TPU v7x, 32 devices: a whole 2x2x4 slice. The times are simulated.
32 devices in a mesh: gy: 8 (over z, x), gx: 4 (over y, core).
Axes of the slice: x: 2, y: 2, z: 4, core: 2. Of those that a mesh axis runs over, the one named last changes fastest.
Arguments:
- ensemble: float32 [64, 64, 512], P(None, 'gy', 'gx'), may hold values from -6 to 6
- flow: float32 [3, 64, 512], P(None, 'gy', 'gx')
- obs_cell: int32 [8, 4, 4], P('gy', 'gx'), may hold values from 0 to 1023
- obs_value: float32 [8, 4, 4], P('gy', 'gx'), may hold values from -6 to 6
- obs_var: float32 [8, 4, 4], P('gy', 'gx'), may hold values from 4 to 16
Outputs:
- analysis: float32 [64, 64, 512], P(None, 'gy', 'gx')
All inputs are finite; a program needn't handle non-finite values.
Results may differ from a plain program's by a relative error of at most 0.0001.
Values sent between devices are 32-bit elements; how exact they have to be, the bound alone decides.
No kernel may reach another device: no remote copies, remote signals or barrier semaphores. Data moves between devices by JAX's collectives and lax.ppermute only.
A program may use at most 64 MiB of HBM per device.

v0:
```python
import jax
import jax.numpy as jnp
from jax import lax
from jax.sharding import PartitionSpec as P


def extended(block, sides, width):
    for axis, dim in sides:
        count = lax.axis_size(axis)
        forward = [(i, i + 1) for i in range(count - 1)]
        backward = [(target, source) for source, target in forward]
        low = lax.ppermute(
            lax.slice_in_dim(block, block.shape[dim] - width, None, axis=dim), axis, forward
        )
        high = lax.ppermute(lax.slice_in_dim(block, 0, width, axis=dim), axis, backward)
        block = jnp.concatenate([low, block, high], axis=dim)
    return block


def advance(padded, coeffs):
    state_grid = padded[:, 1:-1, 1:-1]
    north = padded[:, :-2, 1:-1]
    south = padded[:, 2:, 1:-1]
    west = padded[:, 1:-1, :-2]
    east = padded[:, 1:-1, 2:]
    spread = coeffs[0] * (north + south + west + east - 4.0 * state_grid)
    return state_grid + spread - 0.5 * coeffs[1] * (east - west) - 0.5 * coeffs[2] * (south - north)


def tri_solve(matrix, rhs):
    return lax.linalg.triangular_solve(matrix, rhs, left_side=True, lower=True, transpose_a=True)


def body(ensemble, flow, obs_cell, obs_value, obs_var):
    members = ensemble.shape[0]
    padded, wide_flow = (
        extended(ensemble, (("gy", 1), ("gx", 2)), 2),
        extended(flow, (("gy", 1), ("gx", 2)), 2),
    )
    middle = advance(padded, wide_flow[:, 1:-1, 1:-1])
    predicted_state = advance(middle, flow)
    ensemble_average = jnp.mean(predicted_state, axis=0)
    member_deviation = predicted_state - ensemble_average
    flat_anomaly = member_deviation.reshape(members, -1)
    cells = obs_cell.reshape(-1)
    factor = lax.rsqrt(obs_var.reshape(-1))
    scaled = jnp.take(flat_anomaly, cells, axis=1) * factor
    innovation = (obs_value.reshape(-1) - jnp.take(ensemble_average.reshape(-1), cells)) * factor
    eye = jnp.eye(members, dtype=jnp.float32)
    local_gram = jnp.dot(scaled, scaled.T, precision=lax.Precision.HIGHEST)
    local_target = jnp.dot(scaled, innovation, precision=lax.Precision.HIGHEST)
    gram, target = lax.psum((local_gram, local_target), ("gy", "gx"))
    lower = jnp.linalg.cholesky(gram + (members - 1.0) * eye)
    inverse = tri_solve(lower, eye)
    weights = jnp.dot(
        inverse,
        jnp.dot(inverse.T, target, precision=lax.Precision.HIGHEST),
        precision=lax.Precision.HIGHEST,
    )
    transform = jnp.sqrt(members - 1.0) * inverse + weights[:, None]
    update = jnp.dot(transform.T, flat_anomaly, precision=lax.Precision.HIGHEST)
    return ensemble_average + update.reshape(member_deviation.shape)


def solution(mesh):
    return jax.shard_map(
        body,
        mesh=mesh,
        in_specs=(
            P(None, "gy", "gx"),
            P(None, "gy", "gx"),
            P("gy", "gx", None),
            P("gy", "gx", None),
            P("gy", "gx", None),
        ),
        out_specs=P(None, "gy", "gx"),
        check_vma=False,
    )
```

profile of v0, /device:TPU:0, one launch (start us, length us, event | category | flops | bytes accessed | tf_op | source)
XLA Modules:
  0.0 96.7 jit_solution(7301753496533505068)
XLA Ops:
  0.0 1.1 %fusion.36 = (f32[64,2,128]{2,1,0:T(2,128)S(1)}, f32[64,2,128]{2,1,0:T(2,128)S(1)}) fusion(f32[64,8,128]{2,1,0:T(8,128)} %param.5), kind=kLoop, calls=%fused_computation.74 | loop fusion | bytes 262144 | tf_op jit(solution)/shard_map/slice | solution.py:15
  1.1 4.8 %collective-permute-start = (f32[64,2,128]{2,0,1:T(8,128)S(1)}, f32[64,2,128]{2,0,1:T(8,128)S(1)}, u32[]{:S(2)}, u32[]{:S(2)}) collective-permute-start(f32[64,2,128]{2,0,1:T(8,128)S(1)} %copy.34), channel_id=1, source_target_pairs={{0,4},{4,8},{8,12},{12,16},{16,20},{20,24},{24,28},{1,5},{5,9},{9,... | collective-permute-start | bytes 196616 | tf_op jit(solution)/shard_map/ppermute | solution.py:12
  6.0 1.4 %collective-permute-start.1 = (f32[64,2,128]{2,0,1:T(8,128)S(1)}, f32[64,2,128]{2,0,1:T(8,128)S(1)}, u32[]{:S(2)}, u32[]{:S(2)}) collective-permute-start(f32[64,2,128]{2,0,1:T(8,128)S(1)} %copy.35), channel_id=1, source_target_pairs={{4,0},{8,4},{12,8},{16,12},{20,16},{24,20},{28,24},{5,1},{9,5},{13... | collective-permute-start | bytes 196616 | tf_op jit(solution)/shard_map/ppermute | solution.py:15
  7.5 4.5 %collective-permute-start.4 = (f32[3,2,128]{2,1,0:T(2,128)S(1)}, f32[3,2,128]{2,1,0:T(2,128)S(1)}, u32[]{:S(2)}, u32[]{:S(2)}) collective-permute-start(f32[3,2,128]{2,1,0:T(2,128)S(1)} %get-tuple-element.23), channel_id=1, source_target_pairs={{0,4},{4,8},{8,12},{12,16},{16,20},{20,24},{24,28},{1,5},{5,9},{9,... | collective-permute-start | bytes 9224 | tf_op jit(solution)/shard_map/ppermute | solution.py:12
  12.0 1.3 %collective-permute-start.5 = (f32[3,2,128]{2,1,0:T(2,128)S(1)}, f32[3,2,128]{2,1,0:T(2,128)S(1)}, u32[]{:S(2)}, u32[]{:S(2)}) collective-permute-start(f32[3,2,128]{2,1,0:T(2,128)S(1)} %get-tuple-element.24), channel_id=1, source_target_pairs={{4,0},{8,4},{12,8},{16,12},{20,16},{24,20},{28,24},{5,1},{9,5},{13... | collective-permute-start | bytes 9224 | tf_op jit(solution)/shard_map/ppermute | solution.py:15
  13.4 4.5 %collective-permute-done.5 = f32[3,2,128]{2,1,0:T(2,128)S(1)} collective-permute-done((f32[3,2,128]{2,1,0:T(2,128)S(1)}, f32[3,2,128]{2,1,0:T(2,128)S(1)}, u32[]{:S(2)}, u32[]{:S(2)}) %collective-permute-start.5) | collective-permute-done | bytes 3104 | tf_op jit(solution)/shard_map/ppermute | solution.py:15
  18.0 1.3 %collective-permute-start.6 = (f32[3,12,2]{2,1,0:T(8,128)S(1)}, f32[3,12,2]{2,1,0:T(8,128)S(1)}, u32[]{:S(2)}, u32[]{:S(2)}) collective-permute-start(f32[3,12,2]{2,1,0:T(8,128)S(1)} %get-tuple-element.18), channel_id=1, source_target_pairs={{0,1},{1,2},{2,3},{4,5},{5,6},{6,7},{8,9},{9,10},{10,11},{12,13},{... | collective-permute-start | bytes 872 | tf_op jit(solution)/shard_map/ppermute | solution.py:12
  19.3 1.3 %collective-permute-start.7 = (f32[3,12,2]{2,1,0:T(8,128)S(1)}, f32[3,12,2]{2,1,0:T(8,128)S(1)}, u32[]{:S(2)}, u32[]{:S(2)}) collective-permute-start(f32[3,12,2]{2,1,0:T(8,128)S(1)} %get-tuple-element.19), channel_id=1, source_target_pairs={{1,0},{2,1},{3,2},{5,4},{6,5},{7,6},{9,8},{10,9},{11,10},{13,12},{... | collective-permute-start | bytes 872 | tf_op jit(solution)/shard_map/ppermute | solution.py:15
  20.6 3.5 %collective-permute-done.7 = f32[3,12,2]{2,1,0:T(8,128)S(1)} collective-permute-done((f32[3,12,2]{2,1,0:T(8,128)S(1)}, f32[3,12,2]{2,1,0:T(8,128)S(1)}, u32[]{:S(2)}, u32[]{:S(2)}) %collective-permute-start.7) | collective-permute-done | bytes 320 | tf_op jit(solution)/shard_map/ppermute | solution.py:15
  24.4 0.2 fusion.35
  24.6 4.5 %collective-permute-start.2 = (f32[64,12,2]{2,0,1:T(8,128)S(1)}, f32[64,12,2]{2,0,1:T(8,128)S(1)}, u32[]{:S(2)}, u32[]{:S(2)}) collective-permute-start(f32[64,12,2]{2,0,1:T(8,128)S(1)} %get-tuple-element.9), channel_id=1, source_target_pairs={{0,1},{1,2},{2,3},{4,5},{5,6},{6,7},{8,9},{9,10},{10,11},{12,13},{... | collective-permute-start | bytes 18440 | tf_op jit(solution)/shard_map/ppermute | solution.py:12
  29.1 1.3 %collective-permute-start.3 = (f32[64,12,2]{2,0,1:T(8,128)S(1)}, f32[64,12,2]{2,0,1:T(8,128)S(1)}, u32[]{:S(2)}, u32[]{:S(2)}) collective-permute-start(f32[64,12,2]{2,0,1:T(8,128)S(1)} %get-tuple-element.10), channel_id=1, source_target_pairs={{1,0},{2,1},{3,2},{5,4},{6,5},{7,6},{9,8},{10,9},{11,10},{13,12},{... | collective-permute-start | bytes 18440 | tf_op jit(solution)/shard_map/ppermute | solution.py:15
  30.4 2.2 %collective-permute-done.3 = f32[64,12,2]{2,0,1:T(8,128)S(1)} collective-permute-done((f32[64,12,2]{2,0,1:T(8,128)S(1)}, f32[64,12,2]{2,0,1:T(8,128)S(1)}, u32[]{:S(2)}, u32[]{:S(2)}) %collective-permute-start.3) | collective-permute-done | bytes 6176 | tf_op jit(solution)/shard_map/ppermute | solution.py:15
  32.7 0.4 pad_maximum_fusion
  33.0 0.7 multiply_subtract_fusion
  33.8 0.4 fusion.34
  34.2 0.2 copy.17
  34.4 0.6 gather_fusion
  35.0 0.6 gather_fusion.1
  35.6 0.3 fusion.15
  35.9 0.3 copy-done.4
  36.3 0.2 convolution_bitcast_fusion.2
  36.5 46.1 %all-reduce = (f32[64,64]{1,0:T(8,128)S(1)}, f32[64]{0:T(128)S(1)}) all-reduce(f32[64,64]{1,0:T(8,128)S(1)} %fusion.15, f32[64]{0:T(128)S(1)} %convolution_bitcast_fusion.2), channel_id=1, replica_groups=mesh['gy'=8,'gx'=4] {'gy','gx'}, use_global_device_ids=true, to_apply=%region_1.2 | all-reduce | flops 4160 | bytes 33280 | tf_op jit(solution)/shard_map/psum | solution.py:52
  82.7 5.8 %cholesky.17 = f32[64,64]{1,0:T(8,128)S(1)} custom-call(f32[64,64]{1,0:T(8,128)S(1)} %fusion.7), custom_call_target="Cholesky" | custom-call | tf_op jit(solution)/shard_map/jit(cholesky)/cholesky | solution.py:53
  88.6 0.6 compare_reduce_fusion
  89.3 0.7 fusion.2
  89.9 4.9 %custom-call.6 = f32[1,64,64]{1,2,0:T(8,128)S(1)} custom-call(f32[1,64,64]{2,1,0:T(8,128)S(1)} %fusion.2), custom_call_target="InvertDiagBlocksLowerTriangular" | custom-call | tf_op jit(solution)/shard_map/triangular_solve | solution.py:31
  94.8 0.2 fusion.5
  95.0 0.1 convolution_bitcast_fusion.1
  95.1 0.2 convolution_bitcast_fusion
  95.3 0.5 convolution_add_fusion
  95.8 0.9 copy.21
  (35 shorter events, 0.6 us)
Async XLA Ops:
  1.1 6.4 %copy-start.1 = (f32[3,8,128]{2,1,0:T(8,128)S(1)}, f32[3,8,128]{2,1,0:T(8,128)}, u32[]{:S(2)}) copy-start(f32[3,8,128]{2,1,0:T(8,128)} %param.6) | copy-start | bytes 36868
  1.1 12.2 %copy-start.2 = (s32[1,1,4]{2,1,0:T(1,128)S(1)}, s32[1,1,4]{2,1,0:T(1,128)}, u32[]{:S(2)}) copy-start(s32[1,1,4]{2,1,0:T(1,128)} %param.7) | copy-start | bytes 52
  1.1 12.3 %copy-start.3 = (f32[1,1,4]{2,1,0:T(1,128)S(1)}, f32[1,1,4]{2,1,0:T(1,128)}, u32[]{:S(2)}) copy-start(f32[1,1,4]{2,1,0:T(1,128)} %param.9) | copy-start | bytes 52
  1.1 23.1 %collective-permute-start = (f32[64,2,128]{2,0,1:T(8,128)S(1)}, f32[64,2,128]{2,0,1:T(8,128)S(1)}, u32[]{:S(2)}, u32[]{:S(2)}) collective-permute-start(f32[64,2,128]{2,0,1:T(8,128)S(1)} %copy.34), channel_id=1, source_target_pairs={{0,4},{4,8},{8,12},{12,16},{16,20},{20,24},{24,28},{1,5},{5,9},{9,... | collective-permute-start | bytes 196616 | tf_op jit(solution)/shard_map/ppermute | solution.py:12
  6.0 18.3 %copy-start = (f32[64,8,128]{2,1,0:T(8,128)S(1)}, f32[64,8,128]{2,1,0:T(8,128)}, u32[]{:S(2)}) copy-start(f32[64,8,128]{2,1,0:T(8,128)} %param.5) | copy-start | bytes 786436
  6.0 18.3 %collective-permute-start.1 = (f32[64,2,128]{2,0,1:T(8,128)S(1)}, f32[64,2,128]{2,0,1:T(8,128)S(1)}, u32[]{:S(2)}, u32[]{:S(2)}) collective-permute-start(f32[64,2,128]{2,0,1:T(8,128)S(1)} %copy.35), channel_id=1, source_target_pairs={{4,0},{8,4},{12,8},{16,12},{20,16},{24,20},{28,24},{5,1},{9,5},{13... | collective-permute-start | bytes 196616 | tf_op jit(solution)/shard_map/ppermute | solution.py:15
  7.5 5.9 %collective-permute-start.4 = (f32[3,2,128]{2,1,0:T(2,128)S(1)}, f32[3,2,128]{2,1,0:T(2,128)S(1)}, u32[]{:S(2)}, u32[]{:S(2)}) collective-permute-start(f32[3,2,128]{2,1,0:T(2,128)S(1)} %get-tuple-element.23), channel_id=1, source_target_pairs={{0,4},{4,8},{8,12},{12,16},{16,20},{20,24},{24,28},{1,5},{5,9},{9,... | collective-permute-start | bytes 9224 | tf_op jit(solution)/shard_map/ppermute | solution.py:12
  12.0 5.9 %collective-permute-start.5 = (f32[3,2,128]{2,1,0:T(2,128)S(1)}, f32[3,2,128]{2,1,0:T(2,128)S(1)}, u32[]{:S(2)}, u32[]{:S(2)}) collective-permute-start(f32[3,2,128]{2,1,0:T(2,128)S(1)} %get-tuple-element.24), channel_id=1, source_target_pairs={{4,0},{8,4},{12,8},{16,12},{20,16},{24,20},{28,24},{5,1},{9,5},{13... | collective-permute-start | bytes 9224 | tf_op jit(solution)/shard_map/ppermute | solution.py:15
  18.0 2.6 %collective-permute-start.6 = (f32[3,12,2]{2,1,0:T(8,128)S(1)}, f32[3,12,2]{2,1,0:T(8,128)S(1)}, u32[]{:S(2)}, u32[]{:S(2)}) collective-permute-start(f32[3,12,2]{2,1,0:T(8,128)S(1)} %get-tuple-element.18), channel_id=1, source_target_pairs={{0,1},{1,2},{2,3},{4,5},{5,6},{6,7},{8,9},{9,10},{10,11},{12,13},{... | collective-permute-start | bytes 872 | tf_op jit(solution)/shard_map/ppermute | solution.py:12
  19.3 4.8 %collective-permute-start.7 = (f32[3,12,2]{2,1,0:T(8,128)S(1)}, f32[3,12,2]{2,1,0:T(8,128)S(1)}, u32[]{:S(2)}, u32[]{:S(2)}) collective-permute-start(f32[3,12,2]{2,1,0:T(8,128)S(1)} %get-tuple-element.19), channel_id=1, source_target_pairs={{1,0},{2,1},{3,2},{5,4},{6,5},{7,6},{9,8},{10,9},{11,10},{13,12},{... | collective-permute-start | bytes 872 | tf_op jit(solution)/shard_map/ppermute | solution.py:15
  24.6 5.9 %collective-permute-start.2 = (f32[64,12,2]{2,0,1:T(8,128)S(1)}, f32[64,12,2]{2,0,1:T(8,128)S(1)}, u32[]{:S(2)}, u32[]{:S(2)}) collective-permute-start(f32[64,12,2]{2,0,1:T(8,128)S(1)} %get-tuple-element.9), channel_id=1, source_target_pairs={{0,1},{1,2},{2,3},{4,5},{5,6},{6,7},{8,9},{9,10},{10,11},{12,13},{... | collective-permute-start | bytes 18440 | tf_op jit(solution)/shard_map/ppermute | solution.py:12
  29.1 3.6 %collective-permute-start.3 = (f32[64,12,2]{2,0,1:T(8,128)S(1)}, f32[64,12,2]{2,0,1:T(8,128)S(1)}, u32[]{:S(2)}, u32[]{:S(2)}) collective-permute-start(f32[64,12,2]{2,0,1:T(8,128)S(1)} %get-tuple-element.10), channel_id=1, source_target_pairs={{1,0},{2,1},{3,2},{5,4},{6,5},{7,6},{9,8},{10,9},{11,10},{13,12},{... | collective-permute-start | bytes 18440 | tf_op jit(solution)/shard_map/ppermute | solution.py:15
  35.6 0.7 copy-start.4
where the time goes:
time: 97.1 us; the launch traced here: 96.7 us
  blocking collectives  46.1 us (47%)
  starting transfers between devices  20.5 us (21%)
  other arithmetic  13.8 us (14%)
  waiting for transfers between devices  10.3 us (11%)
  local copies, waits for them, and re-layouts  4.1 us (4%)
  matrix products  1.48 us (2%)
    psum x1, blocking collectives, body(): gram, target = lax.psum((local_gram, local_target), ('gy', 'gx'))  46.1 us
    ppermute x4, starting transfers between devices, extended(): lax.ppermute(lax.slice_in_dim(block, block.shape[dim] - width, None, axis...  15.2 us
    ppermute x4, waiting for transfers between devices, extended(): lax.ppermute(lax.slice_in_dim(block, 0, width, axis=dim), axis, backward)  10.3 us
    another operation x3, other arithmetic, body(): lower = jnp.linalg.cholesky(gram + (members - 1.0) * eye)  6.52 us
    another operation x2, other arithmetic, tri_solve(): lax.linalg.triangular_solve(matrix, rhs, left_side=True, lower=True, tran...  5.55 us
    ppermute x4, starting transfers between devices, extended(): lax.ppermute(lax.slice_in_dim(block, 0, width, axis=dim), axis, backward)  5.3 us
  transfers between devices with their start and end apart: 8, of which 3 were waited for; matrix products, arithmetic and copies ran while one was open for 0% of the time, Pallas kernels for 0%

commit v1 on v0

v1 whole, which is shorter than its diff:
```python
import functools

import jax
import jax.numpy as jnp
from jax import lax
from jax.experimental import pallas as pl
from jax.experimental.pallas import tpu as pltpu
from jax.sharding import PartitionSpec as P

F32 = jnp.float32
HIGHEST = lax.Precision.HIGHEST
PARAMS = pltpu.CompilerParams(vmem_limit_bytes=24 * 1024 * 1024)
VMEM = pl.BlockSpec(memory_space=pltpu.VMEM)
SMEM = pl.BlockSpec(memory_space=pltpu.SMEM)


def lanes(shape):
    return lax.broadcasted_iota(jnp.int32, shape, len(shape) - 1)


def rows_of(shape):
    return lax.broadcasted_iota(jnp.int32, shape, len(shape) - 2)


def shifted(x, amount):
    return pltpu.roll(x, amount % x.shape[-1], x.ndim - 1)


def grid_row(ref, row, members, count):
    return ref[pl.ds(row, members, stride=count), :]


def to_row(column):
    n = column.shape[0]
    wide = jnp.broadcast_to(column, (n, 128))
    return jnp.sum(jnp.where(lanes(wide.shape) == rows_of(wide.shape), wide, 0.0), axis=0, keepdims=True)


def pack_rows(members, count, ens_ref, flow_ref, even_ref, odd_ref):
    is_even = lax.axis_index("gy") % 2 == 0
    top, bottom = [
        (grid_row(ens_ref, a, members, count), grid_row(ens_ref, b, members, count), flow_ref[:, a, :])
        for a, b in ((0, 1), (count - 1, count - 2))
    ]
    for ref, first in ((even_ref, is_even), (odd_ref, jnp.logical_not(is_even))):
        near, second, flow = [jnp.where(first, low, high) for low, high in zip(bottom, top)]
        ref[0:members, :] = near
        ref[members : 2 * members, :] = second
        ref[2 * members : 2 * members + 3, :] = flow
        ref[2 * members + 3 :, :] = jnp.zeros((5, 128), F32)


def halo_rows(even_ref, odd_ref, members):
    is_even = lax.axis_index("gy") % 2 == 0
    parts = []
    for lo, hi in ((0, members), (members, 2 * members), (2 * members, 2 * members + 3)):
        e, o = even_ref[lo:hi, :], odd_ref[lo:hi, :]
        parts.append((jnp.where(is_even, o, e), jnp.where(is_even, e, o)))
    return tuple(p[0] for p in parts), tuple(p[1] for p in parts)


def pack_columns(members, count, ens_ref, flow_ref, row_even_ref, row_odd_ref, even_ref, odd_ref):
    is_even = lax.axis_index("gx") % 2 == 0
    north, south = halo_rows(row_even_ref, row_odd_ref, members)
    field = [north[0]] + [grid_row(ens_ref, r, members, count) for r in range(count)] + [south[0]]
    lane = lanes((members, 128))
    for ref, first in ((even_ref, is_even), (odd_ref, jnp.logical_not(is_even))):
        near_lane = jnp.where(first, 127, 0)
        second_lane = jnp.where(first, 126, 1)
        packed = jnp.zeros((members, 128), F32)
        for i, x in enumerate(field):
            packed = jnp.where(lane == i, pltpu.roll(x, (i + 128 - near_lane) % 128, 1), packed)
            packed = jnp.where(lane == 16 + i, pltpu.roll(x, (16 + i + 128 - second_lane) % 128, 1), packed)
        ref[0:members, :] = packed
        flow_rows = []
        for k in range(3):
            column = jnp.sum(jnp.where(lanes((count, 128)) == near_lane, flow_ref[k], 0.0), axis=1, keepdims=True)
            flow_rows.append(shifted(to_row(column), 1))
        flow_rows.append(jnp.zeros((5, 128), F32))
        ref[members : members + 8, :] = jnp.concatenate(flow_rows, axis=0)


def coefficients(k, u, v):
    return 1.0 - 4.0 * k, k + 0.5 * v, k - 0.5 * v, k + 0.5 * u, k - 0.5 * u


def combine(c, own, north, south, west, east):
    return c[0] * own + c[1] * north + c[2] * south + c[3] * west + c[4] * east


def forecast(
    members, count, n_obs, ens_ref, flow_ref, rows_even_ref, rows_odd_ref, cols_even_ref, cols_odd_ref,
    cell_ref, value_ref, var_ref, out_ref, packet_ref,
):
    north, south = halo_rows(rows_even_ref, rows_odd_ref, members)
    is_even = lax.axis_index("gx") % 2 == 0
    cols_even, cols_odd = cols_even_ref[...], cols_odd_ref[...]
    west = jnp.where(is_even, cols_odd, cols_even)
    east = jnp.where(is_even, cols_even, cols_odd)
    zero = jnp.zeros((members, 128), F32)
    field = [north[1], north[0]] + [grid_row(ens_ref, r, members, count) for r in range(count)] + [south[0], south[1]]
    flows = [[north[2][k : k + 1] for k in range(3)]]
    flows += [[flow_ref[k, r : r + 1, :] for k in range(3)] for r in range(count)]
    flows += [[south[2][k : k + 1] for k in range(3)]]
    coeffs = [coefficients(*f) for f in flows]
    lane = lanes((members, 128))

    def neighbours(x, west_col, east_col, i):
        w = jnp.where(lane == 0, shifted(west_col, -i), shifted(x, 1))
        e = jnp.where(lane == 127, shifted(east_col, 127 - i), shifted(x, -1))
        return w, e

    def own_column(which):
        packed = zero
        for r in range(count):
            packed = jnp.where(lane == r + 1, shifted(field[r + 2], r + 1 - which), packed)
        return packed

    west_x, east_x = west[:members], east[:members]
    middle = []
    for i in range(count + 2):
        x = field[i + 1]
        middle.append(combine(coeffs[i], x, field[i], field[i + 2], *neighbours(x, west_x, east_x, i)))
    side = []
    for block, which in ((west, 0), (east, 127)):
        x = block[:members]
        c = coefficients(*[block[members + k : members + k + 1] for k in range(3)])
        second, own = shifted(x, -16), own_column(which)
        pair = (second, own) if which == 0 else (own, second)
        side.append(combine(c, x, shifted(x, 1), shifted(x, -1), *pair))
    for r in range(count):
        x = middle[r + 1]
        out_ref[r * members : (r + 1) * members, :] = combine(
            coeffs[r + 1], x, middle[r], middle[r + 2], *neighbours(x, side[0], side[1], r + 1)
        )
    sub = rows_of((n_obs, 128))
    at = jnp.zeros((n_obs, 128), F32)
    value = jnp.zeros((n_obs, 128), F32)
    var = jnp.ones((n_obs, 128), F32)
    for j in range(n_obs):
        cell = cell_ref[j]
        row, col = cell // 128, cell % 128
        x = out_ref[pl.ds(pl.multiple_of(row * members, members), members), :]
        column = jnp.sum(jnp.where(lane == col, x, 0.0), axis=1, keepdims=True)
        at = jnp.where(sub == j, to_row(column), at)
        value = jnp.where(sub == j, value_ref[j], value)
        var = jnp.where(sub == j, var_ref[j], var)
    mean = jnp.sum(at, axis=1, keepdims=True) * (1.0 / members)
    obs_lane = lanes((n_obs, 128))
    raw = jnp.where(obs_lane < members, at - mean, jnp.where(obs_lane == members, value - mean, 0.0))
    packet_ref[...] = raw * lax.rsqrt(var)


def analyse(members, count, f_ref, obs_ref, out_ref):
    scaled = obs_ref[...]
    full = lax.dot_general(
        scaled, scaled, (((0,), (0,)), ((), ())), precision=HIGHEST, preferred_element_type=F32
    )
    lane, sub = lanes((members, 128)), rows_of((members, 128))
    a = full[:members, :] + jnp.where(lane == sub, members - 1.0, 0.0)
    for j in range(members):
        row = a[j : j + 1, :]
        column = a[:, j : j + 1]
        below = sub > j
        factor = jnp.where(below, column * (1.0 / row[:, j : j + 1]), 0.0)
        unit = jnp.where(lane[:1] == j, 1.0, row)
        a = jnp.where(below & (lane == j), 0.0, a) - factor * unit
    diagonal = jnp.sum(jnp.where(lane == sub, a, 0.0), axis=1, keepdims=True)
    scale = lax.rsqrt(diagonal)
    inverse = scale * jnp.where(lane < sub, a, jnp.where(lane == sub, 1.0, 0.0))
    reduced = scale * a[:, members : members + 1]
    weights = jnp.sum(reduced * inverse, axis=0, keepdims=True)
    transform = jnp.sqrt(members - 1.0) * inverse + weights
    share = (1.0 - jnp.sum(jnp.where(lane < members, transform, 0.0), axis=1, keepdims=True)) * (1.0 / members)
    transform = (transform + share)[:, :members]
    for r in range(count):
        out_ref[pl.ds(r, members, stride=count), :] = jnp.dot(
            transform, f_ref[r * members : (r + 1) * members, :], precision=HIGHEST, preferred_element_type=F32
        )


def swap(x, axis, offset):
    pairs = [(i, i + 1) for i in range(offset, lax.axis_size(axis) - 1, 2)]
    return lax.ppermute(x, axis, pairs + [(b, a) for a, b in pairs])


def gathered(packet):
    for axis in ("gx", "gy"):
        size = lax.axis_size(axis)
        if size & (size - 1):
            packet = lax.all_gather(packet, axis, tiled=True)
            continue
        step = 1
        while step < size:
            other = lax.ppermute(packet, axis, [(i, i ^ step) for i in range(size)])
            packet = jnp.concatenate([packet, other], axis=0)
            step *= 2
    return packet


def body(ensemble, flow, obs_cell, obs_value, obs_var):
    members, count, width = ensemble.shape
    n_obs = obs_cell.shape[-1]
    ens = ensemble.reshape(members * count, width)
    call = functools.partial(pl.pallas_call, compiler_params=PARAMS)

    def shape(rows):
        return jax.ShapeDtypeStruct((rows, width), F32)

    rows_even, rows_odd = call(
        functools.partial(pack_rows, members, count),
        out_shape=[shape(2 * members + 8)] * 2,
        in_specs=[VMEM] * 2,
        out_specs=[VMEM] * 2,
        name="pack_rows",
    )(ens, flow)
    rows_even, rows_odd = swap(rows_even, "gy", 0), swap(rows_odd, "gy", 1)
    cols_even, cols_odd = call(
        functools.partial(pack_columns, members, count),
        out_shape=[shape(members + 8)] * 2,
        in_specs=[VMEM] * 4,
        out_specs=[VMEM] * 2,
        name="pack_columns",
    )(ens, flow, rows_even, rows_odd)
    cols_even, cols_odd = swap(cols_even, "gx", 0), swap(cols_odd, "gx", 1)
    field, packet = call(
        functools.partial(forecast, members, count, n_obs),
        out_shape=[shape(members * count), shape(n_obs)],
        in_specs=[VMEM] * 6 + [SMEM] * 3,
        out_specs=[VMEM] * 2,
        name="forecast",
    )(ens, flow, rows_even, rows_odd, cols_even, cols_odd, obs_cell.reshape(-1), obs_value.reshape(-1), obs_var.reshape(-1))
    scaled = gathered(packet)
    out = call(
        functools.partial(analyse, members, count),
        out_shape=shape(members * count),
        in_specs=[VMEM] * 2,
        out_specs=VMEM,
        name="analyse",
    )(field, scaled)
    return out.reshape(ensemble.shape)


def solution(mesh):
    return jax.shard_map(
        body,
        mesh=mesh,
        in_specs=(
            P(None, "gy", "gx"),
            P(None, "gy", "gx"),
            P("gy", "gx", None),
            P("gy", "gx", None),
            P("gy", "gx", None),
        ),
        out_specs=P(None, "gy", "gx"),
        check_vma=False,
    )
```

time: 97.1 us -> 44.3 us (0.46)
  blocking collectives: 46.1 us -> 0 us
  other arithmetic: 13.8 us -> 0.02 us
  Pallas kernels: 0 us -> 9.25 us
  starting transfers between devices: 20.5 us -> 22.5 us
  local copies, waits for them, and re-layouts: 4.1 us -> 2.38 us
  matrix products: 1.48 us -> 0 us
    psum x1 -> x0, blocking collectives: 46.1 us -> none  [body(): gram, target = lax.psum((local_gram, local_target), ('gy', 'gx'))]
    another operation x5 -> x0, other arithmetic: 12.1 us -> none  [the longest x3 6.52 us: body(): lower = jnp.linalg.cholesky(gram + (members - 1.0) * eye)]
    pallas_call x0 -> x4, Pallas kernels: none -> 9.25 us  [the longest x1 6.88 us: body(): call(functools.partial(analyse, members, count), out_shape=shape(members...]
    ppermute x8 -> x9, starting transfers between devices: 20.5 us -> 22.5 us  [the longest x5 18.1 us: gathered(): other = lax.ppermute(packet, axis, [(i, i ^ step) for i in range(size)])]
    unnamed x14 -> x10, local copies, waits for them, and re-layouts: 0.43 us -> 2.34 us
    slice x4 -> x0, local copies, waits for them, and re-layouts: 1.34 us -> none  [the longest x1 1.08 us: extended(): lax.slice_in_dim(block, 0, width, axis=dim)]
    dot_general x5 -> x0, matrix products: 1.31 us -> none  [the longest x1 0.51 us: body(): update = jnp.dot(transform.T, flat_anomaly, precision=lax.Precision.HIGHEST)]
    gather x2 -> x0, local copies, waits for them, and re-layouts: 1.19 us -> none  [the longest x1 0.63 us: body(): jnp.take(ensemble_average.reshape(-1), cells)]
  transfers between devices with their start and end apart: 8 -> 9, of which waited for: 3 -> 7; matrix products, arithmetic and copies ran while one was open for 0% -> 0% of each run, Pallas kernels for 0% -> 0%
where the time goes in v1:
time: 44.3 us; the launch traced here: 44.1 us
  starting transfers between devices  22.5 us (51%)
  waiting for transfers between devices  9.93 us (22%)
  Pallas kernels  9.25 us (21%)
  local copies, waits for them, and re-layouts  2.38 us (5%)
    ppermute x5, starting transfers between devices, gathered(): other = lax.ppermute(packet, axis, [(i, i ^ step) for i in range(size)])  18.1 us
    ppermute x5, waiting for transfers between devices, gathered(): other = lax.ppermute(packet, axis, [(i, i ^ step) for i in range(size)])  7.77 us
    pallas_call x1, Pallas kernels, body(): call(functools.partial(analyse, members, count), out_shape=shape(members...  6.88 us
    ppermute x4, starting transfers between devices, swap(): return lax.ppermute(x, axis, pairs + [(b, a) for a, b in pairs])  4.39 us
    unnamed x10, local copies, waits for them, and re-layouts  2.34 us
    ppermute x4, waiting for transfers between devices, swap(): return lax.ppermute(x, axis, pairs + [(b, a) for a, b in pairs])  2.16 us
    pallas_call x1, Pallas kernels, body(): call(functools.partial(forecast, members, count, n_obs), out_shape=[shape...  1.64 us
  transfers between devices with their start and end apart: 9, of which 7 were waited for; matrix products, arithmetic and copies ran while one was open for 0% of the time, Pallas kernels for 0%

profile of v1, /device:TPU:0, one launch (start us, length us, event | category | flops | bytes accessed | tf_op | source)
XLA Modules:
  0.0 44.1 jit_solution(5654743840483788323)
XLA Ops:
  0.0 0.0 copy-start
  0.0 0.9 %copy-done = f32[64,8,128]{2,1,0:T(8,128)S(1)} copy-done((f32[64,8,128]{2,1,0:T(8,128)S(1)}, f32[64,8,128]{2,1,0:T(8,128)}, u32[]{:S(2)}) %copy-start) | copy-done | bytes 262168
  1.0 0.0 copy-start.1
  1.0 0.7 %copy-done.1 = f32[3,8,128]{2,1,0:T(8,128)S(1)} copy-done((f32[3,8,128]{2,1,0:T(8,128)S(1)}, f32[3,8,128]{2,1,0:T(8,128)}, u32[]{:S(2)}) %copy-start.1) | copy-done | bytes 12312
  1.7 3.0 %collective-permute-start = (f32[136,128]{1,0:T(8,128)S(1)}, f32[136,128]{1,0:T(8,128)S(1)}, u32[]{:S(2)}, u32[]{:S(2)}) collective-permute-start(f32[136,128]{1,0:T(8,128)S(1)} %get-tuple-element.11), channel_id=1, source_target_pairs={{0,4},{8,12},{16,20},{24,28},{4,0},{12,8},{20,16},{28,24},{1,5},{9... | collective-permute-start | bytes 208904 | tf_op jit(solution)/shard_map/ppermute | solution.py:184
  4.7 0.7 %collective-permute-start.1 = (f32[136,128]{1,0:T(8,128)S(1)}, f32[136,128]{1,0:T(8,128)S(1)}, u32[]{:S(2)}, u32[]{:S(2)}) collective-permute-start(f32[136,128]{1,0:T(8,128)S(1)} %get-tuple-element.12), channel_id=1, source_target_pairs={{4,8},{12,16},{20,24},{8,4},{16,12},{24,20},{5,9},{13,17},{21,25},... | collective-permute-start | bytes 208904 | tf_op jit(solution)/shard_map/ppermute | solution.py:184
  5.4 1.6 %collective-permute-done.row_even_ref.rows_even_ref = f32[136,128]{1,0:T(8,128)S(1)} collective-permute-done((f32[136,128]{1,0:T(8,128)S(1)}, f32[136,128]{1,0:T(8,128)S(1)}, u32[]{:S(2)}, u32[]{:S(2)}) %collective-permute-start) | collective-permute-done | bytes 69664 | tf_op jit(solution)/shard_map/ppermute | solution.py:184
  7.0 0.0 collective-permute-done.1.row_odd_ref.rows_odd_ref
  7.0 0.7 %pack_columns.1 = (f32[72,128]{1,0:T(8,128)S(1)}, f32[72,128]{1,0:T(8,128)S(1)}) custom-call(f32[512,128]{1,0:T(8,128)S(1)} %bitcast.6, f32[3,8,128]{2,1,0:T(8,128)S(1)} %copy-done.1, f32[136,128]{1,0:T(8,128)S(1)} %collective-permute-done.row_even_ref.rows_even_ref, f32[136,128]{1,0:T(8,128)S(1)} %collective-permute-done.1.row_odd_ref.rows_odd_ref), custom_call_target="tpu_custom_call" | custom-call | tf_op jit(solution)/shard_map/pack_columns/pallas_call | solution.py:218
  7.7 0.1 collective-permute-start.2
  7.8 0.7 %collective-permute-start.3 = (f32[72,128]{1,0:T(8,128)S(1)}, f32[72,128]{1,0:T(8,128)S(1)}, u32[]{:S(2)}, u32[]{:S(2)}) collective-permute-start(f32[72,128]{1,0:T(8,128)S(1)} %get-tuple-element.14), channel_id=1, source_target_pairs={{1,2},{2,1},{5,6},{6,5},{9,10},{10,9},{13,14},{14,13},{17,18},{18,... | collective-permute-start | bytes 110600 | tf_op jit(solution)/shard_map/ppermute | solution.py:184
  8.4 0.5 %collective-permute-done.2.cols_even_ref = f32[72,128]{1,0:T(8,128)S(1)} collective-permute-done((f32[72,128]{1,0:T(8,128)S(1)}, f32[72,128]{1,0:T(8,128)S(1)}, u32[]{:S(2)}, u32[]{:S(2)}) %collective-permute-start.2) | collective-permute-done | bytes 36896 | tf_op jit(solution)/shard_map/ppermute | solution.py:184
  9.0 0.0 collective-permute-done.3.cols_odd_ref
  9.0 0.0 copy-start.2
  9.0 0.0 copy-start.3
  9.0 0.0 copy-start.4
  9.0 0.6 %copy-done.2 = s32[1,1,4]{2,1,0:T(1,128)S(1)} copy-done((s32[1,1,4]{2,1,0:T(1,128)S(1)}, s32[1,1,4]{2,1,0:T(1,128)}, u32[]{:S(2)}) %copy-start.2) | copy-done | bytes 40
  9.6 0.0 copy-done.3
  9.6 0.0 copy-done.4
  9.7 1.6 %forecast.1 = (f32[512,128]{1,0:T(8,128)S(1)}, f32[4,128]{1,0:T(4,128)S(1)}) custom-call(f32[512,128]{1,0:T(8,128)S(1)} %bitcast.7, f32[3,8,128]{2,1,0:T(8,128)S(1)} %copy-done.1, f32[136,128]{1,0:T(8,128)S(1)} %collective-permute-done.row_even_ref.rows_even_ref, f32[136,128]{1,0:T(8,128)S(1)} %collective-permute-done.1.row_odd_ref.rows_odd_ref, ...), custom_call_target="tpu_custom_call" | custom-call | tf_op jit(solution)/shard_map/forecast/pallas_call | solution.py:226
  11.3 4.6 %collective-permute-start.4 = (f32[4,128]{1,0:T(4,128)S(1)}, f32[4,128]{1,0:T(4,128)S(1)}, u32[]{:S(2)}, u32[]{:S(2)}) collective-permute-start(f32[4,128]{1,0:T(4,128)S(1)} %get-tuple-element.16), channel_id=1, source_target_pairs={{0,1},{1,0},{2,3},{3,2},{4,5},{5,4},{6,7},{7,6},{8,9},{9,8},{10,11... | collective-permute-start | bytes 6152 | tf_op jit(solution)/shard_map/ppermute | solution.py:195
  15.9 0.8 %collective-permute-done.4 = f32[4,128]{1,0:T(4,128)S(1)} collective-permute-done((f32[4,128]{1,0:T(4,128)S(1)}, f32[4,128]{1,0:T(4,128)S(1)}, u32[]{:S(2)}, u32[]{:S(2)}) %collective-permute-start.4) | collective-permute-done | bytes 2080 | tf_op jit(solution)/shard_map/ppermute | solution.py:195
  16.7 1.9 %collective-permute-start.5 = (f32[8,128]{1,0:T(8,128)S(1)}, f32[8,128]{1,0:T(8,128)S(1)}, u32[]{:S(2)}, u32[]{:S(2)}) collective-permute-start(f32[8,128]{1,0:T(8,128)S(1)} %pad_maximum_fusion.2), channel_id=1, source_target_pairs={{0,2},{1,3},{2,0},{3,1},{4,6},{5,7},{6,4},{7,5},{8,10},{9,11},{10,... | collective-permute-start | bytes 12296 | tf_op jit(solution)/shard_map/ppermute | solution.py:195
  18.6 1.7 %collective-permute-done.5 = f32[8,128]{1,0:T(8,128)S(1)} collective-permute-done((f32[8,128]{1,0:T(8,128)S(1)}, f32[8,128]{1,0:T(8,128)S(1)}, u32[]{:S(2)}, u32[]{:S(2)}) %collective-permute-start.5) | collective-permute-done | bytes 4128 | tf_op jit(solution)/shard_map/ppermute | solution.py:195
  20.3 5.0 %collective-permute-start.6 = (f32[16,128]{1,0:T(8,128)S(1)}, f32[16,128]{1,0:T(8,128)S(1)}, u32[]{:S(2)}, u32[]{:S(2)}) collective-permute-start(f32[16,128]{1,0:T(8,128)S(1)} %pad_maximum_fusion.1), channel_id=1, source_target_pairs={{0,4},{4,0},{8,12},{12,8},{16,20},{20,16},{24,28},{28,24},{1,5},{5... | collective-permute-start | bytes 24584 | tf_op jit(solution)/shard_map/ppermute | solution.py:195
  25.3 1.6 %collective-permute-done.6 = f32[16,128]{1,0:T(8,128)S(1)} collective-permute-done((f32[16,128]{1,0:T(8,128)S(1)}, f32[16,128]{1,0:T(8,128)S(1)}, u32[]{:S(2)}, u32[]{:S(2)}) %collective-permute-start.6) | collective-permute-done | bytes 8224 | tf_op jit(solution)/shard_map/ppermute | solution.py:195
  26.9 3.5 %collective-permute-start.7 = (f32[32,128]{1,0:T(8,128)S(1)}, f32[32,128]{1,0:T(8,128)S(1)}, u32[]{:S(2)}, u32[]{:S(2)}) collective-permute-start(f32[32,128]{1,0:T(8,128)S(1)} %pad_maximum_fusion), channel_id=1, source_target_pairs={{0,8},{4,12},{8,0},{12,4},{16,24},{20,28},{24,16},{28,20},{1,9},{5... | collective-permute-start | bytes 49160 | tf_op jit(solution)/shard_map/ppermute | solution.py:195
  30.5 1.7 %collective-permute-done.7 = f32[32,128]{1,0:T(8,128)S(1)} collective-permute-done((f32[32,128]{1,0:T(8,128)S(1)}, f32[32,128]{1,0:T(8,128)S(1)}, u32[]{:S(2)}, u32[]{:S(2)}) %collective-permute-start.7) | collective-permute-done | bytes 16416 | tf_op jit(solution)/shard_map/ppermute | solution.py:195
  32.2 3.1 %collective-permute-start.8 = (f32[64,128]{1,0:T(8,128)S(1)}, f32[64,128]{1,0:T(8,128)S(1)}, u32[]{:S(2)}, u32[]{:S(2)}) collective-permute-start(f32[64,128]{1,0:T(8,128)S(1)} %concatenate.22), channel_id=1, source_target_pairs={{0,16},{4,20},{8,24},{12,28},{16,0},{20,4},{24,8},{28,12},{1,17},{... | collective-permute-start | bytes 98312 | tf_op jit(solution)/shard_map/ppermute | solution.py:195
  35.3 1.9 %collective-permute-done.8 = f32[64,128]{1,0:T(8,128)S(1)} collective-permute-done((f32[64,128]{1,0:T(8,128)S(1)}, f32[64,128]{1,0:T(8,128)S(1)}, u32[]{:S(2)}, u32[]{:S(2)}) %collective-permute-start.8) | collective-permute-done | bytes 32800 | tf_op jit(solution)/shard_map/ppermute | solution.py:195
  37.2 6.9 %analyse.1 = f32[512,128]{1,0:T(8,128)} custom-call(f32[512,128]{1,0:T(8,128)S(1)} %get-tuple-element.15.f_ref, f32[128,128]{1,0:T(8,128)S(1)} %concatenate.23.obs_ref), custom_call_target="tpu_custom_call" | custom-call | tf_op jit(solution)/shard_map/analyse/pallas_call | solution.py:234
  (6 shorter events, 0.1 us)
Async XLA Ops:
  0.0 0.9 %copy-start = (f32[64,8,128]{2,1,0:T(8,128)S(1)}, f32[64,8,128]{2,1,0:T(8,128)}, u32[]{:S(2)}) copy-start(f32[64,8,128]{2,1,0:T(8,128)} %param.5) | copy-start | bytes 786436
  1.0 0.7 %copy-start.1 = (f32[3,8,128]{2,1,0:T(8,128)S(1)}, f32[3,8,128]{2,1,0:T(8,128)}, u32[]{:S(2)}) copy-start(f32[3,8,128]{2,1,0:T(8,128)} %flow_ref.5) | copy-start | bytes 36868
  1.7 5.3 %collective-permute-start = (f32[136,128]{1,0:T(8,128)S(1)}, f32[136,128]{1,0:T(8,128)S(1)}, u32[]{:S(2)}, u32[]{:S(2)}) collective-permute-start(f32[136,128]{1,0:T(8,128)S(1)} %get-tuple-element.11), channel_id=1, source_target_pairs={{0,4},{8,12},{16,20},{24,28},{4,0},{12,8},{20,16},{28,24},{1,5},{9... | collective-permute-start | bytes 208904 | tf_op jit(solution)/shard_map/ppermute | solution.py:184
  4.7 2.3 %collective-permute-start.1 = (f32[136,128]{1,0:T(8,128)S(1)}, f32[136,128]{1,0:T(8,128)S(1)}, u32[]{:S(2)}, u32[]{:S(2)}) collective-permute-start(f32[136,128]{1,0:T(8,128)S(1)} %get-tuple-element.12), channel_id=1, source_target_pairs={{4,8},{12,16},{20,24},{8,4},{16,12},{24,20},{5,9},{13,17},{21,25},... | collective-permute-start | bytes 208904 | tf_op jit(solution)/shard_map/ppermute | solution.py:184
  7.7 1.3 %collective-permute-start.2 = (f32[72,128]{1,0:T(8,128)S(1)}, f32[72,128]{1,0:T(8,128)S(1)}, u32[]{:S(2)}, u32[]{:S(2)}) collective-permute-start(f32[72,128]{1,0:T(8,128)S(1)} %get-tuple-element.13), channel_id=1, source_target_pairs={{0,1},{2,3},{1,0},{3,2},{4,5},{6,7},{5,4},{7,6},{8,9},{10,11},{9,8... | collective-permute-start | bytes 110600 | tf_op jit(solution)/shard_map/ppermute | solution.py:184
  7.8 1.2 %collective-permute-start.3 = (f32[72,128]{1,0:T(8,128)S(1)}, f32[72,128]{1,0:T(8,128)S(1)}, u32[]{:S(2)}, u32[]{:S(2)}) collective-permute-start(f32[72,128]{1,0:T(8,128)S(1)} %get-tuple-element.14), channel_id=1, source_target_pairs={{1,2},{2,1},{5,6},{6,5},{9,10},{10,9},{13,14},{14,13},{17,18},{18,... | collective-permute-start | bytes 110600 | tf_op jit(solution)/shard_map/ppermute | solution.py:184
  9.0 0.7 %copy-start.2 = (s32[1,1,4]{2,1,0:T(1,128)S(1)}, s32[1,1,4]{2,1,0:T(1,128)}, u32[]{:S(2)}) copy-start(s32[1,1,4]{2,1,0:T(1,128)} %param.7) | copy-start | bytes 52
  9.0 0.7 %copy-start.3 = (f32[1,1,4]{2,1,0:T(1,128)S(1)}, f32[1,1,4]{2,1,0:T(1,128)}, u32[]{:S(2)}) copy-start(f32[1,1,4]{2,1,0:T(1,128)} %param.8) | copy-start | bytes 52
  9.0 0.7 %copy-start.4 = (f32[1,1,4]{2,1,0:T(1,128)S(1)}, f32[1,1,4]{2,1,0:T(1,128)}, u32[]{:S(2)}) copy-start(f32[1,1,4]{2,1,0:T(1,128)} %param.9) | copy-start | bytes 52
  11.3 5.4 %collective-permute-start.4 = (f32[4,128]{1,0:T(4,128)S(1)}, f32[4,128]{1,0:T(4,128)S(1)}, u32[]{:S(2)}, u32[]{:S(2)}) collective-permute-start(f32[4,128]{1,0:T(4,128)S(1)} %get-tuple-element.16), channel_id=1, source_target_pairs={{0,1},{1,0},{2,3},{3,2},{4,5},{5,4},{6,7},{7,6},{8,9},{9,8},{10,11... | collective-permute-start | bytes 6152 | tf_op jit(solution)/shard_map/ppermute | solution.py:195
  16.7 3.6 %collective-permute-start.5 = (f32[8,128]{1,0:T(8,128)S(1)}, f32[8,128]{1,0:T(8,128)S(1)}, u32[]{:S(2)}, u32[]{:S(2)}) collective-permute-start(f32[8,128]{1,0:T(8,128)S(1)} %pad_maximum_fusion.2), channel_id=1, source_target_pairs={{0,2},{1,3},{2,0},{3,1},{4,6},{5,7},{6,4},{7,5},{8,10},{9,11},{10,... | collective-permute-start | bytes 12296 | tf_op jit(solution)/shard_map/ppermute | solution.py:195
  20.3 6.6 %collective-permute-start.6 = (f32[16,128]{1,0:T(8,128)S(1)}, f32[16,128]{1,0:T(8,128)S(1)}, u32[]{:S(2)}, u32[]{:S(2)}) collective-permute-start(f32[16,128]{1,0:T(8,128)S(1)} %pad_maximum_fusion.1), channel_id=1, source_target_pairs={{0,4},{4,0},{8,12},{12,8},{16,20},{20,16},{24,28},{28,24},{1,5},{5... | collective-permute-start | bytes 24584 | tf_op jit(solution)/shard_map/ppermute | solution.py:195
  26.9 5.2 %collective-permute-start.7 = (f32[32,128]{1,0:T(8,128)S(1)}, f32[32,128]{1,0:T(8,128)S(1)}, u32[]{:S(2)}, u32[]{:S(2)}) collective-permute-start(f32[32,128]{1,0:T(8,128)S(1)} %pad_maximum_fusion), channel_id=1, source_target_pairs={{0,8},{4,12},{8,0},{12,4},{16,24},{20,28},{24,16},{28,20},{1,9},{5... | collective-permute-start | bytes 49160 | tf_op jit(solution)/shard_map/ppermute | solution.py:195
  32.2 5.0 %collective-permute-start.8 = (f32[64,128]{1,0:T(8,128)S(1)}, f32[64,128]{1,0:T(8,128)S(1)}, u32[]{:S(2)}, u32[]{:S(2)}) collective-permute-start(f32[64,128]{1,0:T(8,128)S(1)} %concatenate.22), channel_id=1, source_target_pairs={{0,16},{4,20},{8,24},{12,28},{16,0},{20,4},{24,8},{28,12},{1,17},{... | collective-permute-start | bytes 98312 | tf_op jit(solution)/shard_map/ppermute | solution.py:195

commit v2 on v0

v2 whole, which is shorter than its diff:
```python
import functools

import jax
import jax.numpy as jnp
from jax import lax
from jax.experimental import pallas as pl
from jax.experimental.pallas import tpu as pltpu
from jax.sharding import PartitionSpec as P

F32 = jnp.float32
HIGHEST = lax.Precision.HIGHEST
PARAMS = pltpu.CompilerParams(vmem_limit_bytes=24 * 1024 * 1024)
VMEM = pl.BlockSpec(memory_space=pltpu.VMEM)
SMEM = pl.BlockSpec(memory_space=pltpu.SMEM)


def lanes(shape):
    return lax.broadcasted_iota(jnp.int32, shape, len(shape) - 1)


def rows_of(shape):
    return lax.broadcasted_iota(jnp.int32, shape, len(shape) - 2)


def shifted(x, amount):
    return pltpu.roll(x, amount % x.shape[-1], x.ndim - 1)


EDGE = 16
BLOCK = 4 * EDGE + 8
LEFT, RIGHT, LEFT_MID, RIGHT_MID, OBS = 0, EDGE, 2 * EDGE, 3 * EDGE, 4 * EDGE
ANY = pl.BlockSpec(memory_space=pl.ANY)


def coefficients(k, u, v):
    return 1.0 - 4.0 * k, k + 0.5 * v, k - 0.5 * v, k + 0.5 * u, k - 0.5 * u


def combine(c, own, north, south, west, east):
    return c[0] * own + c[1] * north + c[2] * south + c[3] * west + c[4] * east


def transposed(x):
    return jnp.concatenate([x, jnp.zeros((128 - x.shape[0], 128), F32)], axis=0).T


def load(
    members, count, n_obs, ens_hbm, flow_hbm, cell_hbm, value_hbm, var_hbm,
    field_ref, flow_ref, obs_ref, even_ref, odd_ref, cell_ref, value_ref, var_ref, sems,
):
    order = [0, count - 1, 1, count - 2] + list(range(2, count - 2))
    copies = [pltpu.make_async_copy(flow_hbm, flow_ref, sems.at[count])]
    copies += [
        pltpu.make_async_copy(ens_hbm.at[:, r, :], field_ref.at[pl.ds(r * members, members), :], sems.at[r]) for r in order
    ]
    small = [
        pltpu.make_async_copy(src, dst, sems.at[count + 1 + i])
        for i, (src, dst) in enumerate(((cell_hbm, cell_ref), (value_hbm, value_ref), (var_hbm, var_ref)))
    ]
    for copy in copies + small:
        copy.start()
    for copy in copies + small:
        copy.wait()
    is_even = lax.axis_index("gy") % 2 == 0

    def grid_row(r):
        return field_ref[r * members : (r + 1) * members, :]

    top, bottom = [(grid_row(a), grid_row(b), flow_ref[:, a, :]) for a, b in ((0, 1), (count - 1, count - 2))]
    for ref, first in ((even_ref, is_even), (odd_ref, jnp.logical_not(is_even))):
        near, second, flow = [jnp.where(first, low, high) for low, high in zip(bottom, top)]
        ref[0:members, :] = near
        ref[members : 2 * members, :] = second
        ref[2 * members : 2 * members + 3, :] = flow
        ref[2 * members + 3 :, :] = jnp.zeros((5, 128), F32)
    sub = rows_of((8, 128))
    for i, (ref, rest) in enumerate(((cell_ref, 0.0), (value_ref, 0.0), (var_ref, 1.0))):
        block = jnp.full((8, 128), rest, F32)
        for j in range(n_obs):
            block = jnp.where(sub == j, ref[j].astype(F32), block)
        obs_ref[8 * i : 8 * i + 8, :] = block


def halo_rows(even_ref, odd_ref, members):
    is_even = lax.axis_index("gy") % 2 == 0
    parts = []
    for lo, hi in ((0, members), (members, 2 * members), (2 * members, 2 * members + 3)):
        e, o = even_ref[lo:hi, :], odd_ref[lo:hi, :]
        parts.append((jnp.where(is_even, o, e), jnp.where(is_even, e, o)))
    return tuple(p[0] for p in parts), tuple(p[1] for p in parts)


def tall_coefficients(scratch, flow_ref, north_flow, south_flow, count):
    for k in range(3):
        scratch[k] = jnp.zeros((EDGE, 128), F32)
        scratch[k, 1:2, :] = north_flow[k : k + 1]
        scratch[k, 2 : 2 + count, :] = flow_ref[k]
        scratch[k, 2 + count : 3 + count, :] = south_flow[k : k + 1]
    return coefficients(*[scratch[k] for k in range(3)])


def observe(members, count, n_obs, field_ref, flow_ref, obs_ref, even_ref, odd_ref, out_ref, tall_ref):
    north, south = halo_rows(even_ref, odd_ref, members)
    field = [north[1], north[0]]
    field += [field_ref[r * members : (r + 1) * members, :] for r in range(count)] + [south[0], south[1]]
    coeffs = tall_coefficients(tall_ref, flow_ref, north[2], south[2], count)
    lane, sub = lanes((EDGE, 128)), rows_of((EDGE, 128))
    wide = lanes((members, 128))
    own, up, down, left, right = coeffs
    has_west = lax.axis_index("gx") > 0
    has_east = lax.axis_index("gx") < lax.axis_size("gx") - 1
    zero = jnp.zeros((EDGE, 128), F32)

    def spread(w):
        to_west, to_east = left * w, right * w
        inside = (
            own * w
            + pltpu.roll(up * w, EDGE - 1, 0)
            + pltpu.roll(down * w, 1, 0)
            + jnp.where(lane == 127, 0.0, shifted(to_west, -1))
            + jnp.where(lane == 0, 0.0, shifted(to_east, 1))
        )
        return inside, jnp.where(has_west, to_west[:, 0:1], 0.0), jnp.where(has_east, to_east[:, 127:128], 0.0)

    packed = jnp.zeros((members, 128), F32)
    second = jnp.zeros((members, 128), F32)
    for i in range(1, count + 3):
        x = field[i]
        packed = jnp.where(wide == i, shifted(x, i), packed)
        packed = jnp.where(wide == EDGE + i, shifted(x, EDGE + i - 127), packed)
        if 2 <= i < count + 2:
            second = jnp.where(wide == i, shifted(x, i - 1), second)
            second = jnp.where(wide == EDGE + i, shifted(x, EDGE + i - 126), second)

    def edge_row(low, high):
        both = jnp.where(lane == sub, low[:, 0:1], jnp.where(lane == sub + EDGE, high[:, 127:128], 0.0))
        return jnp.sum(both, axis=0, keepdims=True)

    middle = (
        edge_row(own, own) * packed
        + edge_row(up, up) * shifted(packed, 1)
        + edge_row(down, down) * shifted(packed, -1)
        + edge_row(right, left) * second
    )
    packed = jnp.where(wide < 2 * EDGE, packed, jnp.where(wide < 4 * EDGE, shifted(middle, 2 * EDGE), 0.0))
    meta = jnp.where(lane == 80, left[:, 0:1], jnp.where(lane == 81, right[:, 127:128], zero))
    position = ((sub - 2) * 128 + lane).astype(F32)
    inner = (sub >= 2) & (sub < 2 + count)
    for j in range(n_obs):
        here = jnp.where(inner & (position == obs_ref[j : j + 1, :]), 1.0, 0.0)
        w, mid_west, mid_east = spread(here)
        w, west, east = spread(w)
        total = w[0:1, :] * field[0]
        for i in range(1, count + 4):
            total = total + w[i : i + 1, :] * field[i]
        packed = jnp.where(wide == OBS + j, jnp.sum(total, axis=1, keepdims=True), packed)
        for at, column in ((64, west), (68, east), (72, mid_west), (76, mid_east)):
            meta = jnp.where(lane == at + j, column, meta)
    turned = transposed(packed)
    out_ref[0:EDGE, :] = turned[0:EDGE, :] + meta
    out_ref[EDGE:OBS, :] = turned[EDGE:OBS, :]
    top_lane = lanes((8, 128))
    value, factor = obs_ref[8:16, :], lax.rsqrt(obs_ref[16:24, :])
    out_ref[OBS : OBS + 8, :] = jnp.where(
        top_lane == 64, value, jnp.where(top_lane == 65, factor, turned[OBS : OBS + 8, :])
    )


def place(tile, size):
    return tile if size & (size - 1) else jnp.bitwise_xor(lax.axis_index("gx"), tile)


def block_rows(ref, start, tile, size, rows=EDGE):
    return ref[pl.ds(pl.multiple_of(place(tile, size) * BLOCK + start, 8), rows), :]


def side_columns(ref, tile, size):
    west, east = jnp.maximum(tile - 1, 0), jnp.minimum(tile + 1, size - 1)
    west_meta, east_meta = block_rows(ref, 0, west, size), block_rows(ref, 0, east, size)
    west_mid = block_rows(ref, RIGHT_MID, west, size) + west_meta[:, 81:82] * block_rows(ref, LEFT, tile, size)
    east_mid = block_rows(ref, LEFT_MID, east, size) + east_meta[:, 80:81] * block_rows(ref, RIGHT, tile, size)
    return block_rows(ref, RIGHT, west, size), west_mid, block_rows(ref, LEFT, east, size), east_mid


def complete(members, n_obs, size, blocks_ref, out_ref):
    lane = lanes((n_obs, 128))
    for tile in range(size):
        west, west_mid, east, east_mid = side_columns(blocks_ref, jnp.int32(tile), size)
        meta = block_rows(blocks_ref, 0, jnp.int32(tile), size)
        block = block_rows(blocks_ref, OBS, jnp.int32(tile), size, 8)[:n_obs]
        added = []
        for j in range(n_obs):
            terms = (
                meta[:, 64 + j : 65 + j] * west
                + meta[:, 68 + j : 69 + j] * east
                + meta[:, 72 + j : 73 + j] * west_mid
                + meta[:, 76 + j : 77 + j] * east_mid
            )
            added.append(jnp.sum(terms, axis=0, keepdims=True))
        at = jnp.where(lane < members, block + jnp.concatenate(added, axis=0), 0.0)
        mean = jnp.sum(at, axis=1, keepdims=True) * (1.0 / members)
        raw = jnp.where(lane < members, at - mean, jnp.where(lane == members, block[:, 64:65] - mean, 0.0))
        out_ref[n_obs * tile : n_obs * (tile + 1), :] = raw * block[:, 65:66]


def forecast(members, count, size, field_ref, flow_ref, even_ref, odd_ref, blocks_ref, out_ref, tall_ref):
    north, south = halo_rows(even_ref, odd_ref, members)
    tile = lax.axis_index("gx")
    west, west_mid, east, east_mid = side_columns(blocks_ref, tile, size)
    sides = jnp.concatenate(
        [jnp.where(tile > 0, x, 0.0) for x in (west, west_mid)]
        + [jnp.where(tile < size - 1, x, 0.0) for x in (east, east_mid)],
        axis=0,
    )
    sides = transposed(sides)[:members]
    field = [north[1], north[0]]
    field += [field_ref[r * members : (r + 1) * members, :] for r in range(count)] + [south[0], south[1]]
    tall = tall_coefficients(tall_ref, flow_ref, north[2], south[2], count)
    lane = lanes((members, 128))

    def step(rows, i, start):
        w = jnp.where(lane == 0, shifted(sides, -(start + i)), shifted(rows[i], 1))
        e = jnp.where(lane == 127, shifted(sides, 127 - (start + 2 * EDGE + i)), shifted(rows[i], -1))
        return combine([c[i : i + 1, :] for c in tall], rows[i], rows[i - 1], rows[i + 1], w, e)

    middle = {i: step(field, i, 0) for i in range(1, count + 3)}
    for r in range(count):
        out_ref[r * members : (r + 1) * members, :] = step(middle, r + 2, EDGE)


def analyse(members, count, f_ref, obs_ref, out_ref):
    scaled = obs_ref[...]
    full = lax.dot_general(
        scaled, scaled, (((0,), (0,)), ((), ())), precision=HIGHEST, preferred_element_type=F32
    )
    lane, sub = lanes((members, 128)), rows_of((members, 128))
    a = full[:members, :] + jnp.where(lane == sub, members - 1.0, 0.0)
    for j in range(members):
        row = a[j : j + 1, :]
        column = a[:, j : j + 1]
        below = sub > j
        factor = jnp.where(below, column * (1.0 / row[:, j : j + 1]), 0.0)
        unit = jnp.where(lane[:1] == j, 1.0, row)
        a = jnp.where(below & (lane == j), 0.0, a) - factor * unit
    diagonal = jnp.sum(jnp.where(lane == sub, a, 0.0), axis=1, keepdims=True)
    scale = lax.rsqrt(diagonal)
    inverse = scale * jnp.where(lane < sub, a, jnp.where(lane == sub, 1.0, 0.0))
    reduced = scale * a[:, members : members + 1]
    weights = jnp.sum(reduced * inverse, axis=0, keepdims=True)
    transform = jnp.sqrt(members - 1.0) * inverse + weights
    share = (1.0 - jnp.sum(jnp.where(lane < members, transform, 0.0), axis=1, keepdims=True)) * (1.0 / members)
    transform = (transform + share)[:, :members]
    for r in range(count):
        out_ref[pl.ds(r, members, stride=count), :] = jnp.dot(
            transform, f_ref[r * members : (r + 1) * members, :], precision=HIGHEST, preferred_element_type=F32
        )


def swap(x, axis, offset):
    pairs = [(i, i + 1) for i in range(offset, lax.axis_size(axis) - 1, 2)]
    return lax.ppermute(x, axis, pairs + [(b, a) for a, b in pairs])


def gathered(x, axis):
    size = lax.axis_size(axis)
    if size & (size - 1):
        return lax.all_gather(x, axis, tiled=True)
    step = 1
    while step < size:
        other = lax.ppermute(x, axis, [(i, i ^ step) for i in range(size)])
        x = jnp.concatenate([x, other], axis=0)
        step *= 2
    return x


def body(ensemble, flow, obs_cell, obs_value, obs_var):
    members, count, width = ensemble.shape
    n_obs = obs_cell.shape[-1]
    size = lax.axis_size("gx")
    call = functools.partial(pl.pallas_call, compiler_params=PARAMS)

    def shape(*dims):
        return jax.ShapeDtypeStruct(dims + (width,), F32)

    field, tile_flow, obs, rows_even, rows_odd = call(
        functools.partial(load, members, count, n_obs),
        out_shape=[shape(members * count), shape(3, count), shape(24)] + [shape(2 * members + 8)] * 2,
        in_specs=[ANY] * 5,
        out_specs=[VMEM] * 5,
        scratch_shapes=[pltpu.SMEM((n_obs,), jnp.int32)]
        + [pltpu.SMEM((n_obs,), F32)] * 2
        + [pltpu.SemaphoreType.DMA((count + 4,))],
        name="load",
    )(ensemble, flow, obs_cell.reshape(-1), obs_value.reshape(-1), obs_var.reshape(-1))
    rows_odd = swap(rows_odd, "gy", 1)
    rows_even = swap(rows_even, "gy", 0)
    tall = pltpu.VMEM((3, EDGE, width), F32)
    block = call(
        functools.partial(observe, members, count, n_obs),
        out_shape=shape(BLOCK),
        in_specs=[VMEM] * 5,
        out_specs=VMEM,
        scratch_shapes=[tall],
        name="observe",
    )(field, tile_flow, obs, rows_even, rows_odd)
    blocks = gathered(block, "gx")
    packet = call(
        functools.partial(complete, members, n_obs, size),
        out_shape=shape(n_obs * size),
        in_specs=[VMEM],
        out_specs=VMEM,
        name="complete",
    )(blocks)
    predicted = call(
        functools.partial(forecast, members, count, size),
        out_shape=shape(members * count),
        in_specs=[VMEM] * 5,
        out_specs=VMEM,
        scratch_shapes=[tall],
        cost_estimate=pl.CostEstimate(flops=4 * 10**6, bytes_accessed=6 * 10**5, transcendentals=0),
        name="forecast",
    )(field, tile_flow, rows_even, rows_odd, blocks)
    scaled = gathered(packet, "gy")
    out = call(
        functools.partial(analyse, members, count),
        out_shape=shape(members * count),
        in_specs=[VMEM] * 2,
        out_specs=VMEM,
        name="analyse",
    )(predicted, scaled)
    return out.reshape(ensemble.shape)


def solution(mesh):
    return jax.shard_map(
        body,
        mesh=mesh,
        in_specs=(
            P(None, "gy", "gx"),
            P(None, "gy", "gx"),
            P("gy", "gx", None),
            P("gy", "gx", None),
            P("gy", "gx", None),
        ),
        out_specs=P(None, "gy", "gx"),
        check_vma=False,
    )
```

time: 97.1 us -> 39.8 us (0.41)
  blocking collectives: 46.1 us -> 0 us
  other arithmetic: 13.8 us -> 0.03 us
  Pallas kernels: 0 us -> 10.3 us
  starting transfers between devices: 20.5 us -> 16.9 us
  local copies, waits for them, and re-layouts: 4.1 us -> 2.34 us
  matrix products: 1.48 us -> 0 us
    psum x1 -> x0, blocking collectives: 46.1 us -> none  [body(): gram, target = lax.psum((local_gram, local_target), ('gy', 'gx'))]
    another operation x5 -> x0, other arithmetic: 12.1 us -> none  [the longest x3 6.52 us: body(): lower = jnp.linalg.cholesky(gram + (members - 1.0) * eye)]
    pallas_call x0 -> x5, Pallas kernels: none -> 10.3 us  [the longest x1 6.88 us: body(): call(functools.partial(analyse, members, count), out_shape=shape(members...]
    ppermute x8 -> x7, starting transfers between devices: 20.5 us -> 16.9 us  [the longest x5 13.3 us: gathered(): other = lax.ppermute(x, axis, [(i, i ^ step) for i in range(size)])]
    unnamed x14 -> x10, local copies, waits for them, and re-layouts: 0.43 us -> 2.34 us
    slice x4 -> x0, local copies, waits for them, and re-layouts: 1.34 us -> none  [the longest x1 1.08 us: extended(): lax.slice_in_dim(block, 0, width, axis=dim)]
    dot_general x5 -> x0, matrix products: 1.31 us -> none  [the longest x1 0.51 us: body(): update = jnp.dot(transform.T, flat_anomaly, precision=lax.Precision.HIGHEST)]
    gather x2 -> x0, local copies, waits for them, and re-layouts: 1.19 us -> none  [the longest x1 0.63 us: body(): jnp.take(ensemble_average.reshape(-1), cells)]
  transfers between devices with their start and end apart: 8 -> 7, of which waited for: 3 -> 6; matrix products, arithmetic and copies ran while one was open for 0% -> 0% of each run, Pallas kernels for 0% -> 2%
where the time goes in v2:
time: 39.8 us; the launch traced here: 39.5 us
  starting transfers between devices  16.9 us (42%)
  Pallas kernels  10.3 us (26%)
  waiting for transfers between devices  9.86 us (25%)
  local copies, waits for them, and re-layouts  2.34 us (6%)
    ppermute x5, starting transfers between devices, gathered(): other = lax.ppermute(x, axis, [(i, i ^ step) for i in range(size)])  13.3 us
    ppermute x5, waiting for transfers between devices, gathered(): other = lax.ppermute(x, axis, [(i, i ^ step) for i in range(size)])  8.23 us
    pallas_call x1, Pallas kernels, body(): call(functools.partial(analyse, members, count), out_shape=shape(members...  6.88 us
    ppermute x2, starting transfers between devices, swap(): return lax.ppermute(x, axis, pairs + [(b, a) for a, b in pairs])  3.66 us
    unnamed x10, local copies, waits for them, and re-layouts  2.34 us
    ppermute x2, waiting for transfers between devices, swap(): return lax.ppermute(x, axis, pairs + [(b, a) for a, b in pairs])  1.63 us
    pallas_call x1, Pallas kernels, body(): call(functools.partial(observe, members, count, n_obs), out_shape=shape(B...  1.16 us
    pallas_call x1, Pallas kernels, body(): call(functools.partial(load, members, count, n_obs), out_shape=[shape(mem...  0.88 us
  transfers between devices with their start and end apart: 7, of which 6 were waited for; matrix products, arithmetic and copies ran while one was open for 0% of the time, Pallas kernels for 2%

profile of v2, /device:TPU:0, one launch (start us, length us, event | category | flops | bytes accessed | tf_op | source)
XLA Modules:
  0.0 39.5 jit_solution(6961287624814945140)
XLA Ops:
  0.0 0.0 copy-start.2
  0.0 0.0 copy-start.3
  0.0 0.0 copy-start.4
  0.0 0.6 %copy-done.2 = s32[1,1,4]{2,1,0:T(1,128)S(1)} copy-done((s32[1,1,4]{2,1,0:T(1,128)S(1)}, s32[1,1,4]{2,1,0:T(1,128)}, u32[]{:S(2)}) %copy-start.2) | copy-done | bytes 40
  0.7 0.0 copy-done.3
  0.7 0.0 copy-done.4
  0.7 0.0 copy-start
  0.7 0.9 %copy-done = f32[64,8,128]{2,1,0:T(8,128)S(1)} copy-done((f32[64,8,128]{2,1,0:T(8,128)S(1)}, f32[64,8,128]{2,1,0:T(8,128)}, u32[]{:S(2)}) %copy-start) | copy-done | bytes 262168
  1.6 0.0 copy-start.1
  1.6 0.7 %copy-done.1 = f32[3,8,128]{2,1,0:T(8,128)S(1)} copy-done((f32[3,8,128]{2,1,0:T(8,128)S(1)}, f32[3,8,128]{2,1,0:T(8,128)}, u32[]{:S(2)}) %copy-start.1) | copy-done | bytes 12312
  2.3 0.9 %load.1 = (f32[512,128]{1,0:T(8,128)S(1)}, f32[3,8,128]{2,1,0:T(8,128)S(1)}, f32[24,128]{1,0:T(8,128)S(1)}, f32[136,128]{1,0:T(8,128)S(1)}, f32[136,128]{1,0:T(8,128)S(1)}) custom-call(f32[64,8,128]{2,1,0:T(8,128)S(1)} %copy-done, f32[3,8,128]{2,1,0:T(8,128)S(1)} %copy-done.1, s32[4]{0:T(128)S(1)} %bitcast.4, f32[4]{0:T(128)S(1)} %bitcast.5, f32[4]{0:T(128)S(1)} %bitcast.6), custom_call_target="tpu_custom_call" | custom-call | tf_op jit(solution)/shard_map/load/pallas_call | solution.py:285
  3.2 3.0 %collective-permute-start = (f32[136,128]{1,0:T(8,128)S(1)}, f32[136,128]{1,0:T(8,128)S(1)}, u32[]{:S(2)}, u32[]{:S(2)}) collective-permute-start(f32[136,128]{1,0:T(8,128)S(1)} %get-tuple-element.12), channel_id=1, source_target_pairs={{0,4},{8,12},{16,20},{24,28},{4,0},{12,8},{20,16},{28,24},{1,5},{9... | collective-permute-start | bytes 208904 | tf_op jit(solution)/shard_map/ppermute | solution.py:261
  6.2 0.7 %collective-permute-start.1 = (f32[136,128]{1,0:T(8,128)S(1)}, f32[136,128]{1,0:T(8,128)S(1)}, u32[]{:S(2)}, u32[]{:S(2)}) collective-permute-start(f32[136,128]{1,0:T(8,128)S(1)} %get-tuple-element.13), channel_id=1, source_target_pairs={{4,8},{12,16},{20,24},{8,4},{16,12},{24,20},{5,9},{13,17},{21,25},... | collective-permute-start | bytes 208904 | tf_op jit(solution)/shard_map/ppermute | solution.py:261
  6.9 1.6 %collective-permute-done.even_ref = f32[136,128]{1,0:T(8,128)S(1)} collective-permute-done((f32[136,128]{1,0:T(8,128)S(1)}, f32[136,128]{1,0:T(8,128)S(1)}, u32[]{:S(2)}, u32[]{:S(2)}) %collective-permute-start) | collective-permute-done | bytes 69664 | tf_op jit(solution)/shard_map/ppermute | solution.py:261
  8.5 0.0 collective-permute-done.1.odd_ref
  8.5 1.2 %observe.1 = f32[72,128]{1,0:T(8,128)S(1)} custom-call(f32[512,128]{1,0:T(8,128)S(1)} %get-tuple-element.10.field_ref, f32[3,8,128]{2,1,0:T(8,128)S(1)} %get-tuple-element.11.flow_ref, f32[24,128]{1,0:T(8,128)S(1)} %get-tuple-element.14.obs_ref, f32[136,128]{1,0:T(8,128)S(1)} %collective-permute-done.even_ref, f32[136,128]{1,0:T(8,128)S(1)} %collective-permute-done.1.odd_ref), custom_call_target="tpu_custom_call" | custom-call | tf_op jit(solution)/shard_map/observe/pallas_call | solution.py:298
  9.7 0.1 collective-permute-start.2
  9.8 1.2 %collective-permute-done.2 = f32[72,128]{1,0:T(8,128)S(1)} collective-permute-done((f32[72,128]{1,0:T(8,128)S(1)}, f32[72,128]{1,0:T(8,128)S(1)}, u32[]{:S(2)}, u32[]{:S(2)}) %collective-permute-start.2) | collective-permute-done | bytes 36896 | tf_op jit(solution)/shard_map/ppermute | solution.py:270
  11.0 2.0 %collective-permute-start.3 = (f32[144,128]{1,0:T(8,128)S(1)}, f32[144,128]{1,0:T(8,128)S(1)}, u32[]{:S(2)}, u32[]{:S(2)}) collective-permute-start(f32[144,128]{1,0:T(8,128)S(1)} %pad_maximum_fusion.1), channel_id=1, source_target_pairs={{0,2},{1,3},{2,0},{3,1},{4,6},{5,7},{6,4},{7,5},{8,10},{9,11},{10,... | collective-permute-start | bytes 221192 | tf_op jit(solution)/shard_map/ppermute | solution.py:270
  13.0 2.6 %collective-permute-done.3 = f32[144,128]{1,0:T(8,128)S(1)} collective-permute-done((f32[144,128]{1,0:T(8,128)S(1)}, f32[144,128]{1,0:T(8,128)S(1)}, u32[]{:S(2)}, u32[]{:S(2)}) %collective-permute-start.3) | collective-permute-done | bytes 73760 | tf_op jit(solution)/shard_map/ppermute | solution.py:270
  15.6 0.6 %complete.1 = f32[16,128]{1,0:T(8,128)S(1)} custom-call(f32[288,128]{1,0:T(8,128)S(1)} %pad_maximum_fusion.blocks_ref), custom_call_target="tpu_custom_call" | custom-call | tf_op jit(solution)/shard_map/complete/pallas_call | solution.py:307
  16.3 4.8 %collective-permute-start.4 = (f32[16,128]{1,0:T(8,128)S(1)}, f32[16,128]{1,0:T(8,128)S(1)}, u32[]{:S(2)}, u32[]{:S(2)}) collective-permute-start(f32[16,128]{1,0:T(8,128)S(1)} %complete.1), channel_id=1, source_target_pairs={{0,4},{4,0},{8,12},{12,8},{16,20},{20,16},{24,28},{28,24},{1,5},{5... | collective-permute-start | bytes 24584 | tf_op jit(solution)/shard_map/ppermute | solution.py:270
  21.1 1.6 %collective-permute-done.4 = f32[16,128]{1,0:T(8,128)S(1)} collective-permute-done((f32[16,128]{1,0:T(8,128)S(1)}, f32[16,128]{1,0:T(8,128)S(1)}, u32[]{:S(2)}, u32[]{:S(2)}) %collective-permute-start.4) | collective-permute-done | bytes 8224 | tf_op jit(solution)/shard_map/ppermute | solution.py:270
  22.7 3.3 %collective-permute-start.5 = (f32[32,128]{1,0:T(8,128)S(1)}, f32[32,128]{1,0:T(8,128)S(1)}, u32[]{:S(2)}, u32[]{:S(2)}) collective-permute-start(f32[32,128]{1,0:T(8,128)S(1)} %pad_maximum_fusion.4), channel_id=1, source_target_pairs={{0,8},{4,12},{8,0},{12,4},{16,24},{20,28},{24,16},{28,20},{1,9},{5... | collective-permute-start | bytes 49160 | tf_op jit(solution)/shard_map/ppermute | solution.py:270
  26.0 1.7 %collective-permute-done.5 = f32[32,128]{1,0:T(8,128)S(1)} collective-permute-done((f32[32,128]{1,0:T(8,128)S(1)}, f32[32,128]{1,0:T(8,128)S(1)}, u32[]{:S(2)}, u32[]{:S(2)}) %collective-permute-start.5) | collective-permute-done | bytes 16416 | tf_op jit(solution)/shard_map/ppermute | solution.py:270
  27.7 3.0 %collective-permute-start.6 = (f32[64,128]{1,0:T(8,128)S(1)}, f32[64,128]{1,0:T(8,128)S(1)}, u32[]{:S(2)}, u32[]{:S(2)}) collective-permute-start(f32[64,128]{1,0:T(8,128)S(1)} %pad_maximum_fusion.3), channel_id=1, source_target_pairs={{0,16},{4,20},{8,24},{12,28},{16,0},{20,4},{24,8},{28,12},{1,17},{... | collective-permute-start | bytes 98312 | tf_op jit(solution)/shard_map/ppermute | solution.py:270
  30.8 0.8 %forecast.1.f_ref = f32[512,128]{1,0:T(8,128)S(1)} custom-call(f32[512,128]{1,0:T(8,128)S(1)} %get-tuple-element.10.field_ref, f32[3,8,128]{2,1,0:T(8,128)S(1)} %get-tuple-element.11.flow_ref, f32[136,128]{1,0:T(8,128)S(1)} %collective-permute-done.even_ref, f32[136,128]{1,0:T(8,128)S(1)} %collective-permute-done.1.odd_ref, ...), custom_call_target="tpu_custom_call" | custom-call | flops 4000000 | bytes 600000 | tf_op jit(solution)/shard_map/forecast/pallas_call | solution.py:314
  31.6 1.1 %collective-permute-done.6 = f32[64,128]{1,0:T(8,128)S(1)} collective-permute-done((f32[64,128]{1,0:T(8,128)S(1)}, f32[64,128]{1,0:T(8,128)S(1)}, u32[]{:S(2)}, u32[]{:S(2)}) %collective-permute-start.6) | collective-permute-done | bytes 32800 | tf_op jit(solution)/shard_map/ppermute | solution.py:270
  32.7 6.9 %analyse.1 = f32[512,128]{1,0:T(8,128)} custom-call(f32[512,128]{1,0:T(8,128)S(1)} %forecast.1.f_ref, f32[128,128]{1,0:T(8,128)S(1)} %pad_maximum_fusion.2.obs_ref), custom_call_target="tpu_custom_call" | custom-call | tf_op jit(solution)/shard_map/analyse/pallas_call | solution.py:324
  (5 shorter events, 0.0 us)
Async XLA Ops:
  0.0 0.7 %copy-start.2 = (s32[1,1,4]{2,1,0:T(1,128)S(1)}, s32[1,1,4]{2,1,0:T(1,128)}, u32[]{:S(2)}) copy-start(s32[1,1,4]{2,1,0:T(1,128)} %param.7) | copy-start | bytes 52
  0.0 0.7 %copy-start.3 = (f32[1,1,4]{2,1,0:T(1,128)S(1)}, f32[1,1,4]{2,1,0:T(1,128)}, u32[]{:S(2)}) copy-start(f32[1,1,4]{2,1,0:T(1,128)} %param.8) | copy-start | bytes 52
  0.0 0.7 %copy-start.4 = (f32[1,1,4]{2,1,0:T(1,128)S(1)}, f32[1,1,4]{2,1,0:T(1,128)}, u32[]{:S(2)}) copy-start(f32[1,1,4]{2,1,0:T(1,128)} %param.9) | copy-start | bytes 52
  0.7 0.9 %copy-start = (f32[64,8,128]{2,1,0:T(8,128)S(1)}, f32[64,8,128]{2,1,0:T(8,128)}, u32[]{:S(2)}) copy-start(f32[64,8,128]{2,1,0:T(8,128)} %ens_hbm.1) | copy-start | bytes 786436
  1.6 0.7 %copy-start.1 = (f32[3,8,128]{2,1,0:T(8,128)S(1)}, f32[3,8,128]{2,1,0:T(8,128)}, u32[]{:S(2)}) copy-start(f32[3,8,128]{2,1,0:T(8,128)} %flow_hbm.1) | copy-start | bytes 36868
  3.2 5.3 %collective-permute-start = (f32[136,128]{1,0:T(8,128)S(1)}, f32[136,128]{1,0:T(8,128)S(1)}, u32[]{:S(2)}, u32[]{:S(2)}) collective-permute-start(f32[136,128]{1,0:T(8,128)S(1)} %get-tuple-element.12), channel_id=1, source_target_pairs={{0,4},{8,12},{16,20},{24,28},{4,0},{12,8},{20,16},{28,24},{1,5},{9... | collective-permute-start | bytes 208904 | tf_op jit(solution)/shard_map/ppermute | solution.py:261
  6.2 2.3 %collective-permute-start.1 = (f32[136,128]{1,0:T(8,128)S(1)}, f32[136,128]{1,0:T(8,128)S(1)}, u32[]{:S(2)}, u32[]{:S(2)}) collective-permute-start(f32[136,128]{1,0:T(8,128)S(1)} %get-tuple-element.13), channel_id=1, source_target_pairs={{4,8},{12,16},{20,24},{8,4},{16,12},{24,20},{5,9},{13,17},{21,25},... | collective-permute-start | bytes 208904 | tf_op jit(solution)/shard_map/ppermute | solution.py:261
  9.7 1.3 %collective-permute-start.2 = (f32[72,128]{1,0:T(8,128)S(1)}, f32[72,128]{1,0:T(8,128)S(1)}, u32[]{:S(2)}, u32[]{:S(2)}) collective-permute-start(f32[72,128]{1,0:T(8,128)S(1)} %observe.1), channel_id=1, source_target_pairs={{0,1},{1,0},{2,3},{3,2},{4,5},{5,4},{6,7},{7,6},{8,9},{9,8},{10,11... | collective-permute-start | bytes 110600 | tf_op jit(solution)/shard_map/ppermute | solution.py:270
  11.0 4.6 %collective-permute-start.3 = (f32[144,128]{1,0:T(8,128)S(1)}, f32[144,128]{1,0:T(8,128)S(1)}, u32[]{:S(2)}, u32[]{:S(2)}) collective-permute-start(f32[144,128]{1,0:T(8,128)S(1)} %pad_maximum_fusion.1), channel_id=1, source_target_pairs={{0,2},{1,3},{2,0},{3,1},{4,6},{5,7},{6,4},{7,5},{8,10},{9,11},{10,... | collective-permute-start | bytes 221192 | tf_op jit(solution)/shard_map/ppermute | solution.py:270
  16.3 6.4 %collective-permute-start.4 = (f32[16,128]{1,0:T(8,128)S(1)}, f32[16,128]{1,0:T(8,128)S(1)}, u32[]{:S(2)}, u32[]{:S(2)}) collective-permute-start(f32[16,128]{1,0:T(8,128)S(1)} %complete.1), channel_id=1, source_target_pairs={{0,4},{4,0},{8,12},{12,8},{16,20},{20,16},{24,28},{28,24},{1,5},{5... | collective-permute-start | bytes 24584 | tf_op jit(solution)/shard_map/ppermute | solution.py:270
  22.7 5.0 %collective-permute-start.5 = (f32[32,128]{1,0:T(8,128)S(1)}, f32[32,128]{1,0:T(8,128)S(1)}, u32[]{:S(2)}, u32[]{:S(2)}) collective-permute-start(f32[32,128]{1,0:T(8,128)S(1)} %pad_maximum_fusion.4), channel_id=1, source_target_pairs={{0,8},{4,12},{8,0},{12,4},{16,24},{20,28},{24,16},{28,20},{1,9},{5... | collective-permute-start | bytes 49160 | tf_op jit(solution)/shard_map/ppermute | solution.py:270
  27.7 4.9 %collective-permute-start.6 = (f32[64,128]{1,0:T(8,128)S(1)}, f32[64,128]{1,0:T(8,128)S(1)}, u32[]{:S(2)}, u32[]{:S(2)}) collective-permute-start(f32[64,128]{1,0:T(8,128)S(1)} %pad_maximum_fusion.3), channel_id=1, source_target_pairs={{0,16},{4,20},{8,24},{12,28},{16,0},{20,4},{24,8},{28,12},{1,17},{... | collective-permute-start | bytes 98312 | tf_op jit(solution)/shard_map/ppermute | solution.py:270

commit v3 on v2

--- a/solution.py
+++ b/solution.py
@@ -29,7 +29,7 @@
 EDGE = 16
 BLOCK = 4 * EDGE + 8
 LEFT, RIGHT, LEFT_MID, RIGHT_MID, OBS = 0, EDGE, 2 * EDGE, 3 * EDGE, 4 * EDGE
-ANY = pl.BlockSpec(memory_space=pl.ANY)
+HBM = pl.BlockSpec(memory_space=pltpu.HBM)
 
 
 def coefficients(k, u, v):
@@ -99,7 +99,7 @@
     return coefficients(*[scratch[k] for k in range(3)])
 
 
-def observe(members, count, n_obs, field_ref, flow_ref, obs_ref, even_ref, odd_ref, out_ref, tall_ref):
+def observe(members, count, n_obs, field_ref, flow_ref, obs_ref, odd_ref, even_ref, out_ref, tall_ref):
     north, south = halo_rows(even_ref, odd_ref, members)
     field = [north[1], north[0]]
     field += [field_ref[r * members : (r + 1) * members, :] for r in range(count)] + [south[0], south[1]]
@@ -203,7 +203,7 @@
         out_ref[n_obs * tile : n_obs * (tile + 1), :] = raw * block[:, 65:66]
 
 
-def forecast(members, count, size, field_ref, flow_ref, even_ref, odd_ref, blocks_ref, out_ref, tall_ref):
+def forecast(members, count, size, field_ref, flow_ref, odd_ref, even_ref, blocks_ref, out_ref, tall_ref):
     north, south = halo_rows(even_ref, odd_ref, members)
     tile = lax.axis_index("gx")
     west, west_mid, east, east_mid = side_columns(blocks_ref, tile, size)
@@ -228,6 +228,32 @@
         out_ref[r * members : (r + 1) * members, :] = step(middle, r + 2, EDGE)
 
 
+def eliminated(a, members):
+    size = 8
+    lane, sub = lanes((size, 128)), rows_of((size, 128))
+    part = [a[size * q : size * (q + 1), :] for q in range(members // size)]
+    for p in range(len(part)):
+        column = {
+            (q, j): jnp.broadcast_to(part[q][:, size * p + j : size * p + j + 1], (size, 128))
+            for q in range(p, len(part))
+            for j in range(size)
+        }
+        for j in range(size):
+            at = size * p + j
+            inverse = 1.0 / column[p, j][j : j + 1, :]
+            unit = jnp.where(lane[:1] == at, 1.0, part[p][j : j + 1, :])
+            pivots = [column[p, k][j : j + 1, :] for k in range(j + 1, size)]
+            for q in range(p, len(part)):
+                factor = column[q, j] * inverse
+                if q == p:
+                    factor = jnp.where(sub > j, factor, 0.0)
+                for k in range(j + 1, size):
+                    column[q, k] = column[q, k] - factor * pivots[k - j - 1]
+                cleared = (lane == at) & (sub > j) if q == p else lane == at
+                part[q] = jnp.where(cleared, 0.0, part[q]) - factor * unit
+    return jnp.concatenate(part, axis=0)
+
+
 def analyse(members, count, f_ref, obs_ref, out_ref):
     scaled = obs_ref[...]
     full = lax.dot_general(
@@ -235,13 +261,7 @@
     )
     lane, sub = lanes((members, 128)), rows_of((members, 128))
     a = full[:members, :] + jnp.where(lane == sub, members - 1.0, 0.0)
-    for j in range(members):
-        row = a[j : j + 1, :]
-        column = a[:, j : j + 1]
-        below = sub > j
-        factor = jnp.where(below, column * (1.0 / row[:, j : j + 1]), 0.0)
-        unit = jnp.where(lane[:1] == j, 1.0, row)
-        a = jnp.where(below & (lane == j), 0.0, a) - factor * unit
+    a = eliminated(a, members)
     diagonal = jnp.sum(jnp.where(lane == sub, a, 0.0), axis=1, keepdims=True)
     scale = lax.rsqrt(diagonal)
     inverse = scale * jnp.where(lane < sub, a, jnp.where(lane == sub, 1.0, 0.0))
@@ -282,16 +302,20 @@
     def shape(*dims):
         return jax.ShapeDtypeStruct(dims + (width,), F32)
 
-    field, tile_flow, obs, rows_even, rows_odd = call(
+    field, tile_flow, obs, rows_even, rows_odd = pl.pallas_call(
         functools.partial(load, members, count, n_obs),
+        compiler_params=PARAMS,
         out_shape=[shape(members * count), shape(3, count), shape(24)] + [shape(2 * members + 8)] * 2,
-        in_specs=[ANY] * 5,
+        in_specs=[HBM] * 5,
         out_specs=[VMEM] * 5,
         scratch_shapes=[pltpu.SMEM((n_obs,), jnp.int32)]
         + [pltpu.SMEM((n_obs,), F32)] * 2
         + [pltpu.SemaphoreType.DMA((count + 4,))],
         name="load",
-    )(ensemble, flow, obs_cell.reshape(-1), obs_value.reshape(-1), obs_var.reshape(-1))
+    )(*[
+        pltpu.with_memory_space_constraint(x, pltpu.HBM)
+        for x in (ensemble, flow, obs_cell.reshape(-1), obs_value.reshape(-1), obs_var.reshape(-1))
+    ])
     rows_odd = swap(rows_odd, "gy", 1)
     rows_even = swap(rows_even, "gy", 0)
     tall = pltpu.VMEM((3, EDGE, width), F32)
@@ -302,7 +326,7 @@
         out_specs=VMEM,
         scratch_shapes=[tall],
         name="observe",
-    )(field, tile_flow, obs, rows_even, rows_odd)
+    )(field, tile_flow, obs, rows_odd, rows_even)
     blocks = gathered(block, "gx")
     packet = call(
         functools.partial(complete, members, n_obs, size),
@@ -319,7 +343,7 @@
         scratch_shapes=[tall],
         cost_estimate=pl.CostEstimate(flops=4 * 10**6, bytes_accessed=6 * 10**5, transcendentals=0),
         name="forecast",
-    )(field, tile_flow, rows_even, rows_odd, blocks)
+    )(field, tile_flow, rows_odd, rows_even, blocks)
     scaled = gathered(packet, "gy")
     out = call(
         functools.partial(analyse, members, count),

time: 39.8 us -> 33.6 us (0.84)
  Pallas kernels: 10.3 us -> 6.95 us
  local copies, waits for them, and re-layouts: 2.34 us -> 0 us
  starting transfers between devices: 16.9 us -> 15.6 us
  waiting for transfers between devices: 9.86 us -> 10.8 us
    ppermute x5, starting transfers between devices: 13.3 us -> 9.13 us  [gathered(): other = lax.ppermute(x, axis, [(i, i ^ step) for i in range(size)])]
    pallas_call x1, Pallas kernels: 6.88 us -> 3.32 us  [body(): call(functools.partial(analyse, members, count), out_shape=shape(members...]
    ppermute x2, starting transfers between devices: 3.66 us -> 6.46 us  [swap(): return lax.ppermute(x, axis, pairs + [(b, a) for a, b in pairs])]
    unnamed x10 -> x0, local copies, waits for them, and re-layouts: 2.34 us -> none
    ppermute x2, waiting for transfers between devices: 1.63 us -> 2.29 us  [swap(): return lax.ppermute(x, axis, pairs + [(b, a) for a, b in pairs])]
where the time goes in v3:
time: 33.6 us; the launch traced here: 33.4 us
  starting transfers between devices  15.6 us (46%)
  waiting for transfers between devices  10.8 us (32%)
  Pallas kernels  6.95 us (21%)
    ppermute x5, starting transfers between devices, gathered(): other = lax.ppermute(x, axis, [(i, i ^ step) for i in range(size)])  9.13 us
    ppermute x5, waiting for transfers between devices, gathered(): other = lax.ppermute(x, axis, [(i, i ^ step) for i in range(size)])  8.47 us
    ppermute x2, starting transfers between devices, swap(): return lax.ppermute(x, axis, pairs + [(b, a) for a, b in pairs])  6.46 us
    pallas_call x1, Pallas kernels, body(): call(functools.partial(analyse, members, count), out_shape=shape(members...  3.32 us
    ppermute x2, waiting for transfers between devices, swap(): return lax.ppermute(x, axis, pairs + [(b, a) for a, b in pairs])  2.29 us
    pallas_call x1, Pallas kernels, body(): call(functools.partial(observe, members, count, n_obs), out_shape=shape(B...  1.16 us
    pallas_call x1, Pallas kernels, body(): pl.pallas_call(functools.partial(load, members, count, n_obs), compiler_p...  1.04 us
    pallas_call x1, Pallas kernels, body(): call(functools.partial(forecast, members, count, size), out_shape=shape(m...  0.8 us
  transfers between devices with their start and end apart: 7, of which 6 were waited for; matrix products, arithmetic and copies ran while one was open for 0% of the time, Pallas kernels for 2%

profile of v3, /device:TPU:0, one launch (start us, length us, event | category | flops | bytes accessed | tf_op | source)
XLA Modules:
  0.0 33.4 jit_solution(4807751236124479839)
XLA Ops:
  0.0 1.0 %load.1 = (f32[512,128]{1,0:T(8,128)S(1)}, f32[3,8,128]{2,1,0:T(8,128)S(1)}, f32[24,128]{1,0:T(8,128)S(1)}, f32[136,128]{1,0:T(8,128)S(1)}, f32[136,128]{1,0:T(8,128)S(1)}) custom-call(f32[64,8,128]{2,1,0:T(8,128)} %ens_hbm.1, f32[3,8,128]{2,1,0:T(8,128)} %flow_hbm.1, s32[4]{0:T(128)} %bitcast.4, f32[4]{0:T(128)} %bitcast.5, f32[4]{0:T(128)} %bitcast.6), custom_call_target="tpu_custom_call" | custom-call | tf_op jit(solution)/shard_map/load/pallas_call | solution.py:305
  1.1 0.7 %collective-permute-start = (f32[136,128]{1,0:T(8,128)S(1)}, f32[136,128]{1,0:T(8,128)S(1)}, u32[]{:S(2)}, u32[]{:S(2)}) collective-permute-start(f32[136,128]{1,0:T(8,128)S(1)} %get-tuple-element.12), channel_id=1, source_target_pairs={{4,8},{12,16},{20,24},{8,4},{16,12},{24,20},{5,9},{13,17},{21,25},... | collective-permute-start | bytes 208904 | tf_op jit(solution)/shard_map/ppermute | solution.py:281
  1.7 5.8 %collective-permute-start.1 = (f32[136,128]{1,0:T(8,128)S(1)}, f32[136,128]{1,0:T(8,128)S(1)}, u32[]{:S(2)}, u32[]{:S(2)}) collective-permute-start(f32[136,128]{1,0:T(8,128)S(1)} %get-tuple-element.13), channel_id=1, source_target_pairs={{0,4},{8,12},{16,20},{24,28},{4,0},{12,8},{20,16},{28,24},{1,5},{9... | collective-permute-start | bytes 208904 | tf_op jit(solution)/shard_map/ppermute | solution.py:281
  7.5 0.0 collective-permute-done.odd_ref
  7.5 2.3 %collective-permute-done.1.even_ref = f32[136,128]{1,0:T(8,128)S(1)} collective-permute-done((f32[136,128]{1,0:T(8,128)S(1)}, f32[136,128]{1,0:T(8,128)S(1)}, u32[]{:S(2)}, u32[]{:S(2)}) %collective-permute-start.1) | collective-permute-done | bytes 69664 | tf_op jit(solution)/shard_map/ppermute | solution.py:281
  9.8 1.2 %observe.1 = f32[72,128]{1,0:T(8,128)S(1)} custom-call(f32[512,128]{1,0:T(8,128)S(1)} %get-tuple-element.10.field_ref, f32[3,8,128]{2,1,0:T(8,128)S(1)} %get-tuple-element.11.flow_ref, f32[24,128]{1,0:T(8,128)S(1)} %get-tuple-element.14.obs_ref, f32[136,128]{1,0:T(8,128)S(1)} %collective-permute-done.odd_ref, f32[136,128]{1,0:T(8,128)S(1)} %collective-permute-done.1.even_ref), custom_call_target="tpu_custom_call" | custom-call | tf_op jit(solution)/shard_map/observe/pallas_call | solution.py:322
  11.0 0.1 collective-permute-start.2
  11.0 1.2 %collective-permute-done.2 = f32[72,128]{1,0:T(8,128)S(1)} collective-permute-done((f32[72,128]{1,0:T(8,128)S(1)}, f32[72,128]{1,0:T(8,128)S(1)}, u32[]{:S(2)}, u32[]{:S(2)}) %collective-permute-start.2) | collective-permute-done | bytes 36896 | tf_op jit(solution)/shard_map/ppermute | solution.py:290
  12.3 1.5 %collective-permute-start.3 = (f32[144,128]{1,0:T(8,128)S(1)}, f32[144,128]{1,0:T(8,128)S(1)}, u32[]{:S(2)}, u32[]{:S(2)}) collective-permute-start(f32[144,128]{1,0:T(8,128)S(1)} %pad_maximum_fusion.1), channel_id=1, source_target_pairs={{0,2},{1,3},{2,0},{3,1},{4,6},{5,7},{6,4},{7,5},{8,10},{9,11},{10,... | collective-permute-start | bytes 221192 | tf_op jit(solution)/shard_map/ppermute | solution.py:290
  13.8 2.8 %collective-permute-done.3 = f32[144,128]{1,0:T(8,128)S(1)} collective-permute-done((f32[144,128]{1,0:T(8,128)S(1)}, f32[144,128]{1,0:T(8,128)S(1)}, u32[]{:S(2)}, u32[]{:S(2)}) %collective-permute-start.3) | collective-permute-done | bytes 73760 | tf_op jit(solution)/shard_map/ppermute | solution.py:290
  16.6 0.6 %complete.1 = f32[16,128]{1,0:T(8,128)S(1)} custom-call(f32[288,128]{1,0:T(8,128)S(1)} %pad_maximum_fusion.blocks_ref), custom_call_target="tpu_custom_call" | custom-call | tf_op jit(solution)/shard_map/complete/pallas_call | solution.py:331
  17.3 2.4 %collective-permute-start.4 = (f32[16,128]{1,0:T(8,128)S(1)}, f32[16,128]{1,0:T(8,128)S(1)}, u32[]{:S(2)}, u32[]{:S(2)}) collective-permute-start(f32[16,128]{1,0:T(8,128)S(1)} %complete.1), channel_id=1, source_target_pairs={{0,4},{4,0},{8,12},{12,8},{16,20},{20,16},{24,28},{28,24},{1,5},{5... | collective-permute-start | bytes 24584 | tf_op jit(solution)/shard_map/ppermute | solution.py:290
  19.6 1.6 %collective-permute-done.4 = f32[16,128]{1,0:T(8,128)S(1)} collective-permute-done((f32[16,128]{1,0:T(8,128)S(1)}, f32[16,128]{1,0:T(8,128)S(1)}, u32[]{:S(2)}, u32[]{:S(2)}) %collective-permute-start.4) | collective-permute-done | bytes 8224 | tf_op jit(solution)/shard_map/ppermute | solution.py:290
  21.3 2.1 %collective-permute-start.5 = (f32[32,128]{1,0:T(8,128)S(1)}, f32[32,128]{1,0:T(8,128)S(1)}, u32[]{:S(2)}, u32[]{:S(2)}) collective-permute-start(f32[32,128]{1,0:T(8,128)S(1)} %pad_maximum_fusion.4), channel_id=1, source_target_pairs={{0,8},{4,12},{8,0},{12,4},{16,24},{20,28},{24,16},{28,20},{1,9},{5... | collective-permute-start | bytes 49160 | tf_op jit(solution)/shard_map/ppermute | solution.py:290
  23.4 1.7 %collective-permute-done.5 = f32[32,128]{1,0:T(8,128)S(1)} collective-permute-done((f32[32,128]{1,0:T(8,128)S(1)}, f32[32,128]{1,0:T(8,128)S(1)}, u32[]{:S(2)}, u32[]{:S(2)}) %collective-permute-start.5) | collective-permute-done | bytes 16416 | tf_op jit(solution)/shard_map/ppermute | solution.py:290
  25.1 3.0 %collective-permute-start.6 = (f32[64,128]{1,0:T(8,128)S(1)}, f32[64,128]{1,0:T(8,128)S(1)}, u32[]{:S(2)}, u32[]{:S(2)}) collective-permute-start(f32[64,128]{1,0:T(8,128)S(1)} %pad_maximum_fusion.3), channel_id=1, source_target_pairs={{0,16},{4,20},{8,24},{12,28},{16,0},{20,4},{24,8},{28,12},{1,17},{... | collective-permute-start | bytes 98312 | tf_op jit(solution)/shard_map/ppermute | solution.py:290
  28.1 0.8 %forecast.1.f_ref = f32[512,128]{1,0:T(8,128)S(1)} custom-call(f32[512,128]{1,0:T(8,128)S(1)} %get-tuple-element.10.field_ref, f32[3,8,128]{2,1,0:T(8,128)S(1)} %get-tuple-element.11.flow_ref, f32[136,128]{1,0:T(8,128)S(1)} %collective-permute-done.odd_ref, f32[136,128]{1,0:T(8,128)S(1)} %collective-permute-done.1.even_ref, ...), custom_call_target="tpu_custom_call" | custom-call | flops 4000000 | bytes 600000 | tf_op jit(solution)/shard_map/forecast/pallas_call | solution.py:338
  28.9 1.1 %collective-permute-done.6 = f32[64,128]{1,0:T(8,128)S(1)} collective-permute-done((f32[64,128]{1,0:T(8,128)S(1)}, f32[64,128]{1,0:T(8,128)S(1)}, u32[]{:S(2)}, u32[]{:S(2)}) %collective-permute-start.6) | collective-permute-done | bytes 32800 | tf_op jit(solution)/shard_map/ppermute | solution.py:290
  30.0 3.3 %analyse.1 = f32[512,128]{1,0:T(8,128)} custom-call(f32[512,128]{1,0:T(8,128)S(1)} %forecast.1.f_ref, f32[128,128]{1,0:T(8,128)S(1)} %pad_maximum_fusion.2.obs_ref), custom_call_target="tpu_custom_call" | custom-call | tf_op jit(solution)/shard_map/analyse/pallas_call | solution.py:348
  (5 shorter events, 0.0 us)
Async XLA Ops:
  1.1 6.5 %collective-permute-start = (f32[136,128]{1,0:T(8,128)S(1)}, f32[136,128]{1,0:T(8,128)S(1)}, u32[]{:S(2)}, u32[]{:S(2)}) collective-permute-start(f32[136,128]{1,0:T(8,128)S(1)} %get-tuple-element.12), channel_id=1, source_target_pairs={{4,8},{12,16},{20,24},{8,4},{16,12},{24,20},{5,9},{13,17},{21,25},... | collective-permute-start | bytes 208904 | tf_op jit(solution)/shard_map/ppermute | solution.py:281
  1.7 8.1 %collective-permute-start.1 = (f32[136,128]{1,0:T(8,128)S(1)}, f32[136,128]{1,0:T(8,128)S(1)}, u32[]{:S(2)}, u32[]{:S(2)}) collective-permute-start(f32[136,128]{1,0:T(8,128)S(1)} %get-tuple-element.13), channel_id=1, source_target_pairs={{0,4},{8,12},{16,20},{24,28},{4,0},{12,8},{20,16},{28,24},{1,5},{9... | collective-permute-start | bytes 208904 | tf_op jit(solution)/shard_map/ppermute | solution.py:281
  11.0 1.3 %collective-permute-start.2 = (f32[72,128]{1,0:T(8,128)S(1)}, f32[72,128]{1,0:T(8,128)S(1)}, u32[]{:S(2)}, u32[]{:S(2)}) collective-permute-start(f32[72,128]{1,0:T(8,128)S(1)} %observe.1), channel_id=1, source_target_pairs={{0,1},{1,0},{2,3},{3,2},{4,5},{5,4},{6,7},{7,6},{8,9},{9,8},{10,11... | collective-permute-start | bytes 110600 | tf_op jit(solution)/shard_map/ppermute | solution.py:290
  12.3 4.4 %collective-permute-start.3 = (f32[144,128]{1,0:T(8,128)S(1)}, f32[144,128]{1,0:T(8,128)S(1)}, u32[]{:S(2)}, u32[]{:S(2)}) collective-permute-start(f32[144,128]{1,0:T(8,128)S(1)} %pad_maximum_fusion.1), channel_id=1, source_target_pairs={{0,2},{1,3},{2,0},{3,1},{4,6},{5,7},{6,4},{7,5},{8,10},{9,11},{10,... | collective-permute-start | bytes 221192 | tf_op jit(solution)/shard_map/ppermute | solution.py:290
  17.3 4.0 %collective-permute-start.4 = (f32[16,128]{1,0:T(8,128)S(1)}, f32[16,128]{1,0:T(8,128)S(1)}, u32[]{:S(2)}, u32[]{:S(2)}) collective-permute-start(f32[16,128]{1,0:T(8,128)S(1)} %complete.1), channel_id=1, source_target_pairs={{0,4},{4,0},{8,12},{12,8},{16,20},{20,16},{24,28},{28,24},{1,5},{5... | collective-permute-start | bytes 24584 | tf_op jit(solution)/shard_map/ppermute | solution.py:290
  21.3 3.8 %collective-permute-start.5 = (f32[32,128]{1,0:T(8,128)S(1)}, f32[32,128]{1,0:T(8,128)S(1)}, u32[]{:S(2)}, u32[]{:S(2)}) collective-permute-start(f32[32,128]{1,0:T(8,128)S(1)} %pad_maximum_fusion.4), channel_id=1, source_target_pairs={{0,8},{4,12},{8,0},{12,4},{16,24},{20,28},{24,16},{28,20},{1,9},{5... | collective-permute-start | bytes 49160 | tf_op jit(solution)/shard_map/ppermute | solution.py:290
  25.1 4.9 %collective-permute-start.6 = (f32[64,128]{1,0:T(8,128)S(1)}, f32[64,128]{1,0:T(8,128)S(1)}, u32[]{:S(2)}, u32[]{:S(2)}) collective-permute-start(f32[64,128]{1,0:T(8,128)S(1)} %pad_maximum_fusion.3), channel_id=1, source_target_pairs={{0,16},{4,20},{8,24},{12,28},{16,0},{20,4},{24,8},{28,12},{1,17},{... | collective-permute-start | bytes 98312 | tf_op jit(solution)/shard_map/ppermute | solution.py:290

commit v4 on v3

--- a/solution.py
+++ b/solution.py
@@ -27,9 +27,11 @@
 
 
 EDGE = 16
-BLOCK = 4 * EDGE + 8
-LEFT, RIGHT, LEFT_MID, RIGHT_MID, OBS = 0, EDGE, 2 * EDGE, 3 * EDGE, 4 * EDGE
+BLOCK = EDGE + 16
+MID, OBS = EDGE, EDGE + 8
+VALUE, FACTOR, TO_WEST, TO_EAST, WEIGHTS = 64, 65, 66, 67, 72
 HBM = pl.BlockSpec(memory_space=pltpu.HBM)
+ANY = pl.BlockSpec(memory_space=pl.ANY)
 
 
 def coefficients(k, u, v):
@@ -92,24 +94,27 @@
 
 def tall_coefficients(scratch, flow_ref, north_flow, south_flow, count):
     for k in range(3):
-        scratch[k] = jnp.zeros((EDGE, 128), F32)
-        scratch[k, 1:2, :] = north_flow[k : k + 1]
-        scratch[k, 2 : 2 + count, :] = flow_ref[k]
-        scratch[k, 2 + count : 3 + count, :] = south_flow[k : k + 1]
+        scratch[k, 0:count, :] = flow_ref[k]
+        scratch[k, count:, :] = jnp.zeros((EDGE - count, 128), F32)
+        scratch[k, count : count + 1, :] = south_flow[k : k + 1]
+        scratch[k, EDGE - 1 : EDGE, :] = north_flow[k : k + 1]
     return coefficients(*[scratch[k] for k in range(3)])
+
+
+def tall_field(field_ref, north, south, members, count):
+    field = {-2: north[1], -1: north[0], count: south[0], count + 1: south[1]}
+    field.update({r: field_ref[r * members : (r + 1) * members, :] for r in range(count)})
+    return field
 
 
 def observe(members, count, n_obs, field_ref, flow_ref, obs_ref, odd_ref, even_ref, out_ref, tall_ref):
     north, south = halo_rows(even_ref, odd_ref, members)
-    field = [north[1], north[0]]
-    field += [field_ref[r * members : (r + 1) * members, :] for r in range(count)] + [south[0], south[1]]
-    coeffs = tall_coefficients(tall_ref, flow_ref, north[2], south[2], count)
+    field = tall_field(field_ref, north, south, members, count)
+    own, up, down, left, right = tall_coefficients(tall_ref, flow_ref, north[2], south[2], count)
     lane, sub = lanes((EDGE, 128)), rows_of((EDGE, 128))
     wide = lanes((members, 128))
-    own, up, down, left, right = coeffs
     has_west = lax.axis_index("gx") > 0
     has_east = lax.axis_index("gx") < lax.axis_size("gx") - 1
-    zero = jnp.zeros((EDGE, 128), F32)
 
     def spread(w):
         to_west, to_east = left * w, right * w
@@ -124,13 +129,13 @@
 
     packed = jnp.zeros((members, 128), F32)
     second = jnp.zeros((members, 128), F32)
-    for i in range(1, count + 3):
-        x = field[i]
-        packed = jnp.where(wide == i, shifted(x, i), packed)
-        packed = jnp.where(wide == EDGE + i, shifted(x, EDGE + i - 127), packed)
-        if 2 <= i < count + 2:
-            second = jnp.where(wide == i, shifted(x, i - 1), second)
-            second = jnp.where(wide == EDGE + i, shifted(x, EDGE + i - 126), second)
+    for r in range(-1, count + 1):
+        x, at = field[r], r % EDGE
+        packed = jnp.where(wide == at, shifted(x, at), packed)
+        packed = jnp.where(wide == EDGE + at, shifted(x, EDGE + at - 127), packed)
+        if 0 <= r < count:
+            second = jnp.where(wide == at, shifted(x, at - 1), second)
+            second = jnp.where(wide == EDGE + at, shifted(x, EDGE + at - 126), second)
 
     def edge_row(low, high):
         both = jnp.where(lane == sub, low[:, 0:1], jnp.where(lane == sub + EDGE, high[:, 127:128], 0.0))
@@ -138,94 +143,91 @@
 
     middle = (
         edge_row(own, own) * packed
-        + edge_row(up, up) * shifted(packed, 1)
+        + edge_row(up, up) * jnp.where(wide % EDGE == 0, shifted(packed, 1 - EDGE), shifted(packed, 1))
         + edge_row(down, down) * shifted(packed, -1)
         + edge_row(right, left) * second
     )
-    packed = jnp.where(wide < 2 * EDGE, packed, jnp.where(wide < 4 * EDGE, shifted(middle, 2 * EDGE), 0.0))
-    meta = jnp.where(lane == 80, left[:, 0:1], jnp.where(lane == 81, right[:, 127:128], zero))
-    position = ((sub - 2) * 128 + lane).astype(F32)
-    inner = (sub >= 2) & (sub < 2 + count)
+    packed = jnp.where(wide < 2 * EDGE, packed, 0.0)
+    packed = jnp.where((wide >= 32) & (wide < 40), shifted(middle, 32), packed)
+    packed = jnp.where((wide >= 40) & (wide < 48), shifted(middle, 24), packed)
+    top_lane = lane[:8]
+    meta = jnp.where(top_lane == VALUE, obs_ref[8:16, :], 0.0)
+    meta = jnp.where(top_lane == FACTOR, lax.rsqrt(obs_ref[16:24, :]), meta)
+    meta = jnp.where(top_lane == TO_WEST, left[:8, 0:1], meta)
+    meta = jnp.where(top_lane == TO_EAST, right[:8, 127:128], meta)
+    position = (sub * 128 + lane).astype(F32)
     for j in range(n_obs):
-        here = jnp.where(inner & (position == obs_ref[j : j + 1, :]), 1.0, 0.0)
+        here = jnp.where((sub < count) & (position == obs_ref[j : j + 1, :]), 1.0, 0.0)
         w, mid_west, mid_east = spread(here)
         w, west, east = spread(w)
-        total = w[0:1, :] * field[0]
-        for i in range(1, count + 4):
-            total = total + w[i : i + 1, :] * field[i]
-        packed = jnp.where(wide == OBS + j, jnp.sum(total, axis=1, keepdims=True), packed)
-        for at, column in ((64, west), (68, east), (72, mid_west), (76, mid_east)):
-            meta = jnp.where(lane == at + j, column, meta)
-    turned = transposed(packed)
-    out_ref[0:EDGE, :] = turned[0:EDGE, :] + meta
-    out_ref[EDGE:OBS, :] = turned[EDGE:OBS, :]
-    top_lane = lanes((8, 128))
-    value, factor = obs_ref[8:16, :], lax.rsqrt(obs_ref[16:24, :])
-    out_ref[OBS : OBS + 8, :] = jnp.where(
-        top_lane == 64, value, jnp.where(top_lane == 65, factor, turned[OBS : OBS + 8, :])
-    )
-
-
-def place(tile, size):
-    return tile if size & (size - 1) else jnp.bitwise_xor(lax.axis_index("gx"), tile)
-
-
-def block_rows(ref, start, tile, size, rows=EDGE):
-    return ref[pl.ds(pl.multiple_of(place(tile, size) * BLOCK + start, 8), rows), :]
+        total = w[EDGE - 2 : EDGE - 1, :] * field[-2]
+        for r in range(-1, count + 2):
+            total = total + w[r % EDGE : r % EDGE + 1, :] * field[r]
+        packed = jnp.where(wide == 48 + j, jnp.sum(total, axis=1, keepdims=True), packed)
+        for k, column in enumerate((west[:8], west[8:], east[:8], east[8:], mid_west[:8], mid_east[:8])):
+            meta = jnp.where(top_lane == WEIGHTS + k * n_obs + j, column, meta)
+    turned = jnp.concatenate([packed, jnp.zeros((128 - members, 128), F32)], axis=0).T
+    out_ref[0:EDGE, :] = turned[0:EDGE] + shifted(turned[EDGE : 2 * EDGE], 64)
+    out_ref[MID : MID + 8, :] = turned[32:40] + shifted(turned[40:48], 64)
+    out_ref[OBS : OBS + 8, :] = turned[48:56] + meta
+
+
+def block_rows(ref, start, tile, size, rows):
+    place = tile if size & (size - 1) else jnp.bitwise_xor(lax.axis_index("gx") | 1, tile)
+    return ref[pl.ds(pl.multiple_of(place * BLOCK + start, 8), rows), :]
 
 
 def side_columns(ref, tile, size):
     west, east = jnp.maximum(tile - 1, 0), jnp.minimum(tile + 1, size - 1)
-    west_meta, east_meta = block_rows(ref, 0, west, size), block_rows(ref, 0, east, size)
-    west_mid = block_rows(ref, RIGHT_MID, west, size) + west_meta[:, 81:82] * block_rows(ref, LEFT, tile, size)
-    east_mid = block_rows(ref, LEFT_MID, east, size) + east_meta[:, 80:81] * block_rows(ref, RIGHT, tile, size)
-    return block_rows(ref, RIGHT, west, size), west_mid, block_rows(ref, LEFT, east, size), east_mid
+    own = block_rows(ref, 0, tile, size, EDGE)
+    west_x = shifted(block_rows(ref, 0, west, size, EDGE), 64)
+    east_x = block_rows(ref, 0, east, size, EDGE)
+    west_mid = shifted(block_rows(ref, MID, west, size, 8), 64)
+    west_mid += block_rows(ref, OBS, west, size, 8)[:, TO_EAST : TO_EAST + 1] * own[:8]
+    east_mid = block_rows(ref, MID, east, size, 8)
+    east_mid += block_rows(ref, OBS, east, size, 8)[:, TO_WEST : TO_WEST + 1] * shifted(own[:8], 64)
+    return west_x, east_x, west_mid, east_mid
 
 
 def complete(members, n_obs, size, blocks_ref, out_ref):
     lane = lanes((n_obs, 128))
     for tile in range(size):
-        west, west_mid, east, east_mid = side_columns(blocks_ref, jnp.int32(tile), size)
-        meta = block_rows(blocks_ref, 0, jnp.int32(tile), size)
-        block = block_rows(blocks_ref, OBS, jnp.int32(tile), size, 8)[:n_obs]
+        west, east, west_mid, east_mid = side_columns(blocks_ref, jnp.int32(tile), size)
+        block = block_rows(blocks_ref, OBS, jnp.int32(tile), size, 8)
+        terms = (west[:8], west[8:], east[:8], east[8:], west_mid, east_mid)
         added = []
         for j in range(n_obs):
-            terms = (
-                meta[:, 64 + j : 65 + j] * west
-                + meta[:, 68 + j : 69 + j] * east
-                + meta[:, 72 + j : 73 + j] * west_mid
-                + meta[:, 76 + j : 77 + j] * east_mid
-            )
-            added.append(jnp.sum(terms, axis=0, keepdims=True))
+            at = [WEIGHTS + k * n_obs + j for k in range(len(terms))]
+            total = sum(block[:, a : a + 1] * term for a, term in zip(at, terms))
+            added.append(jnp.sum(total, axis=0, keepdims=True))
+        block = block[:n_obs]
         at = jnp.where(lane < members, block + jnp.concatenate(added, axis=0), 0.0)
         mean = jnp.sum(at, axis=1, keepdims=True) * (1.0 / members)
-        raw = jnp.where(lane < members, at - mean, jnp.where(lane == members, block[:, 64:65] - mean, 0.0))
-        out_ref[n_obs * tile : n_obs * (tile + 1), :] = raw * block[:, 65:66]
+        raw = jnp.where(lane < members, at - mean, jnp.where(lane == members, block[:, VALUE : VALUE + 1] - mean, 0.0))
+        out_ref[n_obs * tile : n_obs * (tile + 1), :] = raw * block[:, FACTOR : FACTOR + 1]
 
 
 def forecast(members, count, size, field_ref, flow_ref, odd_ref, even_ref, blocks_ref, out_ref, tall_ref):
     north, south = halo_rows(even_ref, odd_ref, members)
     tile = lax.axis_index("gx")
-    west, west_mid, east, east_mid = side_columns(blocks_ref, tile, size)
-    sides = jnp.concatenate(
-        [jnp.where(tile > 0, x, 0.0) for x in (west, west_mid)]
-        + [jnp.where(tile < size - 1, x, 0.0) for x in (east, east_mid)],
-        axis=0,
-    )
-    sides = transposed(sides)[:members]
-    field = [north[1], north[0]]
-    field += [field_ref[r * members : (r + 1) * members, :] for r in range(count)] + [south[0], south[1]]
+    west, east, west_mid, east_mid = side_columns(blocks_ref, tile, size)
+    has_west, has_east = tile > 0, tile < size - 1
+    sides = [jnp.where(has_west, west, 0.0), jnp.where(has_east, east, 0.0)]
+    sides += [jnp.where(has_west, west_mid, 0.0), jnp.where(has_east, east_mid, 0.0), jnp.zeros((80, 128), F32)]
+    sides = jnp.concatenate(sides, axis=0).T[:members]
+    field = tall_field(field_ref, north, south, members, count)
     tall = tall_coefficients(tall_ref, flow_ref, north[2], south[2], count)
     lane = lanes((members, 128))
 
-    def step(rows, i, start):
-        w = jnp.where(lane == 0, shifted(sides, -(start + i)), shifted(rows[i], 1))
-        e = jnp.where(lane == 127, shifted(sides, 127 - (start + 2 * EDGE + i)), shifted(rows[i], -1))
-        return combine([c[i : i + 1, :] for c in tall], rows[i], rows[i - 1], rows[i + 1], w, e)
-
-    middle = {i: step(field, i, 0) for i in range(1, count + 3)}
+    def step(rows, r, west_at, east_at):
+        w = jnp.where(lane == 0, shifted(sides, -west_at), shifted(rows[r], 1))
+        e = jnp.where(lane == 127, shifted(sides, 127 - east_at), shifted(rows[r], -1))
+        at = r % EDGE
+        return combine([c[at : at + 1, :] for c in tall], rows[r], rows[r - 1], rows[r + 1], w, e)
+
+    middle = {r: step(field, r, r % EDGE, EDGE + r % EDGE) for r in range(-1, count + 1)}
     for r in range(count):
-        out_ref[r * members : (r + 1) * members, :] = step(middle, r + 2, EDGE)
+        out_ref[r * members : (r + 1) * members, :] = step(middle, r, 2 * EDGE + r, 2 * EDGE + 8 + r)
 
 
 def eliminated(a, members):
@@ -254,8 +256,8 @@
     return jnp.concatenate(part, axis=0)
 
 
-def analyse(members, count, f_ref, obs_ref, out_ref):
-    scaled = obs_ref[...]
+def analyse(members, count, f_ref, obs_ref, even_obs_ref, out_ref):
+    scaled = jnp.where(lax.axis_index("gx") % 2 == 0, even_obs_ref[...], obs_ref[...])
     full = lax.dot_general(
         scaled, scaled, (((0,), (0,)), ((), ())), precision=HIGHEST, preferred_element_type=F32
     )
@@ -281,30 +283,79 @@
     return lax.ppermute(x, axis, pairs + [(b, a) for a, b in pairs])
 
 
-def gathered(x, axis):
-    size = lax.axis_size(axis)
-    if size & (size - 1):
-        return lax.all_gather(x, axis, tiled=True)
+def stack(x_ref, other_ref, *refs):
+    out_ref = refs[-1]
+    out_ref[: x_ref.shape[0], :] = x_ref[...]
+    out_ref[x_ref.shape[0] :, :] = other_ref[...]
+
+
+def stacked(x, other, *ahead):
+    return pl.pallas_call(
+        stack,
+        out_shape=jax.ShapeDtypeStruct((2 * x.shape[0], x.shape[1]), x.dtype),
+        in_specs=[VMEM] * 2 + [ANY] * len(ahead),
+        out_specs=VMEM,
+        compiler_params=PARAMS,
+        name="stack",
+    )(x, other, *ahead)
+
+
+def doubled(x, axis, step, *ahead):
+    ny, nx = lax.axis_size("gy"), lax.axis_size("gx")
+    flip = (step, 0) if axis == "gy" else (0, step)
+    pairs = [(a * nx + b, (a ^ flip[0]) * nx + (b ^ flip[1])) for a in range(ny) for b in range(1, nx, 2)]
+    return stacked(x, lax.ppermute(x, ("gy", "gx"), pairs), *ahead)
+
+
+def handed_on(x):
+    return lax.ppermute(x, "gx", [(i, i - 1) for i in range(1, lax.axis_size("gx"), 2)])
+
+
+def two_power(size):
+    return size & (size - 1) == 0
+
+
+def row_blocks(block):
+    size = lax.axis_size("gx")
+    if size == 1 or not two_power(size):
+        blocks = lax.all_gather(block, "gx", tiled=True)
+        return blocks, blocks
+    blocks = jnp.concatenate([block, lax.ppermute(block, "gx", [(i, i ^ 1) for i in range(size)])], axis=0)
+    step = 2
+    while step < size:
+        blocks = doubled(blocks, "gx", step)
+        step *= 2
+    return blocks, handed_on(blocks)
+
+
+def all_rows(packet, early, late):
+    size = lax.axis_size("gy")
+    if lax.axis_size("gx") == 1 or not two_power(lax.axis_size("gx")) or not two_power(size):
+        if two_power(lax.axis_size("gx")) and lax.axis_size("gx") > 1:
+            own = handed_on(packet)
+            packet = jnp.where(lax.axis_index("gx") % 2 == 0, own, packet)
+        packets = lax.all_gather(packet, "gy", tiled=True)
+        return packets, packets
     step = 1
     while step < size:
-        other = lax.ppermute(x, axis, [(i, i ^ step) for i in range(size)])
-        x = jnp.concatenate([x, other], axis=0)
+        ahead = ([early] if step == 1 else []) + ([late] if 2 * step == size else [])
+        packet = doubled(packet, "gy", step, *ahead)
         step *= 2
-    return x
+    return packet, handed_on(packet)
 
 
 def body(ensemble, flow, obs_cell, obs_value, obs_var):
     members, count, width = ensemble.shape
     n_obs = obs_cell.shape[-1]
     size = lax.axis_size("gx")
+    is_even = lax.axis_index("gx") % 2 == 0
     call = functools.partial(pl.pallas_call, compiler_params=PARAMS)
 
     def shape(*dims):
         return jax.ShapeDtypeStruct(dims + (width,), F32)
 
-    field, tile_flow, obs, rows_even, rows_odd = pl.pallas_call(
+    field, tile_flow, obs, rows_even, rows_odd = call(
         functools.partial(load, members, count, n_obs),
-        compiler_params=PARAMS,
         out_shape=[shape(members * count), shape(3, count), shape(24)] + [shape(2 * members + 8)] * 2,
         in_specs=[HBM] * 5,
         out_specs=[VMEM] * 5,
@@ -327,7 +378,7 @@
         scratch_shapes=[tall],
         name="observe",
     )(field, tile_flow, obs, rows_odd, rows_even)
-    blocks = gathered(block, "gx")
+    blocks, blocks_even = row_blocks(block)
     packet = call(
         functools.partial(complete, members, n_obs, size),
         out_shape=shape(n_obs * size),
@@ -343,15 +394,14 @@
         scratch_shapes=[tall],
         cost_estimate=pl.CostEstimate(flops=4 * 10**6, bytes_accessed=6 * 10**5, transcendentals=0),
         name="forecast",
-    )(field, tile_flow, rows_odd, rows_even, blocks)
-    scaled = gathered(packet, "gy")
+    )(field, tile_flow, rows_odd, rows_even, jnp.where(is_even, blocks_even, blocks))
     out = call(
         functools.partial(analyse, members, count),
         out_shape=shape(members * count),
-        in_specs=[VMEM] * 2,
+        in_specs=[VMEM] * 3,
         out_specs=VMEM,
         name="analyse",
-    )(predicted, scaled)
+    )(predicted, *all_rows(packet, blocks_even, predicted))
     return out.reshape(ensemble.shape)
 
 

time: 33.6 us -> 39.7 us (1.18)
  waiting for transfers between devices: 10.8 us -> 20.7 us
  starting transfers between devices: 15.6 us -> 11.7 us
    ppermute x5 -> x7, waiting for transfers between devices: 8.47 us -> 18.4 us  [the longest x2 17.2 us: handed_on(): lax.ppermute(x, 'gx', [(i, i - 1) for i in range(1, lax.axis_size('gx'),...]
    ppermute x5 -> x7, starting transfers between devices: 9.13 us -> 5.26 us  [the longest x4 2.63 us: doubled(): return stacked(x, lax.ppermute(x, ('gy', 'gx'), pairs), *ahead)]
    pallas_call x1 -> x5, Pallas kernels: 1.04 us -> 1.06 us  [the longest x1 1.04 us: body(): call(functools.partial(load, members, count, n_obs), out_shape=[shape(mem...]
  transfers between devices with their start and end apart: 7 -> 9, of which waited for: 6 -> 4; matrix products, arithmetic and copies ran while one was open for 0% -> 0% of each run, Pallas kernels for 2% -> 3%
where the time goes in v4:
time: 39.7 us; the launch traced here: 39.4 us
  waiting for transfers between devices  20.7 us (52%)
  starting transfers between devices  11.7 us (29%)
  Pallas kernels  6.75 us (17%)
    ppermute x2, waiting for transfers between devices, handed_on(): lax.ppermute(x, 'gx', [(i, i - 1) for i in range(1, lax.axis_size('gx'),...  17.2 us
    ppermute x2, starting transfers between devices, swap(): return lax.ppermute(x, axis, pairs + [(b, a) for a, b in pairs])  6.46 us
    pallas_call x1, Pallas kernels, body(): call(functools.partial(analyse, members, count), out_shape=shape(members...  3.33 us
    ppermute x4, starting transfers between devices, doubled(): return stacked(x, lax.ppermute(x, ('gy', 'gx'), pairs), *ahead)  2.63 us
    ppermute x2, starting transfers between devices, handed_on(): lax.ppermute(x, 'gx', [(i, i - 1) for i in range(1, lax.axis_size('gx'),...  2.58 us
    ppermute x2, waiting for transfers between devices, swap(): return lax.ppermute(x, axis, pairs + [(b, a) for a, b in pairs])  2.29 us
    ppermute x1, waiting for transfers between devices, row_blocks(): lax.ppermute(block, 'gx', [(i, i ^ 1) for i in range(size)])  1.17 us
    pallas_call x1, Pallas kernels, body(): call(functools.partial(observe, members, count, n_obs), out_shape=shape(B...  1.08 us
  transfers between devices with their start and end apart: 9, of which 4 were waited for; matrix products, arithmetic and copies ran while one was open for 0% of the time, Pallas kernels for 3%

profile of v4, /device:TPU:0, one launch (start us, length us, event | category | flops | bytes accessed | tf_op | source)
XLA Modules:
  0.0 39.4 jit_solution(17069803280207621209)
XLA Ops:
  0.0 1.0 %load.1 = (f32[512,128]{1,0:T(8,128)S(1)}, f32[3,8,128]{2,1,0:T(8,128)S(1)}, f32[24,128]{1,0:T(8,128)S(1)}, f32[136,128]{1,0:T(8,128)S(1)}, f32[136,128]{1,0:T(8,128)S(1)}) custom-call(f32[64,8,128]{2,1,0:T(8,128)} %ens_hbm.1, f32[3,8,128]{2,1,0:T(8,128)} %flow_hbm.1, s32[4]{0:T(128)} %bitcast.4, f32[4]{0:T(128)} %bitcast.5, f32[4]{0:T(128)} %bitcast.6), custom_call_target="tpu_custom_call" | custom-call | tf_op jit(solution)/shard_map/load/pallas_call | solution.py:357
  1.1 0.7 %collective-permute-start = (f32[136,128]{1,0:T(8,128)S(1)}, f32[136,128]{1,0:T(8,128)S(1)}, u32[]{:S(2)}, u32[]{:S(2)}) collective-permute-start(f32[136,128]{1,0:T(8,128)S(1)} %get-tuple-element.12), channel_id=1, source_target_pairs={{4,8},{12,16},{20,24},{8,4},{16,12},{24,20},{5,9},{13,17},{21,25},... | collective-permute-start | bytes 208904 | tf_op jit(solution)/shard_map/ppermute | solution.py:283
  1.7 5.8 %collective-permute-start.1 = (f32[136,128]{1,0:T(8,128)S(1)}, f32[136,128]{1,0:T(8,128)S(1)}, u32[]{:S(2)}, u32[]{:S(2)}) collective-permute-start(f32[136,128]{1,0:T(8,128)S(1)} %get-tuple-element.13), channel_id=1, source_target_pairs={{0,4},{8,12},{16,20},{24,28},{4,0},{12,8},{20,16},{28,24},{1,5},{9... | collective-permute-start | bytes 208904 | tf_op jit(solution)/shard_map/ppermute | solution.py:283
  7.5 0.0 collective-permute-done.odd_ref
  7.5 2.3 %collective-permute-done.1.even_ref = f32[136,128]{1,0:T(8,128)S(1)} collective-permute-done((f32[136,128]{1,0:T(8,128)S(1)}, f32[136,128]{1,0:T(8,128)S(1)}, u32[]{:S(2)}, u32[]{:S(2)}) %collective-permute-start.1) | collective-permute-done | bytes 69664 | tf_op jit(solution)/shard_map/ppermute | solution.py:283
  9.8 1.1 %observe.1 = f32[32,128]{1,0:T(8,128)S(1)} custom-call(f32[512,128]{1,0:T(8,128)S(1)} %get-tuple-element.10.field_ref, f32[3,8,128]{2,1,0:T(8,128)S(1)} %get-tuple-element.11.flow_ref, f32[24,128]{1,0:T(8,128)S(1)} %get-tuple-element.14.obs_ref, f32[136,128]{1,0:T(8,128)S(1)} %collective-permute-done.odd_ref, f32[136,128]{1,0:T(8,128)S(1)} %collective-permute-done.1.even_ref), custom_call_target="tpu_custom_call" | custom-call | tf_op jit(solution)/shard_map/observe/pallas_call | solution.py:373
  10.9 0.1 collective-permute-start.2
  11.0 1.2 %collective-permute-done.2 = f32[32,128]{1,0:T(8,128)S(1)} collective-permute-done((f32[32,128]{1,0:T(8,128)S(1)}, f32[32,128]{1,0:T(8,128)S(1)}, u32[]{:S(2)}, u32[]{:S(2)}) %collective-permute-start.2) | collective-permute-done | bytes 16416 | tf_op jit(solution)/shard_map/ppermute | solution.py:323
  12.1 0.7 %collective-permute-start.3 = (f32[64,128]{1,0:T(8,128)S(1)}, f32[64,128]{1,0:T(8,128)S(1)}, u32[]{:S(2)}, u32[]{:S(2)}) collective-permute-start(f32[64,128]{1,0:T(8,128)S(1)} %pad_maximum_fusion.x_ref), channel_id=1, source_target_pairs={{1,3},{3,1},{5,7},{7,5},{9,11},{11,9},{13,15},{15,13},{17,19},{19,... | collective-permute-start | bytes 98312 | tf_op jit(solution)/shard_map/ppermute | solution.py:307
  12.8 0.0 collective-permute-done.3.other_ref
  12.8 1.3 %collective-permute-start.4 = (f32[128,128]{1,0:T(8,128)S(1)}, f32[128,128]{1,0:T(8,128)S(1)}, u32[]{:S(2)}, u32[]{:S(2)}) collective-permute-start(f32[128,128]{1,0:T(8,128)S(1)} %stack.4.blocks_ref), channel_id=1, source_target_pairs={{1,0},{3,2},{5,4},{7,6},{9,8},{11,10},{13,12},{15,14},{17,16},{19,... | collective-permute-start | bytes 196616 | tf_op jit(solution)/shard_map/ppermute | solution.py:311
  14.1 0.5 %complete.1.x_ref = f32[16,128]{1,0:T(8,128)S(1)} custom-call(f32[128,128]{1,0:T(8,128)S(1)} %stack.4.blocks_ref), custom_call_target="tpu_custom_call" | custom-call | tf_op jit(solution)/shard_map/complete/pallas_call | solution.py:382
  14.6 0.7 %collective-permute-start.5 = (f32[16,128]{1,0:T(8,128)S(1)}, f32[16,128]{1,0:T(8,128)S(1)}, u32[]{:S(2)}, u32[]{:S(2)}) collective-permute-start(f32[16,128]{1,0:T(8,128)S(1)} %complete.1.x_ref), channel_id=1, source_target_pairs={{1,5},{3,7},{5,1},{7,3},{9,13},{11,15},{13,9},{15,11},{17,21},{19,... | collective-permute-start | bytes 24584 | tf_op jit(solution)/shard_map/ppermute | solution.py:307
  15.3 0.0 collective-permute-done.5.other_ref
  15.3 3.7 %collective-permute-done.4.refs_0_ = f32[128,128]{1,0:T(8,128)S(1)} collective-permute-done((f32[128,128]{1,0:T(8,128)S(1)}, f32[128,128]{1,0:T(8,128)S(1)}, u32[]{:S(2)}, u32[]{:S(2)}) %collective-permute-start.4) | collective-permute-done | bytes 65568 | tf_op jit(solution)/shard_map/ppermute | solution.py:311
  19.0 0.7 %collective-permute-start.6 = (f32[32,128]{1,0:T(8,128)S(1)}, f32[32,128]{1,0:T(8,128)S(1)}, u32[]{:S(2)}, u32[]{:S(2)}) collective-permute-start(f32[32,128]{1,0:T(8,128)S(1)} %stack.5.x_ref), channel_id=1, source_target_pairs={{1,9},{3,11},{5,13},{7,15},{9,1},{11,3},{13,5},{15,7},{17,25},{19,... | collective-permute-start | bytes 49160 | tf_op jit(solution)/shard_map/ppermute | solution.py:307
  19.6 0.0 collective-permute-done.6.other_ref
  19.7 0.7 %collective-permute-start.7 = (f32[64,128]{1,0:T(8,128)S(1)}, f32[64,128]{1,0:T(8,128)S(1)}, u32[]{:S(2)}, u32[]{:S(2)}) collective-permute-start(f32[64,128]{1,0:T(8,128)S(1)} %stack.6.x_ref), channel_id=1, source_target_pairs={{1,17},{3,19},{5,21},{7,23},{9,25},{11,27},{13,29},{15,31},{17,1},... | collective-permute-start | bytes 98312 | tf_op jit(solution)/shard_map/ppermute | solution.py:307
  20.3 0.8 %forecast.1.refs_0_.f_ref = f32[512,128]{1,0:T(8,128)S(1)} custom-call(f32[512,128]{1,0:T(8,128)S(1)} %get-tuple-element.10.field_ref, f32[3,8,128]{2,1,0:T(8,128)S(1)} %get-tuple-element.11.flow_ref, f32[136,128]{1,0:T(8,128)S(1)} %collective-permute-done.odd_ref, f32[136,128]{1,0:T(8,128)S(1)} %collective-permute-done.1.even_ref, ...), custom_call_target="tpu_custom_call" | custom-call | flops 4000000 | bytes 600000 | tf_op jit(solution)/shard_map/forecast/pallas_call | solution.py:389
  21.1 0.0 collective-permute-done.7.other_ref
  21.1 1.3 %collective-permute-start.8 = (f32[128,128]{1,0:T(8,128)S(1)}, f32[128,128]{1,0:T(8,128)S(1)}, u32[]{:S(2)}, u32[]{:S(2)}) collective-permute-start(f32[128,128]{1,0:T(8,128)S(1)} %stack.7.obs_ref), channel_id=1, source_target_pairs={{1,0},{3,2},{5,4},{7,6},{9,8},{11,10},{13,12},{15,14},{17,16},{19,... | collective-permute-start | bytes 196616 | tf_op jit(solution)/shard_map/ppermute | solution.py:311
  22.4 13.6 %collective-permute-done.8.even_obs_ref = f32[128,128]{1,0:T(8,128)S(1)} collective-permute-done((f32[128,128]{1,0:T(8,128)S(1)}, f32[128,128]{1,0:T(8,128)S(1)}, u32[]{:S(2)}, u32[]{:S(2)}) %collective-permute-start.8) | collective-permute-done | bytes 65568 | tf_op jit(solution)/shard_map/ppermute | solution.py:311
  36.0 3.3 %analyse.1 = f32[512,128]{1,0:T(8,128)} custom-call(f32[512,128]{1,0:T(8,128)S(1)} %forecast.1.refs_0_.f_ref, f32[128,128]{1,0:T(8,128)S(1)} %stack.7.obs_ref, f32[128,128]{1,0:T(8,128)S(1)} %collective-permute-done.8.even_obs_ref), custom_call_target="tpu_custom_call" | custom-call | tf_op jit(solution)/shard_map/analyse/pallas_call | solution.py:398
  (6 shorter events, 0.0 us)
Async XLA Ops:
  1.1 6.5 %collective-permute-start = (f32[136,128]{1,0:T(8,128)S(1)}, f32[136,128]{1,0:T(8,128)S(1)}, u32[]{:S(2)}, u32[]{:S(2)}) collective-permute-start(f32[136,128]{1,0:T(8,128)S(1)} %get-tuple-element.12), channel_id=1, source_target_pairs={{4,8},{12,16},{20,24},{8,4},{16,12},{24,20},{5,9},{13,17},{21,25},... | collective-permute-start | bytes 208904 | tf_op jit(solution)/shard_map/ppermute | solution.py:283
  1.7 8.1 %collective-permute-start.1 = (f32[136,128]{1,0:T(8,128)S(1)}, f32[136,128]{1,0:T(8,128)S(1)}, u32[]{:S(2)}, u32[]{:S(2)}) collective-permute-start(f32[136,128]{1,0:T(8,128)S(1)} %get-tuple-element.13), channel_id=1, source_target_pairs={{0,4},{8,12},{16,20},{24,28},{4,0},{12,8},{20,16},{28,24},{1,5},{9... | collective-permute-start | bytes 208904 | tf_op jit(solution)/shard_map/ppermute | solution.py:283
  10.9 1.2 %collective-permute-start.2 = (f32[32,128]{1,0:T(8,128)S(1)}, f32[32,128]{1,0:T(8,128)S(1)}, u32[]{:S(2)}, u32[]{:S(2)}) collective-permute-start(f32[32,128]{1,0:T(8,128)S(1)} %observe.1), channel_id=1, source_target_pairs={{0,1},{1,0},{2,3},{3,2},{4,5},{5,4},{6,7},{7,6},{8,9},{9,8},{10,11... | collective-permute-start | bytes 49160 | tf_op jit(solution)/shard_map/ppermute | solution.py:323
  12.1 0.7 %collective-permute-start.3 = (f32[64,128]{1,0:T(8,128)S(1)}, f32[64,128]{1,0:T(8,128)S(1)}, u32[]{:S(2)}, u32[]{:S(2)}) collective-permute-start(f32[64,128]{1,0:T(8,128)S(1)} %pad_maximum_fusion.x_ref), channel_id=1, source_target_pairs={{1,3},{3,1},{5,7},{7,5},{9,11},{11,9},{13,15},{15,13},{17,19},{19,... | collective-permute-start | bytes 98312 | tf_op jit(solution)/shard_map/ppermute | solution.py:307
  12.8 6.1 %collective-permute-start.4 = (f32[128,128]{1,0:T(8,128)S(1)}, f32[128,128]{1,0:T(8,128)S(1)}, u32[]{:S(2)}, u32[]{:S(2)}) collective-permute-start(f32[128,128]{1,0:T(8,128)S(1)} %stack.4.blocks_ref), channel_id=1, source_target_pairs={{1,0},{3,2},{5,4},{7,6},{9,8},{11,10},{13,12},{15,14},{17,16},{19,... | collective-permute-start | bytes 196616 | tf_op jit(solution)/shard_map/ppermute | solution.py:311
  14.6 0.7 %collective-permute-start.5 = (f32[16,128]{1,0:T(8,128)S(1)}, f32[16,128]{1,0:T(8,128)S(1)}, u32[]{:S(2)}, u32[]{:S(2)}) collective-permute-start(f32[16,128]{1,0:T(8,128)S(1)} %complete.1.x_ref), channel_id=1, source_target_pairs={{1,5},{3,7},{5,1},{7,3},{9,13},{11,15},{13,9},{15,11},{17,21},{19,... | collective-permute-start | bytes 24584 | tf_op jit(solution)/shard_map/ppermute | solution.py:307
  19.0 0.7 %collective-permute-start.6 = (f32[32,128]{1,0:T(8,128)S(1)}, f32[32,128]{1,0:T(8,128)S(1)}, u32[]{:S(2)}, u32[]{:S(2)}) collective-permute-start(f32[32,128]{1,0:T(8,128)S(1)} %stack.5.x_ref), channel_id=1, source_target_pairs={{1,9},{3,11},{5,13},{7,15},{9,1},{11,3},{13,5},{15,7},{17,25},{19,... | collective-permute-start | bytes 49160 | tf_op jit(solution)/shard_map/ppermute | solution.py:307
  19.7 1.5 %collective-permute-start.7 = (f32[64,128]{1,0:T(8,128)S(1)}, f32[64,128]{1,0:T(8,128)S(1)}, u32[]{:S(2)}, u32[]{:S(2)}) collective-permute-start(f32[64,128]{1,0:T(8,128)S(1)} %stack.6.x_ref), channel_id=1, source_target_pairs={{1,17},{3,19},{5,21},{7,23},{9,25},{11,27},{13,29},{15,31},{17,1},... | collective-permute-start | bytes 98312 | tf_op jit(solution)/shard_map/ppermute | solution.py:307
  21.1 14.9 %collective-permute-start.8 = (f32[128,128]{1,0:T(8,128)S(1)}, f32[128,128]{1,0:T(8,128)S(1)}, u32[]{:S(2)}, u32[]{:S(2)}) collective-permute-start(f32[128,128]{1,0:T(8,128)S(1)} %stack.7.obs_ref), channel_id=1, source_target_pairs={{1,0},{3,2},{5,4},{7,6},{9,8},{11,10},{13,12},{15,14},{17,16},{19,... | collective-permute-start | bytes 196616 | tf_op jit(solution)/shard_map/ppermute | solution.py:311

commit v5 on v4

--- a/solution.py
+++ b/solution.py
@@ -31,7 +31,6 @@
 MID, OBS = EDGE, EDGE + 8
 VALUE, FACTOR, TO_WEST, TO_EAST, WEIGHTS = 64, 65, 66, 67, 72
 HBM = pl.BlockSpec(memory_space=pltpu.HBM)
-ANY = pl.BlockSpec(memory_space=pl.ANY)
 
 
 def coefficients(k, u, v):
@@ -84,11 +83,14 @@
 
 
 def halo_rows(even_ref, odd_ref, members):
-    is_even = lax.axis_index("gy") % 2 == 0
+    at = lax.axis_index("gy")
+    is_even = at % 2 == 0
+    inside = at > 0, at < lax.axis_size("gy") - 1
     parts = []
     for lo, hi in ((0, members), (members, 2 * members), (2 * members, 2 * members + 3)):
         e, o = even_ref[lo:hi, :], odd_ref[lo:hi, :]
-        parts.append((jnp.where(is_even, o, e), jnp.where(is_even, e, o)))
+        pair = jnp.where(is_even, o, e), jnp.where(is_even, e, o)
+        parts.append([jnp.where(here, x, 0.0) for here, x in zip(inside, pair)])
     return tuple(p[0] for p in parts), tuple(p[1] for p in parts)
 
 
@@ -173,8 +175,7 @@
 
 
 def block_rows(ref, start, tile, size, rows):
-    place = tile if size & (size - 1) else jnp.bitwise_xor(lax.axis_index("gx") | 1, tile)
-    return ref[pl.ds(pl.multiple_of(place * BLOCK + start, 8), rows), :]
+    return ref[pl.ds(pl.multiple_of(place_of(tile, size) * BLOCK + start, 8), rows), :]
 
 
 def side_columns(ref, tile, size):
@@ -256,8 +257,8 @@
     return jnp.concatenate(part, axis=0)
 
 
-def analyse(members, count, f_ref, obs_ref, even_obs_ref, out_ref):
-    scaled = jnp.where(lax.axis_index("gx") % 2 == 0, even_obs_ref[...], obs_ref[...])
+def analyse(members, count, f_ref, obs_ref, out_ref):
+    scaled = obs_ref[...]
     full = lax.dot_general(
         scaled, scaled, (((0,), (0,)), ((), ())), precision=HIGHEST, preferred_element_type=F32
     )
@@ -279,76 +280,65 @@
 
 
 def swap(x, axis, offset):
-    pairs = [(i, i + 1) for i in range(offset, lax.axis_size(axis) - 1, 2)]
-    return lax.ppermute(x, axis, pairs + [(b, a) for a, b in pairs])
-
-
-def stack(x_ref, other_ref, *refs):
-    out_ref = refs[-1]
-    out_ref[: x_ref.shape[0], :] = x_ref[...]
-    out_ref[x_ref.shape[0] :, :] = other_ref[...]
-
-
-def stacked(x, other, *ahead):
-    return pl.pallas_call(
-        stack,
-        out_shape=jax.ShapeDtypeStruct((2 * x.shape[0], x.shape[1]), x.dtype),
-        in_specs=[VMEM] * 2 + [ANY] * len(ahead),
-        out_specs=VMEM,
-        compiler_params=PARAMS,
-        name="stack",
-    )(x, other, *ahead)
-
-
-def doubled(x, axis, step, *ahead):
     ny, nx = lax.axis_size("gy"), lax.axis_size("gx")
-    flip = (step, 0) if axis == "gy" else (0, step)
-    pairs = [(a * nx + b, (a ^ flip[0]) * nx + (b ^ flip[1])) for a in range(ny) for b in range(1, nx, 2)]
-    return stacked(x, lax.ppermute(x, ("gy", "gx"), pairs), *ahead)
-
-
-def handed_on(x):
-    return lax.ppermute(x, "gx", [(i, i - 1) for i in range(1, lax.axis_size("gx"), 2)])
+    partner = {i: i for i in range(ny)}
+    for i in range(offset, ny - 1, 2):
+        partner[i], partner[i + 1] = i + 1, i
+    pairs = []
+    for a in range(ny):
+        for b in range(nx):
+            if partner[a] != a:
+                pairs.append((a * nx + b, partner[a] * nx + b))
+            elif nx % 2 == 0:
+                pairs.append((a * nx + b, a * nx + (b ^ 1)))
+    return lax.ppermute(x, ("gy", "gx"), pairs)
 
 
 def two_power(size):
     return size & (size - 1) == 0
 
 
+def doubled(x, flip_y, flip_x):
+    ny, nx = lax.axis_size("gy"), lax.axis_size("gx")
+    pairs = [(a * nx + b, (a ^ flip_y) * nx + (b ^ flip_x)) for a in range(ny) for b in range(nx)]
+    return jnp.concatenate([x, lax.ppermute(x, ("gy", "gx"), pairs)], axis=0)
+
+
 def row_blocks(block):
-    size = lax.axis_size("gx")
-    if size == 1 or not two_power(size):
-        blocks = lax.all_gather(block, "gx", tiled=True)
-        return blocks, blocks
-    blocks = jnp.concatenate([block, lax.ppermute(block, "gx", [(i, i ^ 1) for i in range(size)])], axis=0)
-    step = 2
+    size, step = lax.axis_size("gx"), 1
+    if not two_power(size):
+        return lax.all_gather(block, "gx", tiled=True)
     while step < size:
-        blocks = doubled(blocks, "gx", step)
+        block = doubled(block, 0, step | 1)
         step *= 2
-    return blocks, handed_on(blocks)
-
-
-def all_rows(packet, early, late):
-    size = lax.axis_size("gy")
-    if lax.axis_size("gx") == 1 or not two_power(lax.axis_size("gx")) or not two_power(size):
-        if two_power(lax.axis_size("gx")) and lax.axis_size("gx") > 1:
-            own = handed_on(packet)
-            packet = jnp.where(lax.axis_index("gx") % 2 == 0, own, packet)
-        packets = lax.all_gather(packet, "gy", tiled=True)
-        return packets, packets
-    step = 1
+    return block
+
+
+def place_of(tile, size):
+    if not two_power(size):
+        return tile
+    distance = jnp.bitwise_xor(lax.axis_index("gx"), tile)
+    place, bit = distance, 2
+    while bit < size:
+        place = jnp.bitwise_xor(place, (distance // bit) % 2)
+        bit *= 2
+    return place
+
+
+def all_rows(packet):
+    size, step = lax.axis_size("gy"), 1
+    if not two_power(size):
+        return lax.all_gather(packet, "gy", tiled=True)
     while step < size:
-        ahead = ([early] if step == 1 else []) + ([late] if 2 * step == size else [])
-        packet = doubled(packet, "gy", step, *ahead)
+        packet = doubled(packet, step, 1 - lax.axis_size("gx") % 2)
         step *= 2
-    return packet, handed_on(packet)
+    return packet
 
 
 def body(ensemble, flow, obs_cell, obs_value, obs_var):
     members, count, width = ensemble.shape
     n_obs = obs_cell.shape[-1]
     size = lax.axis_size("gx")
-    is_even = lax.axis_index("gx") % 2 == 0
     call = functools.partial(pl.pallas_call, compiler_params=PARAMS)
 
     def shape(*dims):
@@ -378,7 +368,7 @@
         scratch_shapes=[tall],
         name="observe",
     )(field, tile_flow, obs, rows_odd, rows_even)
-    blocks, blocks_even = row_blocks(block)
+    blocks = row_blocks(block)
     packet = call(
         functools.partial(complete, members, n_obs, size),
         out_shape=shape(n_obs * size),
@@ -394,14 +384,14 @@
         scratch_shapes=[tall],
         cost_estimate=pl.CostEstimate(flops=4 * 10**6, bytes_accessed=6 * 10**5, transcendentals=0),
         name="forecast",
-    )(field, tile_flow, rows_odd, rows_even, jnp.where(is_even, blocks_even, blocks))
+    )(field, tile_flow, rows_odd, rows_even, blocks)
     out = call(
         functools.partial(analyse, members, count),
         out_shape=shape(members * count),
-        in_specs=[VMEM] * 3,
+        in_specs=[VMEM] * 2,
         out_specs=VMEM,
         name="analyse",
-    )(predicted, *all_rows(packet, blocks_even, predicted))
+    )(predicted, all_rows(packet))
     return out.reshape(ensemble.shape)
 
 

time: 39.7 us -> 28.8 us (0.73)
  waiting for transfers between devices: 20.7 us -> 9.11 us
  starting transfers between devices: 11.7 us -> 12.7 us
    ppermute x9 -> x7, waiting for transfers between devices: 20.7 us -> 9.11 us  [the longest x5 6.83 us: doubled(): return jnp.concatenate([x, lax.ppermute(x, ('gy', 'gx'), pairs)], axis=0)]
    ppermute x9 -> x7, starting transfers between devices: 11.7 us -> 12.7 us  [the longest x5 8.13 us: doubled(): return jnp.concatenate([x, lax.ppermute(x, ('gy', 'gx'), pairs)], axis=0)]
  transfers between devices with their start and end apart: 9 -> 7, of which waited for: 4 -> 6; matrix products, arithmetic and copies ran while one was open for 0% -> 0% of each run, Pallas kernels for 3% -> 3%
where the time goes in v5:
time: 28.8 us; the launch traced here: 28.6 us
  starting transfers between devices  12.7 us (44%)
  waiting for transfers between devices  9.11 us (32%)
  Pallas kernels  6.74 us (23%)
    ppermute x5, starting transfers between devices, doubled(): return jnp.concatenate([x, lax.ppermute(x, ('gy', 'gx'), pairs)], axis=0)  8.13 us
    ppermute x5, waiting for transfers between devices, doubled(): return jnp.concatenate([x, lax.ppermute(x, ('gy', 'gx'), pairs)], axis=0)  6.83 us
    ppermute x2, starting transfers between devices, swap(): return lax.ppermute(x, ('gy', 'gx'), pairs)  4.55 us
    pallas_call x1, Pallas kernels, body(): call(functools.partial(analyse, members, count), out_shape=shape(members...  3.32 us
    ppermute x2, waiting for transfers between devices, swap(): return lax.ppermute(x, ('gy', 'gx'), pairs)  2.29 us
    pallas_call x1, Pallas kernels, body(): call(functools.partial(observe, members, count, n_obs), out_shape=shape(B...  1.09 us
    pallas_call x1, Pallas kernels, body(): call(functools.partial(load, members, count, n_obs), out_shape=[shape(mem...  1.04 us
    pallas_call x1, Pallas kernels, body(): call(functools.partial(forecast, members, count, size), out_shape=shape(m...  0.8 us
  transfers between devices with their start and end apart: 7, of which 6 were waited for; matrix products, arithmetic and copies ran while one was open for 0% of the time, Pallas kernels for 3%

profile of v5, /device:TPU:0, one launch (start us, length us, event | category | flops | bytes accessed | tf_op | source)
XLA Modules:
  0.0 28.6 jit_solution(11596176204066427252)
XLA Ops:
  0.0 1.0 %load.1 = (f32[512,128]{1,0:T(8,128)S(1)}, f32[3,8,128]{2,1,0:T(8,128)S(1)}, f32[24,128]{1,0:T(8,128)S(1)}, f32[136,128]{1,0:T(8,128)S(1)}, f32[136,128]{1,0:T(8,128)S(1)}) custom-call(f32[64,8,128]{2,1,0:T(8,128)} %ens_hbm.1, f32[3,8,128]{2,1,0:T(8,128)} %flow_hbm.1, s32[4]{0:T(128)} %bitcast.4, f32[4]{0:T(128)} %bitcast.5, f32[4]{0:T(128)} %bitcast.6), custom_call_target="tpu_custom_call" | custom-call | tf_op jit(solution)/shard_map/load/pallas_call | solution.py:347
  1.1 0.5 %collective-permute-start = (f32[136,128]{1,0:T(8,128)S(1)}, f32[136,128]{1,0:T(8,128)S(1)}, u32[]{:S(2)}, u32[]{:S(2)}) collective-permute-start(f32[136,128]{1,0:T(8,128)S(1)} %get-tuple-element.12), channel_id=1, source_target_pairs={{0,1},{1,0},{2,3},{3,2},{4,8},{5,9},{6,10},{7,11},{8,4},{9,5},{10,... | collective-permute-start | bytes 208904 | tf_op jit(solution)/shard_map/ppermute | solution.py:294
  1.6 4.0 %collective-permute-start.1 = (f32[136,128]{1,0:T(8,128)S(1)}, f32[136,128]{1,0:T(8,128)S(1)}, u32[]{:S(2)}, u32[]{:S(2)}) collective-permute-start(f32[136,128]{1,0:T(8,128)S(1)} %get-tuple-element.13), channel_id=1, source_target_pairs={{0,4},{1,5},{2,6},{3,7},{4,0},{5,1},{6,2},{7,3},{8,12},{9,13},{10,... | collective-permute-start | bytes 208904 | tf_op jit(solution)/shard_map/ppermute | solution.py:294
  5.6 0.0 collective-permute-done.odd_ref
  5.6 2.3 %collective-permute-done.1.even_ref = f32[136,128]{1,0:T(8,128)S(1)} collective-permute-done((f32[136,128]{1,0:T(8,128)S(1)}, f32[136,128]{1,0:T(8,128)S(1)}, u32[]{:S(2)}, u32[]{:S(2)}) %collective-permute-start.1) | collective-permute-done | bytes 69664 | tf_op jit(solution)/shard_map/ppermute | solution.py:294
  7.9 1.1 %observe.1 = f32[32,128]{1,0:T(8,128)S(1)} custom-call(f32[512,128]{1,0:T(8,128)S(1)} %get-tuple-element.10.field_ref, f32[3,8,128]{2,1,0:T(8,128)S(1)} %get-tuple-element.11.flow_ref, f32[24,128]{1,0:T(8,128)S(1)} %get-tuple-element.14.obs_ref, f32[136,128]{1,0:T(8,128)S(1)} %collective-permute-done.odd_ref, f32[136,128]{1,0:T(8,128)S(1)} %collective-permute-done.1.even_ref), custom_call_target="tpu_custom_call" | custom-call | tf_op jit(solution)/shard_map/observe/pallas_call | solution.py:363
  9.0 0.1 collective-permute-start.2
  9.0 1.2 %collective-permute-done.2 = f32[32,128]{1,0:T(8,128)S(1)} collective-permute-done((f32[32,128]{1,0:T(8,128)S(1)}, f32[32,128]{1,0:T(8,128)S(1)}, u32[]{:S(2)}, u32[]{:S(2)}) %collective-permute-start.2) | collective-permute-done | bytes 16416 | tf_op jit(solution)/shard_map/ppermute | solution.py:304
  10.2 1.3 %collective-permute-start.3 = (f32[64,128]{1,0:T(8,128)S(1)}, f32[64,128]{1,0:T(8,128)S(1)}, u32[]{:S(2)}, u32[]{:S(2)}) collective-permute-start(f32[64,128]{1,0:T(8,128)S(1)} %pad_maximum_fusion.2), channel_id=1, source_target_pairs={{0,3},{1,2},{2,1},{3,0},{4,7},{5,6},{6,5},{7,4},{8,11},{9,10},{10,... | collective-permute-start | bytes 98312 | tf_op jit(solution)/shard_map/ppermute | solution.py:304
  11.5 2.1 %collective-permute-done.3 = f32[64,128]{1,0:T(8,128)S(1)} collective-permute-done((f32[64,128]{1,0:T(8,128)S(1)}, f32[64,128]{1,0:T(8,128)S(1)}, u32[]{:S(2)}, u32[]{:S(2)}) %collective-permute-start.3) | collective-permute-done | bytes 32800 | tf_op jit(solution)/shard_map/ppermute | solution.py:304
  13.6 0.5 %complete.1 = f32[16,128]{1,0:T(8,128)S(1)} custom-call(f32[128,128]{1,0:T(8,128)S(1)} %pad_maximum_fusion.blocks_ref), custom_call_target="tpu_custom_call" | custom-call | tf_op jit(solution)/shard_map/complete/pallas_call | solution.py:372
  14.0 2.3 %collective-permute-start.4 = (f32[16,128]{1,0:T(8,128)S(1)}, f32[16,128]{1,0:T(8,128)S(1)}, u32[]{:S(2)}, u32[]{:S(2)}) collective-permute-start(f32[16,128]{1,0:T(8,128)S(1)} %complete.1), channel_id=1, source_target_pairs={{0,5},{1,4},{2,7},{3,6},{4,1},{5,0},{6,3},{7,2},{8,13},{9,12},{10,... | collective-permute-start | bytes 24584 | tf_op jit(solution)/shard_map/ppermute | solution.py:304
  16.3 1.4 %collective-permute-done.4 = f32[16,128]{1,0:T(8,128)S(1)} collective-permute-done((f32[16,128]{1,0:T(8,128)S(1)}, f32[16,128]{1,0:T(8,128)S(1)}, u32[]{:S(2)}, u32[]{:S(2)}) %collective-permute-start.4) | collective-permute-done | bytes 8224 | tf_op jit(solution)/shard_map/ppermute | solution.py:304
  17.7 1.8 %collective-permute-start.5 = (f32[32,128]{1,0:T(8,128)S(1)}, f32[32,128]{1,0:T(8,128)S(1)}, u32[]{:S(2)}, u32[]{:S(2)}) collective-permute-start(f32[32,128]{1,0:T(8,128)S(1)} %pad_maximum_fusion.4), channel_id=1, source_target_pairs={{0,9},{1,8},{2,11},{3,10},{4,13},{5,12},{6,15},{7,14},{8,1},{9,0},... | collective-permute-start | bytes 49160 | tf_op jit(solution)/shard_map/ppermute | solution.py:304
  19.5 1.4 %collective-permute-done.5 = f32[32,128]{1,0:T(8,128)S(1)} collective-permute-done((f32[32,128]{1,0:T(8,128)S(1)}, f32[32,128]{1,0:T(8,128)S(1)}, u32[]{:S(2)}, u32[]{:S(2)}) %collective-permute-start.5) | collective-permute-done | bytes 16416 | tf_op jit(solution)/shard_map/ppermute | solution.py:304
  20.9 2.7 %collective-permute-start.6 = (f32[64,128]{1,0:T(8,128)S(1)}, f32[64,128]{1,0:T(8,128)S(1)}, u32[]{:S(2)}, u32[]{:S(2)}) collective-permute-start(f32[64,128]{1,0:T(8,128)S(1)} %pad_maximum_fusion.3), channel_id=1, source_target_pairs={{0,17},{1,16},{2,19},{3,18},{4,21},{5,20},{6,23},{7,22},{8,25},{9,... | collective-permute-start | bytes 98312 | tf_op jit(solution)/shard_map/ppermute | solution.py:304
  23.7 0.8 %forecast.1.f_ref = f32[512,128]{1,0:T(8,128)S(1)} custom-call(f32[512,128]{1,0:T(8,128)S(1)} %get-tuple-element.10.field_ref, f32[3,8,128]{2,1,0:T(8,128)S(1)} %get-tuple-element.11.flow_ref, f32[136,128]{1,0:T(8,128)S(1)} %collective-permute-done.odd_ref, f32[136,128]{1,0:T(8,128)S(1)} %collective-permute-done.1.even_ref, ...), custom_call_target="tpu_custom_call" | custom-call | flops 4000000 | bytes 600000 | tf_op jit(solution)/shard_map/forecast/pallas_call | solution.py:379
  24.5 0.8 %collective-permute-done.6 = f32[64,128]{1,0:T(8,128)S(1)} collective-permute-done((f32[64,128]{1,0:T(8,128)S(1)}, f32[64,128]{1,0:T(8,128)S(1)}, u32[]{:S(2)}, u32[]{:S(2)}) %collective-permute-start.6) | collective-permute-done | bytes 32800 | tf_op jit(solution)/shard_map/ppermute | solution.py:304
  25.3 3.3 %analyse.1 = f32[512,128]{1,0:T(8,128)} custom-call(f32[512,128]{1,0:T(8,128)S(1)} %forecast.1.f_ref, f32[128,128]{1,0:T(8,128)S(1)} %pad_maximum_fusion.1.obs_ref), custom_call_target="tpu_custom_call" | custom-call | tf_op jit(solution)/shard_map/analyse/pallas_call | solution.py:388
  (5 shorter events, 0.0 us)
Async XLA Ops:
  1.1 4.6 %collective-permute-start = (f32[136,128]{1,0:T(8,128)S(1)}, f32[136,128]{1,0:T(8,128)S(1)}, u32[]{:S(2)}, u32[]{:S(2)}) collective-permute-start(f32[136,128]{1,0:T(8,128)S(1)} %get-tuple-element.12), channel_id=1, source_target_pairs={{0,1},{1,0},{2,3},{3,2},{4,8},{5,9},{6,10},{7,11},{8,4},{9,5},{10,... | collective-permute-start | bytes 208904 | tf_op jit(solution)/shard_map/ppermute | solution.py:294
  1.6 6.3 %collective-permute-start.1 = (f32[136,128]{1,0:T(8,128)S(1)}, f32[136,128]{1,0:T(8,128)S(1)}, u32[]{:S(2)}, u32[]{:S(2)}) collective-permute-start(f32[136,128]{1,0:T(8,128)S(1)} %get-tuple-element.13), channel_id=1, source_target_pairs={{0,4},{1,5},{2,6},{3,7},{4,0},{5,1},{6,2},{7,3},{8,12},{9,13},{10,... | collective-permute-start | bytes 208904 | tf_op jit(solution)/shard_map/ppermute | solution.py:294
  9.0 1.2 %collective-permute-start.2 = (f32[32,128]{1,0:T(8,128)S(1)}, f32[32,128]{1,0:T(8,128)S(1)}, u32[]{:S(2)}, u32[]{:S(2)}) collective-permute-start(f32[32,128]{1,0:T(8,128)S(1)} %observe.1), channel_id=1, source_target_pairs={{0,1},{1,0},{2,3},{3,2},{4,5},{5,4},{6,7},{7,6},{8,9},{9,8},{10,11... | collective-permute-start | bytes 49160 | tf_op jit(solution)/shard_map/ppermute | solution.py:304
  10.2 3.3 %collective-permute-start.3 = (f32[64,128]{1,0:T(8,128)S(1)}, f32[64,128]{1,0:T(8,128)S(1)}, u32[]{:S(2)}, u32[]{:S(2)}) collective-permute-start(f32[64,128]{1,0:T(8,128)S(1)} %pad_maximum_fusion.2), channel_id=1, source_target_pairs={{0,3},{1,2},{2,1},{3,0},{4,7},{5,6},{6,5},{7,4},{8,11},{9,10},{10,... | collective-permute-start | bytes 98312 | tf_op jit(solution)/shard_map/ppermute | solution.py:304
  14.0 3.6 %collective-permute-start.4 = (f32[16,128]{1,0:T(8,128)S(1)}, f32[16,128]{1,0:T(8,128)S(1)}, u32[]{:S(2)}, u32[]{:S(2)}) collective-permute-start(f32[16,128]{1,0:T(8,128)S(1)} %complete.1), channel_id=1, source_target_pairs={{0,5},{1,4},{2,7},{3,6},{4,1},{5,0},{6,3},{7,2},{8,13},{9,12},{10,... | collective-permute-start | bytes 24584 | tf_op jit(solution)/shard_map/ppermute | solution.py:304
  17.7 3.2 %collective-permute-start.5 = (f32[32,128]{1,0:T(8,128)S(1)}, f32[32,128]{1,0:T(8,128)S(1)}, u32[]{:S(2)}, u32[]{:S(2)}) collective-permute-start(f32[32,128]{1,0:T(8,128)S(1)} %pad_maximum_fusion.4), channel_id=1, source_target_pairs={{0,9},{1,8},{2,11},{3,10},{4,13},{5,12},{6,15},{7,14},{8,1},{9,0},... | collective-permute-start | bytes 49160 | tf_op jit(solution)/shard_map/ppermute | solution.py:304
  20.9 4.3 %collective-permute-start.6 = (f32[64,128]{1,0:T(8,128)S(1)}, f32[64,128]{1,0:T(8,128)S(1)}, u32[]{:S(2)}, u32[]{:S(2)}) collective-permute-start(f32[64,128]{1,0:T(8,128)S(1)} %pad_maximum_fusion.3), channel_id=1, source_target_pairs={{0,17},{1,16},{2,19},{3,18},{4,21},{5,20},{6,23},{7,22},{8,25},{9,... | collective-permute-start | bytes 98312 | tf_op jit(solution)/shard_map/ppermute | solution.py:304

commit v6 on v5

--- a/solution.py
+++ b/solution.py
@@ -208,7 +208,7 @@
         out_ref[n_obs * tile : n_obs * (tile + 1), :] = raw * block[:, FACTOR : FACTOR + 1]
 
 
-def forecast(members, count, size, field_ref, flow_ref, odd_ref, even_ref, blocks_ref, out_ref, tall_ref):
+def forecast(members, count, size, field_ref, flow_ref, odd_ref, even_ref, blocks_ref, out_ref, mean_ref, tall_ref):
     north, south = halo_rows(even_ref, odd_ref, members)
     tile = lax.axis_index("gx")
     west, east, west_mid, east_mid = side_columns(blocks_ref, tile, size)
@@ -228,55 +228,74 @@
 
     middle = {r: step(field, r, r % EDGE, EDGE + r % EDGE) for r in range(-1, count + 1)}
     for r in range(count):
-        out_ref[r * members : (r + 1) * members, :] = step(middle, r, 2 * EDGE + r, 2 * EDGE + 8 + r)
+        x = step(middle, r, 2 * EDGE + r, 2 * EDGE + 8 + r)
+        mean = jnp.sum(x, axis=0, keepdims=True) * (1.0 / members)
+        mean_ref[r : r + 1, :] = mean
+        x = x - mean
+        high = x.astype(jnp.bfloat16)
+        at = slice(128 * r, 128 * (r + 1))
+        out_ref[0:members, at] = high
+        out_ref[members : 2 * members, at] = (x - high.astype(F32)).astype(jnp.bfloat16)
+        out_ref[2 * members :, at] = high
 
 
 def eliminated(a, members):
     size = 8
     lane, sub = lanes((size, 128)), rows_of((size, 128))
     part = [a[size * q : size * (q + 1), :] for q in range(members // size)]
+    pivot = []
+
+    def spread(q, c):
+        return jnp.broadcast_to(part[q][:, c : c + 1], (size, 128))
+
+    ahead = {(0, c): spread(0, c) for c in range(size)}
     for p in range(len(part)):
-        column = {
-            (q, j): jnp.broadcast_to(part[q][:, size * p + j : size * p + j + 1], (size, 128))
-            for q in range(p, len(part))
-            for j in range(size)
-        }
+        start, end = size * p, size * (p + 1)
+        rest = range(p, len(part))
+        column = {(q, c): spread(q, c) for q in rest[1:] for c in range(start, end)}
+        column.update(ahead)
+        more = range(end, end + size if p + 1 < len(part) else end)
+        column.update({(q, c): spread(q, c) for q in rest[:2] for c in more})
+        mine = (lane >= start) & (lane < end)
+        for q in rest:
+            part[q] = jnp.where(mine, 0.0, part[q])
+        found = jnp.zeros((size, 128), F32)
         for j in range(size):
-            at = size * p + j
-            inverse = 1.0 / column[p, j][j : j + 1, :]
+            at = start + j
+            value = column[p, at][j : j + 1, :]
+            found = jnp.where(sub == j, value, found)
+            inverse = 1.0 / value
             unit = jnp.where(lane[:1] == at, 1.0, part[p][j : j + 1, :])
-            pivots = [column[p, k][j : j + 1, :] for k in range(j + 1, size)]
-            for q in range(p, len(part)):
-                factor = column[q, j] * inverse
+            pivots = {c: column[p, c][j : j + 1, :] for c in range(at + 1, end + len(more))}
+            for q in rest:
+                factor = column[q, at] * inverse
+                for c in range(at + 1, end + (len(more) if q <= p + 1 else 0)):
+                    column[q, c] = column[q, c] - factor * pivots[c]
                 if q == p:
                     factor = jnp.where(sub > j, factor, 0.0)
-                for k in range(j + 1, size):
-                    column[q, k] = column[q, k] - factor * pivots[k - j - 1]
-                cleared = (lane == at) & (sub > j) if q == p else lane == at
-                part[q] = jnp.where(cleared, 0.0, part[q]) - factor * unit
-    return jnp.concatenate(part, axis=0)
-
-
-def analyse(members, count, f_ref, obs_ref, out_ref):
+                part[q] = part[q] - factor * unit
+        pivot.append(found)
+        ahead = {(p + 1, c): column[p + 1, c] for c in more}
+    return jnp.concatenate(part, axis=0), jnp.concatenate(pivot, axis=0)
+
+
+def analyse(members, count, f_ref, mean_ref, obs_ref, out_ref):
     scaled = obs_ref[...]
     full = lax.dot_general(
         scaled, scaled, (((0,), (0,)), ((), ())), precision=HIGHEST, preferred_element_type=F32
     )
     lane, sub = lanes((members, 128)), rows_of((members, 128))
-    a = full[:members, :] + jnp.where(lane == sub, members - 1.0, 0.0)
-    a = eliminated(a, members)
-    diagonal = jnp.sum(jnp.where(lane == sub, a, 0.0), axis=1, keepdims=True)
-    scale = lax.rsqrt(diagonal)
+    a, pivots = eliminated(full[:members, :] + jnp.where(lane == sub, members - 1.0, 0.0), members)
+    scale = lax.rsqrt(pivots)
     inverse = scale * jnp.where(lane < sub, a, jnp.where(lane == sub, 1.0, 0.0))
     reduced = scale * a[:, members : members + 1]
     weights = jnp.sum(reduced * inverse, axis=0, keepdims=True)
-    transform = jnp.sqrt(members - 1.0) * inverse + weights
-    share = (1.0 - jnp.sum(jnp.where(lane < members, transform, 0.0), axis=1, keepdims=True)) * (1.0 / members)
-    transform = (transform + share)[:, :members]
+    transform = (jnp.sqrt(members - 1.0) * inverse + weights)[:, :members]
+    high = transform.astype(jnp.bfloat16)
+    low = (transform - high.astype(F32)).astype(jnp.bfloat16)
+    update = jnp.dot(jnp.concatenate([high, high, low], axis=1), f_ref[...], preferred_element_type=F32)
     for r in range(count):
-        out_ref[pl.ds(r, members, stride=count), :] = jnp.dot(
-            transform, f_ref[r * members : (r + 1) * members, :], precision=HIGHEST, preferred_element_type=F32
-        )
+        out_ref[pl.ds(r, members, stride=count), :] = update[:, 128 * r : 128 * (r + 1)] + mean_ref[r : r + 1, :]
 
 
 def swap(x, axis, offset):
@@ -326,12 +345,12 @@
 
 
 def all_rows(packet):
-    size, step = lax.axis_size("gy"), 1
-    if not two_power(size):
+    step = lax.axis_size("gy")
+    if not two_power(step):
         return lax.all_gather(packet, "gy", tiled=True)
-    while step < size:
+    while step > 1:
+        step //= 2
         packet = doubled(packet, step, 1 - lax.axis_size("gx") % 2)
-        step *= 2
     return packet
 
 
@@ -376,11 +395,11 @@
         out_specs=VMEM,
         name="complete",
     )(blocks)
-    predicted = call(
+    anomaly, mean = call(
         functools.partial(forecast, members, count, size),
-        out_shape=shape(members * count),
+        out_shape=[jax.ShapeDtypeStruct((3 * members, count * width), jnp.bfloat16), shape(count)],
         in_specs=[VMEM] * 5,
-        out_specs=VMEM,
+        out_specs=[VMEM] * 2,
         scratch_shapes=[tall],
         cost_estimate=pl.CostEstimate(flops=4 * 10**6, bytes_accessed=6 * 10**5, transcendentals=0),
         name="forecast",
@@ -388,10 +407,10 @@
     out = call(
         functools.partial(analyse, members, count),
         out_shape=shape(members * count),
-        in_specs=[VMEM] * 2,
+        in_specs=[VMEM] * 3,
         out_specs=VMEM,
         name="analyse",
-    )(predicted, all_rows(packet))
+    )(anomaly, mean, all_rows(packet))
     return out.reshape(ensemble.shape)
 
 

time: 28.8 us -> 28.1 us (0.976)
  Pallas kernels: 6.74 us -> 6.11 us
  starting transfers between devices: 12.7 us -> 12.4 us
  waiting for transfers between devices: 9.11 us -> 9.4 us
    pallas_call x1, Pallas kernels: 3.32 us -> 2.62 us  [body(): call(functools.partial(analyse, members, count), out_shape=shape(members...]
    ppermute x5, starting transfers between devices: 8.13 us -> 7.81 us  [doubled(): return jnp.concatenate([x, lax.ppermute(x, ('gy', 'gx'), pairs)], axis=0)]
where the time goes in v6:
time: 28.1 us; the launch traced here: 27.9 us
  starting transfers between devices  12.4 us (44%)
  waiting for transfers between devices  9.4 us (33%)
  Pallas kernels  6.11 us (22%)
    ppermute x5, starting transfers between devices, doubled(): return jnp.concatenate([x, lax.ppermute(x, ('gy', 'gx'), pairs)], axis=0)  7.81 us
    ppermute x5, waiting for transfers between devices, doubled(): return jnp.concatenate([x, lax.ppermute(x, ('gy', 'gx'), pairs)], axis=0)  7.11 us
    ppermute x2, starting transfers between devices, swap(): return lax.ppermute(x, ('gy', 'gx'), pairs)  4.55 us
    pallas_call x1, Pallas kernels, body(): call(functools.partial(analyse, members, count), out_shape=shape(members...  2.62 us
    ppermute x2, waiting for transfers between devices, swap(): return lax.ppermute(x, ('gy', 'gx'), pairs)  2.29 us
    pallas_call x1, Pallas kernels, body(): call(functools.partial(observe, members, count, n_obs), out_shape=shape(B...  1.09 us
    pallas_call x1, Pallas kernels, body(): call(functools.partial(load, members, count, n_obs), out_shape=[shape(mem...  1.04 us
    pallas_call x1, Pallas kernels, body(): call(functools.partial(forecast, members, count, size), out_shape=[jax.Sh...  0.87 us
  transfers between devices with their start and end apart: 7, of which 6 were waited for; matrix products, arithmetic and copies ran while one was open for 0% of the time, Pallas kernels for 3%

profile of v6, /device:TPU:0, one launch (start us, length us, event | category | flops | bytes accessed | tf_op | source)
XLA Modules:
  0.0 27.9 jit_solution(13007629474851096585)
XLA Ops:
  0.0 1.0 %load.1 = (f32[512,128]{1,0:T(8,128)S(1)}, f32[3,8,128]{2,1,0:T(8,128)S(1)}, f32[24,128]{1,0:T(8,128)S(1)}, f32[136,128]{1,0:T(8,128)S(1)}, f32[136,128]{1,0:T(8,128)S(1)}) custom-call(f32[64,8,128]{2,1,0:T(8,128)} %ens_hbm.1, f32[3,8,128]{2,1,0:T(8,128)} %flow_hbm.1, s32[4]{0:T(128)} %bitcast.4, f32[4]{0:T(128)} %bitcast.5, f32[4]{0:T(128)} %bitcast.6), custom_call_target="tpu_custom_call" | custom-call | tf_op jit(solution)/shard_map/load/pallas_call | solution.py:366
  1.1 0.5 %collective-permute-start = (f32[136,128]{1,0:T(8,128)S(1)}, f32[136,128]{1,0:T(8,128)S(1)}, u32[]{:S(2)}, u32[]{:S(2)}) collective-permute-start(f32[136,128]{1,0:T(8,128)S(1)} %get-tuple-element.14), channel_id=1, source_target_pairs={{0,1},{1,0},{2,3},{3,2},{4,8},{5,9},{6,10},{7,11},{8,4},{9,5},{10,... | collective-permute-start | bytes 208904 | tf_op jit(solution)/shard_map/ppermute | solution.py:313
  1.6 4.0 %collective-permute-start.1 = (f32[136,128]{1,0:T(8,128)S(1)}, f32[136,128]{1,0:T(8,128)S(1)}, u32[]{:S(2)}, u32[]{:S(2)}) collective-permute-start(f32[136,128]{1,0:T(8,128)S(1)} %get-tuple-element.15), channel_id=1, source_target_pairs={{0,4},{1,5},{2,6},{3,7},{4,0},{5,1},{6,2},{7,3},{8,12},{9,13},{10,... | collective-permute-start | bytes 208904 | tf_op jit(solution)/shard_map/ppermute | solution.py:313
  5.6 0.0 collective-permute-done.odd_ref
  5.6 2.3 %collective-permute-done.1.even_ref = f32[136,128]{1,0:T(8,128)S(1)} collective-permute-done((f32[136,128]{1,0:T(8,128)S(1)}, f32[136,128]{1,0:T(8,128)S(1)}, u32[]{:S(2)}, u32[]{:S(2)}) %collective-permute-start.1) | collective-permute-done | bytes 69664 | tf_op jit(solution)/shard_map/ppermute | solution.py:313
  7.9 1.1 %observe.1 = f32[32,128]{1,0:T(8,128)S(1)} custom-call(f32[512,128]{1,0:T(8,128)S(1)} %get-tuple-element.12.field_ref, f32[3,8,128]{2,1,0:T(8,128)S(1)} %get-tuple-element.13.flow_ref, f32[24,128]{1,0:T(8,128)S(1)} %get-tuple-element.16.obs_ref, f32[136,128]{1,0:T(8,128)S(1)} %collective-permute-done.odd_ref, f32[136,128]{1,0:T(8,128)S(1)} %collective-permute-done.1.even_ref), custom_call_target="tpu_custom_call" | custom-call | tf_op jit(solution)/shard_map/observe/pallas_call | solution.py:382
  9.0 0.1 collective-permute-start.2
  9.0 1.2 %collective-permute-done.2 = f32[32,128]{1,0:T(8,128)S(1)} collective-permute-done((f32[32,128]{1,0:T(8,128)S(1)}, f32[32,128]{1,0:T(8,128)S(1)}, u32[]{:S(2)}, u32[]{:S(2)}) %collective-permute-start.2) | collective-permute-done | bytes 16416 | tf_op jit(solution)/shard_map/ppermute | solution.py:323
  10.2 1.3 %collective-permute-start.3 = (f32[64,128]{1,0:T(8,128)S(1)}, f32[64,128]{1,0:T(8,128)S(1)}, u32[]{:S(2)}, u32[]{:S(2)}) collective-permute-start(f32[64,128]{1,0:T(8,128)S(1)} %pad_maximum_fusion.2), channel_id=1, source_target_pairs={{0,3},{1,2},{2,1},{3,0},{4,7},{5,6},{6,5},{7,4},{8,11},{9,10},{10,... | collective-permute-start | bytes 98312 | tf_op jit(solution)/shard_map/ppermute | solution.py:323
  11.5 2.1 %collective-permute-done.3 = f32[64,128]{1,0:T(8,128)S(1)} collective-permute-done((f32[64,128]{1,0:T(8,128)S(1)}, f32[64,128]{1,0:T(8,128)S(1)}, u32[]{:S(2)}, u32[]{:S(2)}) %collective-permute-start.3) | collective-permute-done | bytes 32800 | tf_op jit(solution)/shard_map/ppermute | solution.py:323
  13.6 0.5 %complete.1 = f32[16,128]{1,0:T(8,128)S(1)} custom-call(f32[128,128]{1,0:T(8,128)S(1)} %pad_maximum_fusion.blocks_ref), custom_call_target="tpu_custom_call" | custom-call | tf_op jit(solution)/shard_map/complete/pallas_call | solution.py:391
  14.0 3.4 %collective-permute-start.4 = (f32[16,128]{1,0:T(8,128)S(1)}, f32[16,128]{1,0:T(8,128)S(1)}, u32[]{:S(2)}, u32[]{:S(2)}) collective-permute-start(f32[16,128]{1,0:T(8,128)S(1)} %complete.1), channel_id=1, source_target_pairs={{0,17},{1,16},{2,19},{3,18},{4,21},{5,20},{6,23},{7,22},{8,25},{9,... | collective-permute-start | bytes 24584 | tf_op jit(solution)/shard_map/ppermute | solution.py:323
  17.4 1.4 %collective-permute-done.4 = f32[16,128]{1,0:T(8,128)S(1)} collective-permute-done((f32[16,128]{1,0:T(8,128)S(1)}, f32[16,128]{1,0:T(8,128)S(1)}, u32[]{:S(2)}, u32[]{:S(2)}) %collective-permute-start.4) | collective-permute-done | bytes 8224 | tf_op jit(solution)/shard_map/ppermute | solution.py:323
  18.8 1.6 %collective-permute-start.5 = (f32[32,128]{1,0:T(8,128)S(1)}, f32[32,128]{1,0:T(8,128)S(1)}, u32[]{:S(2)}, u32[]{:S(2)}) collective-permute-start(f32[32,128]{1,0:T(8,128)S(1)} %pad_maximum_fusion.4), channel_id=1, source_target_pairs={{0,9},{1,8},{2,11},{3,10},{4,13},{5,12},{6,15},{7,14},{8,1},{9,0},... | collective-permute-start | bytes 49160 | tf_op jit(solution)/shard_map/ppermute | solution.py:323
  20.4 1.6 %collective-permute-done.5 = f32[32,128]{1,0:T(8,128)S(1)} collective-permute-done((f32[32,128]{1,0:T(8,128)S(1)}, f32[32,128]{1,0:T(8,128)S(1)}, u32[]{:S(2)}, u32[]{:S(2)}) %collective-permute-start.5) | collective-permute-done | bytes 16416 | tf_op jit(solution)/shard_map/ppermute | solution.py:323
  22.0 1.5 %collective-permute-start.6 = (f32[64,128]{1,0:T(8,128)S(1)}, f32[64,128]{1,0:T(8,128)S(1)}, u32[]{:S(2)}, u32[]{:S(2)}) collective-permute-start(f32[64,128]{1,0:T(8,128)S(1)} %pad_maximum_fusion.3), channel_id=1, source_target_pairs={{0,5},{1,4},{2,7},{3,6},{4,1},{5,0},{6,3},{7,2},{8,13},{9,12},{10,... | collective-permute-start | bytes 98312 | tf_op jit(solution)/shard_map/ppermute | solution.py:323
  23.5 0.9 %forecast.1 = (bf16[192,1024]{1,0:T(8,128)(2,1)S(1)}, f32[8,128]{1,0:T(8,128)S(1)}) custom-call(f32[512,128]{1,0:T(8,128)S(1)} %get-tuple-element.12.field_ref, f32[3,8,128]{2,1,0:T(8,128)S(1)} %get-tuple-element.13.flow_ref, f32[136,128]{1,0:T(8,128)S(1)} %collective-permute-done.odd_ref, f32[136,128]{1,0:T(8,128)S(1)} %collective-permute-done.1.even_ref, ...), custom_call_target="tpu_custom_call" | custom-call | flops 4000000 | bytes 600000 | tf_op jit(solution)/shard_map/forecast/pallas_call | solution.py:398
  24.3 1.0 %collective-permute-done.6 = f32[64,128]{1,0:T(8,128)S(1)} collective-permute-done((f32[64,128]{1,0:T(8,128)S(1)}, f32[64,128]{1,0:T(8,128)S(1)}, u32[]{:S(2)}, u32[]{:S(2)}) %collective-permute-start.6) | collective-permute-done | bytes 32800 | tf_op jit(solution)/shard_map/ppermute | solution.py:323
  25.3 2.6 %analyse.1 = f32[512,128]{1,0:T(8,128)} custom-call(bf16[192,1024]{1,0:T(8,128)(2,1)S(1)} %get-tuple-element.17.f_ref, f32[8,128]{1,0:T(8,128)S(1)} %get-tuple-element.18.mean_ref, f32[128,128]{1,0:T(8,128)S(1)} %pad_maximum_fusion.1.obs_ref), custom_call_target="tpu_custom_call" | custom-call | tf_op jit(solution)/shard_map/analyse/pallas_call | solution.py:407
  (5 shorter events, 0.0 us)
Async XLA Ops:
  1.1 4.6 %collective-permute-start = (f32[136,128]{1,0:T(8,128)S(1)}, f32[136,128]{1,0:T(8,128)S(1)}, u32[]{:S(2)}, u32[]{:S(2)}) collective-permute-start(f32[136,128]{1,0:T(8,128)S(1)} %get-tuple-element.14), channel_id=1, source_target_pairs={{0,1},{1,0},{2,3},{3,2},{4,8},{5,9},{6,10},{7,11},{8,4},{9,5},{10,... | collective-permute-start | bytes 208904 | tf_op jit(solution)/shard_map/ppermute | solution.py:313
  1.6 6.3 %collective-permute-start.1 = (f32[136,128]{1,0:T(8,128)S(1)}, f32[136,128]{1,0:T(8,128)S(1)}, u32[]{:S(2)}, u32[]{:S(2)}) collective-permute-start(f32[136,128]{1,0:T(8,128)S(1)} %get-tuple-element.15), channel_id=1, source_target_pairs={{0,4},{1,5},{2,6},{3,7},{4,0},{5,1},{6,2},{7,3},{8,12},{9,13},{10,... | collective-permute-start | bytes 208904 | tf_op jit(solution)/shard_map/ppermute | solution.py:313
  9.0 1.2 %collective-permute-start.2 = (f32[32,128]{1,0:T(8,128)S(1)}, f32[32,128]{1,0:T(8,128)S(1)}, u32[]{:S(2)}, u32[]{:S(2)}) collective-permute-start(f32[32,128]{1,0:T(8,128)S(1)} %observe.1), channel_id=1, source_target_pairs={{0,1},{1,0},{2,3},{3,2},{4,5},{5,4},{6,7},{7,6},{8,9},{9,8},{10,11... | collective-permute-start | bytes 49160 | tf_op jit(solution)/shard_map/ppermute | solution.py:323
  10.2 3.3 %collective-permute-start.3 = (f32[64,128]{1,0:T(8,128)S(1)}, f32[64,128]{1,0:T(8,128)S(1)}, u32[]{:S(2)}, u32[]{:S(2)}) collective-permute-start(f32[64,128]{1,0:T(8,128)S(1)} %pad_maximum_fusion.2), channel_id=1, source_target_pairs={{0,3},{1,2},{2,1},{3,0},{4,7},{5,6},{6,5},{7,4},{8,11},{9,10},{10,... | collective-permute-start | bytes 98312 | tf_op jit(solution)/shard_map/ppermute | solution.py:323
  14.0 4.7 %collective-permute-start.4 = (f32[16,128]{1,0:T(8,128)S(1)}, f32[16,128]{1,0:T(8,128)S(1)}, u32[]{:S(2)}, u32[]{:S(2)}) collective-permute-start(f32[16,128]{1,0:T(8,128)S(1)} %complete.1), channel_id=1, source_target_pairs={{0,17},{1,16},{2,19},{3,18},{4,21},{5,20},{6,23},{7,22},{8,25},{9,... | collective-permute-start | bytes 24584 | tf_op jit(solution)/shard_map/ppermute | solution.py:323
  18.8 3.2 %collective-permute-start.5 = (f32[32,128]{1,0:T(8,128)S(1)}, f32[32,128]{1,0:T(8,128)S(1)}, u32[]{:S(2)}, u32[]{:S(2)}) collective-permute-start(f32[32,128]{1,0:T(8,128)S(1)} %pad_maximum_fusion.4), channel_id=1, source_target_pairs={{0,9},{1,8},{2,11},{3,10},{4,13},{5,12},{6,15},{7,14},{8,1},{9,0},... | collective-permute-start | bytes 49160 | tf_op jit(solution)/shard_map/ppermute | solution.py:323
  22.0 3.3 %collective-permute-start.6 = (f32[64,128]{1,0:T(8,128)S(1)}, f32[64,128]{1,0:T(8,128)S(1)}, u32[]{:S(2)}, u32[]{:S(2)}) collective-permute-start(f32[64,128]{1,0:T(8,128)S(1)} %pad_maximum_fusion.3), channel_id=1, source_target_pairs={{0,5},{1,4},{2,7},{3,6},{4,1},{5,0},{6,3},{7,2},{8,13},{9,12},{10,... | collective-permute-start | bytes 98312 | tf_op jit(solution)/shard_map/ppermute | solution.py:323

commit v7 on v6

--- a/solution.py
+++ b/solution.py
@@ -31,6 +31,7 @@
 MID, OBS = EDGE, EDGE + 8
 VALUE, FACTOR, TO_WEST, TO_EAST, WEIGHTS = 64, 65, 66, 67, 72
 HBM = pl.BlockSpec(memory_space=pltpu.HBM)
+ANY = pl.BlockSpec(memory_space=pl.ANY)
 
 
 def coefficients(k, u, v):
@@ -45,41 +46,25 @@
     return jnp.concatenate([x, jnp.zeros((128 - x.shape[0], 128), F32)], axis=0).T
 
 
-def load(
-    members, count, n_obs, ens_hbm, flow_hbm, cell_hbm, value_hbm, var_hbm,
-    field_ref, flow_ref, obs_ref, even_ref, odd_ref, cell_ref, value_ref, var_ref, sems,
-):
-    order = [0, count - 1, 1, count - 2] + list(range(2, count - 2))
-    copies = [pltpu.make_async_copy(flow_hbm, flow_ref, sems.at[count])]
-    copies += [
-        pltpu.make_async_copy(ens_hbm.at[:, r, :], field_ref.at[pl.ds(r * members, members), :], sems.at[r]) for r in order
-    ]
-    small = [
-        pltpu.make_async_copy(src, dst, sems.at[count + 1 + i])
-        for i, (src, dst) in enumerate(((cell_hbm, cell_ref), (value_hbm, value_ref), (var_hbm, var_ref)))
-    ]
-    for copy in copies + small:
-        copy.start()
-    for copy in copies + small:
-        copy.wait()
+def load(members, count, ens_hbm, flow_hbm, even_ref, odd_ref, sems):
     is_even = lax.axis_index("gy") % 2 == 0
-
-    def grid_row(r):
-        return field_ref[r * members : (r + 1) * members, :]
-
-    top, bottom = [(grid_row(a), grid_row(b), flow_ref[:, a, :]) for a, b in ((0, 1), (count - 1, count - 2))]
-    for ref, first in ((even_ref, is_even), (odd_ref, jnp.logical_not(is_even))):
-        near, second, flow = [jnp.where(first, low, high) for low, high in zip(bottom, top)]
-        ref[0:members, :] = near
-        ref[members : 2 * members, :] = second
-        ref[2 * members : 2 * members + 3, :] = flow
-        ref[2 * members + 3 :, :] = jnp.zeros((5, 128), F32)
-    sub = rows_of((8, 128))
-    for i, (ref, rest) in enumerate(((cell_ref, 0.0), (value_ref, 0.0), (var_ref, 1.0))):
-        block = jnp.full((8, 128), rest, F32)
-        for j in range(n_obs):
-            block = jnp.where(sub == j, ref[j].astype(F32), block)
-        obs_ref[8 * i : 8 * i + 8, :] = block
+    for ref in (even_ref, odd_ref):
+        ref[2 * members :, :] = jnp.zeros((8, 128), F32)
+
+    def copies(refs):
+        for i, (ref, near, second) in enumerate(zip(refs, (count - 1, 0), (count - 2, 1))):
+            yield pltpu.make_async_copy(ens_hbm.at[:, near, :], ref.at[pl.ds(0, members), :], sems.at[3 * i])
+            yield pltpu.make_async_copy(ens_hbm.at[:, second, :], ref.at[pl.ds(members, members), :], sems.at[3 * i + 1])
+            yield pltpu.make_async_copy(flow_hbm.at[:, near, :], ref.at[pl.ds(2 * members, 3), :], sems.at[3 * i + 2])
+
+    def bring(refs):
+        for copy in list(copies(refs)):
+            copy.start()
+        for copy in list(copies(refs)):
+            copy.wait()
+
+    pl.when(is_even)(lambda: bring((even_ref, odd_ref)))
+    pl.when(jnp.logical_not(is_even))(lambda: bring((odd_ref, even_ref)))
 
 
 def halo_rows(even_ref, odd_ref, members):
@@ -109,35 +94,49 @@
     return field
 
 
-def observe(members, count, n_obs, field_ref, flow_ref, obs_ref, odd_ref, even_ref, out_ref, tall_ref):
-    north, south = halo_rows(even_ref, odd_ref, members)
-    field = tall_field(field_ref, north, south, members, count)
-    own, up, down, left, right = tall_coefficients(tall_ref, flow_ref, north[2], south[2], count)
+def spread(w, coeffs, lane):
+    own, up, down, left, right = coeffs
+    to_west, to_east = left * w, right * w
+    inside = (
+        own * w
+        + pltpu.roll(up * w, EDGE - 1, 0)
+        + pltpu.roll(down * w, 1, 0)
+        + jnp.where(lane == 127, 0.0, shifted(to_west, -1))
+        + jnp.where(lane == 0, 0.0, shifted(to_east, 1))
+    )
+    has_west = lax.axis_index("gx") > 0
+    has_east = lax.axis_index("gx") < lax.axis_size("gx") - 1
+    return inside, jnp.where(has_west, to_west[:, 0:1], 0.0), jnp.where(has_east, to_east[:, 127:128], 0.0)
+
+
+def prepare(
+    members, count, n_obs, ens_hbm, flow_hbm, cell_hbm, value_hbm, var_hbm, sent_ref,
+    field_ref, flow_ref, packed_ref, meta_ref, weight_ref, rest_ref, cell_ref, value_ref, var_ref, tall_ref, sems,
+):
+    copies = [
+        pltpu.make_async_copy(ens_hbm.at[:, r, :], field_ref.at[pl.ds(r * members, members), :], sems.at[r])
+        for r in range(count)
+    ]
+    pairs = ((flow_hbm, flow_ref), (cell_hbm, cell_ref), (value_hbm, value_ref), (var_hbm, var_ref))
+    copies += [pltpu.make_async_copy(src, dst, sems.at[count + i]) for i, (src, dst) in enumerate(pairs)]
+    for copy in copies:
+        copy.start()
+    for copy in copies:
+        copy.wait()
     lane, sub = lanes((EDGE, 128)), rows_of((EDGE, 128))
     wide = lanes((members, 128))
-    has_west = lax.axis_index("gx") > 0
-    has_east = lax.axis_index("gx") < lax.axis_size("gx") - 1
-
-    def spread(w):
-        to_west, to_east = left * w, right * w
-        inside = (
-            own * w
-            + pltpu.roll(up * w, EDGE - 1, 0)
-            + pltpu.roll(down * w, 1, 0)
-            + jnp.where(lane == 127, 0.0, shifted(to_west, -1))
-            + jnp.where(lane == 0, 0.0, shifted(to_east, 1))
-        )
-        return inside, jnp.where(has_west, to_west[:, 0:1], 0.0), jnp.where(has_east, to_east[:, 127:128], 0.0)
-
+    nothing = jnp.zeros((3, 128), F32)
+    coeffs = tall_coefficients(tall_ref, flow_ref, nothing, nothing, count)
+    coeffs = (jnp.where(sub < count, coeffs[0], 0.0),) + coeffs[1:]
+    own, up, down, left, right = coeffs
+    field = [field_ref[r * members : (r + 1) * members, :] for r in range(count)]
     packed = jnp.zeros((members, 128), F32)
     second = jnp.zeros((members, 128), F32)
-    for r in range(-1, count + 1):
-        x, at = field[r], r % EDGE
-        packed = jnp.where(wide == at, shifted(x, at), packed)
-        packed = jnp.where(wide == EDGE + at, shifted(x, EDGE + at - 127), packed)
-        if 0 <= r < count:
-            second = jnp.where(wide == at, shifted(x, at - 1), second)
-            second = jnp.where(wide == EDGE + at, shifted(x, EDGE + at - 126), second)
+    for r, x in enumerate(field):
+        packed = jnp.where(wide == r, shifted(x, r), packed)
+        packed = jnp.where(wide == EDGE + r, shifted(x, EDGE + r - 127), packed)
+        second = jnp.where(wide == r, shifted(x, r - 1), second)
+        second = jnp.where(wide == EDGE + r, shifted(x, EDGE + r - 126), second)
 
     def edge_row(low, high):
         both = jnp.where(lane == sub, low[:, 0:1], jnp.where(lane == sub + EDGE, high[:, 127:128], 0.0))
@@ -145,29 +144,75 @@
 
     middle = (
         edge_row(own, own) * packed
-        + edge_row(up, up) * jnp.where(wide % EDGE == 0, shifted(packed, 1 - EDGE), shifted(packed, 1))
+        + edge_row(up, up) * shifted(packed, 1)
         + edge_row(down, down) * shifted(packed, -1)
         + edge_row(right, left) * second
     )
-    packed = jnp.where(wide < 2 * EDGE, packed, 0.0)
     packed = jnp.where((wide >= 32) & (wide < 40), shifted(middle, 32), packed)
     packed = jnp.where((wide >= 40) & (wide < 48), shifted(middle, 24), packed)
-    top_lane = lane[:8]
-    meta = jnp.where(top_lane == VALUE, obs_ref[8:16, :], 0.0)
-    meta = jnp.where(top_lane == FACTOR, lax.rsqrt(obs_ref[16:24, :]), meta)
+    top_lane, top_sub = lane[:8], sub[:8]
+    blocks = []
+    for ref, rest in ((value_ref, 0.0), (var_ref, 1.0)):
+        block = jnp.full((8, 128), rest, F32)
+        for j in range(n_obs):
+            block = jnp.where(top_sub == j, ref[j], block)
+        blocks.append(block)
+    meta = jnp.where(top_lane == VALUE, blocks[0], 0.0)
+    meta = jnp.where(top_lane == FACTOR, lax.rsqrt(blocks[1]), meta)
     meta = jnp.where(top_lane == TO_WEST, left[:8, 0:1], meta)
     meta = jnp.where(top_lane == TO_EAST, right[:8, 127:128], meta)
-    position = (sub * 128 + lane).astype(F32)
     for j in range(n_obs):
-        here = jnp.where((sub < count) & (position == obs_ref[j : j + 1, :]), 1.0, 0.0)
-        w, mid_west, mid_east = spread(here)
-        w, west, east = spread(w)
-        total = w[EDGE - 2 : EDGE - 1, :] * field[-2]
-        for r in range(-1, count + 2):
-            total = total + w[r % EDGE : r % EDGE + 1, :] * field[r]
+        here = jnp.where((sub < count) & (sub * 128 + lane == cell_ref[j]), 1.0, 0.0)
+        first, mid_west, mid_east = spread(here, coeffs, lane)
+        w, west, east = spread(first, coeffs, lane)
+        weight_ref[j] = first
+        rest_ref[j] = w
+        total = w[0:1, :] * field[0]
+        for r in range(1, count):
+            total = total + w[r : r + 1, :] * field[r]
         packed = jnp.where(wide == 48 + j, jnp.sum(total, axis=1, keepdims=True), packed)
-        for k, column in enumerate((west[:8], west[8:], east[:8], east[8:], mid_west[:8], mid_east[:8])):
-            meta = jnp.where(top_lane == WEIGHTS + k * n_obs + j, column, meta)
+        for k, column in ((0, west), (2, east), (4, mid_west), (5, mid_east)):
+            meta = jnp.where(top_lane == WEIGHTS + k * n_obs + j, column[:8], meta)
+    packed_ref[...] = packed
+    meta_ref[0:8, :] = meta
+    last = count - 1
+    fix = jnp.zeros((8, 128), F32)
+    for at, c, r, col in ((32, up, 0, 0), (40, up, 0, 127), (32 + last, down, last, 0), (40 + last, down, last, 127)):
+        fix = jnp.where(top_lane == at, c[r : r + 1, col : col + 1], fix)
+    meta_ref[8:16, :] = fix
+
+
+def observe(
+    members, count, n_obs, field_ref, flow_ref, packed_ref, meta_ref, weight_ref, rest_ref, odd_ref, even_ref,
+    out_ref, tall_ref,
+):
+    north, south = halo_rows(even_ref, odd_ref, members)
+    lane, sub = lanes((EDGE, 128)), rows_of((EDGE, 128))
+    wide = lanes((members, 128))
+    for k in range(3):
+        tall_ref[k] = jnp.zeros((EDGE, 128), F32)
+        tall_ref[k, count : count + 1, :] = south[2][k : k + 1]
+        tall_ref[k, EDGE - 1 : EDGE, :] = north[2][k : k + 1]
+    coeffs = coefficients(*[tall_ref[k] for k in range(3)])
+    coeffs = (jnp.where((sub == count) | (sub == EDGE - 1), coeffs[0], 0.0),) + coeffs[1:]
+    rows = {-2: north[1], -1: north[0], count: south[0], count + 1: south[1]}
+    tile_rows = {r: field_ref[r * members : (r + 1) * members, :] for r in (0, count - 1)}
+    packed, meta, fix = packed_ref[...], meta_ref[0:8, :], meta_ref[8:9, :]
+    for x, slot, at in ((rows[-1], EDGE - 1, 0), (rows[count], count, count - 1)):
+        packed = jnp.where(wide == slot, shifted(x, slot), packed)
+        packed = jnp.where(wide == EDGE + slot, shifted(x, EDGE + slot - 127), packed)
+        moved = jnp.where(wide == 32 + at, shifted(x, 32 + at), 0.0)
+        moved = jnp.where(wide == 40 + at, shifted(x, 40 + at - 127), moved)
+        packed = packed + fix * moved
+    top_lane = lane[:8]
+    for j in range(n_obs):
+        w, west, east = spread(weight_ref[j], coeffs, lane)
+        all_w = w + rest_ref[j]
+        total = sum(all_w[r % EDGE : r % EDGE + 1, :] * x for r, x in rows.items())
+        total += sum(w[r : r + 1, :] * x for r, x in tile_rows.items())
+        packed = jnp.where(wide == 48 + j, packed + jnp.sum(total, axis=1, keepdims=True), packed)
+        for k, column in ((1, west), (3, east)):
+            meta = jnp.where(top_lane == WEIGHTS + k * n_obs + j, column[8:], meta)
     turned = jnp.concatenate([packed, jnp.zeros((128 - members, 128), F32)], axis=0).T
     out_ref[0:EDGE, :] = turned[0:EDGE] + shifted(turned[EDGE : 2 * EDGE], 64)
     out_ref[MID : MID + 8, :] = turned[32:40] + shifted(turned[40:48], 64)
@@ -363,30 +408,40 @@
     def shape(*dims):
         return jax.ShapeDtypeStruct(dims + (width,), F32)
 
-    field, tile_flow, obs, rows_even, rows_odd = call(
-        functools.partial(load, members, count, n_obs),
-        out_shape=[shape(members * count), shape(3, count), shape(24)] + [shape(2 * members + 8)] * 2,
-        in_specs=[HBM] * 5,
-        out_specs=[VMEM] * 5,
+    inputs = [
+        pltpu.with_memory_space_constraint(x, pltpu.HBM)
+        for x in (ensemble, flow, obs_cell.reshape(-1), obs_value.reshape(-1), obs_var.reshape(-1))
+    ]
+    rows_even, rows_odd = call(
+        functools.partial(load, members, count),
+        out_shape=[shape(2 * members + 8)] * 2,
+        in_specs=[HBM] * 2,
+        out_specs=[VMEM] * 2,
+        scratch_shapes=[pltpu.SemaphoreType.DMA((6,))],
+        name="load",
+    )(*inputs[:2])
+    tall = pltpu.VMEM((3, EDGE, width), F32)
+    field, tile_flow, *ready = call(
+        functools.partial(prepare, members, count, n_obs),
+        out_shape=[shape(members * count), shape(3, count), shape(members), shape(16)] + [shape(n_obs, EDGE)] * 2,
+        in_specs=[HBM] * 5 + [ANY],
+        out_specs=[VMEM] * 6,
         scratch_shapes=[pltpu.SMEM((n_obs,), jnp.int32)]
         + [pltpu.SMEM((n_obs,), F32)] * 2
-        + [pltpu.SemaphoreType.DMA((count + 4,))],
-        name="load",
-    )(*[
-        pltpu.with_memory_space_constraint(x, pltpu.HBM)
-        for x in (ensemble, flow, obs_cell.reshape(-1), obs_value.reshape(-1), obs_var.reshape(-1))
-    ])
+        + [tall, pltpu.SemaphoreType.DMA((count + 4,))],
+        cost_estimate=pl.CostEstimate(flops=4 * 10**6, bytes_accessed=6 * 10**5, transcendentals=0),
+        name="prepare",
+    )(*inputs, rows_even)
     rows_odd = swap(rows_odd, "gy", 1)
     rows_even = swap(rows_even, "gy", 0)
-    tall = pltpu.VMEM((3, EDGE, width), F32)
     block = call(
         functools.partial(observe, members, count, n_obs),
         out_shape=shape(BLOCK),
-        in_specs=[VMEM] * 5,
+        in_specs=[VMEM] * 8,
         out_specs=VMEM,
         scratch_shapes=[tall],
         name="observe",
-    )(field, tile_flow, obs, rows_odd, rows_even)
+    )(field, tile_flow, *ready, rows_odd, rows_even)
     blocks = row_blocks(block)
     packet = call(
         functools.partial(complete, members, n_obs, size),

time: 28.1 us -> 27.3 us (0.972)
  waiting for transfers between devices: 9.4 us -> 7.36 us
  Pallas kernels: 6.11 us -> 7.26 us
    ppermute x2, waiting for transfers between devices: 2.29 us -> 0.25 us  [swap(): return lax.ppermute(x, ('gy', 'gx'), pairs)]
    pallas_call x1 -> x2, Pallas kernels: 1.04 us -> 2.9 us  [the longest x1 2.02 us: body(): call(functools.partial(prepare, members, count, n_obs), out_shape=[shape(...]
    pallas_call x1, Pallas kernels: 1.09 us -> 0.39 us  [body(): call(functools.partial(observe, members, count, n_obs), out_shape=shape(B...]
  transfers between devices with their start and end apart: 7 -> 7, of which waited for: 6 -> 6; matrix products, arithmetic and copies ran while one was open for 0% -> 0% of each run, Pallas kernels for 3% -> 11%
where the time goes in v7:
time: 27.3 us; the launch traced here: 27.1 us
  starting transfers between devices  12.4 us (45%)
  waiting for transfers between devices  7.36 us (27%)
  Pallas kernels  7.26 us (27%)
    ppermute x5, starting transfers between devices, doubled(): return jnp.concatenate([x, lax.ppermute(x, ('gy', 'gx'), pairs)], axis=0)  7.82 us
    ppermute x5, waiting for transfers between devices, doubled(): return jnp.concatenate([x, lax.ppermute(x, ('gy', 'gx'), pairs)], axis=0)  7.11 us
    ppermute x2, starting transfers between devices, swap(): return lax.ppermute(x, ('gy', 'gx'), pairs)  4.55 us
    pallas_call x1, Pallas kernels, body(): call(functools.partial(analyse, members, count), out_shape=shape(members...  2.62 us
    pallas_call x1, Pallas kernels, body(): call(functools.partial(prepare, members, count, n_obs), out_shape=[shape(...  2.02 us
    pallas_call x1, Pallas kernels, body(): call(functools.partial(load, members, count), out_shape=[shape(2 * member...  0.88 us
    pallas_call x1, Pallas kernels, body(): call(functools.partial(forecast, members, count, size), out_shape=[jax.Sh...  0.87 us
  transfers between devices with their start and end apart: 7, of which 6 were waited for; matrix products, arithmetic and copies ran while one was open for 0% of the time, Pallas kernels for 11%

profile of v7, /device:TPU:0, one launch (start us, length us, event | category | flops | bytes accessed | tf_op | source)
XLA Modules:
  0.0 27.1 jit_solution(13826288690627337962)
XLA Ops:
  0.0 0.9 %load.1 = (f32[136,128]{1,0:T(8,128)S(1)}, f32[136,128]{1,0:T(8,128)S(1)}) custom-call(f32[64,8,128]{2,1,0:T(8,128)} %ens_hbm.3, f32[3,8,128]{2,1,0:T(8,128)} %flow_hbm.3), custom_call_target="tpu_custom_call" | custom-call | tf_op jit(solution)/shard_map/load/pallas_call | solution.py:415
  0.9 0.5 %collective-permute-start = (f32[136,128]{1,0:T(8,128)S(1)}, f32[136,128]{1,0:T(8,128)S(1)}, u32[]{:S(2)}, u32[]{:S(2)}) collective-permute-start(f32[136,128]{1,0:T(8,128)S(1)} %get-tuple-element.18), channel_id=1, source_target_pairs={{0,1},{1,0},{2,3},{3,2},{4,8},{5,9},{6,10},{7,11},{8,4},{9,5},{10,... | collective-permute-start | bytes 208904 | tf_op jit(solution)/shard_map/ppermute | solution.py:358
  1.4 4.0 %collective-permute-start.1 = (f32[136,128]{1,0:T(8,128)S(1)}, f32[136,128]{1,0:T(8,128)S(1)}, u32[]{:S(2)}, u32[]{:S(2)}) collective-permute-start(f32[136,128]{1,0:T(8,128)S(1)} %get-tuple-element.15.sent_ref), channel_id=1, source_target_pairs={{0,4},{1,5},{2,6},{3,7},{4,0},{5,1},{6,2},{7,3},{8,12},{9,13},{10,... | collective-permute-start | bytes 208904 | tf_op jit(solution)/shard_map/ppermute | solution.py:358
  5.4 2.0 %prepare.1 = (f32[512,128]{1,0:T(8,128)S(1)}, f32[3,8,128]{2,1,0:T(8,128)S(1)}, f32[64,128]{1,0:T(8,128)S(1)}, f32[16,128]{1,0:T(8,128)S(1)}, f32[4,16,128]{2,1,0:T(8,128)S(1)}, /*index=5*/f32[4,16,128]{2,1,0:T(8,128)S(1)}) custom-call(f32[64,8,128]{2,1,0:T(8,128)} %ens_hbm.3, f32[3,8,128]{2,1,0:T(8,128)} %flow_hbm.3, s32[4]{0:T(128)} %bitcast.4, f32[4]{0:T(128)} %bitcast.5, ...), custom_call_target="tpu_custom_call" | custom-call | flops 4000000 | bytes 600000 | tf_op jit(solution)/shard_map/prepare/pallas_call | solution.py:424
  7.5 0.0 collective-permute-done.odd_ref
  7.5 0.2 collective-permute-done.1.even_ref
  7.7 0.4 %observe.1 = f32[32,128]{1,0:T(8,128)S(1)} custom-call(f32[512,128]{1,0:T(8,128)S(1)} %get-tuple-element.16.field_ref, f32[3,8,128]{2,1,0:T(8,128)S(1)} %get-tuple-element.17.flow_ref, f32[64,128]{1,0:T(8,128)S(1)} %get-tuple-element.19.packed_ref, f32[16,128]{1,0:T(8,128)S(1)} %get-tuple-element.20.meta_ref, ...), custom_call_target="tpu_custom_call" | custom-call | tf_op jit(solution)/shard_map/observe/pallas_call | solution.py:437
  8.1 0.1 collective-permute-start.2
  8.2 1.2 %collective-permute-done.2 = f32[32,128]{1,0:T(8,128)S(1)} collective-permute-done((f32[32,128]{1,0:T(8,128)S(1)}, f32[32,128]{1,0:T(8,128)S(1)}, u32[]{:S(2)}, u32[]{:S(2)}) %collective-permute-start.2) | collective-permute-done | bytes 16416 | tf_op jit(solution)/shard_map/ppermute | solution.py:368
  9.4 1.3 %collective-permute-start.3 = (f32[64,128]{1,0:T(8,128)S(1)}, f32[64,128]{1,0:T(8,128)S(1)}, u32[]{:S(2)}, u32[]{:S(2)}) collective-permute-start(f32[64,128]{1,0:T(8,128)S(1)} %pad_maximum_fusion.2), channel_id=1, source_target_pairs={{0,3},{1,2},{2,1},{3,0},{4,7},{5,6},{6,5},{7,4},{8,11},{9,10},{10,... | collective-permute-start | bytes 98312 | tf_op jit(solution)/shard_map/ppermute | solution.py:368
  10.6 2.1 %collective-permute-done.3 = f32[64,128]{1,0:T(8,128)S(1)} collective-permute-done((f32[64,128]{1,0:T(8,128)S(1)}, f32[64,128]{1,0:T(8,128)S(1)}, u32[]{:S(2)}, u32[]{:S(2)}) %collective-permute-start.3) | collective-permute-done | bytes 32800 | tf_op jit(solution)/shard_map/ppermute | solution.py:368
  12.7 0.5 %complete.1 = f32[16,128]{1,0:T(8,128)S(1)} custom-call(f32[128,128]{1,0:T(8,128)S(1)} %pad_maximum_fusion.blocks_ref), custom_call_target="tpu_custom_call" | custom-call | tf_op jit(solution)/shard_map/complete/pallas_call | solution.py:446
  13.2 3.4 %collective-permute-start.4 = (f32[16,128]{1,0:T(8,128)S(1)}, f32[16,128]{1,0:T(8,128)S(1)}, u32[]{:S(2)}, u32[]{:S(2)}) collective-permute-start(f32[16,128]{1,0:T(8,128)S(1)} %complete.1), channel_id=1, source_target_pairs={{0,17},{1,16},{2,19},{3,18},{4,21},{5,20},{6,23},{7,22},{8,25},{9,... | collective-permute-start | bytes 24584 | tf_op jit(solution)/shard_map/ppermute | solution.py:368
  16.6 1.4 %collective-permute-done.4 = f32[16,128]{1,0:T(8,128)S(1)} collective-permute-done((f32[16,128]{1,0:T(8,128)S(1)}, f32[16,128]{1,0:T(8,128)S(1)}, u32[]{:S(2)}, u32[]{:S(2)}) %collective-permute-start.4) | collective-permute-done | bytes 8224 | tf_op jit(solution)/shard_map/ppermute | solution.py:368
  17.9 1.6 %collective-permute-start.5 = (f32[32,128]{1,0:T(8,128)S(1)}, f32[32,128]{1,0:T(8,128)S(1)}, u32[]{:S(2)}, u32[]{:S(2)}) collective-permute-start(f32[32,128]{1,0:T(8,128)S(1)} %pad_maximum_fusion.4), channel_id=1, source_target_pairs={{0,9},{1,8},{2,11},{3,10},{4,13},{5,12},{6,15},{7,14},{8,1},{9,0},... | collective-permute-start | bytes 49160 | tf_op jit(solution)/shard_map/ppermute | solution.py:368
  19.5 1.6 %collective-permute-done.5 = f32[32,128]{1,0:T(8,128)S(1)} collective-permute-done((f32[32,128]{1,0:T(8,128)S(1)}, f32[32,128]{1,0:T(8,128)S(1)}, u32[]{:S(2)}, u32[]{:S(2)}) %collective-permute-start.5) | collective-permute-done | bytes 16416 | tf_op jit(solution)/shard_map/ppermute | solution.py:368
  21.1 1.5 %collective-permute-start.6 = (f32[64,128]{1,0:T(8,128)S(1)}, f32[64,128]{1,0:T(8,128)S(1)}, u32[]{:S(2)}, u32[]{:S(2)}) collective-permute-start(f32[64,128]{1,0:T(8,128)S(1)} %pad_maximum_fusion.3), channel_id=1, source_target_pairs={{0,5},{1,4},{2,7},{3,6},{4,1},{5,0},{6,3},{7,2},{8,13},{9,12},{10,... | collective-permute-start | bytes 98312 | tf_op jit(solution)/shard_map/ppermute | solution.py:368
  22.6 0.9 %forecast.1 = (bf16[192,1024]{1,0:T(8,128)(2,1)S(1)}, f32[8,128]{1,0:T(8,128)S(1)}) custom-call(f32[512,128]{1,0:T(8,128)S(1)} %get-tuple-element.16.field_ref, f32[3,8,128]{2,1,0:T(8,128)S(1)} %get-tuple-element.17.flow_ref, f32[136,128]{1,0:T(8,128)S(1)} %collective-permute-done.odd_ref, f32[136,128]{1,0:T(8,128)S(1)} %collective-permute-done.1.even_ref, ...), custom_call_target="tpu_custom_call" | custom-call | flops 4000000 | bytes 600000 | tf_op jit(solution)/shard_map/forecast/pallas_call | solution.py:453
  23.5 1.0 %collective-permute-done.6 = f32[64,128]{1,0:T(8,128)S(1)} collective-permute-done((f32[64,128]{1,0:T(8,128)S(1)}, f32[64,128]{1,0:T(8,128)S(1)}, u32[]{:S(2)}, u32[]{:S(2)}) %collective-permute-start.6) | collective-permute-done | bytes 32800 | tf_op jit(solution)/shard_map/ppermute | solution.py:368
  24.4 2.6 %analyse.1 = f32[512,128]{1,0:T(8,128)} custom-call(bf16[192,1024]{1,0:T(8,128)(2,1)S(1)} %get-tuple-element.23.f_ref, f32[8,128]{1,0:T(8,128)S(1)} %get-tuple-element.24.mean_ref, f32[128,128]{1,0:T(8,128)S(1)} %pad_maximum_fusion.1.obs_ref), custom_call_target="tpu_custom_call" | custom-call | tf_op jit(solution)/shard_map/analyse/pallas_call | solution.py:462
  (5 shorter events, 0.0 us)
Async XLA Ops:
  0.9 6.6 %collective-permute-start = (f32[136,128]{1,0:T(8,128)S(1)}, f32[136,128]{1,0:T(8,128)S(1)}, u32[]{:S(2)}, u32[]{:S(2)}) collective-permute-start(f32[136,128]{1,0:T(8,128)S(1)} %get-tuple-element.18), channel_id=1, source_target_pairs={{0,1},{1,0},{2,3},{3,2},{4,8},{5,9},{6,10},{7,11},{8,4},{9,5},{10,... | collective-permute-start | bytes 208904 | tf_op jit(solution)/shard_map/ppermute | solution.py:358
  1.4 6.3 %collective-permute-start.1 = (f32[136,128]{1,0:T(8,128)S(1)}, f32[136,128]{1,0:T(8,128)S(1)}, u32[]{:S(2)}, u32[]{:S(2)}) collective-permute-start(f32[136,128]{1,0:T(8,128)S(1)} %get-tuple-element.15.sent_ref), channel_id=1, source_target_pairs={{0,4},{1,5},{2,6},{3,7},{4,0},{5,1},{6,2},{7,3},{8,12},{9,13},{10,... | collective-permute-start | bytes 208904 | tf_op jit(solution)/shard_map/ppermute | solution.py:358
  8.1 1.2 %collective-permute-start.2 = (f32[32,128]{1,0:T(8,128)S(1)}, f32[32,128]{1,0:T(8,128)S(1)}, u32[]{:S(2)}, u32[]{:S(2)}) collective-permute-start(f32[32,128]{1,0:T(8,128)S(1)} %observe.1), channel_id=1, source_target_pairs={{0,1},{1,0},{2,3},{3,2},{4,5},{5,4},{6,7},{7,6},{8,9},{9,8},{10,11... | collective-permute-start | bytes 49160 | tf_op jit(solution)/shard_map/ppermute | solution.py:368
  9.4 3.3 %collective-permute-start.3 = (f32[64,128]{1,0:T(8,128)S(1)}, f32[64,128]{1,0:T(8,128)S(1)}, u32[]{:S(2)}, u32[]{:S(2)}) collective-permute-start(f32[64,128]{1,0:T(8,128)S(1)} %pad_maximum_fusion.2), channel_id=1, source_target_pairs={{0,3},{1,2},{2,1},{3,0},{4,7},{5,6},{6,5},{7,4},{8,11},{9,10},{10,... | collective-permute-start | bytes 98312 | tf_op jit(solution)/shard_map/ppermute | solution.py:368
  13.2 4.7 %collective-permute-start.4 = (f32[16,128]{1,0:T(8,128)S(1)}, f32[16,128]{1,0:T(8,128)S(1)}, u32[]{:S(2)}, u32[]{:S(2)}) collective-permute-start(f32[16,128]{1,0:T(8,128)S(1)} %complete.1), channel_id=1, source_target_pairs={{0,17},{1,16},{2,19},{3,18},{4,21},{5,20},{6,23},{7,22},{8,25},{9,... | collective-permute-start | bytes 24584 | tf_op jit(solution)/shard_map/ppermute | solution.py:368
  17.9 3.2 %collective-permute-start.5 = (f32[32,128]{1,0:T(8,128)S(1)}, f32[32,128]{1,0:T(8,128)S(1)}, u32[]{:S(2)}, u32[]{:S(2)}) collective-permute-start(f32[32,128]{1,0:T(8,128)S(1)} %pad_maximum_fusion.4), channel_id=1, source_target_pairs={{0,9},{1,8},{2,11},{3,10},{4,13},{5,12},{6,15},{7,14},{8,1},{9,0},... | collective-permute-start | bytes 49160 | tf_op jit(solution)/shard_map/ppermute | solution.py:368
  21.1 3.3 %collective-permute-start.6 = (f32[64,128]{1,0:T(8,128)S(1)}, f32[64,128]{1,0:T(8,128)S(1)}, u32[]{:S(2)}, u32[]{:S(2)}) collective-permute-start(f32[64,128]{1,0:T(8,128)S(1)} %pad_maximum_fusion.3), channel_id=1, source_target_pairs={{0,5},{1,4},{2,7},{3,6},{4,1},{5,0},{6,3},{7,2},{8,13},{9,12},{10,... | collective-permute-start | bytes 98312 | tf_op jit(solution)/shard_map/ppermute | solution.py:368

commit v8 on v7

--- a/solution.py
+++ b/solution.py
@@ -32,6 +32,7 @@
 VALUE, FACTOR, TO_WEST, TO_EAST, WEIGHTS = 64, 65, 66, 67, 72
 HBM = pl.BlockSpec(memory_space=pltpu.HBM)
 ANY = pl.BlockSpec(memory_space=pl.ANY)
+ORDER = (2, 3, 1)
 
 
 def coefficients(k, u, v):
@@ -300,7 +301,7 @@
         column = {(q, c): spread(q, c) for q in rest[1:] for c in range(start, end)}
         column.update(ahead)
         more = range(end, end + size if p + 1 < len(part) else end)
-        column.update({(q, c): spread(q, c) for q in rest[:2] for c in more})
+        column.update({(q, c): spread(q, c) for q in rest[1:2] for c in more})
         mine = (lane >= start) & (lane < end)
         for q in rest:
             part[q] = jnp.where(mine, 0.0, part[q])
@@ -311,10 +312,11 @@
             found = jnp.where(sub == j, value, found)
             inverse = 1.0 / value
             unit = jnp.where(lane[:1] == at, 1.0, part[p][j : j + 1, :])
-            pivots = {c: column[p, c][j : j + 1, :] for c in range(at + 1, end + len(more))}
+            pivots = {c: column[p, c][j : j + 1, :] for c in range(at + 1, end)}
+            pivots.update({c: column[p + 1, at][c - end : c - end + 1, :] for c in more})
             for q in rest:
                 factor = column[q, at] * inverse
-                for c in range(at + 1, end + (len(more) if q <= p + 1 else 0)):
+                for c in range(at + 1, end + (len(more) if q == p + 1 else 0)):
                     column[q, c] = column[q, c] - factor * pivots[c]
                 if q == p:
                     factor = jnp.where(sub > j, factor, 0.0)
@@ -324,8 +326,9 @@
     return jnp.concatenate(part, axis=0), jnp.concatenate(pivot, axis=0)
 
 
-def analyse(members, count, f_ref, mean_ref, obs_ref, out_ref):
-    scaled = obs_ref[...]
+def analyse(members, count, f_ref, mean_ref, *refs):
+    out_ref = refs[-1]
+    scaled = jnp.concatenate([ref[...] for ref in refs[:-1]], axis=0)
     full = lax.dot_general(
         scaled, scaled, (((0,), (0,)), ((), ())), precision=HIGHEST, preferred_element_type=F32
     )
@@ -362,10 +365,14 @@
     return size & (size - 1) == 0
 
 
-def doubled(x, flip_y, flip_x):
+def partner(x, flip_y, flip_x):
     ny, nx = lax.axis_size("gy"), lax.axis_size("gx")
     pairs = [(a * nx + b, (a ^ flip_y) * nx + (b ^ flip_x)) for a in range(ny) for b in range(nx)]
-    return jnp.concatenate([x, lax.ppermute(x, ("gy", "gx"), pairs)], axis=0)
+    return lax.ppermute(x, ("gy", "gx"), pairs)
+
+
+def doubled(x, flip_y, flip_x):
+    return jnp.concatenate([x, partner(x, flip_y, flip_x)], axis=0)
 
 
 def row_blocks(block):
@@ -390,13 +397,15 @@
 
 
 def all_rows(packet):
-    step = lax.axis_size("gy")
-    if not two_power(step):
-        return lax.all_gather(packet, "gy", tiled=True)
-    while step > 1:
+    size = lax.axis_size("gy")
+    if not two_power(size) or size < 4:
+        return [lax.all_gather(packet, "gy", tiled=True)]
+    flip_x = 1 - lax.axis_size("gx") % 2
+    step = size // 2
+    while step > 2:
+        packet = doubled(packet, step, flip_x)
         step //= 2
-        packet = doubled(packet, step, 1 - lax.axis_size("gx") % 2)
-    return packet
+    return [packet] + [partner(packet, flip_y, flip_x) for flip_y in ORDER]
 
 
 def body(ensemble, flow, obs_cell, obs_value, obs_var):
@@ -459,13 +468,14 @@
         cost_estimate=pl.CostEstimate(flops=4 * 10**6, bytes_accessed=6 * 10**5, transcendentals=0),
         name="forecast",
     )(field, tile_flow, rows_odd, rows_even, blocks)
+    packets = all_rows(packet)
     out = call(
         functools.partial(analyse, members, count),
         out_shape=shape(members * count),
-        in_specs=[VMEM] * 3,
+        in_specs=[VMEM] * (2 + len(packets)),
         out_specs=VMEM,
         name="analyse",
-    )(anomaly, mean, all_rows(packet))
+    )(anomaly, mean, *packets)
     return out.reshape(ensemble.shape)
 
 

time: 27.3 us -> 26.9 us (0.985)
  waiting for transfers between devices: 7.36 us -> 7 us
    ppermute x5 -> x6, waiting for transfers between devices: 7.11 us -> 6.75 us  [partner(): return lax.ppermute(x, ('gy', 'gx'), pairs)]
    ppermute x5 -> x6, starting transfers between devices: 7.82 us -> 7.84 us  [partner(): return lax.ppermute(x, ('gy', 'gx'), pairs)]
  transfers between devices with their start and end apart: 7 -> 8, of which waited for: 6 -> 6; matrix products, arithmetic and copies ran while one was open for 0% -> 0% of each run, Pallas kernels for 11% -> 11%
where the time goes in v8:
time: 26.9 us; the launch traced here: 26.7 us
  starting transfers between devices  12.4 us (46%)
  Pallas kernels  7.19 us (27%)
  waiting for transfers between devices  7 us (26%)
    ppermute x6, starting transfers between devices, partner(): return lax.ppermute(x, ('gy', 'gx'), pairs)  7.84 us
    ppermute x6, waiting for transfers between devices, partner(): return lax.ppermute(x, ('gy', 'gx'), pairs)  6.75 us
    ppermute x2, starting transfers between devices, swap(): return lax.ppermute(x, ('gy', 'gx'), pairs)  4.55 us
    pallas_call x1, Pallas kernels, body(): call(functools.partial(analyse, members, count), out_shape=shape(members...  2.55 us
    pallas_call x1, Pallas kernels, body(): call(functools.partial(prepare, members, count, n_obs), out_shape=[shape(...  2.02 us
    pallas_call x1, Pallas kernels, body(): call(functools.partial(load, members, count), out_shape=[shape(2 * member...  0.88 us
    pallas_call x1, Pallas kernels, body(): call(functools.partial(forecast, members, count, size), out_shape=[jax.Sh...  0.87 us
  transfers between devices with their start and end apart: 8, of which 6 were waited for; matrix products, arithmetic and copies ran while one was open for 0% of the time, Pallas kernels for 11%

profile of v8, /device:TPU:0, one launch (start us, length us, event | category | flops | bytes accessed | tf_op | source)
XLA Modules:
  0.0 26.7 jit_solution(7439343296452278074)
XLA Ops:
  0.0 0.9 %load.1 = (f32[136,128]{1,0:T(8,128)S(1)}, f32[136,128]{1,0:T(8,128)S(1)}) custom-call(f32[64,8,128]{2,1,0:T(8,128)} %ens_hbm.3, f32[3,8,128]{2,1,0:T(8,128)} %flow_hbm.3), custom_call_target="tpu_custom_call" | custom-call | tf_op jit(solution)/shard_map/load/pallas_call | solution.py:424
  0.9 0.5 %collective-permute-start = (f32[136,128]{1,0:T(8,128)S(1)}, f32[136,128]{1,0:T(8,128)S(1)}, u32[]{:S(2)}, u32[]{:S(2)}) collective-permute-start(f32[136,128]{1,0:T(8,128)S(1)} %get-tuple-element.18), channel_id=1, source_target_pairs={{0,1},{1,0},{2,3},{3,2},{4,8},{5,9},{6,10},{7,11},{8,4},{9,5},{10,... | collective-permute-start | bytes 208904 | tf_op jit(solution)/shard_map/ppermute | solution.py:361
  1.4 4.0 %collective-permute-start.1 = (f32[136,128]{1,0:T(8,128)S(1)}, f32[136,128]{1,0:T(8,128)S(1)}, u32[]{:S(2)}, u32[]{:S(2)}) collective-permute-start(f32[136,128]{1,0:T(8,128)S(1)} %get-tuple-element.15.sent_ref), channel_id=1, source_target_pairs={{0,4},{1,5},{2,6},{3,7},{4,0},{5,1},{6,2},{7,3},{8,12},{9,13},{10,... | collective-permute-start | bytes 208904 | tf_op jit(solution)/shard_map/ppermute | solution.py:361
  5.4 2.0 %prepare.1 = (f32[512,128]{1,0:T(8,128)S(1)}, f32[3,8,128]{2,1,0:T(8,128)S(1)}, f32[64,128]{1,0:T(8,128)S(1)}, f32[16,128]{1,0:T(8,128)S(1)}, f32[4,16,128]{2,1,0:T(8,128)S(1)}, /*index=5*/f32[4,16,128]{2,1,0:T(8,128)S(1)}) custom-call(f32[64,8,128]{2,1,0:T(8,128)} %ens_hbm.3, f32[3,8,128]{2,1,0:T(8,128)} %flow_hbm.3, s32[4]{0:T(128)} %bitcast.4, f32[4]{0:T(128)} %bitcast.5, ...), custom_call_target="tpu_custom_call" | custom-call | flops 4000000 | bytes 600000 | tf_op jit(solution)/shard_map/prepare/pallas_call | solution.py:433
  7.5 0.0 collective-permute-done.odd_ref
  7.5 0.2 collective-permute-done.1.even_ref
  7.7 0.4 %observe.1 = f32[32,128]{1,0:T(8,128)S(1)} custom-call(f32[512,128]{1,0:T(8,128)S(1)} %get-tuple-element.16.field_ref, f32[3,8,128]{2,1,0:T(8,128)S(1)} %get-tuple-element.17.flow_ref, f32[64,128]{1,0:T(8,128)S(1)} %get-tuple-element.19.packed_ref, f32[16,128]{1,0:T(8,128)S(1)} %get-tuple-element.20.meta_ref, ...), custom_call_target="tpu_custom_call" | custom-call | tf_op jit(solution)/shard_map/observe/pallas_call | solution.py:446
  8.1 0.1 collective-permute-start.2
  8.2 1.2 %collective-permute-done.2 = f32[32,128]{1,0:T(8,128)S(1)} collective-permute-done((f32[32,128]{1,0:T(8,128)S(1)}, f32[32,128]{1,0:T(8,128)S(1)}, u32[]{:S(2)}, u32[]{:S(2)}) %collective-permute-start.2) | collective-permute-done | bytes 16416 | tf_op jit(solution)/shard_map/ppermute | solution.py:371
  9.4 1.3 %collective-permute-start.3 = (f32[64,128]{1,0:T(8,128)S(1)}, f32[64,128]{1,0:T(8,128)S(1)}, u32[]{:S(2)}, u32[]{:S(2)}) collective-permute-start(f32[64,128]{1,0:T(8,128)S(1)} %pad_maximum_fusion.1), channel_id=1, source_target_pairs={{0,3},{1,2},{2,1},{3,0},{4,7},{5,6},{6,5},{7,4},{8,11},{9,10},{10,... | collective-permute-start | bytes 98312 | tf_op jit(solution)/shard_map/ppermute | solution.py:371
  10.6 2.1 %collective-permute-done.3 = f32[64,128]{1,0:T(8,128)S(1)} collective-permute-done((f32[64,128]{1,0:T(8,128)S(1)}, f32[64,128]{1,0:T(8,128)S(1)}, u32[]{:S(2)}, u32[]{:S(2)}) %collective-permute-start.3) | collective-permute-done | bytes 32800 | tf_op jit(solution)/shard_map/ppermute | solution.py:371
  12.7 0.5 %complete.1 = f32[16,128]{1,0:T(8,128)S(1)} custom-call(f32[128,128]{1,0:T(8,128)S(1)} %pad_maximum_fusion.blocks_ref), custom_call_target="tpu_custom_call" | custom-call | tf_op jit(solution)/shard_map/complete/pallas_call | solution.py:455
  13.2 3.4 %collective-permute-start.4 = (f32[16,128]{1,0:T(8,128)S(1)}, f32[16,128]{1,0:T(8,128)S(1)}, u32[]{:S(2)}, u32[]{:S(2)}) collective-permute-start(f32[16,128]{1,0:T(8,128)S(1)} %complete.1), channel_id=1, source_target_pairs={{0,17},{1,16},{2,19},{3,18},{4,21},{5,20},{6,23},{7,22},{8,25},{9,... | collective-permute-start | bytes 24584 | tf_op jit(solution)/shard_map/ppermute | solution.py:371
  16.6 1.4 %collective-permute-done.4 = f32[16,128]{1,0:T(8,128)S(1)} collective-permute-done((f32[16,128]{1,0:T(8,128)S(1)}, f32[16,128]{1,0:T(8,128)S(1)}, u32[]{:S(2)}, u32[]{:S(2)}) %collective-permute-start.4) | collective-permute-done | bytes 8224 | tf_op jit(solution)/shard_map/ppermute | solution.py:371
  17.9 1.5 %collective-permute-start.7 = (f32[32,128]{1,0:T(8,128)S(1)}, f32[32,128]{1,0:T(8,128)S(1)}, u32[]{:S(2)}, u32[]{:S(2)}) collective-permute-start(f32[32,128]{1,0:T(8,128)S(1)} %pad_maximum_fusion.2.refs_0_), channel_id=1, source_target_pairs={{0,5},{1,4},{2,7},{3,6},{4,1},{5,0},{6,3},{7,2},{8,13},{9,12},{10,... | collective-permute-start | bytes 49160 | tf_op jit(solution)/shard_map/ppermute | solution.py:371
  19.4 1.5 %collective-permute-start.6 = (f32[32,128]{1,0:T(8,128)S(1)}, f32[32,128]{1,0:T(8,128)S(1)}, u32[]{:S(2)}, u32[]{:S(2)}) collective-permute-start(f32[32,128]{1,0:T(8,128)S(1)} %pad_maximum_fusion.2.refs_0_), channel_id=1, source_target_pairs={{0,13},{1,12},{2,15},{3,14},{4,9},{5,8},{6,11},{7,10},{8,5},{9,4},... | collective-permute-start | bytes 49160 | tf_op jit(solution)/shard_map/ppermute | solution.py:371
  20.9 0.1 collective-permute-start.5
  21.1 0.9 %forecast.1 = (bf16[192,1024]{1,0:T(8,128)(2,1)S(1)}, f32[8,128]{1,0:T(8,128)S(1)}) custom-call(f32[512,128]{1,0:T(8,128)S(1)} %get-tuple-element.16.field_ref, f32[3,8,128]{2,1,0:T(8,128)S(1)} %get-tuple-element.17.flow_ref, f32[136,128]{1,0:T(8,128)S(1)} %collective-permute-done.odd_ref, f32[136,128]{1,0:T(8,128)S(1)} %collective-permute-done.1.even_ref, ...), custom_call_target="tpu_custom_call" | custom-call | flops 4000000 | bytes 600000 | tf_op jit(solution)/shard_map/forecast/pallas_call | solution.py:462
  21.9 0.0 collective-permute-done.7.refs_3_
  21.9 1.6 %collective-permute-done.6.refs_2_ = f32[32,128]{1,0:T(8,128)S(1)} collective-permute-done((f32[32,128]{1,0:T(8,128)S(1)}, f32[32,128]{1,0:T(8,128)S(1)}, u32[]{:S(2)}, u32[]{:S(2)}) %collective-permute-start.6) | collective-permute-done | bytes 16416 | tf_op jit(solution)/shard_map/ppermute | solution.py:371
  23.5 0.6 %collective-permute-done.5.refs_1_ = f32[32,128]{1,0:T(8,128)S(1)} collective-permute-done((f32[32,128]{1,0:T(8,128)S(1)}, f32[32,128]{1,0:T(8,128)S(1)}, u32[]{:S(2)}, u32[]{:S(2)}) %collective-permute-start.5) | collective-permute-done | bytes 16416 | tf_op jit(solution)/shard_map/ppermute | solution.py:371
  24.1 2.6 %analyse.1 = f32[512,128]{1,0:T(8,128)} custom-call(bf16[192,1024]{1,0:T(8,128)(2,1)S(1)} %get-tuple-element.23.f_ref, f32[8,128]{1,0:T(8,128)S(1)} %get-tuple-element.24.mean_ref, f32[32,128]{1,0:T(8,128)S(1)} %pad_maximum_fusion.2.refs_0_, f32[32,128]{1,0:T(8,128)S(1)} %collective-permute-done.5.refs_1_, f32[32,128]{1,0:T(8,128)S(1)} %collective-permute-done.6.refs_2_, ...), custom_call_target="tpu_custom_call" | custom-call | tf_op jit(solution)/shard_map/analyse/pallas_call | solution.py:472
  (3 shorter events, 0.0 us)
Async XLA Ops:
  0.9 6.6 %collective-permute-start = (f32[136,128]{1,0:T(8,128)S(1)}, f32[136,128]{1,0:T(8,128)S(1)}, u32[]{:S(2)}, u32[]{:S(2)}) collective-permute-start(f32[136,128]{1,0:T(8,128)S(1)} %get-tuple-element.18), channel_id=1, source_target_pairs={{0,1},{1,0},{2,3},{3,2},{4,8},{5,9},{6,10},{7,11},{8,4},{9,5},{10,... | collective-permute-start | bytes 208904 | tf_op jit(solution)/shard_map/ppermute | solution.py:361
  1.4 6.3 %collective-permute-start.1 = (f32[136,128]{1,0:T(8,128)S(1)}, f32[136,128]{1,0:T(8,128)S(1)}, u32[]{:S(2)}, u32[]{:S(2)}) collective-permute-start(f32[136,128]{1,0:T(8,128)S(1)} %get-tuple-element.15.sent_ref), channel_id=1, source_target_pairs={{0,4},{1,5},{2,6},{3,7},{4,0},{5,1},{6,2},{7,3},{8,12},{9,13},{10,... | collective-permute-start | bytes 208904 | tf_op jit(solution)/shard_map/ppermute | solution.py:361
  8.1 1.2 %collective-permute-start.2 = (f32[32,128]{1,0:T(8,128)S(1)}, f32[32,128]{1,0:T(8,128)S(1)}, u32[]{:S(2)}, u32[]{:S(2)}) collective-permute-start(f32[32,128]{1,0:T(8,128)S(1)} %observe.1), channel_id=1, source_target_pairs={{0,1},{1,0},{2,3},{3,2},{4,5},{5,4},{6,7},{7,6},{8,9},{9,8},{10,11... | collective-permute-start | bytes 49160 | tf_op jit(solution)/shard_map/ppermute | solution.py:371
  9.4 3.3 %collective-permute-start.3 = (f32[64,128]{1,0:T(8,128)S(1)}, f32[64,128]{1,0:T(8,128)S(1)}, u32[]{:S(2)}, u32[]{:S(2)}) collective-permute-start(f32[64,128]{1,0:T(8,128)S(1)} %pad_maximum_fusion.1), channel_id=1, source_target_pairs={{0,3},{1,2},{2,1},{3,0},{4,7},{5,6},{6,5},{7,4},{8,11},{9,10},{10,... | collective-permute-start | bytes 98312 | tf_op jit(solution)/shard_map/ppermute | solution.py:371
  13.2 4.7 %collective-permute-start.4 = (f32[16,128]{1,0:T(8,128)S(1)}, f32[16,128]{1,0:T(8,128)S(1)}, u32[]{:S(2)}, u32[]{:S(2)}) collective-permute-start(f32[16,128]{1,0:T(8,128)S(1)} %complete.1), channel_id=1, source_target_pairs={{0,17},{1,16},{2,19},{3,18},{4,21},{5,20},{6,23},{7,22},{8,25},{9,... | collective-permute-start | bytes 24584 | tf_op jit(solution)/shard_map/ppermute | solution.py:371
  17.9 4.0 %collective-permute-start.7 = (f32[32,128]{1,0:T(8,128)S(1)}, f32[32,128]{1,0:T(8,128)S(1)}, u32[]{:S(2)}, u32[]{:S(2)}) collective-permute-start(f32[32,128]{1,0:T(8,128)S(1)} %pad_maximum_fusion.2.refs_0_), channel_id=1, source_target_pairs={{0,5},{1,4},{2,7},{3,6},{4,1},{5,0},{6,3},{7,2},{8,13},{9,12},{10,... | collective-permute-start | bytes 49160 | tf_op jit(solution)/shard_map/ppermute | solution.py:371
  19.4 4.1 %collective-permute-start.6 = (f32[32,128]{1,0:T(8,128)S(1)}, f32[32,128]{1,0:T(8,128)S(1)}, u32[]{:S(2)}, u32[]{:S(2)}) collective-permute-start(f32[32,128]{1,0:T(8,128)S(1)} %pad_maximum_fusion.2.refs_0_), channel_id=1, source_target_pairs={{0,13},{1,12},{2,15},{3,14},{4,9},{5,8},{6,11},{7,10},{8,5},{9,4},... | collective-permute-start | bytes 49160 | tf_op jit(solution)/shard_map/ppermute | solution.py:371
  20.9 3.2 %collective-permute-start.5 = (f32[32,128]{1,0:T(8,128)S(1)}, f32[32,128]{1,0:T(8,128)S(1)}, u32[]{:S(2)}, u32[]{:S(2)}) collective-permute-start(f32[32,128]{1,0:T(8,128)S(1)} %pad_maximum_fusion.2.refs_0_), channel_id=1, source_target_pairs={{0,9},{1,8},{2,11},{3,10},{4,13},{5,12},{6,15},{7,14},{8,1},{9,0},... | collective-permute-start | bytes 49160 | tf_op jit(solution)/shard_map/ppermute | solution.py:371

commit v9 on v8

--- a/solution.py
+++ b/solution.py
@@ -371,8 +371,24 @@
     return lax.ppermute(x, ("gy", "gx"), pairs)
 
 
-def doubled(x, flip_y, flip_x):
-    return jnp.concatenate([x, partner(x, flip_y, flip_x)], axis=0)
+def stack(x_ref, other_ref, *refs):
+    out_ref = refs[-1]
+    out_ref[: x_ref.shape[0], :] = x_ref[...]
+    out_ref[x_ref.shape[0] :, :] = other_ref[...]
+
+
+def doubled(x, flip_y, flip_x, *before):
+    other = partner(x, flip_y, flip_x)
+    if not before:
+        return jnp.concatenate([x, other], axis=0)
+    return pl.pallas_call(
+        stack,
+        out_shape=jax.ShapeDtypeStruct((2 * x.shape[0], x.shape[1]), x.dtype),
+        in_specs=[VMEM] * 2 + [ANY] * len(before),
+        out_specs=VMEM,
+        compiler_params=PARAMS,
+        name="stack",
+    )(x, other, *before)
 
 
 def row_blocks(block):
@@ -396,14 +412,14 @@
     return place
 
 
-def all_rows(packet):
+def all_rows(packet, beside):
     size = lax.axis_size("gy")
     if not two_power(size) or size < 4:
         return [lax.all_gather(packet, "gy", tiled=True)]
     flip_x = 1 - lax.axis_size("gx") % 2
     step = size // 2
     while step > 2:
-        packet = doubled(packet, step, flip_x)
+        packet = doubled(packet, step, flip_x, *([beside] if 2 * step == size else []))
         step //= 2
     return [packet] + [partner(packet, flip_y, flip_x) for flip_y in ORDER]
 
@@ -468,7 +484,7 @@
         cost_estimate=pl.CostEstimate(flops=4 * 10**6, bytes_accessed=6 * 10**5, transcendentals=0),
         name="forecast",
     )(field, tile_flow, rows_odd, rows_even, blocks)
-    packets = all_rows(packet)
+    packets = all_rows(packet, anomaly)
     out = call(
         functools.partial(analyse, members, count),
         out_shape=shape(members * count),

time: 26.9 us -> 26.9 us (level)
  no operation moved by 1% of the time
where the time goes in v9:
time: 26.9 us; the launch traced here: 26.7 us
  starting transfers between devices  12.4 us (46%)
  Pallas kernels  7.19 us (27%)
  waiting for transfers between devices  7.01 us (26%)
    ppermute x6, starting transfers between devices, partner(): return lax.ppermute(x, ('gy', 'gx'), pairs)  7.84 us
    ppermute x6, waiting for transfers between devices, partner(): return lax.ppermute(x, ('gy', 'gx'), pairs)  6.76 us
    ppermute x2, starting transfers between devices, swap(): return lax.ppermute(x, ('gy', 'gx'), pairs)  4.55 us
    pallas_call x1, Pallas kernels, body(): call(functools.partial(analyse, members, count), out_shape=shape(members...  2.55 us
    pallas_call x1, Pallas kernels, body(): call(functools.partial(prepare, members, count, n_obs), out_shape=[shape(...  2.02 us
    pallas_call x1, Pallas kernels, body(): call(functools.partial(load, members, count), out_shape=[shape(2 * member...  0.88 us
    pallas_call x1, Pallas kernels, body(): call(functools.partial(forecast, members, count, size), out_shape=[jax.Sh...  0.87 us
  transfers between devices with their start and end apart: 8, of which 6 were waited for; matrix products, arithmetic and copies ran while one was open for 0% of the time, Pallas kernels for 11%

profile of v9, /device:TPU:0, one launch (start us, length us, event | category | flops | bytes accessed | tf_op | source)
XLA Modules:
  0.0 26.7 jit_solution(5526295736031788877)
XLA Ops:
  0.0 0.9 %load.1 = (f32[136,128]{1,0:T(8,128)S(1)}, f32[136,128]{1,0:T(8,128)S(1)}) custom-call(f32[64,8,128]{2,1,0:T(8,128)} %ens_hbm.3, f32[3,8,128]{2,1,0:T(8,128)} %flow_hbm.3), custom_call_target="tpu_custom_call" | custom-call | tf_op jit(solution)/shard_map/load/pallas_call | solution.py:440
  0.9 0.5 %collective-permute-start = (f32[136,128]{1,0:T(8,128)S(1)}, f32[136,128]{1,0:T(8,128)S(1)}, u32[]{:S(2)}, u32[]{:S(2)}) collective-permute-start(f32[136,128]{1,0:T(8,128)S(1)} %get-tuple-element.18), channel_id=1, source_target_pairs={{0,1},{1,0},{2,3},{3,2},{4,8},{5,9},{6,10},{7,11},{8,4},{9,5},{10,... | collective-permute-start | bytes 208904 | tf_op jit(solution)/shard_map/ppermute | solution.py:361
  1.4 4.0 %collective-permute-start.1 = (f32[136,128]{1,0:T(8,128)S(1)}, f32[136,128]{1,0:T(8,128)S(1)}, u32[]{:S(2)}, u32[]{:S(2)}) collective-permute-start(f32[136,128]{1,0:T(8,128)S(1)} %get-tuple-element.15.sent_ref), channel_id=1, source_target_pairs={{0,4},{1,5},{2,6},{3,7},{4,0},{5,1},{6,2},{7,3},{8,12},{9,13},{10,... | collective-permute-start | bytes 208904 | tf_op jit(solution)/shard_map/ppermute | solution.py:361
  5.4 2.0 %prepare.1 = (f32[512,128]{1,0:T(8,128)S(1)}, f32[3,8,128]{2,1,0:T(8,128)S(1)}, f32[64,128]{1,0:T(8,128)S(1)}, f32[16,128]{1,0:T(8,128)S(1)}, f32[4,16,128]{2,1,0:T(8,128)S(1)}, /*index=5*/f32[4,16,128]{2,1,0:T(8,128)S(1)}) custom-call(f32[64,8,128]{2,1,0:T(8,128)} %ens_hbm.3, f32[3,8,128]{2,1,0:T(8,128)} %flow_hbm.3, s32[4]{0:T(128)} %bitcast.4, f32[4]{0:T(128)} %bitcast.5, ...), custom_call_target="tpu_custom_call" | custom-call | flops 4000000 | bytes 600000 | tf_op jit(solution)/shard_map/prepare/pallas_call | solution.py:449
  7.5 0.0 collective-permute-done.odd_ref
  7.5 0.2 collective-permute-done.1.even_ref
  7.7 0.4 %observe.1 = f32[32,128]{1,0:T(8,128)S(1)} custom-call(f32[512,128]{1,0:T(8,128)S(1)} %get-tuple-element.16.field_ref, f32[3,8,128]{2,1,0:T(8,128)S(1)} %get-tuple-element.17.flow_ref, f32[64,128]{1,0:T(8,128)S(1)} %get-tuple-element.19.packed_ref, f32[16,128]{1,0:T(8,128)S(1)} %get-tuple-element.20.meta_ref, ...), custom_call_target="tpu_custom_call" | custom-call | tf_op jit(solution)/shard_map/observe/pallas_call | solution.py:462
  8.1 0.1 collective-permute-start.2
  8.2 1.2 %collective-permute-done.2 = f32[32,128]{1,0:T(8,128)S(1)} collective-permute-done((f32[32,128]{1,0:T(8,128)S(1)}, f32[32,128]{1,0:T(8,128)S(1)}, u32[]{:S(2)}, u32[]{:S(2)}) %collective-permute-start.2) | collective-permute-done | bytes 16416 | tf_op jit(solution)/shard_map/ppermute | solution.py:371
  9.4 1.3 %collective-permute-start.3 = (f32[64,128]{1,0:T(8,128)S(1)}, f32[64,128]{1,0:T(8,128)S(1)}, u32[]{:S(2)}, u32[]{:S(2)}) collective-permute-start(f32[64,128]{1,0:T(8,128)S(1)} %pad_maximum_fusion.1), channel_id=1, source_target_pairs={{0,3},{1,2},{2,1},{3,0},{4,7},{5,6},{6,5},{7,4},{8,11},{9,10},{10,... | collective-permute-start | bytes 98312 | tf_op jit(solution)/shard_map/ppermute | solution.py:371
  10.6 2.1 %collective-permute-done.3 = f32[64,128]{1,0:T(8,128)S(1)} collective-permute-done((f32[64,128]{1,0:T(8,128)S(1)}, f32[64,128]{1,0:T(8,128)S(1)}, u32[]{:S(2)}, u32[]{:S(2)}) %collective-permute-start.3) | collective-permute-done | bytes 32800 | tf_op jit(solution)/shard_map/ppermute | solution.py:371
  12.7 0.5 %complete.1.x_ref = f32[16,128]{1,0:T(8,128)S(1)} custom-call(f32[128,128]{1,0:T(8,128)S(1)} %pad_maximum_fusion.blocks_ref), custom_call_target="tpu_custom_call" | custom-call | tf_op jit(solution)/shard_map/complete/pallas_call | solution.py:471
  13.2 3.4 %collective-permute-start.4 = (f32[16,128]{1,0:T(8,128)S(1)}, f32[16,128]{1,0:T(8,128)S(1)}, u32[]{:S(2)}, u32[]{:S(2)}) collective-permute-start(f32[16,128]{1,0:T(8,128)S(1)} %complete.1.x_ref), channel_id=1, source_target_pairs={{0,17},{1,16},{2,19},{3,18},{4,21},{5,20},{6,23},{7,22},{8,25},{9,... | collective-permute-start | bytes 24584 | tf_op jit(solution)/shard_map/ppermute | solution.py:371
  16.6 0.9 %forecast.1 = (bf16[192,1024]{1,0:T(8,128)(2,1)S(1)}, f32[8,128]{1,0:T(8,128)S(1)}) custom-call(f32[512,128]{1,0:T(8,128)S(1)} %get-tuple-element.16.field_ref, f32[3,8,128]{2,1,0:T(8,128)S(1)} %get-tuple-element.17.flow_ref, f32[136,128]{1,0:T(8,128)S(1)} %collective-permute-done.odd_ref, f32[136,128]{1,0:T(8,128)S(1)} %collective-permute-done.1.even_ref, ...), custom_call_target="tpu_custom_call" | custom-call | flops 4000000 | bytes 600000 | tf_op jit(solution)/shard_map/forecast/pallas_call | solution.py:478
  17.4 0.5 %collective-permute-done.4.other_ref = f32[16,128]{1,0:T(8,128)S(1)} collective-permute-done((f32[16,128]{1,0:T(8,128)S(1)}, f32[16,128]{1,0:T(8,128)S(1)}, u32[]{:S(2)}, u32[]{:S(2)}) %collective-permute-start.4) | collective-permute-done | bytes 8224 | tf_op jit(solution)/shard_map/ppermute | solution.py:371
  17.9 1.5 %collective-permute-start.7 = (f32[32,128]{1,0:T(8,128)S(1)}, f32[32,128]{1,0:T(8,128)S(1)}, u32[]{:S(2)}, u32[]{:S(2)}) collective-permute-start(f32[32,128]{1,0:T(8,128)S(1)} %stack.1.refs_0_), channel_id=1, source_target_pairs={{0,5},{1,4},{2,7},{3,6},{4,1},{5,0},{6,3},{7,2},{8,13},{9,12},{10,... | collective-permute-start | bytes 49160 | tf_op jit(solution)/shard_map/ppermute | solution.py:371
  19.4 1.5 %collective-permute-start.6 = (f32[32,128]{1,0:T(8,128)S(1)}, f32[32,128]{1,0:T(8,128)S(1)}, u32[]{:S(2)}, u32[]{:S(2)}) collective-permute-start(f32[32,128]{1,0:T(8,128)S(1)} %stack.1.refs_0_), channel_id=1, source_target_pairs={{0,13},{1,12},{2,15},{3,14},{4,9},{5,8},{6,11},{7,10},{8,5},{9,4},... | collective-permute-start | bytes 49160 | tf_op jit(solution)/shard_map/ppermute | solution.py:371
  20.9 0.1 collective-permute-start.5
  21.1 0.0 collective-permute-done.7.refs_3_
  21.1 2.4 %collective-permute-done.6.refs_2_ = f32[32,128]{1,0:T(8,128)S(1)} collective-permute-done((f32[32,128]{1,0:T(8,128)S(1)}, f32[32,128]{1,0:T(8,128)S(1)}, u32[]{:S(2)}, u32[]{:S(2)}) %collective-permute-start.6) | collective-permute-done | bytes 16416 | tf_op jit(solution)/shard_map/ppermute | solution.py:371
  23.5 0.6 %collective-permute-done.5.refs_1_ = f32[32,128]{1,0:T(8,128)S(1)} collective-permute-done((f32[32,128]{1,0:T(8,128)S(1)}, f32[32,128]{1,0:T(8,128)S(1)}, u32[]{:S(2)}, u32[]{:S(2)}) %collective-permute-start.5) | collective-permute-done | bytes 16416 | tf_op jit(solution)/shard_map/ppermute | solution.py:371
  24.1 2.6 %analyse.1 = f32[512,128]{1,0:T(8,128)} custom-call(bf16[192,1024]{1,0:T(8,128)(2,1)S(1)} %get-tuple-element.23.refs_0_.f_ref, f32[8,128]{1,0:T(8,128)S(1)} %get-tuple-element.24.mean_ref, f32[32,128]{1,0:T(8,128)S(1)} %stack.1.refs_0_, f32[32,128]{1,0:T(8,128)S(1)} %collective-permute-done.5.refs_1_, f32[32,128]{1,0:T(8,128)S(1)} %collective-permute-done.6.refs_2_, ...), custom_call_target="tpu_custom_call" | custom-call | tf_op jit(solution)/shard_map/analyse/pallas_call | solution.py:488
  (3 shorter events, 0.0 us)
Async XLA Ops:
  0.9 6.6 %collective-permute-start = (f32[136,128]{1,0:T(8,128)S(1)}, f32[136,128]{1,0:T(8,128)S(1)}, u32[]{:S(2)}, u32[]{:S(2)}) collective-permute-start(f32[136,128]{1,0:T(8,128)S(1)} %get-tuple-element.18), channel_id=1, source_target_pairs={{0,1},{1,0},{2,3},{3,2},{4,8},{5,9},{6,10},{7,11},{8,4},{9,5},{10,... | collective-permute-start | bytes 208904 | tf_op jit(solution)/shard_map/ppermute | solution.py:361
  1.4 6.3 %collective-permute-start.1 = (f32[136,128]{1,0:T(8,128)S(1)}, f32[136,128]{1,0:T(8,128)S(1)}, u32[]{:S(2)}, u32[]{:S(2)}) collective-permute-start(f32[136,128]{1,0:T(8,128)S(1)} %get-tuple-element.15.sent_ref), channel_id=1, source_target_pairs={{0,4},{1,5},{2,6},{3,7},{4,0},{5,1},{6,2},{7,3},{8,12},{9,13},{10,... | collective-permute-start | bytes 208904 | tf_op jit(solution)/shard_map/ppermute | solution.py:361
  8.1 1.2 %collective-permute-start.2 = (f32[32,128]{1,0:T(8,128)S(1)}, f32[32,128]{1,0:T(8,128)S(1)}, u32[]{:S(2)}, u32[]{:S(2)}) collective-permute-start(f32[32,128]{1,0:T(8,128)S(1)} %observe.1), channel_id=1, source_target_pairs={{0,1},{1,0},{2,3},{3,2},{4,5},{5,4},{6,7},{7,6},{8,9},{9,8},{10,11... | collective-permute-start | bytes 49160 | tf_op jit(solution)/shard_map/ppermute | solution.py:371
  9.4 3.3 %collective-permute-start.3 = (f32[64,128]{1,0:T(8,128)S(1)}, f32[64,128]{1,0:T(8,128)S(1)}, u32[]{:S(2)}, u32[]{:S(2)}) collective-permute-start(f32[64,128]{1,0:T(8,128)S(1)} %pad_maximum_fusion.1), channel_id=1, source_target_pairs={{0,3},{1,2},{2,1},{3,0},{4,7},{5,6},{6,5},{7,4},{8,11},{9,10},{10,... | collective-permute-start | bytes 98312 | tf_op jit(solution)/shard_map/ppermute | solution.py:371
  13.2 4.7 %collective-permute-start.4 = (f32[16,128]{1,0:T(8,128)S(1)}, f32[16,128]{1,0:T(8,128)S(1)}, u32[]{:S(2)}, u32[]{:S(2)}) collective-permute-start(f32[16,128]{1,0:T(8,128)S(1)} %complete.1.x_ref), channel_id=1, source_target_pairs={{0,17},{1,16},{2,19},{3,18},{4,21},{5,20},{6,23},{7,22},{8,25},{9,... | collective-permute-start | bytes 24584 | tf_op jit(solution)/shard_map/ppermute | solution.py:371
  17.9 3.2 %collective-permute-start.7 = (f32[32,128]{1,0:T(8,128)S(1)}, f32[32,128]{1,0:T(8,128)S(1)}, u32[]{:S(2)}, u32[]{:S(2)}) collective-permute-start(f32[32,128]{1,0:T(8,128)S(1)} %stack.1.refs_0_), channel_id=1, source_target_pairs={{0,5},{1,4},{2,7},{3,6},{4,1},{5,0},{6,3},{7,2},{8,13},{9,12},{10,... | collective-permute-start | bytes 49160 | tf_op jit(solution)/shard_map/ppermute | solution.py:371
  19.4 4.1 %collective-permute-start.6 = (f32[32,128]{1,0:T(8,128)S(1)}, f32[32,128]{1,0:T(8,128)S(1)}, u32[]{:S(2)}, u32[]{:S(2)}) collective-permute-start(f32[32,128]{1,0:T(8,128)S(1)} %stack.1.refs_0_), channel_id=1, source_target_pairs={{0,13},{1,12},{2,15},{3,14},{4,9},{5,8},{6,11},{7,10},{8,5},{9,4},... | collective-permute-start | bytes 49160 | tf_op jit(solution)/shard_map/ppermute | solution.py:371
  20.9 3.2 %collective-permute-start.5 = (f32[32,128]{1,0:T(8,128)S(1)}, f32[32,128]{1,0:T(8,128)S(1)}, u32[]{:S(2)}, u32[]{:S(2)}) collective-permute-start(f32[32,128]{1,0:T(8,128)S(1)} %stack.1.refs_0_), channel_id=1, source_target_pairs={{0,9},{1,8},{2,11},{3,10},{4,13},{5,12},{6,15},{7,14},{8,1},{9,0},... | collective-permute-start | bytes 49160 | tf_op jit(solution)/shard_map/ppermute | solution.py:371

commit v10 on v8

--- a/solution.py
+++ b/solution.py
@@ -376,9 +376,10 @@
 
 
 def row_blocks(block):
-    size, step = lax.axis_size("gx"), 1
-    if not two_power(size):
+    size, step = lax.axis_size("gx"), 4
+    if not two_power(size) or size < 4:
         return lax.all_gather(block, "gx", tiled=True)
+    block = jnp.concatenate([block] + [partner(block, 0, flip) for flip in (1, 3, 2)], axis=0)
     while step < size:
         block = doubled(block, 0, step | 1)
         step *= 2
@@ -386,7 +387,7 @@
 
 
 def place_of(tile, size):
-    if not two_power(size):
+    if not two_power(size) or size < 4:
         return tile
     distance = jnp.bitwise_xor(lax.axis_index("gx"), tile)
     place, bit = distance, 2

time: 26.9 us -> 27.1 us (level)
  starting transfers between devices: 12.4 us -> 13.2 us
  waiting for transfers between devices: 7 us -> 6.43 us
    ppermute x6 -> x7, starting transfers between devices: 7.84 us -> 8.61 us  [partner(): return lax.ppermute(x, ('gy', 'gx'), pairs)]
    ppermute x6 -> x7, waiting for transfers between devices: 6.75 us -> 6.18 us  [partner(): return lax.ppermute(x, ('gy', 'gx'), pairs)]
  transfers between devices with their start and end apart: 8 -> 9, of which waited for: 6 -> 6; matrix products, arithmetic and copies ran while one was open for 0% -> 0% of each run, Pallas kernels for 11% -> 11%
where the time goes in v10:
time: 27.1 us; the launch traced here: 26.8 us
  starting transfers between devices  13.2 us (49%)
  Pallas kernels  7.2 us (27%)
  waiting for transfers between devices  6.43 us (24%)
    ppermute x7, starting transfers between devices, partner(): return lax.ppermute(x, ('gy', 'gx'), pairs)  8.61 us
    ppermute x7, waiting for transfers between devices, partner(): return lax.ppermute(x, ('gy', 'gx'), pairs)  6.18 us
    ppermute x2, starting transfers between devices, swap(): return lax.ppermute(x, ('gy', 'gx'), pairs)  4.55 us
    pallas_call x1, Pallas kernels, body(): call(functools.partial(analyse, members, count), out_shape=shape(members...  2.55 us
    pallas_call x1, Pallas kernels, body(): call(functools.partial(prepare, members, count, n_obs), out_shape=[shape(...  2.02 us
    pallas_call x1, Pallas kernels, body(): call(functools.partial(load, members, count), out_shape=[shape(2 * member...  0.88 us
    pallas_call x1, Pallas kernels, body(): call(functools.partial(forecast, members, count, size), out_shape=[jax.Sh...  0.87 us
  transfers between devices with their start and end apart: 9, of which 6 were waited for; matrix products, arithmetic and copies ran while one was open for 0% of the time, Pallas kernels for 11%

profile of v10, /device:TPU:0, one launch (start us, length us, event | category | flops | bytes accessed | tf_op | source)
XLA Modules:
  0.0 26.8 jit_solution(3815669883968943124)
XLA Ops:
  0.0 0.9 %load.1 = (f32[136,128]{1,0:T(8,128)S(1)}, f32[136,128]{1,0:T(8,128)S(1)}) custom-call(f32[64,8,128]{2,1,0:T(8,128)} %ens_hbm.3, f32[3,8,128]{2,1,0:T(8,128)} %flow_hbm.3), custom_call_target="tpu_custom_call" | custom-call | tf_op jit(solution)/shard_map/load/pallas_call | solution.py:425
  0.9 0.5 %collective-permute-start = (f32[136,128]{1,0:T(8,128)S(1)}, f32[136,128]{1,0:T(8,128)S(1)}, u32[]{:S(2)}, u32[]{:S(2)}) collective-permute-start(f32[136,128]{1,0:T(8,128)S(1)} %get-tuple-element.18), channel_id=1, source_target_pairs={{0,1},{1,0},{2,3},{3,2},{4,8},{5,9},{6,10},{7,11},{8,4},{9,5},{10,... | collective-permute-start | bytes 208904 | tf_op jit(solution)/shard_map/ppermute | solution.py:361
  1.4 4.0 %collective-permute-start.1 = (f32[136,128]{1,0:T(8,128)S(1)}, f32[136,128]{1,0:T(8,128)S(1)}, u32[]{:S(2)}, u32[]{:S(2)}) collective-permute-start(f32[136,128]{1,0:T(8,128)S(1)} %get-tuple-element.15.sent_ref), channel_id=1, source_target_pairs={{0,4},{1,5},{2,6},{3,7},{4,0},{5,1},{6,2},{7,3},{8,12},{9,13},{10,... | collective-permute-start | bytes 208904 | tf_op jit(solution)/shard_map/ppermute | solution.py:361
  5.4 2.0 %prepare.1 = (f32[512,128]{1,0:T(8,128)S(1)}, f32[3,8,128]{2,1,0:T(8,128)S(1)}, f32[64,128]{1,0:T(8,128)S(1)}, f32[16,128]{1,0:T(8,128)S(1)}, f32[4,16,128]{2,1,0:T(8,128)S(1)}, /*index=5*/f32[4,16,128]{2,1,0:T(8,128)S(1)}) custom-call(f32[64,8,128]{2,1,0:T(8,128)} %ens_hbm.3, f32[3,8,128]{2,1,0:T(8,128)} %flow_hbm.3, s32[4]{0:T(128)} %bitcast.4, f32[4]{0:T(128)} %bitcast.5, ...), custom_call_target="tpu_custom_call" | custom-call | flops 4000000 | bytes 600000 | tf_op jit(solution)/shard_map/prepare/pallas_call | solution.py:434
  7.5 0.0 collective-permute-done.odd_ref
  7.5 0.2 collective-permute-done.1.even_ref
  7.7 0.4 %observe.1 = f32[32,128]{1,0:T(8,128)S(1)} custom-call(f32[512,128]{1,0:T(8,128)S(1)} %get-tuple-element.16.field_ref, f32[3,8,128]{2,1,0:T(8,128)S(1)} %get-tuple-element.17.flow_ref, f32[64,128]{1,0:T(8,128)S(1)} %get-tuple-element.19.packed_ref, f32[16,128]{1,0:T(8,128)S(1)} %get-tuple-element.20.meta_ref, ...), custom_call_target="tpu_custom_call" | custom-call | tf_op jit(solution)/shard_map/observe/pallas_call | solution.py:447
  8.1 1.6 %collective-permute-start.4 = (f32[32,128]{1,0:T(8,128)S(1)}, f32[32,128]{1,0:T(8,128)S(1)}, u32[]{:S(2)}, u32[]{:S(2)}) collective-permute-start(f32[32,128]{1,0:T(8,128)S(1)} %observe.1), channel_id=1, source_target_pairs={{0,2},{1,3},{2,0},{3,1},{4,6},{5,7},{6,4},{7,5},{8,10},{9,11},{10,... | collective-permute-start | bytes 49160 | tf_op jit(solution)/shard_map/ppermute | solution.py:371
  9.7 0.0 collective-permute-start.3
  9.7 0.6 %collective-permute-start.2 = (f32[32,128]{1,0:T(8,128)S(1)}, f32[32,128]{1,0:T(8,128)S(1)}, u32[]{:S(2)}, u32[]{:S(2)}) collective-permute-start(f32[32,128]{1,0:T(8,128)S(1)} %observe.1), channel_id=1, source_target_pairs={{0,1},{1,0},{2,3},{3,2},{4,5},{5,4},{6,7},{7,6},{8,9},{9,8},{10,11... | collective-permute-start | bytes 49160 | tf_op jit(solution)/shard_map/ppermute | solution.py:371
  10.3 1.6 %collective-permute-done.4 = f32[32,128]{1,0:T(8,128)S(1)} collective-permute-done((f32[32,128]{1,0:T(8,128)S(1)}, f32[32,128]{1,0:T(8,128)S(1)}, u32[]{:S(2)}, u32[]{:S(2)}) %collective-permute-start.4) | collective-permute-done | bytes 16416 | tf_op jit(solution)/shard_map/ppermute | solution.py:371
  11.9 0.9 %collective-permute-done.3 = f32[32,128]{1,0:T(8,128)S(1)} collective-permute-done((f32[32,128]{1,0:T(8,128)S(1)}, f32[32,128]{1,0:T(8,128)S(1)}, u32[]{:S(2)}, u32[]{:S(2)}) %collective-permute-start.3) | collective-permute-done | bytes 16416 | tf_op jit(solution)/shard_map/ppermute | solution.py:371
  12.9 0.0 collective-permute-done.2
  12.9 0.5 %complete.1 = f32[16,128]{1,0:T(8,128)S(1)} custom-call(f32[128,128]{1,0:T(8,128)S(1)} %pad_maximum_fusion.blocks_ref), custom_call_target="tpu_custom_call" | custom-call | tf_op jit(solution)/shard_map/complete/pallas_call | solution.py:456
  13.4 2.5 %collective-permute-start.5 = (f32[16,128]{1,0:T(8,128)S(1)}, f32[16,128]{1,0:T(8,128)S(1)}, u32[]{:S(2)}, u32[]{:S(2)}) collective-permute-start(f32[16,128]{1,0:T(8,128)S(1)} %complete.1), channel_id=1, source_target_pairs={{0,17},{1,16},{2,19},{3,18},{4,21},{5,20},{6,23},{7,22},{8,25},{9,... | collective-permute-start | bytes 24584 | tf_op jit(solution)/shard_map/ppermute | solution.py:371
  15.9 1.4 %collective-permute-done.5 = f32[16,128]{1,0:T(8,128)S(1)} collective-permute-done((f32[16,128]{1,0:T(8,128)S(1)}, f32[16,128]{1,0:T(8,128)S(1)}, u32[]{:S(2)}, u32[]{:S(2)}) %collective-permute-start.5) | collective-permute-done | bytes 8224 | tf_op jit(solution)/shard_map/ppermute | solution.py:371
  17.4 2.2 %collective-permute-start.8 = (f32[32,128]{1,0:T(8,128)S(1)}, f32[32,128]{1,0:T(8,128)S(1)}, u32[]{:S(2)}, u32[]{:S(2)}) collective-permute-start(f32[32,128]{1,0:T(8,128)S(1)} %pad_maximum_fusion.1.refs_0_), channel_id=1, source_target_pairs={{0,5},{1,4},{2,7},{3,6},{4,1},{5,0},{6,3},{7,2},{8,13},{9,12},{10,... | collective-permute-start | bytes 49160 | tf_op jit(solution)/shard_map/ppermute | solution.py:371
  19.5 1.6 %collective-permute-start.7 = (f32[32,128]{1,0:T(8,128)S(1)}, f32[32,128]{1,0:T(8,128)S(1)}, u32[]{:S(2)}, u32[]{:S(2)}) collective-permute-start(f32[32,128]{1,0:T(8,128)S(1)} %pad_maximum_fusion.1.refs_0_), channel_id=1, source_target_pairs={{0,13},{1,12},{2,15},{3,14},{4,9},{5,8},{6,11},{7,10},{8,5},{9,4},... | collective-permute-start | bytes 49160 | tf_op jit(solution)/shard_map/ppermute | solution.py:371
  21.1 0.1 collective-permute-start.6
  21.2 0.9 %forecast.1 = (bf16[192,1024]{1,0:T(8,128)(2,1)S(1)}, f32[8,128]{1,0:T(8,128)S(1)}) custom-call(f32[512,128]{1,0:T(8,128)S(1)} %get-tuple-element.16.field_ref, f32[3,8,128]{2,1,0:T(8,128)S(1)} %get-tuple-element.17.flow_ref, f32[136,128]{1,0:T(8,128)S(1)} %collective-permute-done.odd_ref, f32[136,128]{1,0:T(8,128)S(1)} %collective-permute-done.1.even_ref, ...), custom_call_target="tpu_custom_call" | custom-call | flops 4000000 | bytes 600000 | tf_op jit(solution)/shard_map/forecast/pallas_call | solution.py:463
  22.1 0.0 collective-permute-done.8.refs_3_
  22.1 1.5 %collective-permute-done.7.refs_2_ = f32[32,128]{1,0:T(8,128)S(1)} collective-permute-done((f32[32,128]{1,0:T(8,128)S(1)}, f32[32,128]{1,0:T(8,128)S(1)}, u32[]{:S(2)}, u32[]{:S(2)}) %collective-permute-start.7) | collective-permute-done | bytes 16416 | tf_op jit(solution)/shard_map/ppermute | solution.py:371
  23.6 0.7 %collective-permute-done.6.refs_1_ = f32[32,128]{1,0:T(8,128)S(1)} collective-permute-done((f32[32,128]{1,0:T(8,128)S(1)}, f32[32,128]{1,0:T(8,128)S(1)}, u32[]{:S(2)}, u32[]{:S(2)}) %collective-permute-start.6) | collective-permute-done | bytes 16416 | tf_op jit(solution)/shard_map/ppermute | solution.py:371
  24.3 2.6 %analyse.1 = f32[512,128]{1,0:T(8,128)} custom-call(bf16[192,1024]{1,0:T(8,128)(2,1)S(1)} %get-tuple-element.23.f_ref, f32[8,128]{1,0:T(8,128)S(1)} %get-tuple-element.24.mean_ref, f32[32,128]{1,0:T(8,128)S(1)} %pad_maximum_fusion.1.refs_0_, f32[32,128]{1,0:T(8,128)S(1)} %collective-permute-done.6.refs_1_, f32[32,128]{1,0:T(8,128)S(1)} %collective-permute-done.7.refs_2_, ...), custom_call_target="tpu_custom_call" | custom-call | tf_op jit(solution)/shard_map/analyse/pallas_call | solution.py:473
  (2 shorter events, 0.0 us)
Async XLA Ops:
  0.9 6.6 %collective-permute-start = (f32[136,128]{1,0:T(8,128)S(1)}, f32[136,128]{1,0:T(8,128)S(1)}, u32[]{:S(2)}, u32[]{:S(2)}) collective-permute-start(f32[136,128]{1,0:T(8,128)S(1)} %get-tuple-element.18), channel_id=1, source_target_pairs={{0,1},{1,0},{2,3},{3,2},{4,8},{5,9},{6,10},{7,11},{8,4},{9,5},{10,... | collective-permute-start | bytes 208904 | tf_op jit(solution)/shard_map/ppermute | solution.py:361
  1.4 6.3 %collective-permute-start.1 = (f32[136,128]{1,0:T(8,128)S(1)}, f32[136,128]{1,0:T(8,128)S(1)}, u32[]{:S(2)}, u32[]{:S(2)}) collective-permute-start(f32[136,128]{1,0:T(8,128)S(1)} %get-tuple-element.15.sent_ref), channel_id=1, source_target_pairs={{0,4},{1,5},{2,6},{3,7},{4,0},{5,1},{6,2},{7,3},{8,12},{9,13},{10,... | collective-permute-start | bytes 208904 | tf_op jit(solution)/shard_map/ppermute | solution.py:361
  8.1 3.8 %collective-permute-start.4 = (f32[32,128]{1,0:T(8,128)S(1)}, f32[32,128]{1,0:T(8,128)S(1)}, u32[]{:S(2)}, u32[]{:S(2)}) collective-permute-start(f32[32,128]{1,0:T(8,128)S(1)} %observe.1), channel_id=1, source_target_pairs={{0,2},{1,3},{2,0},{3,1},{4,6},{5,7},{6,4},{7,5},{8,10},{9,11},{10,... | collective-permute-start | bytes 49160 | tf_op jit(solution)/shard_map/ppermute | solution.py:371
  9.7 3.2 %collective-permute-start.3 = (f32[32,128]{1,0:T(8,128)S(1)}, f32[32,128]{1,0:T(8,128)S(1)}, u32[]{:S(2)}, u32[]{:S(2)}) collective-permute-start(f32[32,128]{1,0:T(8,128)S(1)} %observe.1), channel_id=1, source_target_pairs={{0,3},{1,2},{2,1},{3,0},{4,7},{5,6},{6,5},{7,4},{8,11},{9,10},{10,... | collective-permute-start | bytes 49160 | tf_op jit(solution)/shard_map/ppermute | solution.py:371
  9.7 3.2 %collective-permute-start.2 = (f32[32,128]{1,0:T(8,128)S(1)}, f32[32,128]{1,0:T(8,128)S(1)}, u32[]{:S(2)}, u32[]{:S(2)}) collective-permute-start(f32[32,128]{1,0:T(8,128)S(1)} %observe.1), channel_id=1, source_target_pairs={{0,1},{1,0},{2,3},{3,2},{4,5},{5,4},{6,7},{7,6},{8,9},{9,8},{10,11... | collective-permute-start | bytes 49160 | tf_op jit(solution)/shard_map/ppermute | solution.py:371
  13.4 4.0 %collective-permute-start.5 = (f32[16,128]{1,0:T(8,128)S(1)}, f32[16,128]{1,0:T(8,128)S(1)}, u32[]{:S(2)}, u32[]{:S(2)}) collective-permute-start(f32[16,128]{1,0:T(8,128)S(1)} %complete.1), channel_id=1, source_target_pairs={{0,17},{1,16},{2,19},{3,18},{4,21},{5,20},{6,23},{7,22},{8,25},{9,... | collective-permute-start | bytes 24584 | tf_op jit(solution)/shard_map/ppermute | solution.py:371
  17.4 4.7 %collective-permute-start.8 = (f32[32,128]{1,0:T(8,128)S(1)}, f32[32,128]{1,0:T(8,128)S(1)}, u32[]{:S(2)}, u32[]{:S(2)}) collective-permute-start(f32[32,128]{1,0:T(8,128)S(1)} %pad_maximum_fusion.1.refs_0_), channel_id=1, source_target_pairs={{0,5},{1,4},{2,7},{3,6},{4,1},{5,0},{6,3},{7,2},{8,13},{9,12},{10,... | collective-permute-start | bytes 49160 | tf_op jit(solution)/shard_map/ppermute | solution.py:371
  19.5 4.1 %collective-permute-start.7 = (f32[32,128]{1,0:T(8,128)S(1)}, f32[32,128]{1,0:T(8,128)S(1)}, u32[]{:S(2)}, u32[]{:S(2)}) collective-permute-start(f32[32,128]{1,0:T(8,128)S(1)} %pad_maximum_fusion.1.refs_0_), channel_id=1, source_target_pairs={{0,13},{1,12},{2,15},{3,14},{4,9},{5,8},{6,11},{7,10},{8,5},{9,4},... | collective-permute-start | bytes 49160 | tf_op jit(solution)/shard_map/ppermute | solution.py:371
  21.1 3.2 %collective-permute-start.6 = (f32[32,128]{1,0:T(8,128)S(1)}, f32[32,128]{1,0:T(8,128)S(1)}, u32[]{:S(2)}, u32[]{:S(2)}) collective-permute-start(f32[32,128]{1,0:T(8,128)S(1)} %pad_maximum_fusion.1.refs_0_), channel_id=1, source_target_pairs={{0,9},{1,8},{2,11},{3,10},{4,13},{5,12},{6,15},{7,14},{8,1},{9,0},... | collective-permute-start | bytes 49160 | tf_op jit(solution)/shard_map/ppermute | solution.py:371

commit v11 on v8

--- a/solution.py
+++ b/solution.py
@@ -8,7 +8,6 @@
 from jax.sharding import PartitionSpec as P
 
 F32 = jnp.float32
-HIGHEST = lax.Precision.HIGHEST
 PARAMS = pltpu.CompilerParams(vmem_limit_bytes=24 * 1024 * 1024)
 VMEM = pl.BlockSpec(memory_space=pltpu.VMEM)
 SMEM = pl.BlockSpec(memory_space=pltpu.SMEM)
@@ -285,7 +284,7 @@
         out_ref[2 * members :, at] = high
 
 
-def eliminated(a, members):
+def eliminated(a, members, column_ref):
     size = 8
     lane, sub = lanes((size, 128)), rows_of((size, 128))
     part = [a[size * q : size * (q + 1), :] for q in range(members // size)]
@@ -313,7 +312,9 @@
             inverse = 1.0 / value
             unit = jnp.where(lane[:1] == at, 1.0, part[p][j : j + 1, :])
             pivots = {c: column[p, c][j : j + 1, :] for c in range(at + 1, end)}
-            pivots.update({c: column[p + 1, at][c - end : c - end + 1, :] for c in more})
+            if more:
+                column_ref[at] = column[p + 1, at]
+            pivots.update({c: column_ref[at, c - end : c - end + 1, :] for c in more})
             for q in rest:
                 factor = column[q, at] * inverse
                 for c in range(at + 1, end + (len(more) if q == p + 1 else 0)):
@@ -326,14 +327,26 @@
     return jnp.concatenate(part, axis=0), jnp.concatenate(pivot, axis=0)
 
 
+def thirds(x):
+    first = x.astype(jnp.bfloat16)
+    rest = x - first.astype(F32)
+    second = rest.astype(jnp.bfloat16)
+    return first, second, (rest - second.astype(F32)).astype(jnp.bfloat16)
+
+
+def product(lefts, rights):
+    left, right = jnp.concatenate(lefts, axis=1), jnp.concatenate(rights, axis=0)
+    return jnp.dot(left, right, preferred_element_type=F32)
+
+
 def analyse(members, count, f_ref, mean_ref, *refs):
-    out_ref = refs[-1]
-    scaled = jnp.concatenate([ref[...] for ref in refs[:-1]], axis=0)
-    full = lax.dot_general(
-        scaled, scaled, (((0,), (0,)), ((), ())), precision=HIGHEST, preferred_element_type=F32
-    )
+    out_ref, column_ref = refs[-2:]
+    scaled = jnp.concatenate([ref[...] for ref in refs[:-2]], axis=0)
+    a1, a2, a3 = thirds(scaled)
+    t1, t2, t3 = thirds(scaled.T[:members])
+    full = product([t1, t2], [a1, a1]) + (product([t1, t2], [a2, a2]) + product([t1, t3], [a3, a1]))
     lane, sub = lanes((members, 128)), rows_of((members, 128))
-    a, pivots = eliminated(full[:members, :] + jnp.where(lane == sub, members - 1.0, 0.0), members)
+    a, pivots = eliminated(full + jnp.where(lane == sub, members - 1.0, 0.0), members, column_ref)
     scale = lax.rsqrt(pivots)
     inverse = scale * jnp.where(lane < sub, a, jnp.where(lane == sub, 1.0, 0.0))
     reduced = scale * a[:, members : members + 1]
@@ -341,7 +354,7 @@
     transform = (jnp.sqrt(members - 1.0) * inverse + weights)[:, :members]
     high = transform.astype(jnp.bfloat16)
     low = (transform - high.astype(F32)).astype(jnp.bfloat16)
-    update = jnp.dot(jnp.concatenate([high, high, low], axis=1), f_ref[...], preferred_element_type=F32)
+    update = product([high, high, low], [f_ref[...]])
     for r in range(count):
         out_ref[pl.ds(r, members, stride=count), :] = update[:, 128 * r : 128 * (r + 1)] + mean_ref[r : r + 1, :]
 
@@ -474,6 +487,7 @@
         out_shape=shape(members * count),
         in_specs=[VMEM] * (2 + len(packets)),
         out_specs=VMEM,
+        scratch_shapes=[pltpu.VMEM((members, 8, width), F32)],
         name="analyse",
     )(anomaly, mean, *packets)
     return out.reshape(ensemble.shape)

time: 26.9 us -> 26.7 us (level)
  no operation moved by 1% of the time
where the time goes in v11:
time: 26.7 us; the launch traced here: 26.4 us
  starting transfers between devices  12.4 us (46%)
  waiting for transfers between devices  7 us (26%)
  Pallas kernels  6.95 us (26%)
    ppermute x6, starting transfers between devices, partner(): return lax.ppermute(x, ('gy', 'gx'), pairs)  7.84 us
    ppermute x6, waiting for transfers between devices, partner(): return lax.ppermute(x, ('gy', 'gx'), pairs)  6.75 us
    ppermute x2, starting transfers between devices, swap(): return lax.ppermute(x, ('gy', 'gx'), pairs)  4.55 us
    pallas_call x1, Pallas kernels, body(): call(functools.partial(analyse, members, count), out_shape=shape(members...  2.31 us
    pallas_call x1, Pallas kernels, body(): call(functools.partial(prepare, members, count, n_obs), out_shape=[shape(...  2.02 us
    pallas_call x1, Pallas kernels, body(): call(functools.partial(load, members, count), out_shape=[shape(2 * member...  0.88 us
    pallas_call x1, Pallas kernels, body(): call(functools.partial(forecast, members, count, size), out_shape=[jax.Sh...  0.87 us
  transfers between devices with their start and end apart: 8, of which 6 were waited for; matrix products, arithmetic and copies ran while one was open for 0% of the time, Pallas kernels for 11%

profile of v11, /device:TPU:0, one launch (start us, length us, event | category | flops | bytes accessed | tf_op | source)
XLA Modules:
  0.0 26.4 jit_solution(4612876389233270808)
XLA Ops:
  0.0 0.9 %load.1 = (f32[136,128]{1,0:T(8,128)S(1)}, f32[136,128]{1,0:T(8,128)S(1)}) custom-call(f32[64,8,128]{2,1,0:T(8,128)} %ens_hbm.3, f32[3,8,128]{2,1,0:T(8,128)} %flow_hbm.3), custom_call_target="tpu_custom_call" | custom-call | tf_op jit(solution)/shard_map/load/pallas_call | solution.py:437
  0.9 0.5 %collective-permute-start = (f32[136,128]{1,0:T(8,128)S(1)}, f32[136,128]{1,0:T(8,128)S(1)}, u32[]{:S(2)}, u32[]{:S(2)}) collective-permute-start(f32[136,128]{1,0:T(8,128)S(1)} %get-tuple-element.18), channel_id=1, source_target_pairs={{0,1},{1,0},{2,3},{3,2},{4,8},{5,9},{6,10},{7,11},{8,4},{9,5},{10,... | collective-permute-start | bytes 208904 | tf_op jit(solution)/shard_map/ppermute | solution.py:374
  1.4 4.0 %collective-permute-start.1 = (f32[136,128]{1,0:T(8,128)S(1)}, f32[136,128]{1,0:T(8,128)S(1)}, u32[]{:S(2)}, u32[]{:S(2)}) collective-permute-start(f32[136,128]{1,0:T(8,128)S(1)} %get-tuple-element.15.sent_ref), channel_id=1, source_target_pairs={{0,4},{1,5},{2,6},{3,7},{4,0},{5,1},{6,2},{7,3},{8,12},{9,13},{10,... | collective-permute-start | bytes 208904 | tf_op jit(solution)/shard_map/ppermute | solution.py:374
  5.4 2.0 %prepare.1 = (f32[512,128]{1,0:T(8,128)S(1)}, f32[3,8,128]{2,1,0:T(8,128)S(1)}, f32[64,128]{1,0:T(8,128)S(1)}, f32[16,128]{1,0:T(8,128)S(1)}, f32[4,16,128]{2,1,0:T(8,128)S(1)}, /*index=5*/f32[4,16,128]{2,1,0:T(8,128)S(1)}) custom-call(f32[64,8,128]{2,1,0:T(8,128)} %ens_hbm.3, f32[3,8,128]{2,1,0:T(8,128)} %flow_hbm.3, s32[4]{0:T(128)} %bitcast.4, f32[4]{0:T(128)} %bitcast.5, ...), custom_call_target="tpu_custom_call" | custom-call | flops 4000000 | bytes 600000 | tf_op jit(solution)/shard_map/prepare/pallas_call | solution.py:446
  7.5 0.0 collective-permute-done.odd_ref
  7.5 0.2 collective-permute-done.1.even_ref
  7.7 0.4 %observe.1 = f32[32,128]{1,0:T(8,128)S(1)} custom-call(f32[512,128]{1,0:T(8,128)S(1)} %get-tuple-element.16.field_ref, f32[3,8,128]{2,1,0:T(8,128)S(1)} %get-tuple-element.17.flow_ref, f32[64,128]{1,0:T(8,128)S(1)} %get-tuple-element.19.packed_ref, f32[16,128]{1,0:T(8,128)S(1)} %get-tuple-element.20.meta_ref, ...), custom_call_target="tpu_custom_call" | custom-call | tf_op jit(solution)/shard_map/observe/pallas_call | solution.py:459
  8.1 0.1 collective-permute-start.2
  8.2 1.2 %collective-permute-done.2 = f32[32,128]{1,0:T(8,128)S(1)} collective-permute-done((f32[32,128]{1,0:T(8,128)S(1)}, f32[32,128]{1,0:T(8,128)S(1)}, u32[]{:S(2)}, u32[]{:S(2)}) %collective-permute-start.2) | collective-permute-done | bytes 16416 | tf_op jit(solution)/shard_map/ppermute | solution.py:384
  9.4 1.3 %collective-permute-start.3 = (f32[64,128]{1,0:T(8,128)S(1)}, f32[64,128]{1,0:T(8,128)S(1)}, u32[]{:S(2)}, u32[]{:S(2)}) collective-permute-start(f32[64,128]{1,0:T(8,128)S(1)} %pad_maximum_fusion.1), channel_id=1, source_target_pairs={{0,3},{1,2},{2,1},{3,0},{4,7},{5,6},{6,5},{7,4},{8,11},{9,10},{10,... | collective-permute-start | bytes 98312 | tf_op jit(solution)/shard_map/ppermute | solution.py:384
  10.6 2.1 %collective-permute-done.3 = f32[64,128]{1,0:T(8,128)S(1)} collective-permute-done((f32[64,128]{1,0:T(8,128)S(1)}, f32[64,128]{1,0:T(8,128)S(1)}, u32[]{:S(2)}, u32[]{:S(2)}) %collective-permute-start.3) | collective-permute-done | bytes 32800 | tf_op jit(solution)/shard_map/ppermute | solution.py:384
  12.7 0.5 %complete.1 = f32[16,128]{1,0:T(8,128)S(1)} custom-call(f32[128,128]{1,0:T(8,128)S(1)} %pad_maximum_fusion.blocks_ref), custom_call_target="tpu_custom_call" | custom-call | tf_op jit(solution)/shard_map/complete/pallas_call | solution.py:468
  13.2 3.4 %collective-permute-start.4 = (f32[16,128]{1,0:T(8,128)S(1)}, f32[16,128]{1,0:T(8,128)S(1)}, u32[]{:S(2)}, u32[]{:S(2)}) collective-permute-start(f32[16,128]{1,0:T(8,128)S(1)} %complete.1), channel_id=1, source_target_pairs={{0,17},{1,16},{2,19},{3,18},{4,21},{5,20},{6,23},{7,22},{8,25},{9,... | collective-permute-start | bytes 24584 | tf_op jit(solution)/shard_map/ppermute | solution.py:384
  16.6 1.4 %collective-permute-done.4 = f32[16,128]{1,0:T(8,128)S(1)} collective-permute-done((f32[16,128]{1,0:T(8,128)S(1)}, f32[16,128]{1,0:T(8,128)S(1)}, u32[]{:S(2)}, u32[]{:S(2)}) %collective-permute-start.4) | collective-permute-done | bytes 8224 | tf_op jit(solution)/shard_map/ppermute | solution.py:384
  17.9 1.5 %collective-permute-start.7 = (f32[32,128]{1,0:T(8,128)S(1)}, f32[32,128]{1,0:T(8,128)S(1)}, u32[]{:S(2)}, u32[]{:S(2)}) collective-permute-start(f32[32,128]{1,0:T(8,128)S(1)} %pad_maximum_fusion.2.refs_0_), channel_id=1, source_target_pairs={{0,5},{1,4},{2,7},{3,6},{4,1},{5,0},{6,3},{7,2},{8,13},{9,12},{10,... | collective-permute-start | bytes 49160 | tf_op jit(solution)/shard_map/ppermute | solution.py:384
  19.4 1.5 %collective-permute-start.6 = (f32[32,128]{1,0:T(8,128)S(1)}, f32[32,128]{1,0:T(8,128)S(1)}, u32[]{:S(2)}, u32[]{:S(2)}) collective-permute-start(f32[32,128]{1,0:T(8,128)S(1)} %pad_maximum_fusion.2.refs_0_), channel_id=1, source_target_pairs={{0,13},{1,12},{2,15},{3,14},{4,9},{5,8},{6,11},{7,10},{8,5},{9,4},... | collective-permute-start | bytes 49160 | tf_op jit(solution)/shard_map/ppermute | solution.py:384
  20.9 0.1 collective-permute-start.5
  21.1 0.9 %forecast.1 = (bf16[192,1024]{1,0:T(8,128)(2,1)S(1)}, f32[8,128]{1,0:T(8,128)S(1)}) custom-call(f32[512,128]{1,0:T(8,128)S(1)} %get-tuple-element.16.field_ref, f32[3,8,128]{2,1,0:T(8,128)S(1)} %get-tuple-element.17.flow_ref, f32[136,128]{1,0:T(8,128)S(1)} %collective-permute-done.odd_ref, f32[136,128]{1,0:T(8,128)S(1)} %collective-permute-done.1.even_ref, ...), custom_call_target="tpu_custom_call" | custom-call | flops 4000000 | bytes 600000 | tf_op jit(solution)/shard_map/forecast/pallas_call | solution.py:475
  21.9 0.0 collective-permute-done.7.refs_3_
  21.9 1.6 %collective-permute-done.6.refs_2_ = f32[32,128]{1,0:T(8,128)S(1)} collective-permute-done((f32[32,128]{1,0:T(8,128)S(1)}, f32[32,128]{1,0:T(8,128)S(1)}, u32[]{:S(2)}, u32[]{:S(2)}) %collective-permute-start.6) | collective-permute-done | bytes 16416 | tf_op jit(solution)/shard_map/ppermute | solution.py:384
  23.5 0.6 %collective-permute-done.5.refs_1_ = f32[32,128]{1,0:T(8,128)S(1)} collective-permute-done((f32[32,128]{1,0:T(8,128)S(1)}, f32[32,128]{1,0:T(8,128)S(1)}, u32[]{:S(2)}, u32[]{:S(2)}) %collective-permute-start.5) | collective-permute-done | bytes 16416 | tf_op jit(solution)/shard_map/ppermute | solution.py:384
  24.1 2.3 %analyse.1 = f32[512,128]{1,0:T(8,128)} custom-call(bf16[192,1024]{1,0:T(8,128)(2,1)S(1)} %get-tuple-element.23.f_ref, f32[8,128]{1,0:T(8,128)S(1)} %get-tuple-element.24.mean_ref, f32[32,128]{1,0:T(8,128)S(1)} %pad_maximum_fusion.2.refs_0_, f32[32,128]{1,0:T(8,128)S(1)} %collective-permute-done.5.refs_1_, f32[32,128]{1,0:T(8,128)S(1)} %collective-permute-done.6.refs_2_, ...), custom_call_target="tpu_custom_call" | custom-call | tf_op jit(solution)/shard_map/analyse/pallas_call | solution.py:485
  (3 shorter events, 0.0 us)
Async XLA Ops:
  0.9 6.6 %collective-permute-start = (f32[136,128]{1,0:T(8,128)S(1)}, f32[136,128]{1,0:T(8,128)S(1)}, u32[]{:S(2)}, u32[]{:S(2)}) collective-permute-start(f32[136,128]{1,0:T(8,128)S(1)} %get-tuple-element.18), channel_id=1, source_target_pairs={{0,1},{1,0},{2,3},{3,2},{4,8},{5,9},{6,10},{7,11},{8,4},{9,5},{10,... | collective-permute-start | bytes 208904 | tf_op jit(solution)/shard_map/ppermute | solution.py:374
  1.4 6.3 %collective-permute-start.1 = (f32[136,128]{1,0:T(8,128)S(1)}, f32[136,128]{1,0:T(8,128)S(1)}, u32[]{:S(2)}, u32[]{:S(2)}) collective-permute-start(f32[136,128]{1,0:T(8,128)S(1)} %get-tuple-element.15.sent_ref), channel_id=1, source_target_pairs={{0,4},{1,5},{2,6},{3,7},{4,0},{5,1},{6,2},{7,3},{8,12},{9,13},{10,... | collective-permute-start | bytes 208904 | tf_op jit(solution)/shard_map/ppermute | solution.py:374
  8.1 1.2 %collective-permute-start.2 = (f32[32,128]{1,0:T(8,128)S(1)}, f32[32,128]{1,0:T(8,128)S(1)}, u32[]{:S(2)}, u32[]{:S(2)}) collective-permute-start(f32[32,128]{1,0:T(8,128)S(1)} %observe.1), channel_id=1, source_target_pairs={{0,1},{1,0},{2,3},{3,2},{4,5},{5,4},{6,7},{7,6},{8,9},{9,8},{10,11... | collective-permute-start | bytes 49160 | tf_op jit(solution)/shard_map/ppermute | solution.py:384
  9.4 3.3 %collective-permute-start.3 = (f32[64,128]{1,0:T(8,128)S(1)}, f32[64,128]{1,0:T(8,128)S(1)}, u32[]{:S(2)}, u32[]{:S(2)}) collective-permute-start(f32[64,128]{1,0:T(8,128)S(1)} %pad_maximum_fusion.1), channel_id=1, source_target_pairs={{0,3},{1,2},{2,1},{3,0},{4,7},{5,6},{6,5},{7,4},{8,11},{9,10},{10,... | collective-permute-start | bytes 98312 | tf_op jit(solution)/shard_map/ppermute | solution.py:384
  13.2 4.7 %collective-permute-start.4 = (f32[16,128]{1,0:T(8,128)S(1)}, f32[16,128]{1,0:T(8,128)S(1)}, u32[]{:S(2)}, u32[]{:S(2)}) collective-permute-start(f32[16,128]{1,0:T(8,128)S(1)} %complete.1), channel_id=1, source_target_pairs={{0,17},{1,16},{2,19},{3,18},{4,21},{5,20},{6,23},{7,22},{8,25},{9,... | collective-permute-start | bytes 24584 | tf_op jit(solution)/shard_map/ppermute | solution.py:384
  17.9 4.0 %collective-permute-start.7 = (f32[32,128]{1,0:T(8,128)S(1)}, f32[32,128]{1,0:T(8,128)S(1)}, u32[]{:S(2)}, u32[]{:S(2)}) collective-permute-start(f32[32,128]{1,0:T(8,128)S(1)} %pad_maximum_fusion.2.refs_0_), channel_id=1, source_target_pairs={{0,5},{1,4},{2,7},{3,6},{4,1},{5,0},{6,3},{7,2},{8,13},{9,12},{10,... | collective-permute-start | bytes 49160 | tf_op jit(solution)/shard_map/ppermute | solution.py:384
  19.4 4.1 %collective-permute-start.6 = (f32[32,128]{1,0:T(8,128)S(1)}, f32[32,128]{1,0:T(8,128)S(1)}, u32[]{:S(2)}, u32[]{:S(2)}) collective-permute-start(f32[32,128]{1,0:T(8,128)S(1)} %pad_maximum_fusion.2.refs_0_), channel_id=1, source_target_pairs={{0,13},{1,12},{2,15},{3,14},{4,9},{5,8},{6,11},{7,10},{8,5},{9,4},... | collective-permute-start | bytes 49160 | tf_op jit(solution)/shard_map/ppermute | solution.py:384
  20.9 3.2 %collective-permute-start.5 = (f32[32,128]{1,0:T(8,128)S(1)}, f32[32,128]{1,0:T(8,128)S(1)}, u32[]{:S(2)}, u32[]{:S(2)}) collective-permute-start(f32[32,128]{1,0:T(8,128)S(1)} %pad_maximum_fusion.2.refs_0_), channel_id=1, source_target_pairs={{0,9},{1,8},{2,11},{3,10},{4,13},{5,12},{6,15},{7,14},{8,1},{9,0},... | collective-permute-start | bytes 49160 | tf_op jit(solution)/shard_map/ppermute | solution.py:384

commit v12 on v11

--- a/solution.py
+++ b/solution.py
@@ -31,7 +31,6 @@
 VALUE, FACTOR, TO_WEST, TO_EAST, WEIGHTS = 64, 65, 66, 67, 72
 HBM = pl.BlockSpec(memory_space=pltpu.HBM)
 ANY = pl.BlockSpec(memory_space=pl.ANY)
-ORDER = (2, 3, 1)
 
 
 def coefficients(k, u, v):
@@ -410,15 +409,16 @@
 
 
 def all_rows(packet):
-    size = lax.axis_size("gy")
-    if not two_power(size) or size < 4:
+    ny, nx = lax.axis_size("gy"), lax.axis_size("gx")
+    if not two_power(ny) or ny < 4 or nx % 2:
         return [lax.all_gather(packet, "gy", tiled=True)]
-    flip_x = 1 - lax.axis_size("gx") % 2
-    step = size // 2
+    step = ny // 2
     while step > 2:
-        packet = doubled(packet, step, flip_x)
+        packet = doubled(packet, step, 1)
         step //= 2
-    return [packet] + [partner(packet, flip_y, flip_x) for flip_y in ORDER]
+    pairs = [(a * nx + b, (a ^ (2 - b % 2)) * nx + (b ^ 1)) for a in range(ny) for b in range(nx)]
+    near = lax.ppermute(packet, ("gy", "gx"), pairs)
+    return [packet, near, partner(packet, 3, 1), partner(near, 0, 1)]
 
 
 def body(ensemble, flow, obs_cell, obs_value, obs_var):

time: 26.7 us -> 26.2 us (0.981)
  waiting for transfers between devices: 7 us -> 6.29 us
    ppermute x0 -> x1, starting transfers between devices: none -> 1.6 us  [all_rows(): near = lax.ppermute(packet, ('gy', 'gx'), pairs)]
    ppermute x6 -> x5, starting transfers between devices: 7.84 us -> 6.46 us  [partner(): return lax.ppermute(x, ('gy', 'gx'), pairs)]
    ppermute x6 -> x5, waiting for transfers between devices: 6.75 us -> 5.9 us  [partner(): return lax.ppermute(x, ('gy', 'gx'), pairs)]
where the time goes in v12:
time: 26.2 us; the launch traced here: 25.9 us
  starting transfers between devices  12.6 us (48%)
  Pallas kernels  6.95 us (27%)
  waiting for transfers between devices  6.29 us (24%)
    ppermute x5, starting transfers between devices, partner(): return lax.ppermute(x, ('gy', 'gx'), pairs)  6.46 us
    ppermute x5, waiting for transfers between devices, partner(): return lax.ppermute(x, ('gy', 'gx'), pairs)  5.9 us
    ppermute x2, starting transfers between devices, swap(): return lax.ppermute(x, ('gy', 'gx'), pairs)  4.55 us
    pallas_call x1, Pallas kernels, body(): call(functools.partial(analyse, members, count), out_shape=shape(members...  2.31 us
    pallas_call x1, Pallas kernels, body(): call(functools.partial(prepare, members, count, n_obs), out_shape=[shape(...  2.02 us
    ppermute x1, starting transfers between devices, all_rows(): near = lax.ppermute(packet, ('gy', 'gx'), pairs)  1.6 us
    pallas_call x1, Pallas kernels, body(): call(functools.partial(load, members, count), out_shape=[shape(2 * member...  0.88 us
    pallas_call x1, Pallas kernels, body(): call(functools.partial(forecast, members, count, size), out_shape=[jax.Sh...  0.87 us
  transfers between devices with their start and end apart: 8, of which 6 were waited for; matrix products, arithmetic and copies ran while one was open for 0% of the time, Pallas kernels for 11%

profile of v12, /device:TPU:0, one launch (start us, length us, event | category | flops | bytes accessed | tf_op | source)
XLA Modules:
  0.0 25.9 jit_solution(7315533656191118917)
XLA Ops:
  0.0 0.9 %load.1 = (f32[136,128]{1,0:T(8,128)S(1)}, f32[136,128]{1,0:T(8,128)S(1)}) custom-call(f32[64,8,128]{2,1,0:T(8,128)} %ens_hbm.3, f32[3,8,128]{2,1,0:T(8,128)} %flow_hbm.3), custom_call_target="tpu_custom_call" | custom-call | tf_op jit(solution)/shard_map/load/pallas_call | solution.py:437
  0.9 0.5 %collective-permute-start = (f32[136,128]{1,0:T(8,128)S(1)}, f32[136,128]{1,0:T(8,128)S(1)}, u32[]{:S(2)}, u32[]{:S(2)}) collective-permute-start(f32[136,128]{1,0:T(8,128)S(1)} %get-tuple-element.18), channel_id=1, source_target_pairs={{0,1},{1,0},{2,3},{3,2},{4,8},{5,9},{6,10},{7,11},{8,4},{9,5},{10,... | collective-permute-start | bytes 208904 | tf_op jit(solution)/shard_map/ppermute | solution.py:373
  1.4 4.0 %collective-permute-start.1 = (f32[136,128]{1,0:T(8,128)S(1)}, f32[136,128]{1,0:T(8,128)S(1)}, u32[]{:S(2)}, u32[]{:S(2)}) collective-permute-start(f32[136,128]{1,0:T(8,128)S(1)} %get-tuple-element.15.sent_ref), channel_id=1, source_target_pairs={{0,4},{1,5},{2,6},{3,7},{4,0},{5,1},{6,2},{7,3},{8,12},{9,13},{10,... | collective-permute-start | bytes 208904 | tf_op jit(solution)/shard_map/ppermute | solution.py:373
  5.4 2.0 %prepare.1 = (f32[512,128]{1,0:T(8,128)S(1)}, f32[3,8,128]{2,1,0:T(8,128)S(1)}, f32[64,128]{1,0:T(8,128)S(1)}, f32[16,128]{1,0:T(8,128)S(1)}, f32[4,16,128]{2,1,0:T(8,128)S(1)}, /*index=5*/f32[4,16,128]{2,1,0:T(8,128)S(1)}) custom-call(f32[64,8,128]{2,1,0:T(8,128)} %ens_hbm.3, f32[3,8,128]{2,1,0:T(8,128)} %flow_hbm.3, s32[4]{0:T(128)} %bitcast.4, f32[4]{0:T(128)} %bitcast.5, ...), custom_call_target="tpu_custom_call" | custom-call | flops 4000000 | bytes 600000 | tf_op jit(solution)/shard_map/prepare/pallas_call | solution.py:446
  7.5 0.0 collective-permute-done.odd_ref
  7.5 0.2 collective-permute-done.1.even_ref
  7.7 0.4 %observe.1 = f32[32,128]{1,0:T(8,128)S(1)} custom-call(f32[512,128]{1,0:T(8,128)S(1)} %get-tuple-element.16.field_ref, f32[3,8,128]{2,1,0:T(8,128)S(1)} %get-tuple-element.17.flow_ref, f32[64,128]{1,0:T(8,128)S(1)} %get-tuple-element.19.packed_ref, f32[16,128]{1,0:T(8,128)S(1)} %get-tuple-element.20.meta_ref, ...), custom_call_target="tpu_custom_call" | custom-call | tf_op jit(solution)/shard_map/observe/pallas_call | solution.py:459
  8.1 0.1 collective-permute-start.2
  8.2 1.2 %collective-permute-done.2 = f32[32,128]{1,0:T(8,128)S(1)} collective-permute-done((f32[32,128]{1,0:T(8,128)S(1)}, f32[32,128]{1,0:T(8,128)S(1)}, u32[]{:S(2)}, u32[]{:S(2)}) %collective-permute-start.2) | collective-permute-done | bytes 16416 | tf_op jit(solution)/shard_map/ppermute | solution.py:383
  9.4 1.3 %collective-permute-start.3 = (f32[64,128]{1,0:T(8,128)S(1)}, f32[64,128]{1,0:T(8,128)S(1)}, u32[]{:S(2)}, u32[]{:S(2)}) collective-permute-start(f32[64,128]{1,0:T(8,128)S(1)} %pad_maximum_fusion.1), channel_id=1, source_target_pairs={{0,3},{1,2},{2,1},{3,0},{4,7},{5,6},{6,5},{7,4},{8,11},{9,10},{10,... | collective-permute-start | bytes 98312 | tf_op jit(solution)/shard_map/ppermute | solution.py:383
  10.6 2.1 %collective-permute-done.3 = f32[64,128]{1,0:T(8,128)S(1)} collective-permute-done((f32[64,128]{1,0:T(8,128)S(1)}, f32[64,128]{1,0:T(8,128)S(1)}, u32[]{:S(2)}, u32[]{:S(2)}) %collective-permute-start.3) | collective-permute-done | bytes 32800 | tf_op jit(solution)/shard_map/ppermute | solution.py:383
  12.7 0.5 %complete.1 = f32[16,128]{1,0:T(8,128)S(1)} custom-call(f32[128,128]{1,0:T(8,128)S(1)} %pad_maximum_fusion.blocks_ref), custom_call_target="tpu_custom_call" | custom-call | tf_op jit(solution)/shard_map/complete/pallas_call | solution.py:468
  13.2 3.4 %collective-permute-start.4 = (f32[16,128]{1,0:T(8,128)S(1)}, f32[16,128]{1,0:T(8,128)S(1)}, u32[]{:S(2)}, u32[]{:S(2)}) collective-permute-start(f32[16,128]{1,0:T(8,128)S(1)} %complete.1), channel_id=1, source_target_pairs={{0,17},{1,16},{2,19},{3,18},{4,21},{5,20},{6,23},{7,22},{8,25},{9,... | collective-permute-start | bytes 24584 | tf_op jit(solution)/shard_map/ppermute | solution.py:383
  16.6 1.4 %collective-permute-done.4 = f32[16,128]{1,0:T(8,128)S(1)} collective-permute-done((f32[16,128]{1,0:T(8,128)S(1)}, f32[16,128]{1,0:T(8,128)S(1)}, u32[]{:S(2)}, u32[]{:S(2)}) %collective-permute-start.4) | collective-permute-done | bytes 8224 | tf_op jit(solution)/shard_map/ppermute | solution.py:383
  17.9 1.6 %collective-permute-start.5 = (f32[32,128]{1,0:T(8,128)S(1)}, f32[32,128]{1,0:T(8,128)S(1)}, u32[]{:S(2)}, u32[]{:S(2)}) collective-permute-start(f32[32,128]{1,0:T(8,128)S(1)} %pad_maximum_fusion.2.refs_0_), channel_id=1, source_target_pairs={{0,9},{1,4},{2,11},{3,6},{4,13},{5,0},{6,15},{7,2},{8,1},{9,12},{1... | collective-permute-start | bytes 49160 | tf_op jit(solution)/shard_map/ppermute | solution.py:420
  19.5 1.4 %collective-permute-start.6 = (f32[32,128]{1,0:T(8,128)S(1)}, f32[32,128]{1,0:T(8,128)S(1)}, u32[]{:S(2)}, u32[]{:S(2)}) collective-permute-start(f32[32,128]{1,0:T(8,128)S(1)} %pad_maximum_fusion.2.refs_0_), channel_id=1, source_target_pairs={{0,13},{1,12},{2,15},{3,14},{4,9},{5,8},{6,11},{7,10},{8,5},{9,4},... | collective-permute-start | bytes 49160 | tf_op jit(solution)/shard_map/ppermute | solution.py:383
  20.9 0.1 collective-permute-done.5.refs_1_
  21.1 0.3 %collective-permute-start.7 = (f32[32,128]{1,0:T(8,128)S(1)}, f32[32,128]{1,0:T(8,128)S(1)}, u32[]{:S(2)}, u32[]{:S(2)}) collective-permute-start(f32[32,128]{1,0:T(8,128)S(1)} %collective-permute-done.5.refs_1_), channel_id=1, source_target_pairs={{0,1},{1,0},{2,3},{3,2},{4,5},{5,4},{6,7},{7,6},{8,9},{9,8},{10,11... | collective-permute-start | bytes 49160 | tf_op jit(solution)/shard_map/ppermute | solution.py:383
  21.4 0.9 %forecast.1 = (bf16[192,1024]{1,0:T(8,128)(2,1)S(1)}, f32[8,128]{1,0:T(8,128)S(1)}) custom-call(f32[512,128]{1,0:T(8,128)S(1)} %get-tuple-element.16.field_ref, f32[3,8,128]{2,1,0:T(8,128)S(1)} %get-tuple-element.17.flow_ref, f32[136,128]{1,0:T(8,128)S(1)} %collective-permute-done.odd_ref, f32[136,128]{1,0:T(8,128)S(1)} %collective-permute-done.1.even_ref, ...), custom_call_target="tpu_custom_call" | custom-call | flops 4000000 | bytes 600000 | tf_op jit(solution)/shard_map/forecast/pallas_call | solution.py:475
  22.3 1.3 %collective-permute-done.6.refs_2_ = f32[32,128]{1,0:T(8,128)S(1)} collective-permute-done((f32[32,128]{1,0:T(8,128)S(1)}, f32[32,128]{1,0:T(8,128)S(1)}, u32[]{:S(2)}, u32[]{:S(2)}) %collective-permute-start.6) | collective-permute-done | bytes 16416 | tf_op jit(solution)/shard_map/ppermute | solution.py:383
  23.6 0.0 collective-permute-done.7.refs_3_
  23.6 2.3 %analyse.1 = f32[512,128]{1,0:T(8,128)} custom-call(bf16[192,1024]{1,0:T(8,128)(2,1)S(1)} %get-tuple-element.23.f_ref, f32[8,128]{1,0:T(8,128)S(1)} %get-tuple-element.24.mean_ref, f32[32,128]{1,0:T(8,128)S(1)} %pad_maximum_fusion.2.refs_0_, f32[32,128]{1,0:T(8,128)S(1)} %collective-permute-done.5.refs_1_, f32[32,128]{1,0:T(8,128)S(1)} %collective-permute-done.6.refs_2_, ...), custom_call_target="tpu_custom_call" | custom-call | tf_op jit(solution)/shard_map/analyse/pallas_call | solution.py:485
  (3 shorter events, 0.0 us)
Async XLA Ops:
  0.9 6.6 %collective-permute-start = (f32[136,128]{1,0:T(8,128)S(1)}, f32[136,128]{1,0:T(8,128)S(1)}, u32[]{:S(2)}, u32[]{:S(2)}) collective-permute-start(f32[136,128]{1,0:T(8,128)S(1)} %get-tuple-element.18), channel_id=1, source_target_pairs={{0,1},{1,0},{2,3},{3,2},{4,8},{5,9},{6,10},{7,11},{8,4},{9,5},{10,... | collective-permute-start | bytes 208904 | tf_op jit(solution)/shard_map/ppermute | solution.py:373
  1.4 6.3 %collective-permute-start.1 = (f32[136,128]{1,0:T(8,128)S(1)}, f32[136,128]{1,0:T(8,128)S(1)}, u32[]{:S(2)}, u32[]{:S(2)}) collective-permute-start(f32[136,128]{1,0:T(8,128)S(1)} %get-tuple-element.15.sent_ref), channel_id=1, source_target_pairs={{0,4},{1,5},{2,6},{3,7},{4,0},{5,1},{6,2},{7,3},{8,12},{9,13},{10,... | collective-permute-start | bytes 208904 | tf_op jit(solution)/shard_map/ppermute | solution.py:373
  8.1 1.2 %collective-permute-start.2 = (f32[32,128]{1,0:T(8,128)S(1)}, f32[32,128]{1,0:T(8,128)S(1)}, u32[]{:S(2)}, u32[]{:S(2)}) collective-permute-start(f32[32,128]{1,0:T(8,128)S(1)} %observe.1), channel_id=1, source_target_pairs={{0,1},{1,0},{2,3},{3,2},{4,5},{5,4},{6,7},{7,6},{8,9},{9,8},{10,11... | collective-permute-start | bytes 49160 | tf_op jit(solution)/shard_map/ppermute | solution.py:383
  9.4 3.3 %collective-permute-start.3 = (f32[64,128]{1,0:T(8,128)S(1)}, f32[64,128]{1,0:T(8,128)S(1)}, u32[]{:S(2)}, u32[]{:S(2)}) collective-permute-start(f32[64,128]{1,0:T(8,128)S(1)} %pad_maximum_fusion.1), channel_id=1, source_target_pairs={{0,3},{1,2},{2,1},{3,0},{4,7},{5,6},{6,5},{7,4},{8,11},{9,10},{10,... | collective-permute-start | bytes 98312 | tf_op jit(solution)/shard_map/ppermute | solution.py:383
  13.2 4.7 %collective-permute-start.4 = (f32[16,128]{1,0:T(8,128)S(1)}, f32[16,128]{1,0:T(8,128)S(1)}, u32[]{:S(2)}, u32[]{:S(2)}) collective-permute-start(f32[16,128]{1,0:T(8,128)S(1)} %complete.1), channel_id=1, source_target_pairs={{0,17},{1,16},{2,19},{3,18},{4,21},{5,20},{6,23},{7,22},{8,25},{9,... | collective-permute-start | bytes 24584 | tf_op jit(solution)/shard_map/ppermute | solution.py:383
  17.9 3.2 %collective-permute-start.5 = (f32[32,128]{1,0:T(8,128)S(1)}, f32[32,128]{1,0:T(8,128)S(1)}, u32[]{:S(2)}, u32[]{:S(2)}) collective-permute-start(f32[32,128]{1,0:T(8,128)S(1)} %pad_maximum_fusion.2.refs_0_), channel_id=1, source_target_pairs={{0,9},{1,4},{2,11},{3,6},{4,13},{5,0},{6,15},{7,2},{8,1},{9,12},{1... | collective-permute-start | bytes 49160 | tf_op jit(solution)/shard_map/ppermute | solution.py:420
  19.5 4.1 %collective-permute-start.6 = (f32[32,128]{1,0:T(8,128)S(1)}, f32[32,128]{1,0:T(8,128)S(1)}, u32[]{:S(2)}, u32[]{:S(2)}) collective-permute-start(f32[32,128]{1,0:T(8,128)S(1)} %pad_maximum_fusion.2.refs_0_), channel_id=1, source_target_pairs={{0,13},{1,12},{2,15},{3,14},{4,9},{5,8},{6,11},{7,10},{8,5},{9,4},... | collective-permute-start | bytes 49160 | tf_op jit(solution)/shard_map/ppermute | solution.py:383
  21.1 2.5 %collective-permute-start.7 = (f32[32,128]{1,0:T(8,128)S(1)}, f32[32,128]{1,0:T(8,128)S(1)}, u32[]{:S(2)}, u32[]{:S(2)}) collective-permute-start(f32[32,128]{1,0:T(8,128)S(1)} %collective-permute-done.5.refs_1_), channel_id=1, source_target_pairs={{0,1},{1,0},{2,3},{3,2},{4,5},{5,4},{6,7},{7,6},{8,9},{9,8},{10,11... | collective-permute-start | bytes 49160 | tf_op jit(solution)/shard_map/ppermute | solution.py:383

commit v13 on v12

--- a/solution.py
+++ b/solution.py
@@ -235,21 +235,24 @@
 
 
 def complete(members, n_obs, size, blocks_ref, out_ref):
-    lane = lanes((n_obs, 128))
+    rows = n_obs * size
+    lane, sub = lanes((rows, 128)), rows_of((rows, 128))
+    at = own = jnp.zeros((rows, 128), F32)
     for tile in range(size):
         west, east, west_mid, east_mid = side_columns(blocks_ref, jnp.int32(tile), size)
         block = block_rows(blocks_ref, OBS, jnp.int32(tile), size, 8)
         terms = (west[:8], west[8:], east[:8], east[8:], west_mid, east_mid)
-        added = []
         for j in range(n_obs):
-            at = [WEIGHTS + k * n_obs + j for k in range(len(terms))]
-            total = sum(block[:, a : a + 1] * term for a, term in zip(at, terms))
-            added.append(jnp.sum(total, axis=0, keepdims=True))
-        block = block[:n_obs]
-        at = jnp.where(lane < members, block + jnp.concatenate(added, axis=0), 0.0)
-        mean = jnp.sum(at, axis=1, keepdims=True) * (1.0 / members)
-        raw = jnp.where(lane < members, at - mean, jnp.where(lane == members, block[:, VALUE : VALUE + 1] - mean, 0.0))
-        out_ref[n_obs * tile : n_obs * (tile + 1), :] = raw * block[:, FACTOR : FACTOR + 1]
+            places = [WEIGHTS + k * n_obs + j for k in range(len(terms))]
+            total = sum(block[:, a : a + 1] * term for a, term in zip(places, terms))
+            row = jnp.sum(total, axis=0, keepdims=True) + block[j : j + 1, :]
+            here = sub == n_obs * tile + j
+            at = jnp.where(here, row, at)
+            own = jnp.where(here, block[j : j + 1, :], own)
+    at = jnp.where(lane < members, at, 0.0)
+    mean = jnp.sum(at, axis=1, keepdims=True) * (1.0 / members)
+    raw = jnp.where(lane < members, at - mean, jnp.where(lane == members, own[:, VALUE : VALUE + 1] - mean, 0.0))
+    out_ref[...] = raw * own[:, FACTOR : FACTOR + 1]
 
 
 def forecast(members, count, size, field_ref, flow_ref, odd_ref, even_ref, blocks_ref, out_ref, mean_ref, tall_ref):
@@ -388,24 +391,25 @@
 
 
 def row_blocks(block):
-    size, step = lax.axis_size("gx"), 1
+    size = step = lax.axis_size("gx")
     if not two_power(size):
         return lax.all_gather(block, "gx", tiled=True)
-    while step < size:
+    while step > 2:
+        step //= 2
         block = doubled(block, 0, step | 1)
-        step *= 2
-    return block
+    return doubled(block, 0, 1) if size > 1 else block
 
 
 def place_of(tile, size):
-    if not two_power(size):
+    if not two_power(size) or size == 1:
         return tile
     distance = jnp.bitwise_xor(lax.axis_index("gx"), tile)
-    place, bit = distance, 2
-    while bit < size:
-        place = jnp.bitwise_xor(place, (distance // bit) % 2)
-        bit *= 2
-    return place
+    place, last, value, bit = 0, distance % 2, 1, size // 2
+    while bit > 1:
+        chosen = (distance // bit) % 2
+        place, last = place + chosen * value, jnp.bitwise_xor(last, chosen)
+        value, bit = 2 * value, bit // 2
+    return place + last * value
 
 
 def all_rows(packet):

time: 26.2 us -> 26 us (level)
  starting transfers between devices: 12.6 us -> 12 us
  waiting for transfers between devices: 6.29 us -> 6.83 us
    ppermute x5, starting transfers between devices: 6.46 us -> 5.86 us  [partner(): return lax.ppermute(x, ('gy', 'gx'), pairs)]
    ppermute x5, waiting for transfers between devices: 5.9 us -> 6.43 us  [partner(): return lax.ppermute(x, ('gy', 'gx'), pairs)]
where the time goes in v13:
time: 26 us; the launch traced here: 25.8 us
  starting transfers between devices  12 us (46%)
  Pallas kernels  6.9 us (27%)
  waiting for transfers between devices  6.83 us (26%)
    ppermute x5, waiting for transfers between devices, partner(): return lax.ppermute(x, ('gy', 'gx'), pairs)  6.43 us
    ppermute x5, starting transfers between devices, partner(): return lax.ppermute(x, ('gy', 'gx'), pairs)  5.86 us
    ppermute x2, starting transfers between devices, swap(): return lax.ppermute(x, ('gy', 'gx'), pairs)  4.55 us
    pallas_call x1, Pallas kernels, body(): call(functools.partial(analyse, members, count), out_shape=shape(members...  2.31 us
    pallas_call x1, Pallas kernels, body(): call(functools.partial(prepare, members, count, n_obs), out_shape=[shape(...  2.02 us
    ppermute x1, starting transfers between devices, all_rows(): near = lax.ppermute(packet, ('gy', 'gx'), pairs)  1.6 us
    pallas_call x1, Pallas kernels, body(): call(functools.partial(load, members, count), out_shape=[shape(2 * member...  0.88 us
    pallas_call x1, Pallas kernels, body(): call(functools.partial(forecast, members, count, size), out_shape=[jax.Sh...  0.87 us
  transfers between devices with their start and end apart: 8, of which 6 were waited for; matrix products, arithmetic and copies ran while one was open for 0% of the time, Pallas kernels for 11%

profile of v13, /device:TPU:0, one launch (start us, length us, event | category | flops | bytes accessed | tf_op | source)
XLA Modules:
  0.0 25.8 jit_solution(12758514083340814085)
XLA Ops:
  0.0 0.9 %load.1 = (f32[136,128]{1,0:T(8,128)S(1)}, f32[136,128]{1,0:T(8,128)S(1)}) custom-call(f32[64,8,128]{2,1,0:T(8,128)} %ens_hbm.3, f32[3,8,128]{2,1,0:T(8,128)} %flow_hbm.3), custom_call_target="tpu_custom_call" | custom-call | tf_op jit(solution)/shard_map/load/pallas_call | solution.py:441
  0.9 0.5 %collective-permute-start = (f32[136,128]{1,0:T(8,128)S(1)}, f32[136,128]{1,0:T(8,128)S(1)}, u32[]{:S(2)}, u32[]{:S(2)}) collective-permute-start(f32[136,128]{1,0:T(8,128)S(1)} %get-tuple-element.18), channel_id=1, source_target_pairs={{0,1},{1,0},{2,3},{3,2},{4,8},{5,9},{6,10},{7,11},{8,4},{9,5},{10,... | collective-permute-start | bytes 208904 | tf_op jit(solution)/shard_map/ppermute | solution.py:376
  1.4 4.0 %collective-permute-start.1 = (f32[136,128]{1,0:T(8,128)S(1)}, f32[136,128]{1,0:T(8,128)S(1)}, u32[]{:S(2)}, u32[]{:S(2)}) collective-permute-start(f32[136,128]{1,0:T(8,128)S(1)} %get-tuple-element.15.sent_ref), channel_id=1, source_target_pairs={{0,4},{1,5},{2,6},{3,7},{4,0},{5,1},{6,2},{7,3},{8,12},{9,13},{10,... | collective-permute-start | bytes 208904 | tf_op jit(solution)/shard_map/ppermute | solution.py:376
  5.4 2.0 %prepare.1 = (f32[512,128]{1,0:T(8,128)S(1)}, f32[3,8,128]{2,1,0:T(8,128)S(1)}, f32[64,128]{1,0:T(8,128)S(1)}, f32[16,128]{1,0:T(8,128)S(1)}, f32[4,16,128]{2,1,0:T(8,128)S(1)}, /*index=5*/f32[4,16,128]{2,1,0:T(8,128)S(1)}) custom-call(f32[64,8,128]{2,1,0:T(8,128)} %ens_hbm.3, f32[3,8,128]{2,1,0:T(8,128)} %flow_hbm.3, s32[4]{0:T(128)} %bitcast.4, f32[4]{0:T(128)} %bitcast.5, ...), custom_call_target="tpu_custom_call" | custom-call | flops 4000000 | bytes 600000 | tf_op jit(solution)/shard_map/prepare/pallas_call | solution.py:450
  7.5 0.0 collective-permute-done.odd_ref
  7.5 0.2 collective-permute-done.1.even_ref
  7.7 0.4 %observe.1 = f32[32,128]{1,0:T(8,128)S(1)} custom-call(f32[512,128]{1,0:T(8,128)S(1)} %get-tuple-element.16.field_ref, f32[3,8,128]{2,1,0:T(8,128)S(1)} %get-tuple-element.17.flow_ref, f32[64,128]{1,0:T(8,128)S(1)} %get-tuple-element.19.packed_ref, f32[16,128]{1,0:T(8,128)S(1)} %get-tuple-element.20.meta_ref, ...), custom_call_target="tpu_custom_call" | custom-call | tf_op jit(solution)/shard_map/observe/pallas_call | solution.py:463
  8.1 0.7 %collective-permute-start.2 = (f32[32,128]{1,0:T(8,128)S(1)}, f32[32,128]{1,0:T(8,128)S(1)}, u32[]{:S(2)}, u32[]{:S(2)}) collective-permute-start(f32[32,128]{1,0:T(8,128)S(1)} %observe.1), channel_id=1, source_target_pairs={{0,3},{1,2},{2,1},{3,0},{4,7},{5,6},{6,5},{7,4},{8,11},{9,10},{10,... | collective-permute-start | bytes 49160 | tf_op jit(solution)/shard_map/ppermute | solution.py:386
  8.8 2.7 %collective-permute-done.2 = f32[32,128]{1,0:T(8,128)S(1)} collective-permute-done((f32[32,128]{1,0:T(8,128)S(1)}, f32[32,128]{1,0:T(8,128)S(1)}, u32[]{:S(2)}, u32[]{:S(2)}) %collective-permute-start.2) | collective-permute-done | bytes 16416 | tf_op jit(solution)/shard_map/ppermute | solution.py:386
  11.4 0.1 collective-permute-start.3
  11.6 1.1 %collective-permute-done.3 = f32[64,128]{1,0:T(8,128)S(1)} collective-permute-done((f32[64,128]{1,0:T(8,128)S(1)}, f32[64,128]{1,0:T(8,128)S(1)}, u32[]{:S(2)}, u32[]{:S(2)}) %collective-permute-start.3) | collective-permute-done | bytes 32800 | tf_op jit(solution)/shard_map/ppermute | solution.py:386
  12.7 0.4 %complete.1 = f32[16,128]{1,0:T(8,128)S(1)} custom-call(f32[128,128]{1,0:T(8,128)S(1)} %pad_maximum_fusion.blocks_ref), custom_call_target="tpu_custom_call" | custom-call | tf_op jit(solution)/shard_map/complete/pallas_call | solution.py:472
  13.1 3.4 %collective-permute-start.4 = (f32[16,128]{1,0:T(8,128)S(1)}, f32[16,128]{1,0:T(8,128)S(1)}, u32[]{:S(2)}, u32[]{:S(2)}) collective-permute-start(f32[16,128]{1,0:T(8,128)S(1)} %complete.1), channel_id=1, source_target_pairs={{0,17},{1,16},{2,19},{3,18},{4,21},{5,20},{6,23},{7,22},{8,25},{9,... | collective-permute-start | bytes 24584 | tf_op jit(solution)/shard_map/ppermute | solution.py:386
  16.4 1.4 %collective-permute-done.4 = f32[16,128]{1,0:T(8,128)S(1)} collective-permute-done((f32[16,128]{1,0:T(8,128)S(1)}, f32[16,128]{1,0:T(8,128)S(1)}, u32[]{:S(2)}, u32[]{:S(2)}) %collective-permute-start.4) | collective-permute-done | bytes 8224 | tf_op jit(solution)/shard_map/ppermute | solution.py:386
  17.8 1.6 %collective-permute-start.5 = (f32[32,128]{1,0:T(8,128)S(1)}, f32[32,128]{1,0:T(8,128)S(1)}, u32[]{:S(2)}, u32[]{:S(2)}) collective-permute-start(f32[32,128]{1,0:T(8,128)S(1)} %pad_maximum_fusion.2.refs_0_), channel_id=1, source_target_pairs={{0,9},{1,4},{2,11},{3,6},{4,13},{5,0},{6,15},{7,2},{8,1},{9,12},{1... | collective-permute-start | bytes 49160 | tf_op jit(solution)/shard_map/ppermute | solution.py:424
  19.4 1.4 %collective-permute-start.6 = (f32[32,128]{1,0:T(8,128)S(1)}, f32[32,128]{1,0:T(8,128)S(1)}, u32[]{:S(2)}, u32[]{:S(2)}) collective-permute-start(f32[32,128]{1,0:T(8,128)S(1)} %pad_maximum_fusion.2.refs_0_), channel_id=1, source_target_pairs={{0,13},{1,12},{2,15},{3,14},{4,9},{5,8},{6,11},{7,10},{8,5},{9,4},... | collective-permute-start | bytes 49160 | tf_op jit(solution)/shard_map/ppermute | solution.py:386
  20.8 0.2 collective-permute-done.5.refs_1_
  21.0 0.3 %collective-permute-start.7 = (f32[32,128]{1,0:T(8,128)S(1)}, f32[32,128]{1,0:T(8,128)S(1)}, u32[]{:S(2)}, u32[]{:S(2)}) collective-permute-start(f32[32,128]{1,0:T(8,128)S(1)} %collective-permute-done.5.refs_1_), channel_id=1, source_target_pairs={{0,1},{1,0},{2,3},{3,2},{4,5},{5,4},{6,7},{7,6},{8,9},{9,8},{10,11... | collective-permute-start | bytes 49160 | tf_op jit(solution)/shard_map/ppermute | solution.py:386
  21.3 0.9 %forecast.1 = (bf16[192,1024]{1,0:T(8,128)(2,1)S(1)}, f32[8,128]{1,0:T(8,128)S(1)}) custom-call(f32[512,128]{1,0:T(8,128)S(1)} %get-tuple-element.16.field_ref, f32[3,8,128]{2,1,0:T(8,128)S(1)} %get-tuple-element.17.flow_ref, f32[136,128]{1,0:T(8,128)S(1)} %collective-permute-done.odd_ref, f32[136,128]{1,0:T(8,128)S(1)} %collective-permute-done.1.even_ref, ...), custom_call_target="tpu_custom_call" | custom-call | flops 4000000 | bytes 600000 | tf_op jit(solution)/shard_map/forecast/pallas_call | solution.py:479
  22.2 1.3 %collective-permute-done.6.refs_2_ = f32[32,128]{1,0:T(8,128)S(1)} collective-permute-done((f32[32,128]{1,0:T(8,128)S(1)}, f32[32,128]{1,0:T(8,128)S(1)}, u32[]{:S(2)}, u32[]{:S(2)}) %collective-permute-start.6) | collective-permute-done | bytes 16416 | tf_op jit(solution)/shard_map/ppermute | solution.py:386
  23.5 0.0 collective-permute-done.7.refs_3_
  23.5 2.3 %analyse.1 = f32[512,128]{1,0:T(8,128)} custom-call(bf16[192,1024]{1,0:T(8,128)(2,1)S(1)} %get-tuple-element.23.f_ref, f32[8,128]{1,0:T(8,128)S(1)} %get-tuple-element.24.mean_ref, f32[32,128]{1,0:T(8,128)S(1)} %pad_maximum_fusion.2.refs_0_, f32[32,128]{1,0:T(8,128)S(1)} %collective-permute-done.5.refs_1_, f32[32,128]{1,0:T(8,128)S(1)} %collective-permute-done.6.refs_2_, ...), custom_call_target="tpu_custom_call" | custom-call | tf_op jit(solution)/shard_map/analyse/pallas_call | solution.py:489
  (3 shorter events, 0.0 us)
Async XLA Ops:
  0.9 6.6 %collective-permute-start = (f32[136,128]{1,0:T(8,128)S(1)}, f32[136,128]{1,0:T(8,128)S(1)}, u32[]{:S(2)}, u32[]{:S(2)}) collective-permute-start(f32[136,128]{1,0:T(8,128)S(1)} %get-tuple-element.18), channel_id=1, source_target_pairs={{0,1},{1,0},{2,3},{3,2},{4,8},{5,9},{6,10},{7,11},{8,4},{9,5},{10,... | collective-permute-start | bytes 208904 | tf_op jit(solution)/shard_map/ppermute | solution.py:376
  1.4 6.3 %collective-permute-start.1 = (f32[136,128]{1,0:T(8,128)S(1)}, f32[136,128]{1,0:T(8,128)S(1)}, u32[]{:S(2)}, u32[]{:S(2)}) collective-permute-start(f32[136,128]{1,0:T(8,128)S(1)} %get-tuple-element.15.sent_ref), channel_id=1, source_target_pairs={{0,4},{1,5},{2,6},{3,7},{4,0},{5,1},{6,2},{7,3},{8,12},{9,13},{10,... | collective-permute-start | bytes 208904 | tf_op jit(solution)/shard_map/ppermute | solution.py:376
  8.1 3.3 %collective-permute-start.2 = (f32[32,128]{1,0:T(8,128)S(1)}, f32[32,128]{1,0:T(8,128)S(1)}, u32[]{:S(2)}, u32[]{:S(2)}) collective-permute-start(f32[32,128]{1,0:T(8,128)S(1)} %observe.1), channel_id=1, source_target_pairs={{0,3},{1,2},{2,1},{3,0},{4,7},{5,6},{6,5},{7,4},{8,11},{9,10},{10,... | collective-permute-start | bytes 49160 | tf_op jit(solution)/shard_map/ppermute | solution.py:386
  11.4 1.2 %collective-permute-start.3 = (f32[64,128]{1,0:T(8,128)S(1)}, f32[64,128]{1,0:T(8,128)S(1)}, u32[]{:S(2)}, u32[]{:S(2)}) collective-permute-start(f32[64,128]{1,0:T(8,128)S(1)} %pad_maximum_fusion.1), channel_id=1, source_target_pairs={{0,1},{1,0},{2,3},{3,2},{4,5},{5,4},{6,7},{7,6},{8,9},{9,8},{10,11... | collective-permute-start | bytes 98312 | tf_op jit(solution)/shard_map/ppermute | solution.py:386
  13.1 4.7 %collective-permute-start.4 = (f32[16,128]{1,0:T(8,128)S(1)}, f32[16,128]{1,0:T(8,128)S(1)}, u32[]{:S(2)}, u32[]{:S(2)}) collective-permute-start(f32[16,128]{1,0:T(8,128)S(1)} %complete.1), channel_id=1, source_target_pairs={{0,17},{1,16},{2,19},{3,18},{4,21},{5,20},{6,23},{7,22},{8,25},{9,... | collective-permute-start | bytes 24584 | tf_op jit(solution)/shard_map/ppermute | solution.py:386
  17.8 3.2 %collective-permute-start.5 = (f32[32,128]{1,0:T(8,128)S(1)}, f32[32,128]{1,0:T(8,128)S(1)}, u32[]{:S(2)}, u32[]{:S(2)}) collective-permute-start(f32[32,128]{1,0:T(8,128)S(1)} %pad_maximum_fusion.2.refs_0_), channel_id=1, source_target_pairs={{0,9},{1,4},{2,11},{3,6},{4,13},{5,0},{6,15},{7,2},{8,1},{9,12},{1... | collective-permute-start | bytes 49160 | tf_op jit(solution)/shard_map/ppermute | solution.py:424
  19.4 4.1 %collective-permute-start.6 = (f32[32,128]{1,0:T(8,128)S(1)}, f32[32,128]{1,0:T(8,128)S(1)}, u32[]{:S(2)}, u32[]{:S(2)}) collective-permute-start(f32[32,128]{1,0:T(8,128)S(1)} %pad_maximum_fusion.2.refs_0_), channel_id=1, source_target_pairs={{0,13},{1,12},{2,15},{3,14},{4,9},{5,8},{6,11},{7,10},{8,5},{9,4},... | collective-permute-start | bytes 49160 | tf_op jit(solution)/shard_map/ppermute | solution.py:386
  21.0 2.5 %collective-permute-start.7 = (f32[32,128]{1,0:T(8,128)S(1)}, f32[32,128]{1,0:T(8,128)S(1)}, u32[]{:S(2)}, u32[]{:S(2)}) collective-permute-start(f32[32,128]{1,0:T(8,128)S(1)} %collective-permute-done.5.refs_1_), channel_id=1, source_target_pairs={{0,1},{1,0},{2,3},{3,2},{4,5},{5,4},{6,7},{7,6},{8,9},{9,8},{10,11... | collective-permute-start | bytes 49160 | tf_op jit(solution)/shard_map/ppermute | solution.py:386

commit v14 on v13

--- a/solution.py
+++ b/solution.py
@@ -241,10 +241,16 @@
     for tile in range(size):
         west, east, west_mid, east_mid = side_columns(blocks_ref, jnp.int32(tile), size)
         block = block_rows(blocks_ref, OBS, jnp.int32(tile), size, 8)
-        terms = (west[:8], west[8:], east[:8], east[8:], west_mid, east_mid)
+        terms = []
+        if tile > 0:
+            terms += [(0, west[:8]), (1, west[8:]), (4, west_mid)]
+        if tile < size - 1:
+            terms += [(2, east[:8]), (3, east[8:]), (5, east_mid)]
         for j in range(n_obs):
-            places = [WEIGHTS + k * n_obs + j for k in range(len(terms))]
-            total = sum(block[:, a : a + 1] * term for a, term in zip(places, terms))
+            total = jnp.zeros((8, 128), F32)
+            for k, term in terms:
+                place = WEIGHTS + k * n_obs + j
+                total = total + block[:, place : place + 1] * term
             row = jnp.sum(total, axis=0, keepdims=True) + block[j : j + 1, :]
             here = sub == n_obs * tile + j
             at = jnp.where(here, row, at)

time: 26 us -> 26 us (level)
  no operation moved by 1% of the time
where the time goes in v14:
time: 26 us; the launch traced here: 25.7 us
  starting transfers between devices  12 us (46%)
  Pallas kernels  6.86 us (26%)
  waiting for transfers between devices  6.82 us (26%)
    ppermute x5, waiting for transfers between devices, partner(): return lax.ppermute(x, ('gy', 'gx'), pairs)  6.42 us
    ppermute x5, starting transfers between devices, partner(): return lax.ppermute(x, ('gy', 'gx'), pairs)  5.86 us
    ppermute x2, starting transfers between devices, swap(): return lax.ppermute(x, ('gy', 'gx'), pairs)  4.55 us
    pallas_call x1, Pallas kernels, body(): call(functools.partial(analyse, members, count), out_shape=shape(members...  2.32 us
    pallas_call x1, Pallas kernels, body(): call(functools.partial(prepare, members, count, n_obs), out_shape=[shape(...  2.02 us
    ppermute x1, starting transfers between devices, all_rows(): near = lax.ppermute(packet, ('gy', 'gx'), pairs)  1.6 us
    pallas_call x1, Pallas kernels, body(): call(functools.partial(load, members, count), out_shape=[shape(2 * member...  0.88 us
    pallas_call x1, Pallas kernels, body(): call(functools.partial(forecast, members, count, size), out_shape=[jax.Sh...  0.87 us
  transfers between devices with their start and end apart: 8, of which 6 were waited for; matrix products, arithmetic and copies ran while one was open for 0% of the time, Pallas kernels for 11%

profile of v14, /device:TPU:0, one launch (start us, length us, event | category | flops | bytes accessed | tf_op | source)
XLA Modules:
  0.0 25.7 jit_solution(17395027375379947986)
XLA Ops:
  0.0 0.9 %load.1 = (f32[136,128]{1,0:T(8,128)S(1)}, f32[136,128]{1,0:T(8,128)S(1)}) custom-call(f32[64,8,128]{2,1,0:T(8,128)} %ens_hbm.3, f32[3,8,128]{2,1,0:T(8,128)} %flow_hbm.3), custom_call_target="tpu_custom_call" | custom-call | tf_op jit(solution)/shard_map/load/pallas_call | solution.py:447
  0.9 0.5 %collective-permute-start = (f32[136,128]{1,0:T(8,128)S(1)}, f32[136,128]{1,0:T(8,128)S(1)}, u32[]{:S(2)}, u32[]{:S(2)}) collective-permute-start(f32[136,128]{1,0:T(8,128)S(1)} %get-tuple-element.18), channel_id=1, source_target_pairs={{0,1},{1,0},{2,3},{3,2},{4,8},{5,9},{6,10},{7,11},{8,4},{9,5},{10,... | collective-permute-start | bytes 208904 | tf_op jit(solution)/shard_map/ppermute | solution.py:382
  1.4 4.0 %collective-permute-start.1 = (f32[136,128]{1,0:T(8,128)S(1)}, f32[136,128]{1,0:T(8,128)S(1)}, u32[]{:S(2)}, u32[]{:S(2)}) collective-permute-start(f32[136,128]{1,0:T(8,128)S(1)} %get-tuple-element.15.sent_ref), channel_id=1, source_target_pairs={{0,4},{1,5},{2,6},{3,7},{4,0},{5,1},{6,2},{7,3},{8,12},{9,13},{10,... | collective-permute-start | bytes 208904 | tf_op jit(solution)/shard_map/ppermute | solution.py:382
  5.4 2.0 %prepare.1 = (f32[512,128]{1,0:T(8,128)S(1)}, f32[3,8,128]{2,1,0:T(8,128)S(1)}, f32[64,128]{1,0:T(8,128)S(1)}, f32[16,128]{1,0:T(8,128)S(1)}, f32[4,16,128]{2,1,0:T(8,128)S(1)}, /*index=5*/f32[4,16,128]{2,1,0:T(8,128)S(1)}) custom-call(f32[64,8,128]{2,1,0:T(8,128)} %ens_hbm.3, f32[3,8,128]{2,1,0:T(8,128)} %flow_hbm.3, s32[4]{0:T(128)} %bitcast.4, f32[4]{0:T(128)} %bitcast.5, ...), custom_call_target="tpu_custom_call" | custom-call | flops 4000000 | bytes 600000 | tf_op jit(solution)/shard_map/prepare/pallas_call | solution.py:456
  7.5 0.0 collective-permute-done.odd_ref
  7.5 0.2 collective-permute-done.1.even_ref
  7.7 0.4 %observe.1 = f32[32,128]{1,0:T(8,128)S(1)} custom-call(f32[512,128]{1,0:T(8,128)S(1)} %get-tuple-element.16.field_ref, f32[3,8,128]{2,1,0:T(8,128)S(1)} %get-tuple-element.17.flow_ref, f32[64,128]{1,0:T(8,128)S(1)} %get-tuple-element.19.packed_ref, f32[16,128]{1,0:T(8,128)S(1)} %get-tuple-element.20.meta_ref, ...), custom_call_target="tpu_custom_call" | custom-call | tf_op jit(solution)/shard_map/observe/pallas_call | solution.py:469
  8.1 0.7 %collective-permute-start.2 = (f32[32,128]{1,0:T(8,128)S(1)}, f32[32,128]{1,0:T(8,128)S(1)}, u32[]{:S(2)}, u32[]{:S(2)}) collective-permute-start(f32[32,128]{1,0:T(8,128)S(1)} %observe.1), channel_id=1, source_target_pairs={{0,3},{1,2},{2,1},{3,0},{4,7},{5,6},{6,5},{7,4},{8,11},{9,10},{10,... | collective-permute-start | bytes 49160 | tf_op jit(solution)/shard_map/ppermute | solution.py:392
  8.8 2.7 %collective-permute-done.2 = f32[32,128]{1,0:T(8,128)S(1)} collective-permute-done((f32[32,128]{1,0:T(8,128)S(1)}, f32[32,128]{1,0:T(8,128)S(1)}, u32[]{:S(2)}, u32[]{:S(2)}) %collective-permute-start.2) | collective-permute-done | bytes 16416 | tf_op jit(solution)/shard_map/ppermute | solution.py:392
  11.4 0.1 collective-permute-start.3
  11.6 1.1 %collective-permute-done.3 = f32[64,128]{1,0:T(8,128)S(1)} collective-permute-done((f32[64,128]{1,0:T(8,128)S(1)}, f32[64,128]{1,0:T(8,128)S(1)}, u32[]{:S(2)}, u32[]{:S(2)}) %collective-permute-start.3) | collective-permute-done | bytes 32800 | tf_op jit(solution)/shard_map/ppermute | solution.py:392
  12.7 0.4 %complete.1 = f32[16,128]{1,0:T(8,128)S(1)} custom-call(f32[128,128]{1,0:T(8,128)S(1)} %pad_maximum_fusion.blocks_ref), custom_call_target="tpu_custom_call" | custom-call | tf_op jit(solution)/shard_map/complete/pallas_call | solution.py:478
  13.0 3.4 %collective-permute-start.4 = (f32[16,128]{1,0:T(8,128)S(1)}, f32[16,128]{1,0:T(8,128)S(1)}, u32[]{:S(2)}, u32[]{:S(2)}) collective-permute-start(f32[16,128]{1,0:T(8,128)S(1)} %complete.1), channel_id=1, source_target_pairs={{0,17},{1,16},{2,19},{3,18},{4,21},{5,20},{6,23},{7,22},{8,25},{9,... | collective-permute-start | bytes 24584 | tf_op jit(solution)/shard_map/ppermute | solution.py:392
  16.4 1.4 %collective-permute-done.4 = f32[16,128]{1,0:T(8,128)S(1)} collective-permute-done((f32[16,128]{1,0:T(8,128)S(1)}, f32[16,128]{1,0:T(8,128)S(1)}, u32[]{:S(2)}, u32[]{:S(2)}) %collective-permute-start.4) | collective-permute-done | bytes 8224 | tf_op jit(solution)/shard_map/ppermute | solution.py:392
  17.8 1.6 %collective-permute-start.5 = (f32[32,128]{1,0:T(8,128)S(1)}, f32[32,128]{1,0:T(8,128)S(1)}, u32[]{:S(2)}, u32[]{:S(2)}) collective-permute-start(f32[32,128]{1,0:T(8,128)S(1)} %pad_maximum_fusion.2.refs_0_), channel_id=1, source_target_pairs={{0,9},{1,4},{2,11},{3,6},{4,13},{5,0},{6,15},{7,2},{8,1},{9,12},{1... | collective-permute-start | bytes 49160 | tf_op jit(solution)/shard_map/ppermute | solution.py:430
  19.4 1.4 %collective-permute-start.6 = (f32[32,128]{1,0:T(8,128)S(1)}, f32[32,128]{1,0:T(8,128)S(1)}, u32[]{:S(2)}, u32[]{:S(2)}) collective-permute-start(f32[32,128]{1,0:T(8,128)S(1)} %pad_maximum_fusion.2.refs_0_), channel_id=1, source_target_pairs={{0,13},{1,12},{2,15},{3,14},{4,9},{5,8},{6,11},{7,10},{8,5},{9,4},... | collective-permute-start | bytes 49160 | tf_op jit(solution)/shard_map/ppermute | solution.py:392
  20.8 0.2 collective-permute-done.5.refs_1_
  20.9 0.3 %collective-permute-start.7 = (f32[32,128]{1,0:T(8,128)S(1)}, f32[32,128]{1,0:T(8,128)S(1)}, u32[]{:S(2)}, u32[]{:S(2)}) collective-permute-start(f32[32,128]{1,0:T(8,128)S(1)} %collective-permute-done.5.refs_1_), channel_id=1, source_target_pairs={{0,1},{1,0},{2,3},{3,2},{4,5},{5,4},{6,7},{7,6},{8,9},{9,8},{10,11... | collective-permute-start | bytes 49160 | tf_op jit(solution)/shard_map/ppermute | solution.py:392
  21.2 0.9 %forecast.1 = (bf16[192,1024]{1,0:T(8,128)(2,1)S(1)}, f32[8,128]{1,0:T(8,128)S(1)}) custom-call(f32[512,128]{1,0:T(8,128)S(1)} %get-tuple-element.16.field_ref, f32[3,8,128]{2,1,0:T(8,128)S(1)} %get-tuple-element.17.flow_ref, f32[136,128]{1,0:T(8,128)S(1)} %collective-permute-done.odd_ref, f32[136,128]{1,0:T(8,128)S(1)} %collective-permute-done.1.even_ref, ...), custom_call_target="tpu_custom_call" | custom-call | flops 4000000 | bytes 600000 | tf_op jit(solution)/shard_map/forecast/pallas_call | solution.py:485
  22.1 1.3 %collective-permute-done.6.refs_2_ = f32[32,128]{1,0:T(8,128)S(1)} collective-permute-done((f32[32,128]{1,0:T(8,128)S(1)}, f32[32,128]{1,0:T(8,128)S(1)}, u32[]{:S(2)}, u32[]{:S(2)}) %collective-permute-start.6) | collective-permute-done | bytes 16416 | tf_op jit(solution)/shard_map/ppermute | solution.py:392
  23.4 0.0 collective-permute-done.7.refs_3_
  23.4 2.3 %analyse.1 = f32[512,128]{1,0:T(8,128)} custom-call(bf16[192,1024]{1,0:T(8,128)(2,1)S(1)} %get-tuple-element.23.f_ref, f32[8,128]{1,0:T(8,128)S(1)} %get-tuple-element.24.mean_ref, f32[32,128]{1,0:T(8,128)S(1)} %pad_maximum_fusion.2.refs_0_, f32[32,128]{1,0:T(8,128)S(1)} %collective-permute-done.5.refs_1_, f32[32,128]{1,0:T(8,128)S(1)} %collective-permute-done.6.refs_2_, ...), custom_call_target="tpu_custom_call" | custom-call | tf_op jit(solution)/shard_map/analyse/pallas_call | solution.py:495
  (3 shorter events, 0.0 us)
Async XLA Ops:
  0.9 6.6 %collective-permute-start = (f32[136,128]{1,0:T(8,128)S(1)}, f32[136,128]{1,0:T(8,128)S(1)}, u32[]{:S(2)}, u32[]{:S(2)}) collective-permute-start(f32[136,128]{1,0:T(8,128)S(1)} %get-tuple-element.18), channel_id=1, source_target_pairs={{0,1},{1,0},{2,3},{3,2},{4,8},{5,9},{6,10},{7,11},{8,4},{9,5},{10,... | collective-permute-start | bytes 208904 | tf_op jit(solution)/shard_map/ppermute | solution.py:382
  1.4 6.3 %collective-permute-start.1 = (f32[136,128]{1,0:T(8,128)S(1)}, f32[136,128]{1,0:T(8,128)S(1)}, u32[]{:S(2)}, u32[]{:S(2)}) collective-permute-start(f32[136,128]{1,0:T(8,128)S(1)} %get-tuple-element.15.sent_ref), channel_id=1, source_target_pairs={{0,4},{1,5},{2,6},{3,7},{4,0},{5,1},{6,2},{7,3},{8,12},{9,13},{10,... | collective-permute-start | bytes 208904 | tf_op jit(solution)/shard_map/ppermute | solution.py:382
  8.1 3.3 %collective-permute-start.2 = (f32[32,128]{1,0:T(8,128)S(1)}, f32[32,128]{1,0:T(8,128)S(1)}, u32[]{:S(2)}, u32[]{:S(2)}) collective-permute-start(f32[32,128]{1,0:T(8,128)S(1)} %observe.1), channel_id=1, source_target_pairs={{0,3},{1,2},{2,1},{3,0},{4,7},{5,6},{6,5},{7,4},{8,11},{9,10},{10,... | collective-permute-start | bytes 49160 | tf_op jit(solution)/shard_map/ppermute | solution.py:392
  11.4 1.2 %collective-permute-start.3 = (f32[64,128]{1,0:T(8,128)S(1)}, f32[64,128]{1,0:T(8,128)S(1)}, u32[]{:S(2)}, u32[]{:S(2)}) collective-permute-start(f32[64,128]{1,0:T(8,128)S(1)} %pad_maximum_fusion.1), channel_id=1, source_target_pairs={{0,1},{1,0},{2,3},{3,2},{4,5},{5,4},{6,7},{7,6},{8,9},{9,8},{10,11... | collective-permute-start | bytes 98312 | tf_op jit(solution)/shard_map/ppermute | solution.py:392
  13.0 4.7 %collective-permute-start.4 = (f32[16,128]{1,0:T(8,128)S(1)}, f32[16,128]{1,0:T(8,128)S(1)}, u32[]{:S(2)}, u32[]{:S(2)}) collective-permute-start(f32[16,128]{1,0:T(8,128)S(1)} %complete.1), channel_id=1, source_target_pairs={{0,17},{1,16},{2,19},{3,18},{4,21},{5,20},{6,23},{7,22},{8,25},{9,... | collective-permute-start | bytes 24584 | tf_op jit(solution)/shard_map/ppermute | solution.py:392
  17.8 3.2 %collective-permute-start.5 = (f32[32,128]{1,0:T(8,128)S(1)}, f32[32,128]{1,0:T(8,128)S(1)}, u32[]{:S(2)}, u32[]{:S(2)}) collective-permute-start(f32[32,128]{1,0:T(8,128)S(1)} %pad_maximum_fusion.2.refs_0_), channel_id=1, source_target_pairs={{0,9},{1,4},{2,11},{3,6},{4,13},{5,0},{6,15},{7,2},{8,1},{9,12},{1... | collective-permute-start | bytes 49160 | tf_op jit(solution)/shard_map/ppermute | solution.py:430
  19.4 4.1 %collective-permute-start.6 = (f32[32,128]{1,0:T(8,128)S(1)}, f32[32,128]{1,0:T(8,128)S(1)}, u32[]{:S(2)}, u32[]{:S(2)}) collective-permute-start(f32[32,128]{1,0:T(8,128)S(1)} %pad_maximum_fusion.2.refs_0_), channel_id=1, source_target_pairs={{0,13},{1,12},{2,15},{3,14},{4,9},{5,8},{6,11},{7,10},{8,5},{9,4},... | collective-permute-start | bytes 49160 | tf_op jit(solution)/shard_map/ppermute | solution.py:392
  20.9 2.5 %collective-permute-start.7 = (f32[32,128]{1,0:T(8,128)S(1)}, f32[32,128]{1,0:T(8,128)S(1)}, u32[]{:S(2)}, u32[]{:S(2)}) collective-permute-start(f32[32,128]{1,0:T(8,128)S(1)} %collective-permute-done.5.refs_1_), channel_id=1, source_target_pairs={{0,1},{1,0},{2,3},{3,2},{4,5},{5,4},{6,7},{7,6},{8,9},{9,8},{10,11... | collective-permute-start | bytes 49160 | tf_op jit(solution)/shard_map/ppermute | solution.py:392

commit v15 on v14

--- a/solution.py
+++ b/solution.py
@@ -26,8 +26,9 @@
 
 
 EDGE = 16
-BLOCK = EDGE + 16
-MID, OBS = EDGE, EDGE + 8
+BLOCK = 24
+MID, OBS = 8, 16
+FORECAST = 4
 VALUE, FACTOR, TO_WEST, TO_EAST, WEIGHTS = 64, 65, 66, 67, 72
 HBM = pl.BlockSpec(memory_space=pltpu.HBM)
 ANY = pl.BlockSpec(memory_space=pl.ANY)
@@ -133,28 +134,27 @@
     second = jnp.zeros((members, 128), F32)
     for r, x in enumerate(field):
         packed = jnp.where(wide == r, shifted(x, r), packed)
-        packed = jnp.where(wide == EDGE + r, shifted(x, EDGE + r - 127), packed)
+        packed = jnp.where(wide == 8 + r, shifted(x, 8 + r - 127), packed)
         second = jnp.where(wide == r, shifted(x, r - 1), second)
-        second = jnp.where(wide == EDGE + r, shifted(x, EDGE + r - 126), second)
+        second = jnp.where(wide == 8 + r, shifted(x, 8 + r - 126), second)
 
     def edge_row(low, high):
-        both = jnp.where(lane == sub, low[:, 0:1], jnp.where(lane == sub + EDGE, high[:, 127:128], 0.0))
+        both = jnp.where(lane == sub, low[:, 0:1], jnp.where(lane == sub + 8, high[:, 127:128], 0.0))
         return jnp.sum(both, axis=0, keepdims=True)
 
     middle = (
         edge_row(own, own) * packed
-        + edge_row(up, up) * shifted(packed, 1)
-        + edge_row(down, down) * shifted(packed, -1)
+        + edge_row(up, up) * jnp.where(wide % 8 == 0, 0.0, shifted(packed, 1))
+        + edge_row(down, down) * jnp.where(wide % 8 == 7, 0.0, shifted(packed, -1))
         + edge_row(right, left) * second
     )
-    packed = jnp.where((wide >= 32) & (wide < 40), shifted(middle, 32), packed)
-    packed = jnp.where((wide >= 40) & (wide < 48), shifted(middle, 24), packed)
+    packed = jnp.where((wide >= 16) & (wide < 32), shifted(middle, 16), packed)
     top_lane, top_sub = lane[:8], sub[:8]
     blocks = []
     for ref, rest in ((value_ref, 0.0), (var_ref, 1.0)):
         block = jnp.full((8, 128), rest, F32)
         for j in range(n_obs):
-            block = jnp.where(top_sub == j, ref[j], block)
+            block = jnp.where(top_sub == FORECAST + j, ref[j], block)
         blocks.append(block)
     meta = jnp.where(top_lane == VALUE, blocks[0], 0.0)
     meta = jnp.where(top_lane == FACTOR, lax.rsqrt(blocks[1]), meta)
@@ -169,14 +169,14 @@
         total = w[0:1, :] * field[0]
         for r in range(1, count):
             total = total + w[r : r + 1, :] * field[r]
-        packed = jnp.where(wide == 48 + j, jnp.sum(total, axis=1, keepdims=True), packed)
+        packed = jnp.where(wide == 32 + FORECAST + j, jnp.sum(total, axis=1, keepdims=True), packed)
         for k, column in ((0, west), (2, east), (4, mid_west), (5, mid_east)):
             meta = jnp.where(top_lane == WEIGHTS + k * n_obs + j, column[:8], meta)
     packed_ref[...] = packed
     meta_ref[0:8, :] = meta
     last = count - 1
     fix = jnp.zeros((8, 128), F32)
-    for at, c, r, col in ((32, up, 0, 0), (40, up, 0, 127), (32 + last, down, last, 0), (40 + last, down, last, 127)):
+    for at, c, r, col in ((16, up, 0, 0), (24, up, 0, 127), (16 + last, down, last, 0), (24 + last, down, last, 127)):
         fix = jnp.where(top_lane == at, c[r : r + 1, col : col + 1], fix)
     meta_ref[8:16, :] = fix
 
@@ -197,41 +197,41 @@
     rows = {-2: north[1], -1: north[0], count: south[0], count + 1: south[1]}
     tile_rows = {r: field_ref[r * members : (r + 1) * members, :] for r in (0, count - 1)}
     packed, meta, fix = packed_ref[...], meta_ref[0:8, :], meta_ref[8:9, :]
-    for x, slot, at in ((rows[-1], EDGE - 1, 0), (rows[count], count, count - 1)):
-        packed = jnp.where(wide == slot, shifted(x, slot), packed)
-        packed = jnp.where(wide == EDGE + slot, shifted(x, EDGE + slot - 127), packed)
-        moved = jnp.where(wide == 32 + at, shifted(x, 32 + at), 0.0)
-        moved = jnp.where(wide == 40 + at, shifted(x, 40 + at - 127), moved)
+    for x, to, at in ((rows[-1], 34, 0), (rows[count], 32, count - 1)):
+        packed = jnp.where(wide == to, shifted(x, to), packed)
+        packed = jnp.where(wide == to + 1, shifted(x, to + 1 - 127), packed)
+        moved = jnp.where(wide == 16 + at, shifted(x, 16 + at), 0.0)
+        moved = jnp.where(wide == 24 + at, shifted(x, 24 + at - 127), moved)
         packed = packed + fix * moved
-    top_lane = lane[:8]
+    top_lane, top_sub = lane[:8], sub[:8]
     for j in range(n_obs):
         w, west, east = spread(weight_ref[j], coeffs, lane)
         all_w = w + rest_ref[j]
         total = sum(all_w[r % EDGE : r % EDGE + 1, :] * x for r, x in rows.items())
         total += sum(w[r : r + 1, :] * x for r, x in tile_rows.items())
-        packed = jnp.where(wide == 48 + j, packed + jnp.sum(total, axis=1, keepdims=True), packed)
-        for k, column in ((1, west), (3, east)):
-            meta = jnp.where(top_lane == WEIGHTS + k * n_obs + j, column[8:], meta)
+        packed = jnp.where(wide == 32 + FORECAST + j, packed + jnp.sum(total, axis=1, keepdims=True), packed)
+        outer = jnp.zeros((8, 128), F32)
+        for at, column, slot in ((0, east, count), (1, west, count), (2, east, EDGE - 1), (3, west, EDGE - 1)):
+            outer = jnp.where(top_sub == at, column[slot : slot + 1], outer)
+        meta = jnp.where(top_lane == WEIGHTS + n_obs + j, outer, meta)
     turned = jnp.concatenate([packed, jnp.zeros((128 - members, 128), F32)], axis=0).T
-    out_ref[0:EDGE, :] = turned[0:EDGE] + shifted(turned[EDGE : 2 * EDGE], 64)
-    out_ref[MID : MID + 8, :] = turned[32:40] + shifted(turned[40:48], 64)
-    out_ref[OBS : OBS + 8, :] = turned[48:56] + meta
-
-
-def block_rows(ref, start, tile, size, rows):
-    return ref[pl.ds(pl.multiple_of(place_of(tile, size) * BLOCK + start, 8), rows), :]
+    out_ref[0:8, :] = turned[0:8] + shifted(turned[8:16], 64)
+    out_ref[MID : MID + 8, :] = turned[16:24] + shifted(turned[24:32], 64)
+    out_ref[OBS : OBS + 8, :] = turned[32:40] + meta
+
+
+def block_rows(ref, start, tile, size):
+    return ref[pl.ds(pl.multiple_of(place_of(tile, size) * BLOCK + start, 8), 8), :]
 
 
 def side_columns(ref, tile, size):
     west, east = jnp.maximum(tile - 1, 0), jnp.minimum(tile + 1, size - 1)
-    own = block_rows(ref, 0, tile, size, EDGE)
-    west_x = shifted(block_rows(ref, 0, west, size, EDGE), 64)
-    east_x = block_rows(ref, 0, east, size, EDGE)
-    west_mid = shifted(block_rows(ref, MID, west, size, 8), 64)
-    west_mid += block_rows(ref, OBS, west, size, 8)[:, TO_EAST : TO_EAST + 1] * own[:8]
-    east_mid = block_rows(ref, MID, east, size, 8)
-    east_mid += block_rows(ref, OBS, east, size, 8)[:, TO_WEST : TO_WEST + 1] * shifted(own[:8], 64)
-    return west_x, east_x, west_mid, east_mid
+    own = block_rows(ref, 0, tile, size)
+    rest = block_rows(ref, OBS, west, size), block_rows(ref, OBS, east, size)
+    columns = shifted(block_rows(ref, 0, west, size), 64), block_rows(ref, 0, east, size)
+    west_mid = shifted(block_rows(ref, MID, west, size), 64) + rest[0][:, TO_EAST : TO_EAST + 1] * own
+    east_mid = block_rows(ref, MID, east, size) + rest[1][:, TO_WEST : TO_WEST + 1] * shifted(own, 64)
+    return columns, (west_mid, east_mid), rest
 
 
 def complete(members, n_obs, size, blocks_ref, out_ref):
@@ -239,22 +239,24 @@
     lane, sub = lanes((rows, 128)), rows_of((rows, 128))
     at = own = jnp.zeros((rows, 128), F32)
     for tile in range(size):
-        west, east, west_mid, east_mid = side_columns(blocks_ref, jnp.int32(tile), size)
-        block = block_rows(blocks_ref, OBS, jnp.int32(tile), size, 8)
-        terms = []
+        columns, mids, rest = side_columns(blocks_ref, jnp.int32(tile), size)
+        block = block_rows(blocks_ref, OBS, jnp.int32(tile), size)
+        odd = rows_of((8, 128)) % 2 == 1
+        terms = [(1, jnp.where(odd, *rest) if 0 < tile < size - 1 else rest[tile == 0])]
         if tile > 0:
-            terms += [(0, west[:8]), (1, west[8:]), (4, west_mid)]
+            terms += [(0, columns[0]), (4, mids[0])]
         if tile < size - 1:
-            terms += [(2, east[:8]), (3, east[8:]), (5, east_mid)]
+            terms += [(2, columns[1]), (5, mids[1])]
         for j in range(n_obs):
             total = jnp.zeros((8, 128), F32)
             for k, term in terms:
                 place = WEIGHTS + k * n_obs + j
                 total = total + block[:, place : place + 1] * term
-            row = jnp.sum(total, axis=0, keepdims=True) + block[j : j + 1, :]
+            observed = block[FORECAST + j : FORECAST + j + 1, :]
+            row = jnp.sum(total, axis=0, keepdims=True) + observed
             here = sub == n_obs * tile + j
             at = jnp.where(here, row, at)
-            own = jnp.where(here, block[j : j + 1, :], own)
+            own = jnp.where(here, observed, own)
     at = jnp.where(lane < members, at, 0.0)
     mean = jnp.sum(at, axis=1, keepdims=True) * (1.0 / members)
     raw = jnp.where(lane < members, at - mean, jnp.where(lane == members, own[:, VALUE : VALUE + 1] - mean, 0.0))
@@ -264,10 +266,9 @@
 def forecast(members, count, size, field_ref, flow_ref, odd_ref, even_ref, blocks_ref, out_ref, mean_ref, tall_ref):
     north, south = halo_rows(even_ref, odd_ref, members)
     tile = lax.axis_index("gx")
-    west, east, west_mid, east_mid = side_columns(blocks_ref, tile, size)
-    has_west, has_east = tile > 0, tile < size - 1
-    sides = [jnp.where(has_west, west, 0.0), jnp.where(has_east, east, 0.0)]
-    sides += [jnp.where(has_west, west_mid, 0.0), jnp.where(has_east, east_mid, 0.0), jnp.zeros((80, 128), F32)]
+    inside = tile > 0, tile < size - 1
+    sides = [jnp.where(here, x, 0.0) for pair in side_columns(blocks_ref, tile, size) for here, x in zip(inside, pair)]
+    sides.append(jnp.zeros((80, 128), F32))
     sides = jnp.concatenate(sides, axis=0).T[:members]
     field = tall_field(field_ref, north, south, members, count)
     tall = tall_coefficients(tall_ref, flow_ref, north[2], south[2], count)
@@ -279,9 +280,10 @@
         at = r % EDGE
         return combine([c[at : at + 1, :] for c in tall], rows[r], rows[r - 1], rows[r + 1], w, e)
 
-    middle = {r: step(field, r, r % EDGE, EDGE + r % EDGE) for r in range(-1, count + 1)}
+    middle = {r: step(field, r, r, 8 + r) for r in range(count)}
+    middle.update({-1: step(field, -1, 35, 42), count: step(field, count, 33, 40)})
     for r in range(count):
-        x = step(middle, r, 2 * EDGE + r, 2 * EDGE + 8 + r)
+        x = step(middle, r, 16 + r, 24 + r)
         mean = jnp.sum(x, axis=0, keepdims=True) * (1.0 / members)
         mean_ref[r : r + 1, :] = mean
         x = x - mean

time: 26 us -> 25.8 us (level)
  no operation moved by 1% of the time
where the time goes in v15:
time: 25.8 us; the launch traced here: 25.6 us
  starting transfers between devices  12 us (47%)
  Pallas kernels  6.79 us (26%)
  waiting for transfers between devices  6.75 us (26%)
    ppermute x5, waiting for transfers between devices, partner(): return lax.ppermute(x, ('gy', 'gx'), pairs)  6.35 us
    ppermute x5, starting transfers between devices, partner(): return lax.ppermute(x, ('gy', 'gx'), pairs)  5.82 us
    ppermute x2, starting transfers between devices, swap(): return lax.ppermute(x, ('gy', 'gx'), pairs)  4.55 us
    pallas_call x1, Pallas kernels, body(): call(functools.partial(analyse, members, count), out_shape=shape(members...  2.31 us
    pallas_call x1, Pallas kernels, body(): call(functools.partial(prepare, members, count, n_obs), out_shape=[shape(...  2.01 us
    ppermute x1, starting transfers between devices, all_rows(): near = lax.ppermute(packet, ('gy', 'gx'), pairs)  1.6 us
    pallas_call x1, Pallas kernels, body(): call(functools.partial(load, members, count), out_shape=[shape(2 * member...  0.88 us
    pallas_call x1, Pallas kernels, body(): call(functools.partial(forecast, members, count, size), out_shape=[jax.Sh...  0.83 us
  transfers between devices with their start and end apart: 8, of which 6 were waited for; matrix products, arithmetic and copies ran while one was open for 0% of the time, Pallas kernels for 11%

profile of v15, /device:TPU:0, one launch (start us, length us, event | category | flops | bytes accessed | tf_op | source)
XLA Modules:
  0.0 25.6 jit_solution(2309682149948379849)
XLA Ops:
  0.0 0.9 %load.1 = (f32[136,128]{1,0:T(8,128)S(1)}, f32[136,128]{1,0:T(8,128)S(1)}) custom-call(f32[64,8,128]{2,1,0:T(8,128)} %ens_hbm.3, f32[3,8,128]{2,1,0:T(8,128)} %flow_hbm.3), custom_call_target="tpu_custom_call" | custom-call | tf_op jit(solution)/shard_map/load/pallas_call | solution.py:449
  0.9 0.5 %collective-permute-start = (f32[136,128]{1,0:T(8,128)S(1)}, f32[136,128]{1,0:T(8,128)S(1)}, u32[]{:S(2)}, u32[]{:S(2)}) collective-permute-start(f32[136,128]{1,0:T(8,128)S(1)} %get-tuple-element.18), channel_id=1, source_target_pairs={{0,1},{1,0},{2,3},{3,2},{4,8},{5,9},{6,10},{7,11},{8,4},{9,5},{10,... | collective-permute-start | bytes 208904 | tf_op jit(solution)/shard_map/ppermute | solution.py:384
  1.4 4.0 %collective-permute-start.1 = (f32[136,128]{1,0:T(8,128)S(1)}, f32[136,128]{1,0:T(8,128)S(1)}, u32[]{:S(2)}, u32[]{:S(2)}) collective-permute-start(f32[136,128]{1,0:T(8,128)S(1)} %get-tuple-element.15.sent_ref), channel_id=1, source_target_pairs={{0,4},{1,5},{2,6},{3,7},{4,0},{5,1},{6,2},{7,3},{8,12},{9,13},{10,... | collective-permute-start | bytes 208904 | tf_op jit(solution)/shard_map/ppermute | solution.py:384
  5.4 2.0 %prepare.1 = (f32[512,128]{1,0:T(8,128)S(1)}, f32[3,8,128]{2,1,0:T(8,128)S(1)}, f32[64,128]{1,0:T(8,128)S(1)}, f32[16,128]{1,0:T(8,128)S(1)}, f32[4,16,128]{2,1,0:T(8,128)S(1)}, /*index=5*/f32[4,16,128]{2,1,0:T(8,128)S(1)}) custom-call(f32[64,8,128]{2,1,0:T(8,128)} %ens_hbm.3, f32[3,8,128]{2,1,0:T(8,128)} %flow_hbm.3, s32[4]{0:T(128)} %bitcast.4, f32[4]{0:T(128)} %bitcast.5, ...), custom_call_target="tpu_custom_call" | custom-call | flops 4000000 | bytes 600000 | tf_op jit(solution)/shard_map/prepare/pallas_call | solution.py:458
  7.5 0.0 collective-permute-done.odd_ref
  7.5 0.3 collective-permute-done.1.even_ref
  7.7 0.4 %observe.1 = f32[24,128]{1,0:T(8,128)S(1)} custom-call(f32[512,128]{1,0:T(8,128)S(1)} %get-tuple-element.16.field_ref, f32[3,8,128]{2,1,0:T(8,128)S(1)} %get-tuple-element.17.flow_ref, f32[64,128]{1,0:T(8,128)S(1)} %get-tuple-element.19.packed_ref, f32[16,128]{1,0:T(8,128)S(1)} %get-tuple-element.20.meta_ref, ...), custom_call_target="tpu_custom_call" | custom-call | tf_op jit(solution)/shard_map/observe/pallas_call | solution.py:471
  8.1 0.6 %collective-permute-start.2 = (f32[24,128]{1,0:T(8,128)S(1)}, f32[24,128]{1,0:T(8,128)S(1)}, u32[]{:S(2)}, u32[]{:S(2)}) collective-permute-start(f32[24,128]{1,0:T(8,128)S(1)} %observe.1), channel_id=1, source_target_pairs={{0,3},{1,2},{2,1},{3,0},{4,7},{5,6},{6,5},{7,4},{8,11},{9,10},{10,... | collective-permute-start | bytes 36872 | tf_op jit(solution)/shard_map/ppermute | solution.py:394
  8.7 2.6 %collective-permute-done.2 = f32[24,128]{1,0:T(8,128)S(1)} collective-permute-done((f32[24,128]{1,0:T(8,128)S(1)}, f32[24,128]{1,0:T(8,128)S(1)}, u32[]{:S(2)}, u32[]{:S(2)}) %collective-permute-start.2) | collective-permute-done | bytes 12320 | tf_op jit(solution)/shard_map/ppermute | solution.py:394
  11.3 0.1 collective-permute-start.3
  11.4 1.1 %collective-permute-done.3 = f32[48,128]{1,0:T(8,128)S(1)} collective-permute-done((f32[48,128]{1,0:T(8,128)S(1)}, f32[48,128]{1,0:T(8,128)S(1)}, u32[]{:S(2)}, u32[]{:S(2)}) %collective-permute-start.3) | collective-permute-done | bytes 24608 | tf_op jit(solution)/shard_map/ppermute | solution.py:394
  12.5 0.4 %complete.1 = f32[16,128]{1,0:T(8,128)S(1)} custom-call(f32[96,128]{1,0:T(8,128)S(1)} %pad_maximum_fusion.blocks_ref), custom_call_target="tpu_custom_call" | custom-call | tf_op jit(solution)/shard_map/complete/pallas_call | solution.py:480
  12.9 3.3 %collective-permute-start.4 = (f32[16,128]{1,0:T(8,128)S(1)}, f32[16,128]{1,0:T(8,128)S(1)}, u32[]{:S(2)}, u32[]{:S(2)}) collective-permute-start(f32[16,128]{1,0:T(8,128)S(1)} %complete.1), channel_id=1, source_target_pairs={{0,17},{1,16},{2,19},{3,18},{4,21},{5,20},{6,23},{7,22},{8,25},{9,... | collective-permute-start | bytes 24584 | tf_op jit(solution)/shard_map/ppermute | solution.py:394
  16.2 1.4 %collective-permute-done.4 = f32[16,128]{1,0:T(8,128)S(1)} collective-permute-done((f32[16,128]{1,0:T(8,128)S(1)}, f32[16,128]{1,0:T(8,128)S(1)}, u32[]{:S(2)}, u32[]{:S(2)}) %collective-permute-start.4) | collective-permute-done | bytes 8224 | tf_op jit(solution)/shard_map/ppermute | solution.py:394
  17.6 1.6 %collective-permute-start.5 = (f32[32,128]{1,0:T(8,128)S(1)}, f32[32,128]{1,0:T(8,128)S(1)}, u32[]{:S(2)}, u32[]{:S(2)}) collective-permute-start(f32[32,128]{1,0:T(8,128)S(1)} %pad_maximum_fusion.2.refs_0_), channel_id=1, source_target_pairs={{0,9},{1,4},{2,11},{3,6},{4,13},{5,0},{6,15},{7,2},{8,1},{9,12},{1... | collective-permute-start | bytes 49160 | tf_op jit(solution)/shard_map/ppermute | solution.py:432
  19.2 1.4 %collective-permute-start.6 = (f32[32,128]{1,0:T(8,128)S(1)}, f32[32,128]{1,0:T(8,128)S(1)}, u32[]{:S(2)}, u32[]{:S(2)}) collective-permute-start(f32[32,128]{1,0:T(8,128)S(1)} %pad_maximum_fusion.2.refs_0_), channel_id=1, source_target_pairs={{0,13},{1,12},{2,15},{3,14},{4,9},{5,8},{6,11},{7,10},{8,5},{9,4},... | collective-permute-start | bytes 49160 | tf_op jit(solution)/shard_map/ppermute | solution.py:394
  20.6 0.1 collective-permute-done.5.refs_1_
  20.7 0.3 %collective-permute-start.7 = (f32[32,128]{1,0:T(8,128)S(1)}, f32[32,128]{1,0:T(8,128)S(1)}, u32[]{:S(2)}, u32[]{:S(2)}) collective-permute-start(f32[32,128]{1,0:T(8,128)S(1)} %collective-permute-done.5.refs_1_), channel_id=1, source_target_pairs={{0,1},{1,0},{2,3},{3,2},{4,5},{5,4},{6,7},{7,6},{8,9},{9,8},{10,11... | collective-permute-start | bytes 49160 | tf_op jit(solution)/shard_map/ppermute | solution.py:394
  21.1 0.8 %forecast.1 = (bf16[192,1024]{1,0:T(8,128)(2,1)S(1)}, f32[8,128]{1,0:T(8,128)S(1)}) custom-call(f32[512,128]{1,0:T(8,128)S(1)} %get-tuple-element.16.field_ref, f32[3,8,128]{2,1,0:T(8,128)S(1)} %get-tuple-element.17.flow_ref, f32[136,128]{1,0:T(8,128)S(1)} %collective-permute-done.odd_ref, f32[136,128]{1,0:T(8,128)S(1)} %collective-permute-done.1.even_ref, ...), custom_call_target="tpu_custom_call" | custom-call | flops 4000000 | bytes 600000 | tf_op jit(solution)/shard_map/forecast/pallas_call | solution.py:487
  21.9 1.3 %collective-permute-done.6.refs_2_ = f32[32,128]{1,0:T(8,128)S(1)} collective-permute-done((f32[32,128]{1,0:T(8,128)S(1)}, f32[32,128]{1,0:T(8,128)S(1)}, u32[]{:S(2)}, u32[]{:S(2)}) %collective-permute-start.6) | collective-permute-done | bytes 16416 | tf_op jit(solution)/shard_map/ppermute | solution.py:394
  23.2 0.0 collective-permute-done.7.refs_3_
  23.2 2.3 %analyse.1 = f32[512,128]{1,0:T(8,128)} custom-call(bf16[192,1024]{1,0:T(8,128)(2,1)S(1)} %get-tuple-element.23.f_ref, f32[8,128]{1,0:T(8,128)S(1)} %get-tuple-element.24.mean_ref, f32[32,128]{1,0:T(8,128)S(1)} %pad_maximum_fusion.2.refs_0_, f32[32,128]{1,0:T(8,128)S(1)} %collective-permute-done.5.refs_1_, f32[32,128]{1,0:T(8,128)S(1)} %collective-permute-done.6.refs_2_, ...), custom_call_target="tpu_custom_call" | custom-call | tf_op jit(solution)/shard_map/analyse/pallas_call | solution.py:497
  (3 shorter events, 0.0 us)
Async XLA Ops:
  0.9 6.6 %collective-permute-start = (f32[136,128]{1,0:T(8,128)S(1)}, f32[136,128]{1,0:T(8,128)S(1)}, u32[]{:S(2)}, u32[]{:S(2)}) collective-permute-start(f32[136,128]{1,0:T(8,128)S(1)} %get-tuple-element.18), channel_id=1, source_target_pairs={{0,1},{1,0},{2,3},{3,2},{4,8},{5,9},{6,10},{7,11},{8,4},{9,5},{10,... | collective-permute-start | bytes 208904 | tf_op jit(solution)/shard_map/ppermute | solution.py:384
  1.4 6.3 %collective-permute-start.1 = (f32[136,128]{1,0:T(8,128)S(1)}, f32[136,128]{1,0:T(8,128)S(1)}, u32[]{:S(2)}, u32[]{:S(2)}) collective-permute-start(f32[136,128]{1,0:T(8,128)S(1)} %get-tuple-element.15.sent_ref), channel_id=1, source_target_pairs={{0,4},{1,5},{2,6},{3,7},{4,0},{5,1},{6,2},{7,3},{8,12},{9,13},{10,... | collective-permute-start | bytes 208904 | tf_op jit(solution)/shard_map/ppermute | solution.py:384
  8.1 3.2 %collective-permute-start.2 = (f32[24,128]{1,0:T(8,128)S(1)}, f32[24,128]{1,0:T(8,128)S(1)}, u32[]{:S(2)}, u32[]{:S(2)}) collective-permute-start(f32[24,128]{1,0:T(8,128)S(1)} %observe.1), channel_id=1, source_target_pairs={{0,3},{1,2},{2,1},{3,0},{4,7},{5,6},{6,5},{7,4},{8,11},{9,10},{10,... | collective-permute-start | bytes 36872 | tf_op jit(solution)/shard_map/ppermute | solution.py:394
  11.3 1.2 %collective-permute-start.3 = (f32[48,128]{1,0:T(8,128)S(1)}, f32[48,128]{1,0:T(8,128)S(1)}, u32[]{:S(2)}, u32[]{:S(2)}) collective-permute-start(f32[48,128]{1,0:T(8,128)S(1)} %pad_maximum_fusion.1), channel_id=1, source_target_pairs={{0,1},{1,0},{2,3},{3,2},{4,5},{5,4},{6,7},{7,6},{8,9},{9,8},{10,11... | collective-permute-start | bytes 73736 | tf_op jit(solution)/shard_map/ppermute | solution.py:394
  12.9 4.7 %collective-permute-start.4 = (f32[16,128]{1,0:T(8,128)S(1)}, f32[16,128]{1,0:T(8,128)S(1)}, u32[]{:S(2)}, u32[]{:S(2)}) collective-permute-start(f32[16,128]{1,0:T(8,128)S(1)} %complete.1), channel_id=1, source_target_pairs={{0,17},{1,16},{2,19},{3,18},{4,21},{5,20},{6,23},{7,22},{8,25},{9,... | collective-permute-start | bytes 24584 | tf_op jit(solution)/shard_map/ppermute | solution.py:394
  17.6 3.2 %collective-permute-start.5 = (f32[32,128]{1,0:T(8,128)S(1)}, f32[32,128]{1,0:T(8,128)S(1)}, u32[]{:S(2)}, u32[]{:S(2)}) collective-permute-start(f32[32,128]{1,0:T(8,128)S(1)} %pad_maximum_fusion.2.refs_0_), channel_id=1, source_target_pairs={{0,9},{1,4},{2,11},{3,6},{4,13},{5,0},{6,15},{7,2},{8,1},{9,12},{1... | collective-permute-start | bytes 49160 | tf_op jit(solution)/shard_map/ppermute | solution.py:432
  19.2 4.1 %collective-permute-start.6 = (f32[32,128]{1,0:T(8,128)S(1)}, f32[32,128]{1,0:T(8,128)S(1)}, u32[]{:S(2)}, u32[]{:S(2)}) collective-permute-start(f32[32,128]{1,0:T(8,128)S(1)} %pad_maximum_fusion.2.refs_0_), channel_id=1, source_target_pairs={{0,13},{1,12},{2,15},{3,14},{4,9},{5,8},{6,11},{7,10},{8,5},{9,4},... | collective-permute-start | bytes 49160 | tf_op jit(solution)/shard_map/ppermute | solution.py:394
  20.7 2.5 %collective-permute-start.7 = (f32[32,128]{1,0:T(8,128)S(1)}, f32[32,128]{1,0:T(8,128)S(1)}, u32[]{:S(2)}, u32[]{:S(2)}) collective-permute-start(f32[32,128]{1,0:T(8,128)S(1)} %collective-permute-done.5.refs_1_), channel_id=1, source_target_pairs={{0,1},{1,0},{2,3},{3,2},{4,5},{5,4},{6,7},{7,6},{8,9},{9,8},{10,11... | collective-permute-start | bytes 49160 | tf_op jit(solution)/shard_map/ppermute | solution.py:394

commit v16 on v15

--- a/solution.py
+++ b/solution.py
@@ -182,7 +182,7 @@
 
 
 def observe(
-    members, count, n_obs, field_ref, flow_ref, packed_ref, meta_ref, weight_ref, rest_ref, odd_ref, even_ref,
+    members, count, n_obs, field_ref, flow_ref, packed_ref, meta_ref, weight_ref, rest_ref, even_ref, odd_ref,
     out_ref, tall_ref,
 ):
     north, south = halo_rows(even_ref, odd_ref, members)
@@ -475,7 +475,7 @@
         out_specs=VMEM,
         scratch_shapes=[tall],
         name="observe",
-    )(field, tile_flow, *ready, rows_odd, rows_even)
+    )(field, tile_flow, *ready, rows_even, rows_odd)
     blocks = row_blocks(block)
     packet = call(
         functools.partial(complete, members, n_obs, size),

time: 25.8 us -> 25.8 us (level)
  no operation moved by 1% of the time
where the time goes in v16:
time: 25.8 us; the launch traced here: 25.6 us
  starting transfers between devices  12 us (47%)
  Pallas kernels  6.79 us (26%)
  waiting for transfers between devices  6.75 us (26%)
    ppermute x5, waiting for transfers between devices, partner(): return lax.ppermute(x, ('gy', 'gx'), pairs)  6.35 us
    ppermute x5, starting transfers between devices, partner(): return lax.ppermute(x, ('gy', 'gx'), pairs)  5.82 us
    ppermute x2, starting transfers between devices, swap(): return lax.ppermute(x, ('gy', 'gx'), pairs)  4.55 us
    pallas_call x1, Pallas kernels, body(): call(functools.partial(analyse, members, count), out_shape=shape(members...  2.31 us
    pallas_call x1, Pallas kernels, body(): call(functools.partial(prepare, members, count, n_obs), out_shape=[shape(...  2.01 us
    ppermute x1, starting transfers between devices, all_rows(): near = lax.ppermute(packet, ('gy', 'gx'), pairs)  1.6 us
    pallas_call x1, Pallas kernels, body(): call(functools.partial(load, members, count), out_shape=[shape(2 * member...  0.88 us
    pallas_call x1, Pallas kernels, body(): call(functools.partial(forecast, members, count, size), out_shape=[jax.Sh...  0.83 us
  transfers between devices with their start and end apart: 8, of which 6 were waited for; matrix products, arithmetic and copies ran while one was open for 0% of the time, Pallas kernels for 11%

profile of v16, /device:TPU:0, one launch (start us, length us, event | category | flops | bytes accessed | tf_op | source)
XLA Modules:
  0.0 25.6 jit_solution(9150704135468328289)
XLA Ops:
  0.0 0.9 %load.1 = (f32[136,128]{1,0:T(8,128)S(1)}, f32[136,128]{1,0:T(8,128)S(1)}) custom-call(f32[64,8,128]{2,1,0:T(8,128)} %ens_hbm.3, f32[3,8,128]{2,1,0:T(8,128)} %flow_hbm.3), custom_call_target="tpu_custom_call" | custom-call | tf_op jit(solution)/shard_map/load/pallas_call | solution.py:449
  0.9 0.5 %collective-permute-start = (f32[136,128]{1,0:T(8,128)S(1)}, f32[136,128]{1,0:T(8,128)S(1)}, u32[]{:S(2)}, u32[]{:S(2)}) collective-permute-start(f32[136,128]{1,0:T(8,128)S(1)} %get-tuple-element.18), channel_id=1, source_target_pairs={{0,1},{1,0},{2,3},{3,2},{4,8},{5,9},{6,10},{7,11},{8,4},{9,5},{10,... | collective-permute-start | bytes 208904 | tf_op jit(solution)/shard_map/ppermute | solution.py:384
  1.4 4.0 %collective-permute-start.1 = (f32[136,128]{1,0:T(8,128)S(1)}, f32[136,128]{1,0:T(8,128)S(1)}, u32[]{:S(2)}, u32[]{:S(2)}) collective-permute-start(f32[136,128]{1,0:T(8,128)S(1)} %get-tuple-element.15.sent_ref), channel_id=1, source_target_pairs={{0,4},{1,5},{2,6},{3,7},{4,0},{5,1},{6,2},{7,3},{8,12},{9,13},{10,... | collective-permute-start | bytes 208904 | tf_op jit(solution)/shard_map/ppermute | solution.py:384
  5.4 2.0 %prepare.1 = (f32[512,128]{1,0:T(8,128)S(1)}, f32[3,8,128]{2,1,0:T(8,128)S(1)}, f32[64,128]{1,0:T(8,128)S(1)}, f32[16,128]{1,0:T(8,128)S(1)}, f32[4,16,128]{2,1,0:T(8,128)S(1)}, /*index=5*/f32[4,16,128]{2,1,0:T(8,128)S(1)}) custom-call(f32[64,8,128]{2,1,0:T(8,128)} %ens_hbm.3, f32[3,8,128]{2,1,0:T(8,128)} %flow_hbm.3, s32[4]{0:T(128)} %bitcast.4, f32[4]{0:T(128)} %bitcast.5, ...), custom_call_target="tpu_custom_call" | custom-call | flops 4000000 | bytes 600000 | tf_op jit(solution)/shard_map/prepare/pallas_call | solution.py:458
  7.5 0.0 collective-permute-done.odd_ref
  7.5 0.3 collective-permute-done.1.even_ref
  7.7 0.4 %observe.1 = f32[24,128]{1,0:T(8,128)S(1)} custom-call(f32[512,128]{1,0:T(8,128)S(1)} %get-tuple-element.16.field_ref, f32[3,8,128]{2,1,0:T(8,128)S(1)} %get-tuple-element.17.flow_ref, f32[64,128]{1,0:T(8,128)S(1)} %get-tuple-element.19.packed_ref, f32[16,128]{1,0:T(8,128)S(1)} %get-tuple-element.20.meta_ref, ...), custom_call_target="tpu_custom_call" | custom-call | tf_op jit(solution)/shard_map/observe/pallas_call | solution.py:471
  8.1 0.6 %collective-permute-start.2 = (f32[24,128]{1,0:T(8,128)S(1)}, f32[24,128]{1,0:T(8,128)S(1)}, u32[]{:S(2)}, u32[]{:S(2)}) collective-permute-start(f32[24,128]{1,0:T(8,128)S(1)} %observe.1), channel_id=1, source_target_pairs={{0,3},{1,2},{2,1},{3,0},{4,7},{5,6},{6,5},{7,4},{8,11},{9,10},{10,... | collective-permute-start | bytes 36872 | tf_op jit(solution)/shard_map/ppermute | solution.py:394
  8.7 2.6 %collective-permute-done.2 = f32[24,128]{1,0:T(8,128)S(1)} collective-permute-done((f32[24,128]{1,0:T(8,128)S(1)}, f32[24,128]{1,0:T(8,128)S(1)}, u32[]{:S(2)}, u32[]{:S(2)}) %collective-permute-start.2) | collective-permute-done | bytes 12320 | tf_op jit(solution)/shard_map/ppermute | solution.py:394
  11.3 0.1 collective-permute-start.3
  11.4 1.1 %collective-permute-done.3 = f32[48,128]{1,0:T(8,128)S(1)} collective-permute-done((f32[48,128]{1,0:T(8,128)S(1)}, f32[48,128]{1,0:T(8,128)S(1)}, u32[]{:S(2)}, u32[]{:S(2)}) %collective-permute-start.3) | collective-permute-done | bytes 24608 | tf_op jit(solution)/shard_map/ppermute | solution.py:394
  12.5 0.4 %complete.1 = f32[16,128]{1,0:T(8,128)S(1)} custom-call(f32[96,128]{1,0:T(8,128)S(1)} %pad_maximum_fusion.blocks_ref), custom_call_target="tpu_custom_call" | custom-call | tf_op jit(solution)/shard_map/complete/pallas_call | solution.py:480
  12.9 3.3 %collective-permute-start.4 = (f32[16,128]{1,0:T(8,128)S(1)}, f32[16,128]{1,0:T(8,128)S(1)}, u32[]{:S(2)}, u32[]{:S(2)}) collective-permute-start(f32[16,128]{1,0:T(8,128)S(1)} %complete.1), channel_id=1, source_target_pairs={{0,17},{1,16},{2,19},{3,18},{4,21},{5,20},{6,23},{7,22},{8,25},{9,... | collective-permute-start | bytes 24584 | tf_op jit(solution)/shard_map/ppermute | solution.py:394
  16.2 1.4 %collective-permute-done.4 = f32[16,128]{1,0:T(8,128)S(1)} collective-permute-done((f32[16,128]{1,0:T(8,128)S(1)}, f32[16,128]{1,0:T(8,128)S(1)}, u32[]{:S(2)}, u32[]{:S(2)}) %collective-permute-start.4) | collective-permute-done | bytes 8224 | tf_op jit(solution)/shard_map/ppermute | solution.py:394
  17.6 1.6 %collective-permute-start.5 = (f32[32,128]{1,0:T(8,128)S(1)}, f32[32,128]{1,0:T(8,128)S(1)}, u32[]{:S(2)}, u32[]{:S(2)}) collective-permute-start(f32[32,128]{1,0:T(8,128)S(1)} %pad_maximum_fusion.2.refs_0_), channel_id=1, source_target_pairs={{0,9},{1,4},{2,11},{3,6},{4,13},{5,0},{6,15},{7,2},{8,1},{9,12},{1... | collective-permute-start | bytes 49160 | tf_op jit(solution)/shard_map/ppermute | solution.py:432
  19.2 1.4 %collective-permute-start.6 = (f32[32,128]{1,0:T(8,128)S(1)}, f32[32,128]{1,0:T(8,128)S(1)}, u32[]{:S(2)}, u32[]{:S(2)}) collective-permute-start(f32[32,128]{1,0:T(8,128)S(1)} %pad_maximum_fusion.2.refs_0_), channel_id=1, source_target_pairs={{0,13},{1,12},{2,15},{3,14},{4,9},{5,8},{6,11},{7,10},{8,5},{9,4},... | collective-permute-start | bytes 49160 | tf_op jit(solution)/shard_map/ppermute | solution.py:394
  20.6 0.1 collective-permute-done.5.refs_1_
  20.7 0.3 %collective-permute-start.7 = (f32[32,128]{1,0:T(8,128)S(1)}, f32[32,128]{1,0:T(8,128)S(1)}, u32[]{:S(2)}, u32[]{:S(2)}) collective-permute-start(f32[32,128]{1,0:T(8,128)S(1)} %collective-permute-done.5.refs_1_), channel_id=1, source_target_pairs={{0,1},{1,0},{2,3},{3,2},{4,5},{5,4},{6,7},{7,6},{8,9},{9,8},{10,11... | collective-permute-start | bytes 49160 | tf_op jit(solution)/shard_map/ppermute | solution.py:394
  21.1 0.8 %forecast.1 = (bf16[192,1024]{1,0:T(8,128)(2,1)S(1)}, f32[8,128]{1,0:T(8,128)S(1)}) custom-call(f32[512,128]{1,0:T(8,128)S(1)} %get-tuple-element.16.field_ref, f32[3,8,128]{2,1,0:T(8,128)S(1)} %get-tuple-element.17.flow_ref, f32[136,128]{1,0:T(8,128)S(1)} %collective-permute-done.odd_ref, f32[136,128]{1,0:T(8,128)S(1)} %collective-permute-done.1.even_ref, ...), custom_call_target="tpu_custom_call" | custom-call | flops 4000000 | bytes 600000 | tf_op jit(solution)/shard_map/forecast/pallas_call | solution.py:487
  21.9 1.3 %collective-permute-done.6.refs_2_ = f32[32,128]{1,0:T(8,128)S(1)} collective-permute-done((f32[32,128]{1,0:T(8,128)S(1)}, f32[32,128]{1,0:T(8,128)S(1)}, u32[]{:S(2)}, u32[]{:S(2)}) %collective-permute-start.6) | collective-permute-done | bytes 16416 | tf_op jit(solution)/shard_map/ppermute | solution.py:394
  23.2 0.0 collective-permute-done.7.refs_3_
  23.2 2.3 %analyse.1 = f32[512,128]{1,0:T(8,128)} custom-call(bf16[192,1024]{1,0:T(8,128)(2,1)S(1)} %get-tuple-element.23.f_ref, f32[8,128]{1,0:T(8,128)S(1)} %get-tuple-element.24.mean_ref, f32[32,128]{1,0:T(8,128)S(1)} %pad_maximum_fusion.2.refs_0_, f32[32,128]{1,0:T(8,128)S(1)} %collective-permute-done.5.refs_1_, f32[32,128]{1,0:T(8,128)S(1)} %collective-permute-done.6.refs_2_, ...), custom_call_target="tpu_custom_call" | custom-call | tf_op jit(solution)/shard_map/analyse/pallas_call | solution.py:497
  (3 shorter events, 0.0 us)
Async XLA Ops:
  0.9 6.6 %collective-permute-start = (f32[136,128]{1,0:T(8,128)S(1)}, f32[136,128]{1,0:T(8,128)S(1)}, u32[]{:S(2)}, u32[]{:S(2)}) collective-permute-start(f32[136,128]{1,0:T(8,128)S(1)} %get-tuple-element.18), channel_id=1, source_target_pairs={{0,1},{1,0},{2,3},{3,2},{4,8},{5,9},{6,10},{7,11},{8,4},{9,5},{10,... | collective-permute-start | bytes 208904 | tf_op jit(solution)/shard_map/ppermute | solution.py:384
  1.4 6.3 %collective-permute-start.1 = (f32[136,128]{1,0:T(8,128)S(1)}, f32[136,128]{1,0:T(8,128)S(1)}, u32[]{:S(2)}, u32[]{:S(2)}) collective-permute-start(f32[136,128]{1,0:T(8,128)S(1)} %get-tuple-element.15.sent_ref), channel_id=1, source_target_pairs={{0,4},{1,5},{2,6},{3,7},{4,0},{5,1},{6,2},{7,3},{8,12},{9,13},{10,... | collective-permute-start | bytes 208904 | tf_op jit(solution)/shard_map/ppermute | solution.py:384
  8.1 3.2 %collective-permute-start.2 = (f32[24,128]{1,0:T(8,128)S(1)}, f32[24,128]{1,0:T(8,128)S(1)}, u32[]{:S(2)}, u32[]{:S(2)}) collective-permute-start(f32[24,128]{1,0:T(8,128)S(1)} %observe.1), channel_id=1, source_target_pairs={{0,3},{1,2},{2,1},{3,0},{4,7},{5,6},{6,5},{7,4},{8,11},{9,10},{10,... | collective-permute-start | bytes 36872 | tf_op jit(solution)/shard_map/ppermute | solution.py:394
  11.3 1.2 %collective-permute-start.3 = (f32[48,128]{1,0:T(8,128)S(1)}, f32[48,128]{1,0:T(8,128)S(1)}, u32[]{:S(2)}, u32[]{:S(2)}) collective-permute-start(f32[48,128]{1,0:T(8,128)S(1)} %pad_maximum_fusion.1), channel_id=1, source_target_pairs={{0,1},{1,0},{2,3},{3,2},{4,5},{5,4},{6,7},{7,6},{8,9},{9,8},{10,11... | collective-permute-start | bytes 73736 | tf_op jit(solution)/shard_map/ppermute | solution.py:394
  12.9 4.7 %collective-permute-start.4 = (f32[16,128]{1,0:T(8,128)S(1)}, f32[16,128]{1,0:T(8,128)S(1)}, u32[]{:S(2)}, u32[]{:S(2)}) collective-permute-start(f32[16,128]{1,0:T(8,128)S(1)} %complete.1), channel_id=1, source_target_pairs={{0,17},{1,16},{2,19},{3,18},{4,21},{5,20},{6,23},{7,22},{8,25},{9,... | collective-permute-start | bytes 24584 | tf_op jit(solution)/shard_map/ppermute | solution.py:394
  17.6 3.2 %collective-permute-start.5 = (f32[32,128]{1,0:T(8,128)S(1)}, f32[32,128]{1,0:T(8,128)S(1)}, u32[]{:S(2)}, u32[]{:S(2)}) collective-permute-start(f32[32,128]{1,0:T(8,128)S(1)} %pad_maximum_fusion.2.refs_0_), channel_id=1, source_target_pairs={{0,9},{1,4},{2,11},{3,6},{4,13},{5,0},{6,15},{7,2},{8,1},{9,12},{1... | collective-permute-start | bytes 49160 | tf_op jit(solution)/shard_map/ppermute | solution.py:432
  19.2 4.1 %collective-permute-start.6 = (f32[32,128]{1,0:T(8,128)S(1)}, f32[32,128]{1,0:T(8,128)S(1)}, u32[]{:S(2)}, u32[]{:S(2)}) collective-permute-start(f32[32,128]{1,0:T(8,128)S(1)} %pad_maximum_fusion.2.refs_0_), channel_id=1, source_target_pairs={{0,13},{1,12},{2,15},{3,14},{4,9},{5,8},{6,11},{7,10},{8,5},{9,4},... | collective-permute-start | bytes 49160 | tf_op jit(solution)/shard_map/ppermute | solution.py:394
  20.7 2.5 %collective-permute-start.7 = (f32[32,128]{1,0:T(8,128)S(1)}, f32[32,128]{1,0:T(8,128)S(1)}, u32[]{:S(2)}, u32[]{:S(2)}) collective-permute-start(f32[32,128]{1,0:T(8,128)S(1)} %collective-permute-done.5.refs_1_), channel_id=1, source_target_pairs={{0,1},{1,0},{2,3},{3,2},{4,5},{5,4},{6,7},{7,6},{8,9},{9,8},{10,11... | collective-permute-start | bytes 49160 | tf_op jit(solution)/shard_map/ppermute | solution.py:394
